TPU v7x, 32 devices: a whole 2x2x4 slice. The times are simulated.
32 devices in a mesh: section: 2 (over core), dp: 8 (over z, x), seq: 2 (over y).
Axes of the slice: x: 2, y: 2, z: 4, core: 2. Of those that a mesh axis runs over, the one named last changes fastest.
Arguments:
- inputs: bfloat16 [2, 16, 256, 384], P(None, 'dp', 'seq'), may hold values from -6 to 6
- cotangent: bfloat16 [2, 16, 256, 384], P(None, 'dp', 'seq'), may hold values from -6 to 6
- time_ids: int32 [2, 16], replicated, may hold values from 0 to 999
- row_counts: int32 [2, 8], P(None, 'dp'), may hold values from 1 to 2, as said below
- cond_table: bfloat16 [1000, 384], replicated, may hold values from -6 to 6
- modulation_weight: bfloat16 [2, 384, 2304], P('section', ('dp', 'seq')), may hold values from -0.3125 to 0.3125
- attention_weight: bfloat16 [2, 384, 1152], P('section', ('dp', 'seq')), may hold values from -0.3125 to 0.3125
- output_weight: bfloat16 [2, 384, 384], P('section', ('dp', 'seq')), may hold values from -1.25 to 1.25
- expand_weight: bfloat16 [2, 384, 1536], P('section', ('dp', 'seq')), may hold values from -0.3125 to 0.3125
- shrink_weight: bfloat16 [2, 1536, 384], P('section', ('dp', 'seq')), may hold values from -0.15625 to 0.15625
- biases: bfloat16 [2, 5376], P('section', ('dp', 'seq')), may hold values from -1.5 to 1.5
Outputs:
- activations: bfloat16 [2, 2, 16, 256, 384], P('section', None, 'dp', 'seq')
- input_grads: float32 [2, 2, 16, 256, 384], P('section', None, 'dp', 'seq')
- table_grad: float32 [1000, 384], replicated
- modulation_grad: float32 [2, 384, 2304], P('section', ('dp', 'seq'))
- attention_grad: float32 [2, 384, 1152], P('section', ('dp', 'seq'))
- output_grad: float32 [2, 384, 384], P('section', ('dp', 'seq'))
- expand_grad: float32 [2, 384, 1536], P('section', ('dp', 'seq'))
- shrink_grad: float32 [2, 1536, 384], P('section', ('dp', 'seq'))
- biases_grad: float32 [2, 5376], P('section', ('dp', 'seq'))
Inputs may be any that keep to these rules, and one draw needn't show every extreme that they name: `row_counts`: entry [m, r] is how many latents data row r holds in micro-batch m: its slots r * 2 to r * 2 + entry - 1 are live, the others are padding. In every micro-batch some row holds 2.
All inputs are finite; a program needn't handle non-finite values.
Results may differ from a plain program's by a relative error of at most 0.018.
The roundings to bfloat16 on the way count: a program that leaves them out, or rounds other values in their place, can miss the bound.
Values may be sent and summed in bfloat16 or wider, within the bound.
No kernel may reach another device: no remote copies, remote signals or barrier semaphores. Data moves between devices by JAX's collectives and lax.ppermute only.
A program may use at most 128 MiB of HBM per device.

v0:
```python
from functools import partial

import jax
import jax.numpy as jnp
from jax import lax
from jax.sharding import PartitionSpec as P

HEADS = 6
HEAD = 64


epsilon = 1e-06


def from_behind(block, axis, distance):
    devices = range(lax.axis_size(axis))
    route = [(i - distance, i) for i in devices if i - distance in devices]
    return lax.ppermute(block, axis, route)


def normalize_rows(values):
    centre = jnp.mean(values, axis=-1, keepdims=True)
    centred = values - centre
    spread = jnp.mean(centred * centred, axis=-1, keepdims=True)
    factor = lax.rsqrt(spread + epsilon)
    return (centred * factor, factor)


def normalize_back(normed, factor, grad_normed):
    mean_grad = jnp.mean(grad_normed, axis=-1, keepdims=True)
    mean_cross = jnp.mean(grad_normed * normed, axis=-1, keepdims=True)
    return factor * (grad_normed - mean_grad - normed * mean_cross)


def matmul(former, latter):
    return jnp.dot(former, latter, preferred_element_type=jnp.float32)


def matmul_transposed(former, latter):
    return lax.dot_general(
        former, latter, (((1,), (1,)), ((), ())), preferred_element_type=jnp.float32
    )


def outer_sum(former, latter):
    return lax.dot_general(
        former, latter, (((0,), (0,)), ((), ())), preferred_element_type=jnp.float32
    )


def pick(buffer, position):
    return lax.dynamic_index_in_dim(buffer, position, 0, keepdims=False)


def store(buffer, position, contents, active):
    current = pick(buffer, position)
    updated = jnp.where(active, contents.astype(buffer.dtype), current)
    return lax.dynamic_update_index_in_dim(buffer, updated, position, 0)


def blanks(layouts):
    return tuple((jnp.zeros(extent, number_type) for extent, number_type in layouts))


def split_heads(tensor):
    return tensor.reshape(tensor.shape[0], tensor.shape[1], HEADS, HEAD)


def modulation_parts(modulation):
    return [member[:, None, :] for member in jnp.split(modulation, 6, axis=-1)]


def unpack(gathered):
    modulation_matrix, attention_matrix, output_matrix, expand_matrix, shrink_matrix, bias_full = [
        member[0] for member in gathered
    ]
    model_width = modulation_matrix.shape[0]
    hidden_width = expand_matrix.shape[1]
    boundaries = [
        6 * model_width,
        7 * model_width,
        8 * model_width,
        9 * model_width,
        9 * model_width + hidden_width,
    ]
    bias_parts = tuple(jnp.split(bias_full.astype(jnp.float32), boundaries))
    return (
        modulation_matrix,
        attention_matrix,
        output_matrix,
        expand_matrix,
        shrink_matrix,
        bias_parts,
    )


def attention_scores(queries, keys_full):
    return jnp.einsum(
        "cthe,clhe->chtl",
        split_heads(queries),
        split_heads(keys_full),
        preferred_element_type=jnp.float32,
    ) * HEAD ** (-0.5)


def forward_front(section_input, silu_now, weights):
    modulation_matrix, attention_matrix, _, _, _, bias_parts = weights
    inputs_wide = section_input.astype(jnp.float32)
    slot_count, tokens, model_width = inputs_wide.shape
    modulation = matmul(silu_now, modulation_matrix) + bias_parts[0]
    members = modulation_parts(modulation)
    normed_one, _ = normalize_rows(inputs_wide)
    hidden_one = (normed_one * (1.0 + members[1]) + members[0]).astype(jnp.bfloat16)
    projected = matmul(hidden_one.reshape(-1, model_width), attention_matrix).reshape(
        slot_count, tokens, 3 * model_width
    )
    queries = (projected[..., :model_width] + bias_parts[1]).astype(jnp.bfloat16)
    keys_local = projected[..., model_width : 2 * model_width].astype(jnp.bfloat16)
    values_local = (projected[..., 2 * model_width :] + bias_parts[2]).astype(jnp.bfloat16)
    return (modulation, queries, keys_local, values_local)


def forward_back(section_input, modulation, queries, keys_full, values_full, weights):
    _, _, output_matrix, expand_matrix, shrink_matrix, bias_parts = weights
    inputs_wide = section_input.astype(jnp.float32)
    slot_count, tokens, model_width = inputs_wide.shape
    members = modulation_parts(modulation)
    scores = attention_scores(queries, keys_full)
    highest = jnp.max(scores, axis=-1, keepdims=True)
    log_total = highest + jnp.log(jnp.sum(jnp.exp(scores - highest), axis=-1, keepdims=True))
    soft_weights = jnp.exp(scores - log_total).astype(jnp.bfloat16)
    attended = jnp.einsum(
        "chtl,clhe->cthe",
        soft_weights,
        split_heads(values_full),
        preferred_element_type=jnp.float32,
    )
    attended = attended.reshape(slot_count, tokens, model_width).astype(jnp.bfloat16)
    attention_branch = (
        matmul(attended.reshape(-1, model_width), output_matrix).reshape(
            slot_count, tokens, model_width
        )
        + bias_parts[3]
    )
    middle = inputs_wide + members[2] * attention_branch
    normed_two, _ = normalize_rows(middle)
    hidden_two = (normed_two * (1.0 + members[4]) + members[3]).astype(jnp.bfloat16)
    expanded = matmul(hidden_two.reshape(-1, model_width), expand_matrix) + bias_parts[4]
    activated = jax.nn.gelu(expanded, approximate=True).astype(jnp.bfloat16)
    branch = (matmul(activated, shrink_matrix) + bias_parts[5]).reshape(
        slot_count, tokens, model_width
    )
    result = middle + members[5] * branch
    return (result, log_total, attended, attention_branch, expanded, branch)


def backward_back(
    grad_out,
    section_input,
    modulation,
    queries,
    keys_full,
    values_full,
    log_total,
    attention_branch,
    expanded,
    branch,
    weights,
):
    _, _, output_matrix, expand_matrix, shrink_matrix, _ = weights
    inputs_wide = section_input.astype(jnp.float32)
    slot_count, tokens, model_width = inputs_wide.shape
    length = keys_full.shape[1]
    members = modulation_parts(modulation)
    middle = inputs_wide + members[2] * attention_branch
    normed_two, factor_two = normalize_rows(middle)
    hidden_two = (normed_two * (1.0 + members[4]) + members[3]).astype(jnp.bfloat16)
    grad_branch = (members[5] * grad_out).astype(jnp.bfloat16)
    gate_two_grad = jnp.sum(grad_out * branch, axis=1)
    grad_activated = matmul_transposed(grad_branch.reshape(-1, model_width), shrink_matrix)
    activated, gelu_back = jax.vjp(partial(jax.nn.gelu, approximate=True), expanded)
    grad_expanded = gelu_back(grad_activated)[0].astype(jnp.bfloat16)
    grad_hidden_two = matmul_transposed(grad_expanded, expand_matrix).reshape(
        slot_count, tokens, model_width
    )
    shift_two_grad = jnp.sum(grad_hidden_two, axis=1)
    scale_two_grad = jnp.sum(grad_hidden_two * normed_two, axis=1)
    grad_middle = grad_out + normalize_back(
        normed_two, factor_two, grad_hidden_two * (1.0 + members[4])
    )
    gate_one_grad = jnp.sum(grad_middle * attention_branch, axis=1)
    grad_attention = (members[2] * grad_middle).astype(jnp.bfloat16)
    grad_attended = matmul_transposed(grad_attention.reshape(-1, model_width), output_matrix)
    grad_attended = grad_attended.reshape(slot_count, tokens, model_width).astype(jnp.bfloat16)
    scores = attention_scores(queries, keys_full)
    soft_exact = jnp.exp(scores - log_total)
    grad_soft = jnp.einsum(
        "cthe,clhe->chtl",
        split_heads(grad_attended),
        split_heads(values_full),
        preferred_element_type=jnp.float32,
    )
    inner_sum = jnp.sum(grad_soft * soft_exact, axis=-1, keepdims=True)
    grad_scores = (soft_exact * (grad_soft - inner_sum)).astype(jnp.bfloat16)
    score_scale = HEAD ** (-0.5)
    grad_queries = (
        jnp.einsum(
            "chtl,clhe->cthe",
            grad_scores,
            split_heads(keys_full),
            preferred_element_type=jnp.float32,
        )
        * score_scale
    )
    grad_queries = grad_queries.reshape(slot_count, tokens, model_width).astype(jnp.bfloat16)
    key_terms = (
        jnp.einsum(
            "chtl,cthe->clhe", grad_scores, split_heads(queries), preferred_element_type=jnp.float32
        )
        * score_scale
    )
    first_tail = key_terms.reshape(slot_count, length, model_width)
    value_terms = jnp.einsum(
        "chtl,cthe->clhe",
        soft_exact.astype(jnp.bfloat16),
        split_heads(grad_attended),
        preferred_element_type=jnp.float32,
    )
    second_tail = value_terms.reshape(slot_count, length, model_width)
    return (
        grad_middle,
        grad_queries,
        first_tail,
        second_tail,
        gate_one_grad,
        shift_two_grad,
        scale_two_grad,
        gate_two_grad,
        hidden_two.reshape(-1, model_width),
        grad_expanded,
        activated.astype(jnp.bfloat16),
        grad_branch.reshape(-1, model_width),
        grad_attention.reshape(-1, model_width),
    )


def backward_front(
    grad_middle, grad_queries, key_grad, value_grad, section_input, modulation, weights
):
    _, attention_matrix, _, _, _, _ = weights
    inputs_wide = section_input.astype(jnp.float32)
    slot_count, tokens, model_width = inputs_wide.shape
    members = modulation_parts(modulation)
    normed_one, factor_one = normalize_rows(inputs_wide)
    hidden_one = (normed_one * (1.0 + members[1]) + members[0]).astype(jnp.bfloat16)
    grad_projected = jnp.concatenate([grad_queries, key_grad, value_grad], axis=-1).reshape(
        -1, 3 * model_width
    )
    grad_hidden_one = matmul_transposed(grad_projected, attention_matrix).reshape(
        slot_count, tokens, model_width
    )
    shift_one_grad = jnp.sum(grad_hidden_one, axis=1)
    scale_one_grad = jnp.sum(grad_hidden_one * normed_one, axis=1)
    grad_inputs = grad_middle + normalize_back(
        normed_one, factor_one, grad_hidden_one * (1.0 + members[1])
    )
    return (
        grad_inputs,
        hidden_one.reshape(-1, model_width),
        grad_projected,
        shift_one_grad,
        scale_one_grad,
    )


def weight_terms(
    silu_rows,
    modulation_rows,
    hidden_one,
    grad_projected,
    attended,
    grad_attention,
    hidden_two,
    grad_expanded,
    activated,
    grad_branch,
    seq_gate,
):
    model_width = hidden_one.shape[1]
    modulation_term = outer_sum(silu_rows, modulation_rows) * seq_gate
    attention_term = outer_sum(hidden_one, grad_projected)
    output_term = outer_sum(attended, grad_attention)
    expand_term = outer_sum(hidden_two, grad_expanded)
    shrink_term = outer_sum(activated, grad_branch)
    bias_term = jnp.concatenate(
        [
            jnp.sum(modulation_rows, axis=0, dtype=jnp.float32) * seq_gate,
            jnp.sum(grad_projected[:, :model_width], axis=0, dtype=jnp.float32),
            jnp.sum(grad_projected[:, 2 * model_width :], axis=0, dtype=jnp.float32),
            jnp.sum(grad_attention, axis=0, dtype=jnp.float32),
            jnp.sum(grad_expanded, axis=0, dtype=jnp.float32),
            jnp.sum(grad_branch, axis=0, dtype=jnp.float32),
        ]
    )
    return tuple(
        (
            member[None]
            for member in (
                modulation_term,
                attention_term,
                output_term,
                expand_term,
                shrink_term,
                bias_term,
            )
        )
    )


def per_device(
    inputs,
    cotangent,
    time_ids,
    row_counts,
    cond_table,
    modulation_weight,
    attention_weight,
    output_weight,
    expand_weight,
    shrink_weight,
    biases,
):
    section_rank = lax.axis_index("section")
    seq_rank = lax.axis_index("seq")
    data_rank = lax.axis_index("dp")
    seq_gate = (seq_rank == 0).astype(jnp.float32)
    batches, slot_count, tokens, model_width = inputs.shape
    length = tokens * lax.axis_size("seq")
    table_rows = cond_table.shape[0]
    shards = (
        modulation_weight,
        attention_weight,
        output_weight,
        expand_weight,
        shrink_weight,
        biases,
    )
    weights = unpack(
        (
            lax.all_gather(shards[0], ("dp", "seq"), axis=1, tiled=True),
            lax.all_gather(shards[1], ("dp", "seq"), axis=1, tiled=True),
            lax.all_gather(shards[2], ("dp", "seq"), axis=1, tiled=True),
            lax.all_gather(shards[3], ("dp", "seq"), axis=1, tiled=True),
            lax.all_gather(shards[4], ("dp", "seq"), axis=1, tiled=True),
            lax.all_gather(shards[5], ("dp", "seq"), axis=1, tiled=True),
        )
    )
    hidden_width = weights[3].shape[1]
    flat_rows = slot_count * tokens
    own_ids = lax.dynamic_slice_in_dim(time_ids, data_rank * slot_count, slot_count, 1)
    selector = (
        own_ids[:, :, None] == jnp.arange(table_rows, dtype=jnp.int32)[None, None, :]
    ).astype(jnp.float32)
    conditions = matmul(selector.astype(jnp.bfloat16).reshape(-1, table_rows), cond_table).reshape(
        batches, slot_count, model_width
    )
    silu_all = jax.nn.silu(conditions).astype(jnp.bfloat16)
    live_mask = (jnp.arange(slot_count, dtype=jnp.int32)[None, :] < row_counts).astype(jnp.float32)
    narrow = ((slot_count, tokens, model_width), jnp.bfloat16)
    wide = ((slot_count, tokens, model_width), jnp.float32)
    per_slot = ((slot_count, model_width), jnp.float32)
    long_terms = ((slot_count, length, model_width), jnp.float32)
    row_totals = ((slot_count, HEADS, tokens, 1), jnp.float32)
    row_narrow = ((flat_rows, model_width), jnp.bfloat16)
    row_hidden = ((flat_rows, hidden_width), jnp.bfloat16)
    front_layouts = [((slot_count, 6 * model_width), jnp.float32), narrow, narrow, narrow]
    back_layouts = [wide, row_totals, narrow, wide, ((flat_rows, hidden_width), jnp.float32), wide]
    tail_layouts = [long_terms, long_terms]
    grad_back_layouts = (
        [wide, narrow]
        + tail_layouts
        + [
            per_slot,
            per_slot,
            per_slot,
            per_slot,
            row_narrow,
            row_hidden,
            row_hidden,
            row_narrow,
            row_narrow,
        ]
    )
    grad_front_layouts = [
        wide,
        row_narrow,
        ((flat_rows, 3 * model_width), jnp.bfloat16),
        per_slot,
        per_slot,
    ]
    kept_inputs = jnp.zeros((batches, slot_count, tokens, model_width), jnp.bfloat16)
    kept_modulation = jnp.zeros((batches, slot_count, 6 * model_width), jnp.float32)
    kept_queries = jnp.zeros((batches, slot_count, tokens, model_width), jnp.bfloat16)
    kept_keys = jnp.zeros((batches, slot_count, length, model_width), jnp.bfloat16)
    kept_values = jnp.zeros((batches, slot_count, length, model_width), jnp.bfloat16)
    kept_totals = jnp.zeros((batches, slot_count, HEADS, tokens, 1), jnp.float32)
    kept_attended = jnp.zeros((batches, slot_count, tokens, model_width), jnp.bfloat16)
    kept_branch_one = jnp.zeros((batches, slot_count, tokens, model_width), jnp.float32)
    kept_expanded = jnp.zeros((batches, flat_rows, hidden_width), jnp.float32)
    kept_branch_two = jnp.zeros((batches, slot_count, tokens, model_width), jnp.float32)
    outputs_local = jnp.zeros((batches, slot_count, tokens, model_width), jnp.bfloat16)
    received = jnp.zeros((slot_count, tokens, model_width), jnp.bfloat16)
    for moment in range(batches + 1):
        micro_batch = moment - section_rank
        active = (micro_batch >= 0) & (micro_batch < batches)
        position = jnp.clip(micro_batch, 0, batches - 1)
        section_input = jnp.where(section_rank == 0, inputs[min(moment, batches - 1)], received)
        silu_now = pick(silu_all, position)
        modulation, queries, keys_local, values_local = lax.cond(
            active,
            lambda: forward_front(section_input, silu_now, weights),
            lambda: blanks(front_layouts),
        )
        keys_full, values_full = (
            lax.all_gather(keys_local, "seq", axis=1, tiled=True),
            lax.all_gather(values_local, "seq", axis=1, tiled=True),
        )
        result, log_total, attended, branch_one, expanded, branch_two = lax.cond(
            active,
            lambda: forward_back(
                section_input, modulation, queries, keys_full, values_full, weights
            ),
            lambda: blanks(back_layouts),
        )
        outgoing = result.astype(jnp.bfloat16)
        live_now = pick(live_mask, position)[:, None, None].astype(jnp.bfloat16)
        kept_inputs = store(kept_inputs, position, section_input, active)
        kept_modulation = store(kept_modulation, position, modulation, active)
        kept_queries = store(kept_queries, position, queries, active)
        kept_keys = store(kept_keys, position, keys_full, active)
        kept_values = store(kept_values, position, values_full, active)
        kept_totals = store(kept_totals, position, log_total, active)
        kept_attended = store(kept_attended, position, attended, active)
        kept_branch_one = store(kept_branch_one, position, branch_one, active)
        kept_expanded = store(kept_expanded, position, expanded, active)
        kept_branch_two = store(kept_branch_two, position, branch_two, active)
        outputs_local = store(outputs_local, position, outgoing * live_now, active)
        if moment < batches:
            received = from_behind(outgoing, "section", 1)
    back_weights = unpack(
        (
            lax.all_gather(shards[0], ("dp", "seq"), axis=1, tiled=True),
            lax.all_gather(shards[1], ("dp", "seq"), axis=1, tiled=True),
            lax.all_gather(shards[2], ("dp", "seq"), axis=1, tiled=True),
            lax.all_gather(shards[3], ("dp", "seq"), axis=1, tiled=True),
            lax.all_gather(shards[4], ("dp", "seq"), axis=1, tiled=True),
            lax.all_gather(shards[5], ("dp", "seq"), axis=1, tiled=True),
        )
    )
    modulation_matrix = back_weights[0]
    received_grad = jnp.zeros((slot_count, tokens, model_width), jnp.bfloat16)
    grads_local = jnp.zeros((batches, slot_count, tokens, model_width), jnp.float32)
    keep_hidden_one = jnp.zeros((batches, flat_rows, model_width), jnp.bfloat16)
    keep_grad_projected = jnp.zeros((batches, flat_rows, 3 * model_width), jnp.bfloat16)
    keep_grad_attention = jnp.zeros((batches, flat_rows, model_width), jnp.bfloat16)
    keep_hidden_two = jnp.zeros((batches, flat_rows, model_width), jnp.bfloat16)
    keep_grad_expanded = jnp.zeros((batches, flat_rows, hidden_width), jnp.bfloat16)
    keep_activated = jnp.zeros((batches, flat_rows, hidden_width), jnp.bfloat16)
    keep_grad_branch = jnp.zeros((batches, flat_rows, model_width), jnp.bfloat16)
    keep_modulation_grads = jnp.zeros((batches, slot_count, 6 * model_width), jnp.bfloat16)
    keep_cond_grads = jnp.zeros((batches, slot_count, model_width), jnp.float32)
    for moment in range(batches + 1):
        micro_batch = moment - 1 + section_rank
        active = (micro_batch >= 0) & (micro_batch < batches)
        position = jnp.clip(micro_batch, 0, batches - 1)
        last_index = min(moment, batches - 1)
        seed_grad = cotangent[last_index].astype(jnp.float32) * live_mask[last_index][:, None, None]
        grad_out = jnp.where(section_rank == 1, seed_grad, received_grad.astype(jnp.float32))
        section_input = pick(kept_inputs, position)
        modulation = pick(kept_modulation, position)
        queries = pick(kept_queries, position)
        keys_full = pick(kept_keys, position)
        values_full = pick(kept_values, position)
        log_total = pick(kept_totals, position)
        attended = pick(kept_attended, position)
        branch_one = pick(kept_branch_one, position)
        expanded = pick(kept_expanded, position)
        branch_two = pick(kept_branch_two, position)
        (
            grad_middle,
            grad_queries,
            first_tail,
            second_tail,
            gate_one_grad,
            shift_two_grad,
            scale_two_grad,
            gate_two_grad,
            hidden_two,
            grad_expanded,
            activated,
            grad_branch,
            grad_attention,
        ) = lax.cond(
            active,
            lambda: backward_back(
                grad_out,
                section_input,
                modulation,
                queries,
                keys_full,
                values_full,
                log_total,
                branch_one,
                expanded,
                branch_two,
                back_weights,
            ),
            lambda: blanks(grad_back_layouts),
        )
        key_grad, value_grad = (
            lax.psum_scatter(
                first_tail.astype(jnp.bfloat16), "seq", scatter_dimension=1, tiled=True
            ).astype(jnp.float32),
            lax.psum_scatter(
                second_tail.astype(jnp.bfloat16), "seq", scatter_dimension=1, tiled=True
            ).astype(jnp.float32),
        )
        grad_inputs, hidden_one, grad_projected, shift_one_grad, scale_one_grad = lax.cond(
            active,
            lambda: backward_front(
                grad_middle,
                grad_queries,
                key_grad.astype(jnp.bfloat16),
                value_grad.astype(jnp.bfloat16),
                section_input,
                modulation,
                back_weights,
            ),
            lambda: blanks(grad_front_layouts),
        )
        modulation_partial = jnp.concatenate(
            [
                shift_one_grad,
                scale_one_grad,
                gate_one_grad,
                shift_two_grad,
                scale_two_grad,
                gate_two_grad,
            ],
            axis=-1,
        )
        modulation_grad_low = lax.psum(modulation_partial, "seq").astype(jnp.bfloat16)
        conditions_now = pick(conditions, position)
        _, silu_back = jax.vjp(jax.nn.silu, conditions_now)
        cond_grad = silu_back(matmul_transposed(modulation_grad_low, modulation_matrix))[0]
        grads_local = store(grads_local, position, grad_inputs, active)
        keep_hidden_one = store(keep_hidden_one, position, hidden_one, active)
        keep_grad_projected = store(keep_grad_projected, position, grad_projected, active)
        keep_grad_attention = store(keep_grad_attention, position, grad_attention, active)
        keep_hidden_two = store(keep_hidden_two, position, hidden_two, active)
        keep_grad_expanded = store(keep_grad_expanded, position, grad_expanded, active)
        keep_activated = store(keep_activated, position, activated, active)
        keep_grad_branch = store(keep_grad_branch, position, grad_branch, active)
        keep_modulation_grads = store(keep_modulation_grads, position, modulation_grad_low, active)
        keep_cond_grads = store(keep_cond_grads, position, cond_grad, active)
        if moment < batches:
            received_grad = from_behind(grad_inputs.astype(jnp.bfloat16), "section", -1)
    every_cond = lax.all_gather(keep_cond_grads[None], ("section", "dp"), axis=0, tiled=True)
    data_rows = every_cond.shape[0] // 2
    section_total = jnp.sum(
        every_cond.reshape(2, data_rows, batches, slot_count, model_width), axis=0
    )
    slot_grads = jnp.transpose(section_total, (1, 0, 2, 3)).reshape(-1, model_width)
    every_selector = (
        time_ids.reshape(-1)[:, None] == jnp.arange(table_rows, dtype=jnp.int32)[None, :]
    ).astype(jnp.float32)
    table_grad = lax.dot_general(
        every_selector,
        slot_grads,
        (((0,), (0,)), ((), ())),
        precision=lax.Precision.HIGHEST,
        preferred_element_type=jnp.float32,
    )
    grad_terms = weight_terms(
        silu_all.reshape(-1, model_width),
        keep_modulation_grads.reshape(-1, 6 * model_width),
        keep_hidden_one.reshape(-1, model_width),
        keep_grad_projected.reshape(-1, 3 * model_width),
        kept_attended.reshape(-1, model_width),
        keep_grad_attention.reshape(-1, model_width),
        keep_hidden_two.reshape(-1, model_width),
        keep_grad_expanded.reshape(-1, hidden_width),
        keep_activated.reshape(-1, hidden_width),
        keep_grad_branch.reshape(-1, model_width),
        seq_gate,
    )
    weight_grads = lax.psum_scatter(grad_terms, ("dp", "seq"), scatter_dimension=1, tiled=True)
    return (
        outputs_local[None],
        grads_local[None],
        table_grad,
        weight_grads[0],
        weight_grads[1],
        weight_grads[2],
        weight_grads[3],
        weight_grads[4],
        weight_grads[5],
    )


def solution(mesh):
    in_specs = (
        P(None, "dp", "seq", None),
        P(None, "dp", "seq", None),
        P(),
        P(None, "dp"),
        P(),
        P("section", ("dp", "seq"), None),
        P("section", ("dp", "seq"), None),
        P("section", ("dp", "seq"), None),
        P("section", ("dp", "seq"), None),
        P("section", ("dp", "seq"), None),
        P("section", ("dp", "seq")),
    )
    out_specs = (
        P("section", None, "dp", "seq", None),
        P("section", None, "dp", "seq", None),
        P(),
        P("section", ("dp", "seq"), None),
        P("section", ("dp", "seq"), None),
        P("section", ("dp", "seq"), None),
        P("section", ("dp", "seq"), None),
        P("section", ("dp", "seq"), None),
        P("section", ("dp", "seq")),
    )
    return jax.shard_map(
        per_device, mesh=mesh, in_specs=in_specs, out_specs=out_specs, check_vma=False
    )
```

profile of v0, /device:TPU:9, one launch (start us, length us, event | category | flops | bytes accessed | tf_op | source)
XLA Modules:
  0.0 1362.0 jit_solution(1954327718230454118)
XLA Ops:
  12.4 57.9 %all-reduce = bf16[5376]{0:T(1024)(128)(2,1)S(1)} all-reduce(bf16[5376]{0:T(1024)(128)(2,1)S(1)} %dynamic-update-slice), channel_id=1, replica_groups=mesh['section'=2,'dp'=8,'seq'=2] {'dp','seq'}, use_global_device_ids=true, to_apply=%add | all-reduce | flops 5376 | bytes 21504
  73.0 29.6 %all_gather.49 = bf16[1,384,384]{2,1,0:T(8,128)(2,1)S(1)} all-gather(bf16[1,24,384]{2,1,0:T(8,128)(2,1)S(1)} %copy-done.133), channel_id=1, replica_groups=mesh['section'=2,'dp'=8,'seq'=2] {'dp','seq'}, dimensions={1}, use_global_device_ids=true | all-gather | bytes 313344 | tf_op jit(solution)/shard_map/all_gather | solution.py:352
  104.3 38.5 %all_gather.46 = bf16[1,384,1152]{2,1,0:T(8,128)(2,1)S(1)} all-gather(bf16[1,24,1152]{2,1,0:T(8,128)(2,1)S(1)} %copy-done.122), channel_id=1, replica_groups=mesh['section'=2,'dp'=8,'seq'=2] {'dp','seq'}, dimensions={1}, use_global_device_ids=true | all-gather | bytes 940032 | tf_op jit(solution)/shard_map/all_gather | solution.py:351
  143.7 5.6 all_gather.47
  149.3 5.9 all_gather.48
  156.1 32.4 %all-gather.8.cloned.1.call-done = bf16[1,1536,384]{2,1,0:T(8,128)(2,1)} async-done(((bf16[1,96,384]{2,1,0:T(8,128)(2,1)}), bf16[1,1536,384]{2,1,0:T(8,128)(2,1)}) %all-gather.8.cloned.1.call-update) | async-done | bytes 1179664 | tf_op jit(solution)/shard_map/all_gather | solution.py:354
  211.6 4.1 conditional.14
  217.5 5.5 all_gather.52
  224.8 7.5 all_gather.53
  232.3 16.9 %conditional.15 = (f32[2,6,128,1]{2,1,0,3:T(8,128)S(1)}, f32[2,128,384]{2,1,0:T(8,128)}, f32[256,1536]{1,0:T(8,128)}, f32[2,128,384]{2,1,0:T(8,128)}, bf16[2,128...) conditional(s32[]{:T(128)} %convert_element_type.531, () %tuple.136, (bf16[2,128,384]{2,1,0:T(8,128)(2,1)}, ...), branch_computations={%region_14.15_spmd, %region_15.20_spmd} | conditional | flops 789085696 | bytes 23657688 | solution.py:428
  272.2 4.1 conditional.16
  278.0 5.5 all_gather.54
  285.3 7.4 all_gather.55
  300.8 17.8 %conditional.17 = (f32[2,6,128,1]{2,1,0,3:T(8,128)S(1)}, f32[2,128,384]{2,1,0:T(8,128)}, f32[256,1536]{1,0:T(8,128)}, f32[2,128,384]{2,1,0:T(8,128)}, bf16[2,128...) conditional(s32[]{:T(128)} %convert_element_type.534, () %tuple.140, (bf16[2,128,384]{2,1,0:T(8,128)(2,1)}, ...), branch_computations={%region_24.25_spmd, %region_25.30_spmd} | conditional | flops 789085696 | bytes 22078624 | solution.py:428
  325.0 31.4 %conditional.18 = (f32[2,128,384]{2,1,0:T(8,128)}, bf16[2,128,384]{1,2,0:T(8,128)(2,1)}, bf16[2,256,384]{1,2,0:T(8,128)(2,1)}, bf16[2,256,384]{1,2,0:T(8,128)(2,...) conditional(s32[]{:T(128)} %convert_element_type.537, ...), branch_computations={%region_30.31_spmd, %region_31.41_spmd} | conditional | flops 947745280 | bytes 44272000 | solution.py:503
  327.9 4.1 fusion.118
  378.6 7.2 reduce-scatter.23.cloned.1.call-done
  385.8 10.6 conditional.19
  405.8 30.4 %conditional.20 = (f32[2,128,384]{2,1,0:T(8,128)}, bf16[2,128,384]{1,2,0:T(8,128)(2,1)}, bf16[2,256,384]{1,2,0:T(8,128)(2,1)}, bf16[2,256,384]{1,2,0:T(8,128)(2,...) conditional(s32[]{:T(128)} %convert_element_type.542, ...), branch_computations={%region_51.52_spmd, %region_52.62_spmd} | conditional | flops 947253760 | bytes 49678716 | solution.py:503
  459.3 7.1 reduce-scatter.27.cloned.1.call-done
  466.4 8.4 conditional.21
  483.5 8.8 conditional.22
  506.6 16.7 %reduce-scatter.29.cloned.1.call-done = bf16[2,128,384]{2,1,0:T(8,128)(2,1)} async-done(((bf16[2,256,384]{2,1,0:T(8,128)(2,1)}), bf16[2,128,384]{2,1,0:T(8,128)(2,1)}) %reduce-scatter.29.cloned.1.call-update) | async-done | bytes 196624 | tf_op jit(solution)/shard_map/reduce_scatter | solution.py:521
  523.3 16.1 %reduce-scatter.31.cloned.1.call-done = bf16[2,128,384]{2,1,0:T(8,128)(2,1)} async-done(((bf16[2,256,384]{2,1,0:T(8,128)(2,1)}), bf16[2,128,384]{2,1,0:T(8,128)(2,1)}) %reduce-scatter.31.cloned.1.call-update) | async-done | bytes 196624 | tf_op jit(solution)/shard_map/reduce_scatter | solution.py:524
  545.7 6.3 all-reduce.3
  603.5 37.1 %all_gather.56 = f32[16,2,2,384]{3,2,1,0:T(2,128)S(1)} all-gather(f32[1,2,2,384]{3,2,1,0:T(2,128)S(1)} %constant_dynamic-update-slice_fusion.28), channel_id=1, replica_groups=mesh['section'=2,'dp'=8,'seq'=2] {'section','dp'}, dimensions={0}, use_global_device_ids=true | all-gather | bytes 104448 | tf_op jit(solution)/shard_map/all_gather | solution.py:568
  643.8 51.2 %reduce-scatter.39.cloned.1.call-done = f32[336,1]{1,0:T(8,128)} async-done(((f32[5376,1]{1,0:T(8,128)}), f32[336,1]{1,0:T(8,128)}) %reduce-scatter.39.cloned.1.call-update) | async-done | bytes 1360
  696.5 125.7 %reduce-scatter.43.cloned.1.call-done = f32[1,24,384]{2,1,0:T(8,128)} async-done(((f32[1,384,384]{2,1,0:T(8,128)}), f32[1,24,384]{2,1,0:T(8,128)}) %reduce-scatter.43.cloned.1.call-update) | async-done | bytes 36880
  822.2 129.9 %reduce-scatter.41.cloned.1.call-done = f32[1,24,1152]{2,1,0:T(8,128)} async-done(((f32[1,384,1152]{2,1,0:T(8,128)}), f32[1,24,1152]{2,1,0:T(8,128)}) %reduce-scatter.41.cloned.1.call-update) | async-done | bytes 110608
  952.1 132.2 %reduce-scatter.35.cloned.1.call-done = f32[1,24,1536]{2,1,0:T(8,128)} async-done(((f32[1,384,1536]{2,1,0:T(8,128)}), f32[1,24,1536]{2,1,0:T(8,128)}) %reduce-scatter.35.cloned.1.call-update) | async-done | bytes 147472 | tf_op jit(solution)/shard_map/reduce_scatter | solution.py:597
  1084.2 132.9 %reduce-scatter.37.cloned.1.call-done = f32[1,96,384]{2,1,0:T(8,128)} async-done(((f32[1,1536,384]{2,1,0:T(8,128)}), f32[1,96,384]{2,1,0:T(8,128)}) %reduce-scatter.37.cloned.1.call-update) | async-done | bytes 147472 | tf_op jit(solution)/shard_map/reduce_scatter | solution.py:597
  1217.1 137.9 %reduce-scatter.33.cloned.1.call-done = f32[1,24,2304]{2,1,0:T(8,128)} async-done(((f32[1,384,2304]{2,1,0:T(8,128)}), f32[1,24,2304]{2,1,0:T(8,128)}) %reduce-scatter.33.cloned.1.call-update) | async-done | bytes 221200 | tf_op jit(solution)/shard_map/reduce_scatter | solution.py:597
  (678 shorter events, 351.5 us)
Async XLA Ops:
  7.2 96.3 %copy-start = (bf16[1000,384]{1,0:T(8,128)(2,1)S(1)}, bf16[1000,384]{1,0:T(8,128)(2,1)}, u32[]{:S(2)}) copy-start(bf16[1000,384]{1,0:T(8,128)(2,1)} %param.39) | copy-start | bytes 2304004
  7.2 65.8 %copy-start.133 = (bf16[1,24,384]{2,1,0:T(8,128)(2,1)S(1)}, bf16[1,24,384]{2,1,0:T(8,128)(2,1)}, u32[]{:S(2)}) copy-start(bf16[1,24,384]{2,1,0:T(8,128)(2,1)} %param.42) | copy-start | bytes 55300
  7.2 95.3 %copy-start.160 = (s32[2,1]{0,1:T(1,128)S(1)}, s32[2,1]{0,1:T(1,128)}, u32[]{:S(2)}) copy-start(s32[2,1]{0,1:T(1,128)} %param.38) | copy-start | bytes 28
  7.2 95.4 %copy-start.92 = (bf16[2,2,128,384]{3,2,1,0:T(8,128)(2,1)S(1)}, bf16[2,2,128,384]{3,2,1,0:T(8,128)(2,1)}, u32[]{:S(2)}) copy-start(bf16[2,2,128,384]{3,2,1,0:T(8,128)(2,1)} %param.36) | copy-start | bytes 1179652
  7.2 135.7 %all-gather.4.cloned.1.call-start = ((), (), s32[]{:S(2)}) async-start(), calls=%async_computation.12 | async-start | bytes 1880064 | tf_op jit(solution)/shard_map/all_gather | solution.py:350
  8.0 148.1 %all-gather.6.cloned.1.call-start = ((), (), s32[]{:S(2)}) async-start(), calls=%async_computation.13 | async-start | bytes 1253376 | tf_op jit(solution)/shard_map/all_gather | solution.py:353
  8.7 179.8 %all-gather.8.cloned.1.call-start = ((), (), s32[]{:S(2)}) async-start(), calls=%async_computation.14 | async-start | bytes 1253376 | tf_op jit(solution)/shard_map/all_gather | solution.py:354
  9.4 369.1 %reduce-scatter.21.cloned.1.call-start = ((), (), s32[]{:S(2)}) async-start(), calls=%async_computation.15 | async-start | bytes 589824 | tf_op jit(solution)/shard_map/reduce_scatter | solution.py:521
  70.3 118.2 %copy-start.150 = (f32[384]{0:T(512)}, f32[384]{0:T(512)S(1)}, u32[]{:S(2)}) copy-start(f32[384]{0:T(512)S(1)} %get-tuple-element.1336) | copy-start | bytes 4612
  70.3 34.0 %copy-start.122 = (bf16[1,24,1152]{2,1,0:T(8,128)(2,1)S(1)}, bf16[1,24,1152]{2,1,0:T(8,128)(2,1)}, u32[]{:S(2)}) copy-start(bf16[1,24,1152]{2,1,0:T(8,128)(2,1)} %param.41) | copy-start | bytes 165892
  71.4 71.5 %copy-start.49 = (bf16[2,2,128,384]{3,2,1,0:T(8,128)(2,1)}, bf16[2,2,128,384]{3,2,1,0:T(8,128)(2,1)S(1)}, u32[]{:S(2)}) copy-start(bf16[2,2,128,384]{3,2,1,0:T(8,128)(2,1)S(1)} %get-tuple-element.1467) | copy-start | bytes 1179652
  102.6 40.3 %copy-start.147 = (f32[2,2]{1,0:T(2,128)}, f32[2,2]{1,0:T(2,128)S(1)}, u32[]{:S(2)}) copy-start(f32[2,2]{1,0:T(2,128)S(1)} %compare_convert_fusion.1) | copy-start | bytes 52
  104.3 167.1 %copy-start.124 = (bf16[2,2,384]{2,1,0:T(2,128)(2,1)}, bf16[2,2,384]{2,1,0:T(2,128)(2,1)S(1)}, u32[]{:S(2)}) copy-start(bf16[2,2,384]{2,1,0:T(2,128)(2,1)S(1)} %get-tuple-element.1475) | copy-start | bytes 9220
  142.9 68.0 %copy-start.12 = (bf16[1,384,1152]{2,1,0:T(8,128)(2,1)}, bf16[1,384,1152]{2,1,0:T(8,128)(2,1)S(1)}, u32[]{:S(2)}) copy-start(bf16[1,384,1152]{2,1,0:T(8,128)(2,1)S(1)} %all_gather.46) | copy-start | bytes 2654212
  192.2 17.6 %collective-permute-start = (bf16[2,128,384]{2,1,0:T(8,128)(2,1)}, bf16[2,128,384]{2,1,0:T(8,128)(2,1)}, u32[]{:S(2)}, u32[]{:S(2)}) collective-permute-start(bf16[2,128,384]{2,1,0:T(8,128)(2,1)} %get-tuple-element.867), channel_id=1, source_target_pairs={{0,16},{1,17},{2,18},{3,19},{4,20},{5,21},{6,22},{7,23},{8,24},{9,... | collective-permute-start | bytes 589832 | tf_op jit(solution)/shard_map/ppermute | solution.py:18
  215.7 16.6 %copy-start.3 = (bf16[1,384,1536]{2,1,0:T(8,128)(2,1)S(1)}, bf16[1,384,1536]{2,1,0:T(8,128)(2,1)}, u32[]{:S(2)}) copy-start(bf16[1,384,1536]{2,1,0:T(8,128)(2,1)} %all-gather.6.cloned.1.call-done) | copy-start | bytes 3538948
  249.2 22.2 %collective-permute-start.1 = (bf16[2,128,384]{2,1,0:T(8,128)(2,1)}, bf16[2,128,384]{2,1,0:T(8,128)(2,1)S(1)}, u32[]{:S(2)}, u32[]{:S(2)}) collective-permute-start(bf16[2,128,384]{2,1,0:T(8,128)(2,1)} %get-tuple-element.872), channel_id=1, source_target_pairs={{0,16},{1,17},{2,18},{3,19},{4,20},{5,21},{6,22},{7,23},{8,24},{9,... | collective-permute-start | bytes 589832 | tf_op jit(solution)/shard_map/ppermute | solution.py:18
  324.1 81.5 %copy-start.71 = (pred[2,128,384]{2,1,0:T(8,128)(4,1)}, pred[2,128,384]{2,1,0:T(8,128)(4,1)S(1)}, u32[]{:S(2)}) copy-start(pred[2,128,384]{2,1,0:T(8,128)(4,1)S(1)} %select_n.593) | copy-start | bytes 294916
  358.4 27.5 %reduce-scatter.23.cloned.1.call-start = ((), (), s32[]{:S(2)}) async-start(), calls=%async_computation.16 | async-start | bytes 589824 | tf_op jit(solution)/shard_map/reduce_scatter | solution.py:524
  368.0 91.3 %reduce-scatter.25.cloned.1.call-start = ((), (), s32[]{:S(2)}) async-start(), calls=%async_computation.17 | async-start | bytes 589824 | tf_op jit(solution)/shard_map/reduce_scatter | solution.py:521
  397.6 8.0 collective-permute-start.2
  438.1 28.3 %reduce-scatter.27.cloned.1.call-start = ((), (), s32[]{:S(2)}) async-start(), calls=%async_computation.18 | async-start | bytes 589824 | tf_op jit(solution)/shard_map/reduce_scatter | solution.py:524
  448.2 75.1 %reduce-scatter.29.cloned.1.call-start = ((), (), s32[]{:S(2)}) async-start(), calls=%async_computation.19 | async-start | bytes 589824 | tf_op jit(solution)/shard_map/reduce_scatter | solution.py:521
  475.9 7.6 collective-permute-start.3
  494.4 44.9 %reduce-scatter.31.cloned.1.call-start = ((), (), s32[]{:S(2)}) async-start(), calls=%async_computation.20 | async-start | bytes 589824 | tf_op jit(solution)/shard_map/reduce_scatter | solution.py:524
  502.2 192.7 %reduce-scatter.39.cloned.1.call-start = ((), (), s32[]{:S(2)}) async-start(), calls=%async_computation.24 | async-start | bytes 2924544
  557.2 265.0 %reduce-scatter.43.cloned.1.call-start = ((), (), s32[]{:S(2)}) async-start(), calls=%async_computation.26 | async-start | bytes 626688
  559.6 392.4 %reduce-scatter.41.cloned.1.call-start = ((), (), s32[]{:S(2)}) async-start(), calls=%async_computation.25 | async-start | bytes 1880064
  563.9 520.4 %reduce-scatter.35.cloned.1.call-start = ((), (), s32[]{:S(2)}) async-start(), calls=%async_computation.22 | async-start | bytes 2506752 | tf_op jit(solution)/shard_map/reduce_scatter | solution.py:597
  568.8 648.3 %reduce-scatter.37.cloned.1.call-start = ((), (), s32[]{:S(2)}) async-start(), calls=%async_computation.23 | async-start | bytes 2506752 | tf_op jit(solution)/shard_map/reduce_scatter | solution.py:597
  591.3 763.8 %reduce-scatter.33.cloned.1.call-start = ((), (), s32[]{:S(2)}) async-start(), calls=%async_computation.21 | async-start | bytes 3760128 | tf_op jit(solution)/shard_map/reduce_scatter | solution.py:597
  640.6 714.4 %copy-start.1 = (bf16[1000,384]{1,0:T(8,128)(2,1)S(1)}, bf16[1000,384]{1,0:T(8,128)(2,1)}, u32[]{:S(2)}) copy-start(bf16[1000,384]{1,0:T(8,128)(2,1)} %param.39) | copy-start | bytes 2304004
  (124 other events, 492.5 us)
Sparse Core Ops, SparseCore 0:
  10.9 58.8 all-gather.3
  72.6 54.9 all-gather.5
  130.4 58.0 all-gather.7
  358.5 11.9 reduce-scatter.20
  372.7 13.1 reduce-scatter.22
  438.3 12.5 reduce-scatter.24
  453.2 13.1 reduce-scatter.26
  494.5 28.6 reduce-scatter.28
  526.2 13.1 reduce-scatter.30
  557.3 137.5 reduce-scatter.38
  700.9 121.2 reduce-scatter.42
  827.5 124.5 reduce-scatter.40
  957.6 126.6 reduce-scatter.34
  1090.3 126.7 reduce-scatter.36
  1222.6 132.3 reduce-scatter.32
where the time goes:
time: 1380 us; the launch traced here: 1360 us
  waiting for transfers between devices  791 us (57%)
  blocking collectives  207 us (15%)
  local copies, waits for them, and re-layouts  157 us (11%)
  other arithmetic  109 us (8%)
  matrix products  72.1 us (5%)
  between operations  16.6 us (1%)
    reduce_scatter x3, waiting for transfers between devices, per_device(): lax.psum_scatter(grad_terms, ('dp', 'seq'), scatter_dimension=1, tiled=True)  403 us
    unnamed x18, waiting for transfers between devices  309 us
    unnamed x1, blocking collectives  57.9 us
    dynamic_update_slice x51, other arithmetic, store(): return lax.dynamic_update_index_in_dim(buffer, updated, position, 0)  49.6 us
    dynamic_slice x40, local copies, waits for them, and re-layouts, pick(): return lax.dynamic_index_in_dim(buffer, position, 0, keepdims=False)  46.4 us
    all_gather x1, blocking collectives, per_device(): lax.all_gather(shards[1], ('dp', 'seq'), axis=1, tiled=True)  38.5 us
    all_gather x1, blocking collectives, per_device(): lax.all_gather(keep_cond_grads[None], ('section', 'dp'), axis=0, tiled=True)  37.1 us
    all_gather x1, waiting for transfers between devices, per_device(): lax.all_gather(shards[4], ('dp', 'seq'), axis=1, tiled=True)  32.4 us
  transfers between devices with their start and end apart: 19, of which 11 were waited for; matrix products, arithmetic and copies ran while one was open for 11% of the time, Pallas kernels for 0%

commit v1 on v0

v1 whole, which is shorter than its diff:
```python
from functools import partial

import jax
import jax.numpy as jnp
from jax import lax
from jax.sharding import PartitionSpec as P

HEADS = 6
HEAD = 64
SCALE = HEAD ** (-0.5)
epsilon = 1e-06
RING = ("dp", "seq")


def normalize_rows(values):
    centre = jnp.mean(values, axis=-1, keepdims=True)
    centred = values - centre
    spread = jnp.mean(centred * centred, axis=-1, keepdims=True)
    factor = lax.rsqrt(spread + epsilon)
    return (centred * factor, factor)


def normalize_back(normed, factor, grad_normed):
    mean_grad = jnp.mean(grad_normed, axis=-1, keepdims=True)
    mean_cross = jnp.mean(grad_normed * normed, axis=-1, keepdims=True)
    return factor * (grad_normed - mean_grad - normed * mean_cross)


def matmul(former, latter):
    return jnp.dot(former, latter, preferred_element_type=jnp.float32)


def matmul_transposed(former, latter):
    return lax.dot_general(
        former, latter, (((1,), (1,)), ((), ())), preferred_element_type=jnp.float32
    )


def outer_sum(former, latter):
    return lax.dot_general(
        former, latter, (((0,), (0,)), ((), ())), preferred_element_type=jnp.float32
    )


def split_heads(tensor):
    return tensor.reshape(tensor.shape[0], HEADS, HEAD)


def forward(inputs_wide, members, weights):
    attention_matrix, output_matrix, expand_matrix, shrink_matrix, biases = weights
    width = inputs_wide.shape[-1]
    shift_one, scale_one, gate_one, shift_two, scale_two, gate_two = members
    normed_one, _ = normalize_rows(inputs_wide)
    hidden_one = (normed_one * (1.0 + scale_one) + shift_one).astype(jnp.bfloat16)
    projected = matmul(hidden_one, attention_matrix)
    queries = (projected[:, :width] + biases[1]).astype(jnp.bfloat16)
    keys = projected[:, width : 2 * width].astype(jnp.bfloat16)
    values = (projected[:, 2 * width :] + biases[2]).astype(jnp.bfloat16)
    scores = (
        jnp.einsum(
            "the,lhe->htl",
            split_heads(queries),
            split_heads(keys),
            preferred_element_type=jnp.float32,
        )
        * SCALE
    )
    highest = jnp.max(scores, axis=-1, keepdims=True)
    log_total = highest + jnp.log(jnp.sum(jnp.exp(scores - highest), axis=-1, keepdims=True))
    soft = jnp.exp(scores - log_total).astype(jnp.bfloat16)
    attended = jnp.einsum(
        "htl,lhe->the", soft, split_heads(values), preferred_element_type=jnp.float32
    )
    attended = attended.reshape(inputs_wide.shape).astype(jnp.bfloat16)
    branch_one = matmul(attended, output_matrix) + biases[3]
    middle = inputs_wide + gate_one * branch_one
    normed_two, _ = normalize_rows(middle)
    hidden_two = (normed_two * (1.0 + scale_two) + shift_two).astype(jnp.bfloat16)
    expanded = matmul(hidden_two, expand_matrix) + biases[4]
    activated = jax.nn.gelu(expanded, approximate=True).astype(jnp.bfloat16)
    branch_two = matmul(activated, shrink_matrix) + biases[5]
    result = middle + gate_two * branch_two
    kept = (queries, keys, values, log_total, attended, branch_one, expanded, branch_two)
    return result, kept


def backward(grad_out, inputs_wide, members, weights, kept):
    attention_matrix, output_matrix, expand_matrix, shrink_matrix, _ = weights
    queries, keys, values, log_total, attended, branch_one, expanded, branch_two = kept
    shift_one, scale_one, gate_one, shift_two, scale_two, gate_two = members
    shape = inputs_wide.shape
    normed_one, factor_one = normalize_rows(inputs_wide)
    hidden_one = (normed_one * (1.0 + scale_one) + shift_one).astype(jnp.bfloat16)
    middle = inputs_wide + gate_one * branch_one
    normed_two, factor_two = normalize_rows(middle)
    hidden_two = (normed_two * (1.0 + scale_two) + shift_two).astype(jnp.bfloat16)
    grad_branch = (gate_two * grad_out).astype(jnp.bfloat16)
    gate_two_grad = jnp.sum(grad_out * branch_two, axis=0)
    grad_activated = matmul_transposed(grad_branch, shrink_matrix)
    activated, gelu_back = jax.vjp(partial(jax.nn.gelu, approximate=True), expanded)
    activated = activated.astype(jnp.bfloat16)
    grad_expanded = gelu_back(grad_activated)[0].astype(jnp.bfloat16)
    grad_hidden_two = matmul_transposed(grad_expanded, expand_matrix)
    shift_two_grad = jnp.sum(grad_hidden_two, axis=0)
    scale_two_grad = jnp.sum(grad_hidden_two * normed_two, axis=0)
    grad_middle = grad_out + normalize_back(
        normed_two, factor_two, grad_hidden_two * (1.0 + scale_two)
    )
    gate_one_grad = jnp.sum(grad_middle * branch_one, axis=0)
    grad_attention = (gate_one * grad_middle).astype(jnp.bfloat16)
    grad_attended = matmul_transposed(grad_attention, output_matrix).astype(jnp.bfloat16)
    scores = (
        jnp.einsum(
            "the,lhe->htl",
            split_heads(queries),
            split_heads(keys),
            preferred_element_type=jnp.float32,
        )
        * SCALE
    )
    soft_exact = jnp.exp(scores - log_total)
    grad_soft = jnp.einsum(
        "the,lhe->htl",
        split_heads(grad_attended),
        split_heads(values),
        preferred_element_type=jnp.float32,
    )
    inner = jnp.sum(grad_soft * soft_exact, axis=-1, keepdims=True)
    grad_scores = (soft_exact * (grad_soft - inner)).astype(jnp.bfloat16)
    grad_queries = (
        jnp.einsum(
            "htl,lhe->the", grad_scores, split_heads(keys), preferred_element_type=jnp.float32
        )
        * SCALE
    )
    grad_keys = (
        jnp.einsum(
            "htl,the->lhe", grad_scores, split_heads(queries), preferred_element_type=jnp.float32
        )
        * SCALE
    )
    grad_values = jnp.einsum(
        "htl,the->lhe",
        soft_exact.astype(jnp.bfloat16),
        split_heads(grad_attended),
        preferred_element_type=jnp.float32,
    )
    grad_projected = jnp.concatenate(
        [
            member.reshape(shape).astype(jnp.bfloat16)
            for member in (grad_queries, grad_keys, grad_values)
        ],
        axis=-1,
    )
    grad_hidden_one = matmul_transposed(grad_projected, attention_matrix)
    shift_one_grad = jnp.sum(grad_hidden_one, axis=0)
    scale_one_grad = jnp.sum(grad_hidden_one * normed_one, axis=0)
    grad_inputs = grad_middle + normalize_back(
        normed_one, factor_one, grad_hidden_one * (1.0 + scale_one)
    )
    grad_modulation = jnp.concatenate(
        [
            shift_one_grad,
            scale_one_grad,
            gate_one_grad,
            shift_two_grad,
            scale_two_grad,
            gate_two_grad,
        ]
    ).astype(jnp.bfloat16)
    width = shape[1]
    column_sums = [
        jnp.sum(member, axis=0, dtype=jnp.float32)
        for member in (
            grad_projected[:, :width],
            grad_projected[:, 2 * width :],
            grad_attention,
            grad_expanded,
            grad_branch,
        )
    ]
    matrix_grads = (
        outer_sum(hidden_one, grad_projected),
        outer_sum(attended, grad_attention),
        outer_sum(hidden_two, grad_expanded),
        outer_sum(activated, grad_branch),
    )
    return grad_inputs, grad_modulation, jnp.concatenate(column_sums), matrix_grads


def pair_swap(block, axis):
    return lax.ppermute(block, axis, [(0, 1), (1, 0)])


def ring_exchange(block, size, step):
    route = [(i, step(i)) for i in range(size)]
    return lax.ppermute(block, RING, route)


def scatter_sum(block, rank, size):
    half = block.shape[-1] // 2
    pieces = [block[..., :half], block[..., half:]]
    left = size
    low_bits = 0
    while left > 4:
        orders = [(0, 1), (1, 0)] if left % 4 == 0 and left >= 16 else [(0,), (0,)]
        for turn in range(len(orders[0])):
            updated = []
            for piece, order in zip(pieces, orders):
                bit = low_bits + order[turn]
                mine = (rank >> bit) & 1
                if len(order) == 2 and turn == 0:
                    shaped = piece.reshape(-1, 2, 2, *piece.shape[1:])
                    at = 2 - order[turn]
                else:
                    shaped = piece.reshape(-1, 2, *piece.shape[1:])
                    at = 1
                keep = lax.dynamic_index_in_dim(shaped, mine, at, keepdims=False)
                send = lax.dynamic_index_in_dim(shaped, 1 - mine, at, keepdims=False)
                got = ring_exchange(send, size, lambda i, bit=bit: i ^ (1 << bit))
                total = (keep.astype(jnp.float32) + got.astype(jnp.float32)).astype(jnp.bfloat16)
                updated.append(total.reshape(-1, *piece.shape[1:]))
            pieces = updated
        low_bits += len(orders[0])
        left //= 2 ** len(orders[0])
    block = jnp.concatenate(pieces, axis=-1)
    high = rank >> low_bits
    total = lax.dynamic_index_in_dim(block, high, 0, keepdims=False).astype(jnp.float32)
    stride = 1 << low_bits
    for turn in range(1, left):
        send = lax.dynamic_index_in_dim(block, (high + turn) % left, 0, keepdims=False)
        got = ring_exchange(send, size, lambda i, turn=turn: (i + turn * stride) % size)
        total = total + got.astype(jnp.float32)
    return total


def per_device(
    inputs,
    cotangent,
    time_ids,
    row_counts,
    cond_table,
    modulation_weight,
    attention_weight,
    output_weight,
    expand_weight,
    shrink_weight,
    biases,
):
    section_rank = lax.axis_index("section")
    data_rank = lax.axis_index("dp")
    seq_rank = lax.axis_index("seq")
    sections = lax.axis_size("section")
    seq_size = lax.axis_size("seq")
    ring_size = lax.axis_size("dp") * seq_size
    ring_rank = data_rank * seq_size + seq_rank
    batches, slots, tokens, width = inputs.shape
    assert batches == sections == 2 and seq_size % slots == 0
    sharers = seq_size // slots
    slot = seq_rank // sharers
    length = tokens * seq_size
    rows = attention_weight.shape[1]
    ratio = shrink_weight.shape[1] // rows
    hidden = ratio * width
    bias_columns = biases.shape[1] // rows
    table_rows = cond_table.shape[0]

    packed = jnp.concatenate(
        [
            attention_weight[0],
            output_weight[0],
            expand_weight[0],
            shrink_weight[0].reshape(rows, ratio, width).reshape(rows, ratio * width),
            modulation_weight[0],
            jnp.pad(biases.reshape(rows, bias_columns), ((0, 0), (0, 128 - bias_columns))),
        ],
        axis=1,
    )
    own_pack = lax.all_gather(packed, RING, axis=0, tiled=True)
    other_pack = pair_swap(own_pack, "section")

    def unpack(pack):
        edges = [0, 3 * width, 4 * width, 4 * width + hidden, 4 * width + 2 * hidden]
        att, out, up, down = [pack[:, a:b] for a, b in zip(edges[:-1], edges[1:])]
        down = down.reshape(hidden, width)
        modulation_matrix = pack[:, edges[-1] : edges[-1] + 6 * width]
        bias = pack[:, edges[-1] + 6 * width :][:, :bias_columns].reshape(-1).astype(jnp.float32)
        cuts = [6 * width, 7 * width, 8 * width, 9 * width, 9 * width + hidden]
        return modulation_matrix, (att, out, up, down, jnp.split(bias, cuts))

    is_first = section_rank == 0
    first_mod, first_weights = unpack(jnp.where(is_first, own_pack, other_pack))
    second_mod, second_weights = unpack(jnp.where(is_first, other_pack, own_pack))

    both = jnp.stack(
        [
            lax.dynamic_index_in_dim(inputs, section_rank, 0, keepdims=False),
            lax.dynamic_index_in_dim(cotangent, section_rank, 0, keepdims=False),
        ],
        axis=1,
    )
    both = jnp.repeat(both, sharers, axis=0)
    both = lax.all_to_all(both, "seq", 0, 0, tiled=True)
    both = jnp.swapaxes(both, 0, 1).reshape(2, length, width)
    live = (
        slot < lax.dynamic_index_in_dim(row_counts, section_rank, 0, keepdims=False)[0]
    ).astype(jnp.float32)
    flat_ids = time_ids.reshape(-1)
    selector = (
        flat_ids[:, None] == jnp.arange(table_rows, dtype=jnp.int32)[None, :]
    ).astype(jnp.bfloat16)
    conditions = matmul(selector, cond_table)
    silu_all = jax.nn.silu(conditions).astype(jnp.bfloat16)
    latent = section_rank * time_ids.shape[1] + data_rank * slots + slot
    condition = lax.dynamic_slice_in_dim(conditions, latent, 1, 0)
    silu_now = lax.dynamic_slice_in_dim(silu_all, latent, 1, 0)

    def members_of(modulation_matrix, weights):
        return jnp.split(matmul(silu_now, modulation_matrix) + weights[4][0], 6, axis=-1)

    first_input = both[0].astype(jnp.float32)
    first_members = members_of(first_mod, first_weights)
    second_members = members_of(second_mod, second_weights)
    first_out, first_kept = forward(first_input, first_members, first_weights)
    first_low = first_out.astype(jnp.bfloat16)
    second_input = first_low.astype(jnp.float32)
    second_out, second_kept = forward(second_input, second_members, second_weights)
    second_grad, second_dmod, second_sums, second_terms = backward(
        both[1].astype(jnp.float32) * live,
        second_input,
        second_members,
        second_weights,
        second_kept,
    )
    second_grad_low = second_grad.astype(jnp.bfloat16)
    first_grad, first_dmod, first_sums, first_terms = backward(
        second_grad_low.astype(jnp.float32),
        first_input,
        first_members,
        first_weights,
        first_kept,
    )

    def to_owners(first, second):
        pieces = jnp.stack([first, second]).reshape(2 * seq_size, tokens, width)
        pieces = lax.all_to_all(pieces, ("section", "seq"), 0, 0, tiled=True)
        return pieces.reshape(batches, slots, sharers, tokens, width)[:, :, 0]

    live_low = live.astype(jnp.bfloat16)
    activations = to_owners(first_low * live_low, second_out.astype(jnp.bfloat16) * live_low)
    input_grads = to_owners(first_grad.astype(jnp.bfloat16), second_grad_low).astype(jnp.float32)

    def pack_terms(terms):
        att, out, up, down = [term * (1.0 / sharers) for term in terms]
        down = down.reshape(width, ratio * width)
        whole = jnp.concatenate([att, out, up, down], axis=1).astype(jnp.bfloat16)
        half = whole.shape[1] // 2
        return jnp.stack([whole[:, :half], whole[:, half:]])

    halves = jnp.stack([pack_terms(first_terms), pack_terms(second_terms)], axis=1)
    keep = lax.dynamic_index_in_dim(halves, section_rank, 0, keepdims=False)
    send = lax.dynamic_index_in_dim(halves, 1 - section_rank, 0, keepdims=False)
    chip_sum = (
        keep.astype(jnp.float32) + pair_swap(send, "section").astype(jnp.float32)
    ).astype(jnp.bfloat16)
    half = chip_sum.shape[-1]
    ring_terms = jnp.swapaxes(chip_sum.reshape(2, ring_size, rows, half), 0, 1)
    owned = scatter_sum(ring_terms.reshape(ring_size, 2 * rows, half), ring_rank, ring_size)
    owned = owned.reshape(2, rows, half)
    mine = lax.dynamic_index_in_dim(owned, section_rank, 0, keepdims=False)
    theirs = pair_swap(
        lax.dynamic_index_in_dim(owned, 1 - section_rank, 0, keepdims=False), "section"
    )
    full = jnp.where(
        is_first,
        jnp.concatenate([mine, theirs], axis=1),
        jnp.concatenate([theirs, mine], axis=1),
    )
    edges = [0, 3 * width, 4 * width, 4 * width + hidden, 4 * width + 2 * hidden]
    att, out, up, down = [full[:, a:b] for a, b in zip(edges[:-1], edges[1:])]
    down = down.reshape(rows * ratio, width)

    _, silu_back = jax.vjp(jax.nn.silu, condition)
    grad_condition = silu_back(
        matmul_transposed(first_dmod[None], first_mod)
        + matmul_transposed(second_dmod[None], second_mod)
    )[0][0]
    row = jnp.concatenate(
        [
            first_dmod.astype(jnp.float32),
            first_sums,
            second_dmod.astype(jnp.float32),
            second_sums,
            grad_condition,
        ]
    )
    every = lax.all_gather(row[None], ("section", "dp", "seq"), axis=0, tiled=True)
    every = every[::sharers]
    per_section = every[:, : 2 * bias_columns * width].reshape(every.shape[0], 2, -1)
    section_rows = lax.dynamic_index_in_dim(per_section, section_rank, 1, keepdims=False)
    bias_total = jnp.sum(section_rows, axis=0)
    bias_grad = lax.dynamic_slice_in_dim(
        bias_total, ring_rank * biases.shape[1], biases.shape[1], 0
    )
    silu_own = lax.dynamic_slice_in_dim(silu_all, ring_rank * rows, rows, 1)
    modulation_grad = outer_sum(silu_own, section_rows[:, : 6 * width].astype(jnp.bfloat16))
    table_grad = lax.dot_general(
        selector.astype(jnp.float32),
        every[:, 2 * bias_columns * width :],
        (((0,), (0,)), ((), ())),
        precision=lax.Precision.HIGHEST,
        preferred_element_type=jnp.float32,
    )
    return (
        activations[None],
        input_grads[None],
        table_grad,
        modulation_grad[None],
        att[None],
        out[None],
        up[None],
        down[None],
        bias_grad[None],
    )


def solution(mesh):
    shard = P("section", ("dp", "seq"), None)
    in_specs = (
        P(None, "dp", "seq", None),
        P(None, "dp", "seq", None),
        P(),
        P(None, "dp"),
        P(),
        shard,
        shard,
        shard,
        shard,
        shard,
        P("section", ("dp", "seq")),
    )
    out_specs = (
        P("section", None, "dp", "seq", None),
        P("section", None, "dp", "seq", None),
        P(),
        shard,
        shard,
        shard,
        shard,
        shard,
        P("section", ("dp", "seq")),
    )
    return jax.shard_map(
        per_device, mesh=mesh, in_specs=in_specs, out_specs=out_specs, check_vma=False
    )
```

time: 1380 us -> 377 us (0.27)
  waiting for transfers between devices: 791 us -> 150 us
  blocking collectives: 207 us -> 0 us
  local copies, waits for them, and re-layouts: 157 us -> 73.5 us
  other arithmetic: 109 us -> 43.2 us
    reduce_scatter x9 -> x0, waiting for transfers between devices: 450 us -> none  [the longest x3 403 us: per_device(): lax.psum_scatter(grad_terms, ('dp', 'seq'), scatter_dimension=1, tiled=True)]
    unnamed x18 -> x2, waiting for transfers between devices: 309 us -> 0.03 us
    all_gather x9 -> x0, blocking collectives: 143 us -> none  [the longest x1 38.5 us: per_device(): lax.all_gather(shards[1], ('dp', 'seq'), axis=1, tiled=True)]
    all_gather x3 -> x2, waiting for transfers between devices: 32.4 us -> 94.1 us  [the longest x1 86.3 us: per_device(): own_pack = lax.all_gather(packed, RING, axis=0, tiled=True)]
    unnamed x1 -> x0, blocking collectives: 57.9 us -> none
    dynamic_update_slice x51 -> x0, other arithmetic: 49.6 us -> none  [store(): return lax.dynamic_update_index_in_dim(buffer, updated, position, 0)]
    dynamic_slice x41 -> x4, local copies, waits for them, and re-layouts: 47.2 us -> 2.76 us  [the longest x1 1.06 us: scatter_sum(): keep = lax.dynamic_index_in_dim(shaped, mine, at, keepdims=False)]
    all_to_all x0 -> x3, waiting for transfers between devices: none -> 28.8 us  [the longest x2 24.4 us: to_owners(): pieces = lax.all_to_all(pieces, ('section', 'seq'), 0, 0, tiled=True)]
  transfers between devices with their start and end apart: 19 -> 15, of which waited for: 11 -> 10; matrix products, arithmetic and copies ran while one was open for 11% -> 18% of each run, Pallas kernels for 0% -> 0%
where the time goes in v1:
time: 377 us; the launch traced here: 370 us
  waiting for transfers between devices  150 us (40%)
  local copies, waits for them, and re-layouts  73.5 us (19%)
  matrix products  65.6 us (17%)
  other arithmetic  43.2 us (11%)
  starting transfers between devices  21.4 us (6%)
  between operations  16.7 us (4%)
    all_gather x1, waiting for transfers between devices, per_device(): own_pack = lax.all_gather(packed, RING, axis=0, tiled=True)  86.3 us
    unnamed x245, local copies, waits for them, and re-layouts  27.5 us
    ppermute x7, waiting for transfers between devices, ring_exchange(): return lax.ppermute(block, RING, route)  26.7 us
    all_to_all x2, waiting for transfers between devices, to_owners(): pieces = lax.all_to_all(pieces, ('section', 'seq'), 0, 0, tiled=True)  24.4 us
    dot_general x10, matrix products, matmul_transposed(): lax.dot_general(former, latter, (((1,), (1,)), ((), ())), preferred_eleme...  22.7 us
    dot_general x11, matrix products, matmul(): return jnp.dot(former, latter, preferred_element_type=jnp.float32)  19.2 us
    dot_general x9, matrix products, outer_sum(): lax.dot_general(former, latter, (((0,), (0,)), ((), ())), preferred_eleme...  11 us
    select_n x1, other arithmetic, per_device(): first_mod, first_weights = unpack(jnp.where(is_first, own_pack, other_pack))  9.19 us
  transfers between devices with their start and end apart: 15, of which 10 were waited for; matrix products, arithmetic and copies ran while one was open for 18% of the time, Pallas kernels for 0%

profile of v1, /device:TPU:9, one launch (start us, length us, event | category | flops | bytes accessed | tf_op | source)
XLA Modules:
  0.0 370.1 jit_solution(14787306759159518034)
XLA Ops:
  13.2 86.3 %all-gather.5.cloned.1.call-done = bf16[384,7040]{1,0:T(8,128)(2,1)} async-done(((bf16[24,7040]{1,0:T(8,128)(2,1)}), bf16[384,7040]{1,0:T(8,128)(2,1)}) %all-gather.5.cloned.1.call-update) | async-done | bytes 5406736 | tf_op jit(solution)/shard_map/all_gather | solution.py:279
  103.3 3.5 all-to-all-start
  109.1 4.4 %all-to-all-done = bf16[2,2,128,384]{3,2,1,0:T(8,128)(2,1)S(1)} async-done(((bf16[2,2,128,384]{3,2,1,0:T(8,128)(2,1)}), bf16[2,2,128,384]{3,2,1,0:T(8,128)(2,1)S(1)}, u32[]{:S(2)}, u32[]{:S(2)}) %all-to-all-start) | async-done | bytes 393248 | tf_op jit(solution)/shard_map/all_to_all | solution.py:303
  113.6 9.2 %broadcast_select_fusion.1 = (bf16[384,7040]{1,0:T(8,128)(2,1)}, bf16[384,7040]{1,0:T(8,128)(2,1)}) fusion(bf16[384,7040]{1,0:T(8,128)(2,1)} %all-gather.5.cloned.1.call-done, bf16[384,7040]{1,0:T(8,128)(2,1)} %collective-permute-done, pred[]{:T(512)S(6)} %eq.26), kind=kLoop, calls=%fused_computation.7 | loop fusion | flops 5406720 | bytes 21626880 | tf_op jit(solution)/shard_map/jit(_where)/select_n | solution.py:292
  144.6 2.1 fusion.158
  161.3 2.1 fusion.157
  163.6 2.0 convolution_add_fusion
  165.7 2.0 convert_reduce_fusion
  167.7 2.6 multiply_reduce_fusion.2
  170.3 2.3 fusion.91
  179.0 2.1 convert_reduce_fusion.6
  183.4 2.6 fusion.82
  187.5 2.2 convert_reduce_fusion.1
  193.2 2.6 multiply_reduce_fusion.4
  208.0 3.2 reshape.366
  216.3 2.3 fusion.2
  233.1 3.4 fusion.106
  240.7 2.8 multiply_reduce_fusion.5
  250.2 2.1 fusion.48
  252.3 2.1 fusion.45
  256.8 3.4 fusion
  263.0 4.1 %all-to-all-start.1 = ((bf16[4,128,384]{2,1,0:T(8,128)(2,1)}), bf16[4,128,384]{2,1,0:T(8,128)(2,1)}, u32[]{:S(2)}, u32[]{:S(2)}) async-start(bf16[4,128,384]{2,1,0:T(8,128)(2,1)} %bitcast.262), calls=%async_computation.1 | async-start | bytes 786432 | tf_op jit(solution)/shard_map/all_to_all | solution.py:346
  268.9 19.6 %all-to-all-done.1 = bf16[4,128,384]{2,1,0:T(8,128)(2,1)} async-done(((bf16[4,128,384]{2,1,0:T(8,128)(2,1)}), bf16[4,128,384]{2,1,0:T(8,128)(2,1)}, u32[]{:S(2)}, u32[]{:S(2)}) %all-to-all-start.1) | async-done | bytes 393248 | tf_op jit(solution)/shard_map/all_to_all | solution.py:346
  288.5 4.9 %all-to-all-start.2 = ((bf16[4,128,384]{2,1,0:T(8,128)(2,1)}), bf16[4,128,384]{2,1,0:T(8,128)(2,1)}, u32[]{:S(2)}, u32[]{:S(2)}) async-start(bf16[4,128,384]{2,1,0:T(8,128)(2,1)} %bitcast.261), calls=%async_computation.2 | async-start | bytes 786432 | tf_op jit(solution)/shard_map/all_to_all | solution.py:346
  296.7 4.9 %all-to-all-done.2 = bf16[4,128,384]{2,1,0:T(8,128)(2,1)} async-done(((bf16[4,128,384]{2,1,0:T(8,128)(2,1)}), bf16[4,128,384]{2,1,0:T(8,128)(2,1)}, u32[]{:S(2)}, u32[]{:S(2)}) %all-to-all-start.2) | async-done | bytes 393248 | tf_op jit(solution)/shard_map/all_to_all | solution.py:346
  303.5 7.9 %all-gather.7.cloned.1.call-done = f32[32,1,11136]{2,1,0:T(1,128)} async-done(((f32[1,1,11136]{2,1,0:T(1,128)}), f32[32,1,11136]{2,1,0:T(1,128)}) %all-gather.7.cloned.1.call-update) | async-done | bytes 1425424 | tf_op jit(solution)/shard_map/all_gather | solution.py:397
  313.9 3.3 reshape.365
  322.5 7.9 %collective-permute-done.3 = bf16[4,48,1152]{2,1,0:T(8,128)(2,1)S(1)} collective-permute-done((bf16[4,48,1152]{2,1,0:T(8,128)(2,1)S(1)}, bf16[4,48,1152]{2,1,0:T(8,128)(2,1)S(1)}, u32[]{:S(2)}, u32[]{:S(2)}) %collective-permute-start.3) | collective-permute-done | bytes 442400 | tf_op jit(solution)/shard_map/ppermute | solution.py:197
  330.5 2.3 collective-permute-done.5
  339.3 11.6 %collective-permute-done.7 = bf16[48,2304]{1,0:T(8,128)(2,1)S(1)} collective-permute-done((bf16[48,2304]{1,0:T(8,128)(2,1)S(1)}, bf16[48,2304]{1,0:T(8,128)(2,1)S(1)}, u32[]{:S(2)}, u32[]{:S(2)}) %collective-permute-start.7) | collective-permute-done | bytes 221216 | tf_op jit(solution)/shard_map/ppermute | solution.py:197
  350.9 4.5 %collective-permute-done.8 = bf16[48,2304]{1,0:T(8,128)(2,1)S(1)} collective-permute-done((bf16[48,2304]{1,0:T(8,128)(2,1)S(1)}, bf16[48,2304]{1,0:T(8,128)(2,1)S(1)}, u32[]{:S(2)}, u32[]{:S(2)}) %collective-permute-start.8) | collective-permute-done | bytes 221216 | tf_op jit(solution)/shard_map/ppermute | solution.py:197
  356.1 2.2 fusion.131
  (413 shorter events, 135.2 us)
Async XLA Ops:
  7.2 101.0 %copy-start = (bf16[1000,384]{1,0:T(8,128)(2,1)S(1)}, bf16[1000,384]{1,0:T(8,128)(2,1)}, u32[]{:S(2)}) copy-start(bf16[1000,384]{1,0:T(8,128)(2,1)} %param.15) | copy-start | bytes 2304004
  7.2 92.3 %all-gather.5.cloned.1.call-start = ((), (), s32[]{:S(2)}) async-start(), calls=%async_computation.3 | async-start | bytes 5744640 | tf_op jit(solution)/shard_map/all_gather | solution.py:279
  11.5 95.3 %copy-start.106 = (s32[2,1]{0,1:T(1,128)S(1)}, s32[2,1]{0,1:T(1,128)}, u32[]{:S(2)}) copy-start(s32[2,1]{0,1:T(1,128)} %param.14) | copy-start | bytes 28
  11.5 96.6 %copy-start.105 = (s32[2,16]{1,0:T(2,128)S(1)}, s32[2,16]{1,0:T(2,128)}, u32[]{:S(2)}) copy-start(s32[2,16]{1,0:T(2,128)} %param.13) | copy-start | bytes 388
  99.5 14.2 %collective-permute-start = (bf16[384,7040]{1,0:T(8,128)(2,1)}, bf16[384,7040]{1,0:T(8,128)(2,1)}, u32[]{:S(2)}, u32[]{:S(2)}) collective-permute-start(bf16[384,7040]{1,0:T(8,128)(2,1)} %all-gather.5.cloned.1.call-done), channel_id=1, source_target_pairs={{0,16},{16,0},{1,17},{17,1},{2,18},{18,2},{3,19},{19,3},{4,20},{20... | collective-permute-start | bytes 16220168 | tf_op jit(solution)/shard_map/ppermute | solution.py:192
  103.3 10.2 %all-to-all-start = ((bf16[2,2,128,384]{3,2,1,0:T(8,128)(2,1)}), bf16[2,2,128,384]{3,2,1,0:T(8,128)(2,1)S(1)}, u32[]{:S(2)}, u32[]{:S(2)}) async-start(bf16[2,2,128,384]{3,2,1,0:T(8,128)(2,1)} %pad_maximum_fusion.8), calls=%async_computation | async-start | bytes 786432 | tf_op jit(solution)/shard_map/all_to_all | solution.py:303
  106.8 204.6 %all-gather.7.cloned.1.call-start = ((), (), s32[]{:S(2)}) async-start(), calls=%async_computation.4 | async-start | bytes 1469952 | tf_op jit(solution)/shard_map/all_gather | solution.py:397
  108.2 14.7 %copy-start.103 = (s32[32]{0:T(128)}, s32[32]{0:T(128)S(1)}, u32[]{:S(2)}) copy-start(s32[32]{0:T(128)S(1)} %eq.22) | copy-start | bytes 388
  109.1 15.6 %copy-start.51 = (bf16[32,384]{1,0:T(8,128)(2,1)}, bf16[32,384]{1,0:T(8,128)(2,1)S(1)}, u32[]{:S(2)}) copy-start(bf16[32,384]{1,0:T(8,128)(2,1)S(1)} %get-tuple-element.99) | copy-start | bytes 73732
  113.5 31.1 %copy-start.8 = (bf16[2,2,128,384]{3,2,1,0:T(8,128)(2,1)}, bf16[2,2,128,384]{3,2,1,0:T(8,128)(2,1)S(1)}, u32[]{:S(2)}) copy-start(bf16[2,2,128,384]{3,2,1,0:T(8,128)(2,1)S(1)} %all-to-all-done) | copy-start | bytes 1179652
  113.6 21.6 %copy-start.81 = (f32[256]{0:T(256)}, f32[256]{0:T(256)S(1)}, u32[]{:S(2)}) copy-start(f32[256]{0:T(256)S(1)} %get-tuple-element.97) | copy-start | bytes 3076
  163.4 12.2 %copy-start.3 = (f32[256,384]{1,0:T(8,128)}, f32[256,384]{1,0:T(8,128)S(1)}, u32[]{:S(2)}) copy-start(f32[256,384]{1,0:T(8,128)S(1)} %get-tuple-element.53) | copy-start | bytes 1179652
  187.0 10.5 %copy-start.14 = (bf16[256,384]{1,0:T(8,128)(2,1)}, bf16[256,384]{1,0:T(8,128)(2,1)S(1)}, u32[]{:S(2)}) copy-start(bf16[256,384]{1,0:T(8,128)(2,1)S(1)} %get-tuple-element.49) | copy-start | bytes 589828
  216.3 7.8 %copy-start.99 = (bf16[384]{0:T(512)(128)(2,1)S(1)}, bf16[384]{0:T(512)(128)(2,1)}, u32[]{:S(2)}) copy-start(bf16[384]{0:T(512)(128)(2,1)} %get-tuple-element.82) | copy-start | bytes 2308
  216.3 16.8 %copy-start.63 = (f32[384]{0:T(512)S(1)}, f32[384]{0:T(512)}, u32[]{:S(2)}) copy-start(f32[384]{0:T(512)} %copy-done.62) | copy-start | bytes 4612
  219.1 37.7 %collective-permute-start.1 = (bf16[2,384,2304]{2,1,0:T(8,128)(2,1)}, bf16[2,384,2304]{2,1,0:T(8,128)(2,1)}, u32[]{:S(2)}, u32[]{:S(2)}) collective-permute-start(bf16[2,384,2304]{2,1,0:T(8,128)(2,1)} %fusion.2), channel_id=1, source_target_pairs={{0,16},{16,0},{1,17},{17,1},{2,18},{18,2},{3,19},{19,3},{4,20},{20... | collective-permute-start | bytes 10616840 | tf_op jit(solution)/shard_map/ppermute | solution.py:192
  250.2 5.8 %copy-start.92 = (f32[384]{0:T(512)S(1)}, f32[384]{0:T(512)}, u32[]{:S(2)}) copy-start(f32[384]{0:T(512)} %reduce_sum.469) | copy-start | bytes 4612
  250.2 5.8 %copy-start.100 = (f32[384]{0:T(512)S(1)}, f32[384]{0:T(512)}, u32[]{:S(2)}) copy-start(f32[384]{0:T(512)} %get-tuple-element.79) | copy-start | bytes 4612
  250.2 5.9 %copy-start.96 = (f32[1536]{0:T(1024)S(1)}, f32[1536]{0:T(1024)}, u32[]{:S(2)}) copy-start(f32[1536]{0:T(1024)} %get-tuple-element.41) | copy-start | bytes 18436
  250.2 5.9 %copy-start.83 = (f32[384]{0:T(512)S(1)}, f32[384]{0:T(512)}, u32[]{:S(2)}) copy-start(f32[384]{0:T(512)} %get-tuple-element.87) | copy-start | bytes 4612
  261.7 55.5 %collective-permute-start.2 = (bf16[4,2,48,1152]{3,2,1,0:T(8,128)(2,1)}, bf16[4,2,48,1152]{3,2,1,0:T(8,128)(2,1)}, u32[]{:S(2)}, u32[]{:S(2)}) collective-permute-start(bf16[4,2,48,1152]{3,2,1,0:T(8,128)(2,1)} %dynamic-slice_bitcast_fusion), channel_id=1, source_target_pairs={{0,1},{1,0},{2,3},{3,2},{4,5},{5,4},{6,7},{7,6},{8,9},{9,8},{10,11... | collective-permute-start | bytes 2654216 | tf_op jit(solution)/shard_map/ppermute | solution.py:197
  263.0 25.5 %all-to-all-start.1 = ((bf16[4,128,384]{2,1,0:T(8,128)(2,1)}), bf16[4,128,384]{2,1,0:T(8,128)(2,1)}, u32[]{:S(2)}, u32[]{:S(2)}) async-start(bf16[4,128,384]{2,1,0:T(8,128)(2,1)} %bitcast.262), calls=%async_computation.1 | async-start | bytes 786432 | tf_op jit(solution)/shard_map/all_to_all | solution.py:346
  288.5 13.0 %all-to-all-start.2 = ((bf16[4,128,384]{2,1,0:T(8,128)(2,1)}), bf16[4,128,384]{2,1,0:T(8,128)(2,1)}, u32[]{:S(2)}, u32[]{:S(2)}) async-start(bf16[4,128,384]{2,1,0:T(8,128)(2,1)} %bitcast.261), calls=%async_computation.2 | async-start | bytes 786432 | tf_op jit(solution)/shard_map/all_to_all | solution.py:346
  295.5 24.5 %collective-permute-start.4 = (bf16[4,2,48,1152]{3,2,0,1:T(8,128)(2,1)}, bf16[4,2,48,1152]{3,2,0,1:T(8,128)(2,1)}, u32[]{:S(2)}, u32[]{:S(2)}) collective-permute-start(bf16[4,2,48,1152]{3,2,0,1:T(8,128)(2,1)} %bitcast.224), channel_id=1, source_target_pairs={{0,2},{1,3},{2,0},{3,1},{4,6},{5,7},{6,4},{7,5},{8,10},{9,11},{10,... | collective-permute-start | bytes 2654216 | tf_op jit(solution)/shard_map/ppermute | solution.py:197
  318.8 11.6 %collective-permute-start.3 = (bf16[4,48,1152]{2,1,0:T(8,128)(2,1)S(1)}, bf16[4,48,1152]{2,1,0:T(8,128)(2,1)S(1)}, u32[]{:S(2)}, u32[]{:S(2)}) collective-permute-start(bf16[4,48,1152]{2,1,0:T(8,128)(2,1)S(1)} %dynamic-slice_bitcast_fusion.2), channel_id=1, source_target_pairs={{0,2},{1,3},{2,0},{3,1},{4,6},{5,7},{6,4},{7,5},{8,10},{9,11},{10,... | collective-permute-start | bytes 1327112 | tf_op jit(solution)/shard_map/ppermute | solution.py:197
  321.4 11.4 %collective-permute-start.5 = (bf16[4,48,1152]{2,1,0:T(8,128)(2,1)S(1)}, bf16[4,48,1152]{2,1,0:T(8,128)(2,1)S(1)}, u32[]{:S(2)}, u32[]{:S(2)}) collective-permute-start(bf16[4,48,1152]{2,1,0:T(8,128)(2,1)S(1)} %dynamic-slice_bitcast_fusion.1), channel_id=1, source_target_pairs={{0,1},{1,0},{2,3},{3,2},{4,5},{5,4},{6,7},{7,6},{8,9},{9,8},{10,11... | collective-permute-start | bytes 1327112 | tf_op jit(solution)/shard_map/ppermute | solution.py:197
  333.0 6.3 %collective-permute-start.6 = (bf16[48,2304]{1,0:T(8,128)(2,1)S(1)}, bf16[48,2304]{1,0:T(8,128)(2,1)S(1)}, u32[]{:S(2)}, u32[]{:S(2)}) collective-permute-start(bf16[48,2304]{1,0:T(8,128)(2,1)S(1)} %get-tuple-element.70), channel_id=1, source_target_pairs={{0,4},{1,5},{2,6},{3,7},{4,8},{5,9},{6,10},{7,11},{8,12},{9,13},{1... | collective-permute-start | bytes 663560 | tf_op jit(solution)/shard_map/ppermute | solution.py:197
  333.5 17.4 %collective-permute-start.7 = (bf16[48,2304]{1,0:T(8,128)(2,1)S(1)}, bf16[48,2304]{1,0:T(8,128)(2,1)S(1)}, u32[]{:S(2)}, u32[]{:S(2)}) collective-permute-start(bf16[48,2304]{1,0:T(8,128)(2,1)S(1)} %get-tuple-element.71), channel_id=1, source_target_pairs={{0,8},{1,9},{2,10},{3,11},{4,12},{5,13},{6,14},{7,15},{8,0},{9,1},... | collective-permute-start | bytes 663560 | tf_op jit(solution)/shard_map/ppermute | solution.py:197
  335.3 20.1 %collective-permute-start.8 = (bf16[48,2304]{1,0:T(8,128)(2,1)S(1)}, bf16[48,2304]{1,0:T(8,128)(2,1)S(1)}, u32[]{:S(2)}, u32[]{:S(2)}) collective-permute-start(bf16[48,2304]{1,0:T(8,128)(2,1)S(1)} %get-tuple-element.72), channel_id=1, source_target_pairs={{0,12},{1,13},{2,14},{3,15},{4,0},{5,1},{6,2},{7,3},{8,4},{9,5},{1... | collective-permute-start | bytes 663560 | tf_op jit(solution)/shard_map/ppermute | solution.py:197
  337.6 18.6 %copy-start.104 = (s32[32]{0:T(128)S(1)}, s32[32]{0:T(128)}, u32[]{:S(2)}) copy-start(s32[32]{0:T(128)} %copy-done.103) | copy-start | bytes 388
  355.6 2.8 collective-permute-start.9
  356.1 6.7 %copy-start.1 = (bf16[1000,384]{1,0:T(8,128)(2,1)S(1)}, bf16[1000,384]{1,0:T(8,128)(2,1)}, u32[]{:S(2)}) copy-start(bf16[1000,384]{1,0:T(8,128)(2,1)} %param.15) | copy-start | bytes 2304004
  (91 other events, 221.3 us)
Sparse Core Ops, SparseCore 0:
  13.3 86.0 all-gather.4
  256.9 54.3 all-gather.6

commit v2 on v1

v2 whole, which is shorter than its diff:
```python
from functools import partial

import jax
import jax.numpy as jnp
from jax import lax
from jax.experimental import pallas as pl
from jax.experimental.pallas import tpu as pltpu
from jax.sharding import PartitionSpec as P

HEADS = 6
HEAD = 64
SCALE = HEAD ** (-0.5)
epsilon = 1e-06
RING = ("dp", "seq")
INNER = (2.0 / 3.141592653589793) ** 0.5
CUBE = 0.044715


def matmul(former, latter):
    return jnp.dot(former, latter, preferred_element_type=jnp.float32)


def matmul_transposed(former, latter):
    return lax.dot_general(
        former, latter, (((1,), (1,)), ((), ())), preferred_element_type=jnp.float32
    )


def outer_sum(former, latter):
    return lax.dot_general(
        former, latter, (((0,), (0,)), ((), ())), preferred_element_type=jnp.float32
    )


def low(values):
    return values.astype(jnp.bfloat16)


def normalize_rows(values):
    centre = jnp.mean(values, axis=-1, keepdims=True)
    centred = values - centre
    spread = jnp.mean(centred * centred, axis=-1, keepdims=True)
    factor = lax.rsqrt(spread + epsilon)
    return (centred * factor, factor)


def normalize_back(normed, factor, grad_normed):
    mean_grad = jnp.mean(grad_normed, axis=-1, keepdims=True)
    mean_cross = jnp.mean(grad_normed * normed, axis=-1, keepdims=True)
    return factor * (grad_normed - mean_grad - normed * mean_cross)


def column_sum(values):
    return jnp.sum(values.astype(jnp.float32), axis=0, keepdims=True)


def section_kernel(layout, backward, *refs):
    width, hidden, rows, ratio, ring_size, share, bias_count = layout
    own_ref, x_ref, silu_ref = refs[:3]
    refs = refs[3:]
    if backward:
        dy_ref = refs[0]
        refs = refs[1:]
    pack_refs = refs[:2]
    refs = refs[2:]
    if backward:
        y_ref, dx_ref, row_ref, keep_ref, send_ref = refs[:5]
        refs = refs[5:]
    else:
        y_ref = refs[0]
        refs = refs[1:]
    mod_w, att_w, out_w, up_w, down_p, bias_p, sems = refs[:7]
    bias_s, down_w, down_s, block_s, qkv_s, att_s, u_s = refs[7:14]
    if backward:
        soft_s, slope_s, da_s, dqkv_s, halves, out_sems = refs[14:]

    own = own_ref[0] == 1
    held = (att_w, out_w, up_w, mod_w, down_p, bias_p)
    sizes = (3 * width, width, hidden, 6 * width, hidden, 128)
    starts = [sum(sizes[:i]) for i in range(len(sizes))]

    def fetches(source):
        return [
            pltpu.make_async_copy(
                pack_refs[source].at[:, start : start + size], target, sems.at[i]
            )
            for i, (target, start, size) in enumerate(zip(held, starts, sizes))
        ]

    @pl.when(own)
    def _():
        for copy in fetches(0):
            copy.start()

    @pl.when(jnp.logical_not(own))
    def _():
        for copy in fetches(1):
            copy.start()

    arrivals = fetches(0)

    def bias(a, b):
        return bias_s[:, a:b]

    x = x_ref[...].astype(jnp.float32)
    normed_one, factor_one = normalize_rows(x)
    arrivals[5].wait()
    bias_rows = bias_p[...].astype(jnp.float32)
    for d in range(ring_size):
        for i in range(0, bias_count, 128):
            wide = min(128, bias_count - i)
            start = d * bias_count + i
            row = d * rows + i // 128
            bias_s[:, start : start + wide] = bias_rows[row : row + 1, :wide]
    arrivals[3].wait()
    modulation = matmul(silu_ref[...], mod_w[...])[0:1, :] + bias(0, 6 * width)
    shift_one, scale_one, gate_one, shift_two, scale_two, gate_two = [
        modulation[:, i * width : (i + 1) * width] for i in range(6)
    ]
    hidden_one = low(normed_one * (1.0 + scale_one) + shift_one)
    at = 6 * width
    arrivals[0].wait()
    qkv_s[:, :width] = low(matmul(hidden_one, att_w[:, :width]) + bias(at, at + width))
    qkv_s[:, width : 2 * width] = low(matmul(hidden_one, att_w[:, width : 2 * width]))
    qkv_s[:, 2 * width :] = low(
        matmul(hidden_one, att_w[:, 2 * width :]) + bias(at + width, at + 2 * width)
    )

    def part(ref, member, head):
        start = member * width + head * HEAD
        return ref[:, start : start + HEAD]

    for head in range(HEADS):
        scores = matmul_transposed(part(qkv_s, 0, head), part(qkv_s, 1, head)) * SCALE
        raised = jnp.exp(scores - jnp.max(scores, axis=-1, keepdims=True))
        soft = raised * (1.0 / jnp.sum(raised, axis=-1, keepdims=True))
        if backward:
            soft_s[head] = soft
        attended = matmul(low(soft), part(qkv_s, 2, head))
        att_s[:, head * HEAD : (head + 1) * HEAD] = low(attended)
    arrivals[1].wait()
    branch_one = matmul(att_s[...], out_w[...]) + bias(at + 2 * width, at + 3 * width)
    middle = x + gate_one * branch_one
    normed_two, factor_two = normalize_rows(middle)
    hidden_two = low(normed_two * (1.0 + scale_two) + shift_two)
    arrivals[2].wait()
    at += 3 * width
    for j in range(ratio):
        cut = slice(j * width, (j + 1) * width)
        a = matmul(hidden_two, up_w[:, cut]) + bias(at + j * width, at + (j + 1) * width)
        square = a * a
        turn = jnp.tanh(INNER * (a + CUBE * (a * square)))
        half_one = 0.5 * (1.0 + turn)
        u_s[:, cut] = low(a * half_one)
        if backward:
            slope_s[:, cut] = half_one + (0.5 * INNER) * a * (1.0 - turn * turn) * (
                1.0 + (3.0 * CUBE) * square
            )
    arrivals[4].wait()
    block_s[...] = down_p[...].astype(jnp.float32)
    for d in range(ring_size):
        for j in range(ratio):
            down_s[(d * ratio + j) * rows : (d * ratio + j + 1) * rows, :] = block_s[
                d * rows : (d + 1) * rows, j * width : (j + 1) * width
            ]
    down_w[...] = low(down_s[...])
    branch_two = matmul(u_s[...], down_w[...]) + bias(at + hidden, at + hidden + width)
    y_ref[...] = low(middle + gate_two * branch_two)
    if not backward:
        return

    grad_out = dy_ref[...].astype(jnp.float32)
    grad_branch = low(gate_two * grad_out)
    sums_at = 6 * width
    row_ref[:, 5 * width : 6 * width] = column_sum(grad_out * branch_two)
    row_ref[:, sums_at + 3 * width + hidden : sums_at + 4 * width + hidden] = column_sum(
        grad_branch
    )
    for j in range(ratio):
        cut = slice(j * width, (j + 1) * width)
        grad_expanded = low(slope_s[:, cut] * matmul_transposed(grad_branch, down_w[cut, :]))
        da_s[:, cut] = grad_expanded
        row_ref[:, sums_at + (3 + j) * width : sums_at + (4 + j) * width] = column_sum(
            grad_expanded
        )
    split = (4 * width + 2 * hidden) // 2 - 4 * width
    up_first = low(outer_sum(hidden_two, da_s[:, :split]) * share)
    halves[0, :, 4 * width :] = up_first
    halves[1, :, : hidden - split] = low(outer_sum(hidden_two, da_s[:, split:]) * share)
    down_s[...] = outer_sum(u_s[...], grad_branch) * share
    for d in range(ring_size):
        for j in range(ratio):
            block_s[d * rows : (d + 1) * rows, j * width : (j + 1) * width] = down_s[
                (d * ratio + j) * rows : (d * ratio + j + 1) * rows, :
            ]
    halves[1, :, hidden - split :] = low(block_s[...])
    rank = own_ref[1]
    second_out = [
        pltpu.make_async_copy(halves.at[1], keep_ref, out_sems.at[1]),
        pltpu.make_async_copy(halves.at[1], send_ref, out_sems.at[1]),
    ]

    @pl.when(rank == 1)
    def _():
        second_out[0].start()

    @pl.when(rank != 1)
    def _():
        second_out[1].start()

    grad_hidden_two = matmul_transposed(da_s[...], up_w[...])
    row_ref[:, 3 * width : 4 * width] = column_sum(grad_hidden_two)
    row_ref[:, 4 * width : 5 * width] = column_sum(grad_hidden_two * normed_two)
    grad_middle = grad_out + normalize_back(
        normed_two, factor_two, grad_hidden_two * (1.0 + scale_two)
    )
    row_ref[:, 2 * width : 3 * width] = column_sum(grad_middle * branch_one)
    grad_attention = low(gate_one * grad_middle)
    row_ref[:, sums_at + 2 * width : sums_at + 3 * width] = column_sum(grad_attention)
    halves[0, :, 3 * width : 4 * width] = low(outer_sum(att_s[...], grad_attention) * share)
    grad_attended = low(matmul_transposed(grad_attention, out_w[...]))
    for head in range(HEADS):
        soft = soft_s[head]
        grad_head = grad_attended[:, head * HEAD : (head + 1) * HEAD]
        grad_soft = matmul_transposed(grad_head, part(qkv_s, 2, head))
        inner = jnp.sum(grad_soft * soft, axis=-1, keepdims=True)
        grad_scores = low(soft * (grad_soft - inner))
        grads = (
            matmul(grad_scores, part(qkv_s, 1, head)) * SCALE,
            outer_sum(grad_scores, part(qkv_s, 0, head)) * SCALE,
            outer_sum(low(soft), grad_head),
        )
        for member, grad in enumerate(grads):
            start = member * width + head * HEAD
            dqkv_s[:, start : start + HEAD] = low(grad)
    row_ref[:, sums_at : sums_at + width] = column_sum(dqkv_s[:, :width])
    row_ref[:, sums_at + width : sums_at + 2 * width] = column_sum(dqkv_s[:, 2 * width :])
    halves[0, :, : 3 * width] = low(outer_sum(hidden_one, dqkv_s[...]) * share)
    first_out = [
        pltpu.make_async_copy(halves.at[0], keep_ref, out_sems.at[0]),
        pltpu.make_async_copy(halves.at[0], send_ref, out_sems.at[0]),
    ]

    @pl.when(rank == 0)
    def _():
        first_out[0].start()

    @pl.when(rank != 0)
    def _():
        first_out[1].start()

    grad_hidden_one = matmul_transposed(dqkv_s[...], att_w[...])
    row_ref[:, :width] = column_sum(grad_hidden_one)
    row_ref[:, width : 2 * width] = column_sum(grad_hidden_one * normed_one)
    dx_ref[...] = low(
        grad_middle
        + normalize_back(normed_one, factor_one, grad_hidden_one * (1.0 + scale_one))
    )
    grad_modulation = low(row_ref[:, : 6 * width])
    row_ref[:, : 6 * width] = grad_modulation.astype(jnp.float32)
    spread = jnp.broadcast_to(row_ref[:, : 6 * width], (16, 6 * width))
    row_ref[:, sums_at + 4 * width + hidden :] = matmul_transposed(low(spread), mod_w[...])[0:1, :]
    second_out[0].wait()
    first_out[0].wait()


def run_section(layout, flags, x, silu, packs, dy=None):
    width, hidden, rows, ratio, ring_size, share, bias_count = layout
    length = x.shape[0]
    backward = dy is not None
    vmem = pl.BlockSpec(memory_space=pltpu.VMEM)
    hbm = pl.BlockSpec(memory_space=pl.ANY)
    bf16, f32 = jnp.bfloat16, jnp.float32
    half = 2 * width + hidden
    shapes = [jax.ShapeDtypeStruct((length, width), bf16)]
    out_specs = [vmem]
    scratch = [
        pltpu.VMEM((width, 6 * width), bf16),
        pltpu.VMEM((width, 3 * width), bf16),
        pltpu.VMEM((width, width), bf16),
        pltpu.VMEM((width, hidden), bf16),
        pltpu.VMEM((width, hidden), bf16),
        pltpu.VMEM((width, 128), bf16),
        pltpu.SemaphoreType.DMA((6,)),
        pltpu.VMEM((1, bias_count * ring_size), f32),
        pltpu.VMEM((hidden, width), bf16),
        pltpu.VMEM((hidden, width), f32),
        pltpu.VMEM((width, hidden), f32),
        pltpu.VMEM((length, 3 * width), bf16),
        pltpu.VMEM((length, width), bf16),
        pltpu.VMEM((length, hidden), bf16),
    ]
    operands = [flags, x, silu]
    if backward:
        operands.append(dy)
        shapes += [
            jax.ShapeDtypeStruct((length, width), bf16),
            jax.ShapeDtypeStruct((1, 11 * width + hidden), f32),
            jax.ShapeDtypeStruct((width, half), bf16),
            jax.ShapeDtypeStruct((width, half), bf16),
        ]
        out_specs += [vmem, vmem, hbm, hbm]
        scratch += [
            pltpu.VMEM((HEADS, length, length), f32),
            pltpu.VMEM((length, hidden), f32),
            pltpu.VMEM((length, hidden), bf16),
            pltpu.VMEM((length, 3 * width), bf16),
            pltpu.VMEM((2, width, half), bf16),
            pltpu.SemaphoreType.DMA((2,)),
        ]
    specs = [pl.BlockSpec(memory_space=pltpu.SMEM)] + [vmem] * (len(operands) - 1) + [hbm] * 2
    work = 2 * length * width * (4 * width + 2 * hidden + 2 * length)
    moved = 2 * width * (10 * width + 2 * hidden)
    return pl.pallas_call(
        partial(section_kernel, layout, backward),
        out_shape=shapes,
        in_specs=specs,
        out_specs=out_specs,
        scratch_shapes=scratch,
        compiler_params=pltpu.CompilerParams(
            vmem_limit_bytes=(36 if length <= 256 else 56) * 1024 * 1024
        ),
        cost_estimate=pl.CostEstimate(
            flops=(3 if backward else 1) * work,
            bytes_accessed=(2 if backward else 1) * moved,
            transcendentals=HEADS * length * length + length * hidden,
        ),
    )(*operands, *packs)


def pair_swap(block, axis):
    return lax.ppermute(block, axis, [(0, 1), (1, 0)])


def ring_exchange(block, size, step):
    route = [(i, step(i)) for i in range(size)]
    return lax.ppermute(block, RING, route)


def scatter_sum(block, rank, size):
    half = block.shape[-1] // 2
    pieces = [block[..., :half], block[..., half:]]
    left = size
    low_bits = 0
    while left > 4:
        orders = [(0, 1), (1, 0)] if left % 4 == 0 and left >= 16 else [(0,), (0,)]
        for turn in range(len(orders[0])):
            updated = []
            for piece, order in zip(pieces, orders):
                bit = low_bits + order[turn]
                mine = (rank >> bit) & 1
                if len(order) == 2 and turn == 0:
                    shaped = piece.reshape(-1, 2, 2, *piece.shape[1:])
                    at = 2 - order[turn]
                else:
                    shaped = piece.reshape(-1, 2, *piece.shape[1:])
                    at = 1
                keep = lax.dynamic_index_in_dim(shaped, mine, at, keepdims=False)
                send = lax.dynamic_index_in_dim(shaped, 1 - mine, at, keepdims=False)
                got = ring_exchange(send, size, lambda i, bit=bit: i ^ (1 << bit))
                total = (keep.astype(jnp.float32) + got.astype(jnp.float32)).astype(jnp.bfloat16)
                updated.append(total.reshape(-1, *piece.shape[1:]))
            pieces = updated
        low_bits += len(orders[0])
        left //= 2 ** len(orders[0])
    block = jnp.concatenate(pieces, axis=-1)
    high = rank >> low_bits
    total = lax.dynamic_index_in_dim(block, high, 0, keepdims=False).astype(jnp.float32)
    stride = 1 << low_bits
    for turn in range(1, left):
        send = lax.dynamic_index_in_dim(block, (high + turn) % left, 0, keepdims=False)
        got = ring_exchange(send, size, lambda i, turn=turn: (i + turn * stride) % size)
        total = total + got.astype(jnp.float32)
    return total


def per_device(
    inputs,
    cotangent,
    time_ids,
    row_counts,
    cond_table,
    modulation_weight,
    attention_weight,
    output_weight,
    expand_weight,
    shrink_weight,
    biases,
):
    section_rank = lax.axis_index("section")
    data_rank = lax.axis_index("dp")
    seq_rank = lax.axis_index("seq")
    sections = lax.axis_size("section")
    seq_size = lax.axis_size("seq")
    ring_size = lax.axis_size("dp") * seq_size
    ring_rank = data_rank * seq_size + seq_rank
    batches, slots, tokens, width = inputs.shape
    assert batches == sections == 2 and seq_size % slots == 0
    sharers = seq_size // slots
    slot = seq_rank // sharers
    length = tokens * seq_size
    rows = attention_weight.shape[1]
    ratio = shrink_weight.shape[1] // rows
    hidden = ratio * width
    bias_count = biases.shape[1]
    bias_rows = -(-bias_count // 128)
    assert bias_rows <= rows and hidden == expand_weight.shape[2]
    table_rows = cond_table.shape[0]
    is_first = section_rank == 0
    layout = (width, hidden, rows, ratio, ring_size, 1.0 / sharers, bias_count)

    bias_block = jnp.pad(biases[0], (0, bias_rows * 128 - bias_count)).reshape(bias_rows, 128)
    packed = jnp.concatenate(
        [
            attention_weight[0],
            output_weight[0],
            expand_weight[0],
            modulation_weight[0],
            *[shrink_weight[0, j * rows : (j + 1) * rows] for j in range(ratio)],
            jnp.pad(bias_block, ((0, rows - bias_rows), (0, 0))),
        ],
        axis=1,
    )
    own_pack = lax.all_gather(packed, RING, axis=0, tiled=True)
    packs = (own_pack, pair_swap(own_pack, "section"))

    live = (
        slot < lax.dynamic_index_in_dim(row_counts, section_rank, 0, keepdims=False)[0]
    ).astype(jnp.bfloat16)
    both = jnp.stack(
        [
            lax.dynamic_index_in_dim(inputs, section_rank, 0, keepdims=False),
            lax.dynamic_index_in_dim(cotangent, section_rank, 0, keepdims=False),
        ],
        axis=1,
    )
    both = jnp.repeat(both, sharers, axis=0)
    both = lax.all_to_all(both, "seq", 0, 0, tiled=True)
    first_input = both[:, 0].reshape(length, width)
    last_grad = both[:, 1].reshape(length, width) * live
    flat_ids = time_ids.reshape(-1)
    selector = (
        flat_ids[:, None] == jnp.arange(table_rows, dtype=jnp.int32)[None, :]
    ).astype(jnp.bfloat16)
    conditions = matmul(selector, cond_table)
    silu_all = jax.nn.silu(conditions).astype(jnp.bfloat16)
    latent = section_rank * time_ids.shape[1] + data_rank * slots + slot
    condition = lax.dynamic_slice_in_dim(conditions, latent, 1, 0)
    silu_now = jnp.broadcast_to(lax.dynamic_slice_in_dim(silu_all, latent, 1, 0), (16, width))

    first_flags = jnp.stack([is_first, ~is_first]).astype(jnp.int32)
    second_flags = jnp.stack([~is_first, ~is_first]).astype(jnp.int32)
    (first_low,) = run_section(layout, first_flags, first_input, silu_now, packs)
    second_low, second_grad, second_row, second_keep, second_send = run_section(
        layout, second_flags, first_low, silu_now, packs, last_grad
    )
    second_got = pair_swap(second_send, "section")
    _, first_grad, first_row, first_keep, first_send = run_section(
        layout, first_flags, first_input, silu_now, packs, second_grad
    )
    first_got = pair_swap(first_send, "section")

    def to_owners(first, second):
        pieces = jnp.stack([first, second]).reshape(2 * seq_size, tokens, width)
        pieces = lax.all_to_all(pieces, ("section", "seq"), 0, 0, tiled=True)
        return pieces.reshape(batches, slots, sharers, tokens, width)[:, :, 0]

    activations = to_owners(first_low * live, second_low * live)
    input_grads = to_owners(first_grad, second_grad).astype(jnp.float32)

    half = first_keep.shape[1]

    def chip_sum(keep, got):
        total = keep.astype(jnp.float32) + got.astype(jnp.float32)
        return total.astype(jnp.bfloat16).reshape(ring_size, 1, rows, half)

    ring_terms = jnp.concatenate(
        [chip_sum(first_keep, first_got), chip_sum(second_keep, second_got)], axis=1
    )
    owned = scatter_sum(ring_terms.reshape(ring_size, 2 * rows, half), ring_rank, ring_size)
    owned = owned.reshape(2, rows, half)
    mine = lax.dynamic_index_in_dim(owned, section_rank, 0, keepdims=False)
    theirs = pair_swap(
        lax.dynamic_index_in_dim(owned, 1 - section_rank, 0, keepdims=False), "section"
    )
    full = jnp.where(
        is_first,
        jnp.concatenate([mine, theirs], axis=1),
        jnp.concatenate([theirs, mine], axis=1),
    )
    edges = [0, 3 * width, 4 * width, 4 * width + hidden]
    att, out, up = [full[:, a:b] for a, b in zip(edges[:-1], edges[1:])]
    down = jnp.concatenate(
        [full[:, edges[3] + j * width : edges[3] + (j + 1) * width] for j in range(ratio)], axis=0
    )

    per_row = 10 * width + hidden
    _, silu_back = jax.vjp(jax.nn.silu, condition)
    grad_condition = silu_back(first_row[:, per_row:] + second_row[:, per_row:])[0]
    row = jnp.concatenate([first_row[:, :per_row], second_row[:, :per_row], grad_condition], axis=1)
    every = lax.all_gather(row, ("section", "dp", "seq"), axis=0, tiled=True)[::sharers]
    section_rows = jnp.where(is_first, every[:, :per_row], every[:, per_row : 2 * per_row])
    bias_total = jnp.sum(section_rows, axis=0)
    bias_grad = lax.dynamic_slice_in_dim(bias_total, ring_rank * bias_count, bias_count, 0)
    silu_own = lax.dynamic_slice_in_dim(silu_all, ring_rank * rows, rows, 1)
    modulation_grad = outer_sum(silu_own, section_rows[:, : 6 * width].astype(jnp.bfloat16))
    table_grad = lax.dot_general(
        selector.astype(jnp.float32),
        every[:, 2 * per_row :],
        (((0,), (0,)), ((), ())),
        precision=lax.Precision.HIGHEST,
        preferred_element_type=jnp.float32,
    )
    return (
        activations[None],
        input_grads[None],
        table_grad,
        modulation_grad[None],
        att[None],
        out[None],
        up[None],
        down[None],
        bias_grad[None],
    )


def solution(mesh):
    shard = P("section", ("dp", "seq"), None)
    in_specs = (
        P(None, "dp", "seq", None),
        P(None, "dp", "seq", None),
        P(),
        P(None, "dp"),
        P(),
        shard,
        shard,
        shard,
        shard,
        shard,
        P("section", ("dp", "seq")),
    )
    out_specs = (
        P("section", None, "dp", "seq", None),
        P("section", None, "dp", "seq", None),
        P(),
        shard,
        shard,
        shard,
        shard,
        shard,
        P("section", ("dp", "seq")),
    )
    return jax.shard_map(
        per_device, mesh=mesh, in_specs=in_specs, out_specs=out_specs, check_vma=False
    )
```

time: 377 us -> 274 us (0.73); the launches traced: 370 us -> 271 us
  matrix products: 65.6 us -> 3.46 us
  local copies, waits for them, and re-layouts: 73.5 us -> 25.3 us
  Pallas kernels: 0 us -> 36.8 us
  other arithmetic: 43.2 us -> 14.1 us
    pallas_call x0 -> x3, Pallas kernels: none -> 36.8 us  [run_section(): pl.pallas_call(partial(section_kernel, layout, backward), out_shape=shape...]
    dot_general x23 -> x1, matrix products: 35.5 us -> 2.2 us  [per_device(): lax.dot_general(selector.astype(jnp.float32), every[:, 2 * per_row:], (((...]
    dot_general x11 -> x1, matrix products: 19.2 us -> 0.3 us  [matmul(): return jnp.dot(former, latter, preferred_element_type=jnp.float32)]
    unnamed x245 -> x26, local copies, waits for them, and re-layouts: 27.5 us -> 14 us
    reshape x7 -> x1, local copies, waits for them, and re-layouts: 10.9 us -> 0.01 us  [per_device(): jnp.pad(biases[0], (0, bias_rows * 128 - bias_count))]
    dot_general x9 -> x1, matrix products: 11 us -> 0.97 us  [outer_sum(): lax.dot_general(former, latter, (((0,), (0,)), ((), ())), preferred_eleme...]
    select_n x1 -> x0, other arithmetic: 9.19 us -> none  [per_device(): first_mod, first_weights = unpack(jnp.where(is_first, own_pack, other_pack))]
    ppermute x7, waiting for transfers between devices: 26.7 us -> 35 us  [ring_exchange(): return lax.ppermute(block, RING, route)]
  transfers between devices with their start and end apart: 15 -> 16, of which waited for: 10 -> 10; matrix products, arithmetic and copies ran while one was open for 18% -> 9% of each run, Pallas kernels for 0% -> 6%
where the time goes in v2:
time: 274 us; the launch traced here: 271 us
  waiting for transfers between devices  152 us (55%)
  Pallas kernels  36.8 us (13%)
  local copies, waits for them, and re-layouts  25.3 us (9%)
  starting transfers between devices  24.2 us (9%)
  between operations  15 us (5%)
  other arithmetic  14.1 us (5%)
  matrix products  3.46 us (1%)
    all_gather x1, waiting for transfers between devices, per_device(): own_pack = lax.all_gather(packed, RING, axis=0, tiled=True)  86.3 us
    pallas_call x3, Pallas kernels, run_section(): pl.pallas_call(partial(section_kernel, layout, backward), out_shape=shape...  36.8 us
    ppermute x7, waiting for transfers between devices, ring_exchange(): return lax.ppermute(block, RING, route)  35 us
    all_to_all x2, waiting for transfers between devices, to_owners(): pieces = lax.all_to_all(pieces, ('section', 'seq'), 0, 0, tiled=True)  24.9 us
    unnamed x26, local copies, waits for them, and re-layouts  14 us
    all_to_all x2, starting transfers between devices, to_owners(): pieces = lax.all_to_all(pieces, ('section', 'seq'), 0, 0, tiled=True)  8.87 us
    ppermute x7, starting transfers between devices, ring_exchange(): return lax.ppermute(block, RING, route)  7.8 us
  transfers between devices with their start and end apart: 16, of which 10 were waited for; matrix products, arithmetic and copies ran while one was open for 9% of the time, Pallas kernels for 6%

profile of v2, /device:TPU:9, one launch (start us, length us, event | category | flops | bytes accessed | tf_op | source)
XLA Modules:
  0.0 271.2 jit_solution(15577749738262842015)
XLA Ops:
  15.1 86.3 %all-gather.4.cloned.1.call-done.refs_3_.refs_4_ = bf16[384,7040]{1,0:T(8,128)(2,1)} async-done(((bf16[24,7040]{1,0:T(8,128)(2,1)}), bf16[384,7040]{1,0:T(8,128)(2,1)}) %all-gather.4.cloned.1.call-update) | async-done | bytes 5406736 | tf_op jit(solution)/shard_map/all_gather | solution.py:424
  101.3 2.0 collective-permute-start
  105.1 3.5 %all-to-all-start = ((bf16[2,2,128,384]{3,2,1,0:T(8,128)(2,1)}), bf16[2,2,128,384]{3,2,1,0:T(8,128)(2,1)S(1)}, u32[]{:S(2)}, u32[]{:S(2)}) async-start(bf16[2,2,128,384]{3,2,1,0:T(8,128)(2,1)} %pad_maximum_fusion.1), calls=%async_computation | async-start | bytes 786432 | tf_op jit(solution)/shard_map/all_to_all | solution.py:438
  110.4 4.9 %all-to-all-done = bf16[2,2,128,384]{3,2,1,0:T(8,128)(2,1)S(1)} async-done(((bf16[2,2,128,384]{3,2,1,0:T(8,128)(2,1)}), bf16[2,2,128,384]{3,2,1,0:T(8,128)(2,1)S(1)}, u32[]{:S(2)}, u32[]{:S(2)}) %all-to-all-start) | async-done | bytes 393248 | tf_op jit(solution)/shard_map/all_to_all | solution.py:438
  115.4 2.5 copy-done.1
  117.9 7.6 %shard_map.178.refs_1_ = bf16[256,384]{1,0:T(8,128)(2,1)S(1)} custom-call(s32[2]{0:T(128)S(1)} %get-tuple-element.47.refs_0_, bf16[256,384]{1,0:T(8,128)(2,1)S(1)} %bitcast.102, bf16[16,384]{1,0:T(8,128)(2,1)S(1)} %broadcast_in_dim.28.refs_2_, bf16[384,7040]{1,0:T(8,128)(2,1)S(1)} %copy-done.1, bf16[384,7040]{1,0:T(8,128)(2,1)} %collective-permute-done.refs_4_.refs_5_), custom_call_target="tpu_custom_call" | custom-call | flops 1006632960 | bytes 5308416 | tf_op jit(solution)/shard_map/pallas_call | solution.py:314
  125.5 13.3 %shard_map.179 = (bf16[256,384]{1,0:T(8,128)(2,1)S(1)}, bf16[256,384]{1,0:T(8,128)(2,1)S(1)}, f32[1,5760]{1,0:T(1,128)S(1)}, bf16[384,2304]{1,0:T(8,128)(2,1)S(1)}, bf16[384,2304]{1,0:T(8,128)(2,1)}) custom-call(s32[2]{0:T(128)S(1)} %get-tuple-element.48.refs_0_, bf16[256,384]{1,0:T(8,128)(2,1)S(1)} %shard_map.178.refs_1_, ...), custom_call_target="tpu_custom_call" | custom-call | flops 3019898880 | bytes 10616832 | tf_op jit(solution)/shard_map/pallas_call | solution.py:314
  139.6 16.0 %shard_map.180 = (bf16[256,384]{1,0:T(8,128)(2,1)}, bf16[256,384]{1,0:T(8,128)(2,1)S(1)}, f32[1,5760]{1,0:T(1,128)S(1)}, bf16[384,2304]{1,0:T(8,128)(2,1)S(1)}, bf16[384,2304]{1,0:T(8,128)(2,1)}) custom-call(s32[2]{0:T(128)S(1)} %get-tuple-element.47.refs_0_, bf16[256,384]{1,0:T(8,128)(2,1)S(1)} %bitcast.103, bf16[16,384]{1,0:T(8,128)(2,1)S(1)} %broadcast_in_dim.28.refs_2_, ...), custom_call_target="tpu_custom_call" | custom-call | flops 3019898880 | bytes 10616832 | tf_op jit(solution)/shard_map/pallas_call | solution.py:314
  155.6 1.2 copy-done.2
  157.6 2.0 add_convert_fusion
  159.6 1.2 collective-permute-done.1
  160.8 1.9 add_convert_fusion.1
  163.1 1.5 fusion.25
  166.4 4.5 %all-to-all-start.1 = ((bf16[4,128,384]{2,1,0:T(8,128)(2,1)}), bf16[4,128,384]{2,1,0:T(8,128)(2,1)}, u32[]{:S(2)}, u32[]{:S(2)}) async-start(bf16[4,128,384]{2,1,0:T(8,128)(2,1)} %bitcast.117), calls=%async_computation.1 | async-start | bytes 786432 | tf_op jit(solution)/shard_map/all_to_all | solution.py:465
  171.7 20.2 %all-to-all-done.1 = bf16[4,128,384]{2,1,0:T(8,128)(2,1)} async-done(((bf16[4,128,384]{2,1,0:T(8,128)(2,1)}), bf16[4,128,384]{2,1,0:T(8,128)(2,1)}, u32[]{:S(2)}, u32[]{:S(2)}) %all-to-all-start.1) | async-done | bytes 393248 | tf_op jit(solution)/shard_map/all_to_all | solution.py:465
  191.9 4.4 %all-to-all-start.2 = ((bf16[4,128,384]{2,1,0:T(8,128)(2,1)}), bf16[4,128,384]{2,1,0:T(8,128)(2,1)S(1)}, u32[]{:S(2)}, u32[]{:S(2)}) async-start(bf16[4,128,384]{2,1,0:T(8,128)(2,1)} %bitcast.116), calls=%async_computation.2 | async-start | bytes 786432 | tf_op jit(solution)/shard_map/all_to_all | solution.py:465
  196.3 2.5 constant_dynamic-slice_fusion.1
  200.9 4.7 %all-to-all-done.2 = bf16[4,128,384]{2,1,0:T(8,128)(2,1)S(1)} async-done(((bf16[4,128,384]{2,1,0:T(8,128)(2,1)}), bf16[4,128,384]{2,1,0:T(8,128)(2,1)S(1)}, u32[]{:S(2)}, u32[]{:S(2)}) %all-to-all-start.2) | async-done | bytes 393248 | tf_op jit(solution)/shard_map/all_to_all | solution.py:465
  206.6 1.5 fusion.1
  208.1 1.2 collective-permute-start.4
  209.3 12.0 %collective-permute-done.5 = bf16[4,2,48,1152]{3,2,0,1:T(8,128)(2,1)} collective-permute-done((bf16[4,2,48,1152]{3,2,0,1:T(8,128)(2,1)}, bf16[4,2,48,1152]{3,2,0,1:T(8,128)(2,1)}, u32[]{:S(2)}, u32[]{:S(2)}) %collective-permute-start.5) | collective-permute-done | bytes 884768 | tf_op jit(solution)/shard_map/ppermute | solution.py:337
  221.3 1.4 fusion
  224.6 1.4 copy.35
  226.0 4.8 %collective-permute-done.4 = bf16[4,48,1152]{2,1,0:T(8,128)(2,1)S(1)} collective-permute-done((bf16[4,48,1152]{2,1,0:T(8,128)(2,1)S(1)}, bf16[4,48,1152]{2,1,0:T(8,128)(2,1)S(1)}, u32[]{:S(2)}, u32[]{:S(2)}) %collective-permute-start.4) | collective-permute-done | bytes 442400 | tf_op jit(solution)/shard_map/ppermute | solution.py:337
  230.9 3.2 %collective-permute-done.6 = bf16[4,48,1152]{2,1,0:T(8,128)(2,1)} collective-permute-done((bf16[4,48,1152]{2,1,0:T(8,128)(2,1)}, bf16[4,48,1152]{2,1,0:T(8,128)(2,1)}, u32[]{:S(2)}, u32[]{:S(2)}) %collective-permute-start.6) | collective-permute-done | bytes 442400 | tf_op jit(solution)/shard_map/ppermute | solution.py:337
  236.1 1.5 collective-permute-start.8
  237.6 2.0 collective-permute-start.7
  241.3 10.3 %collective-permute-done.8 = bf16[48,2304]{1,0:T(8,128)(2,1)S(1)} collective-permute-done((bf16[48,2304]{1,0:T(8,128)(2,1)S(1)}, bf16[48,2304]{1,0:T(8,128)(2,1)S(1)}, u32[]{:S(2)}, u32[]{:S(2)}) %collective-permute-start.8) | collective-permute-done | bytes 221216 | tf_op jit(solution)/shard_map/ppermute | solution.py:337
  251.7 4.7 %collective-permute-done.7 = bf16[48,2304]{1,0:T(8,128)(2,1)S(1)} collective-permute-done((bf16[48,2304]{1,0:T(8,128)(2,1)S(1)}, bf16[48,2304]{1,0:T(8,128)(2,1)S(1)}, u32[]{:S(2)}, u32[]{:S(2)}) %collective-permute-start.7) | collective-permute-done | bytes 221216 | tf_op jit(solution)/shard_map/ppermute | solution.py:337
  256.6 1.2 collective-permute-start.10
  257.7 2.2 fusion.14
  262.6 1.8 copy.46
  (78 shorter events, 27.0 us)
Async XLA Ops:
  7.2 101.6 %copy-start = (bf16[1000,384]{1,0:T(8,128)(2,1)S(1)}, bf16[1000,384]{1,0:T(8,128)(2,1)}, u32[]{:S(2)}) copy-start(bf16[1000,384]{1,0:T(8,128)(2,1)} %param.15) | copy-start | bytes 2304004
  7.2 101.5 %copy-start.6 = (s32[2,16]{1,0:T(2,128)S(1)}, s32[2,16]{1,0:T(2,128)}, u32[]{:S(2)}) copy-start(s32[2,16]{1,0:T(2,128)} %param.13) | copy-start | bytes 388
  7.2 94.1 %all-gather.4.cloned.1.call-start = ((), (), s32[]{:S(2)}) async-start(), calls=%async_computation.3 | async-start | bytes 5744640 | tf_op jit(solution)/shard_map/all_gather | solution.py:424
  14.3 0.7 copy-start.5
  14.3 94.8 %copy-start.7 = (s32[2,1]{0,1:T(1,128)S(1)}, s32[2,1]{0,1:T(1,128)}, u32[]{:S(2)}) copy-start(s32[2,1]{0,1:T(1,128)} %param.14) | copy-start | bytes 28
  101.3 14.1 %collective-permute-start = (bf16[384,7040]{1,0:T(8,128)(2,1)}, bf16[384,7040]{1,0:T(8,128)(2,1)}, u32[]{:S(2)}, u32[]{:S(2)}) collective-permute-start(bf16[384,7040]{1,0:T(8,128)(2,1)} %all-gather.4.cloned.1.call-done.refs_3_.refs_4_), channel_id=1, source_target_pairs={{0,16},{16,0},{1,17},{17,1},{2,18},{18,2},{3,19},{19,3},{4,20},{20... | collective-permute-start | bytes 16220168 | tf_op jit(solution)/shard_map/ppermute | solution.py:332
  105.1 10.2 %all-to-all-start = ((bf16[2,2,128,384]{3,2,1,0:T(8,128)(2,1)}), bf16[2,2,128,384]{3,2,1,0:T(8,128)(2,1)S(1)}, u32[]{:S(2)}, u32[]{:S(2)}) async-start(bf16[2,2,128,384]{3,2,1,0:T(8,128)(2,1)} %pad_maximum_fusion.1), calls=%async_computation | async-start | bytes 786432 | tf_op jit(solution)/shard_map/all_to_all | solution.py:438
  108.6 116.0 %all-gather.6.cloned.1.call-start = ((), (), s32[]{:S(2)}) async-start(), calls=%async_computation.4 | async-start | bytes 1469952 | tf_op jit(solution)/shard_map/all_gather | solution.py:501
  115.4 2.5 copy-start.1
  138.8 18.8 %collective-permute-start.2 = (bf16[384,2304]{1,0:T(8,128)(2,1)}, bf16[384,2304]{1,0:T(8,128)(2,1)}, u32[]{:S(2)}, u32[]{:S(2)}) collective-permute-start(bf16[384,2304]{1,0:T(8,128)(2,1)} %get-tuple-element.26), channel_id=1, source_target_pairs={{0,16},{16,0},{1,17},{17,1},{2,18},{18,2},{3,19},{19,3},{4,20},{20... | collective-permute-start | bytes 5308424 | tf_op jit(solution)/shard_map/ppermute | solution.py:332
  155.6 1.2 copy-start.2
  156.8 4.0 %collective-permute-start.1 = (bf16[384,2304]{1,0:T(8,128)(2,1)}, bf16[384,2304]{1,0:T(8,128)(2,1)}, u32[]{:S(2)}, u32[]{:S(2)}) collective-permute-start(bf16[384,2304]{1,0:T(8,128)(2,1)} %get-tuple-element.24), channel_id=1, source_target_pairs={{0,16},{16,0},{1,17},{17,1},{2,18},{18,2},{3,19},{19,3},{4,20},{20... | collective-permute-start | bytes 5308424 | tf_op jit(solution)/shard_map/ppermute | solution.py:332
  157.6 3.3 %copy-start.3 = (bf16[384,2304]{1,0:T(8,128)(2,1)S(1)}, bf16[384,2304]{1,0:T(8,128)(2,1)}, u32[]{:S(2)}) copy-start(bf16[384,2304]{1,0:T(8,128)(2,1)} %copy-done.2) | copy-start | bytes 5308420
  165.6 41.0 %collective-permute-start.3 = (bf16[4,2,48,1152]{3,2,1,0:T(8,128)(2,1)}, bf16[4,2,48,1152]{3,2,1,0:T(8,128)(2,1)}, u32[]{:S(2)}, u32[]{:S(2)}) collective-permute-start(bf16[4,2,48,1152]{3,2,1,0:T(8,128)(2,1)} %dynamic-slice_bitcast_fusion), channel_id=1, source_target_pairs={{0,1},{1,0},{2,3},{3,2},{4,5},{5,4},{6,7},{7,6},{8,9},{9,8},{10,11... | collective-permute-start | bytes 2654216 | tf_op jit(solution)/shard_map/ppermute | solution.py:337
  166.4 25.5 %all-to-all-start.1 = ((bf16[4,128,384]{2,1,0:T(8,128)(2,1)}), bf16[4,128,384]{2,1,0:T(8,128)(2,1)}, u32[]{:S(2)}, u32[]{:S(2)}) async-start(bf16[4,128,384]{2,1,0:T(8,128)(2,1)} %bitcast.117), calls=%async_computation.1 | async-start | bytes 786432 | tf_op jit(solution)/shard_map/all_to_all | solution.py:465
  191.9 13.7 %all-to-all-start.2 = ((bf16[4,128,384]{2,1,0:T(8,128)(2,1)}), bf16[4,128,384]{2,1,0:T(8,128)(2,1)S(1)}, u32[]{:S(2)}, u32[]{:S(2)}) async-start(bf16[4,128,384]{2,1,0:T(8,128)(2,1)} %bitcast.116), calls=%async_computation.2 | async-start | bytes 786432 | tf_op jit(solution)/shard_map/all_to_all | solution.py:465
  199.8 21.5 %collective-permute-start.5 = (bf16[4,2,48,1152]{3,2,0,1:T(8,128)(2,1)}, bf16[4,2,48,1152]{3,2,0,1:T(8,128)(2,1)}, u32[]{:S(2)}, u32[]{:S(2)}) collective-permute-start(bf16[4,2,48,1152]{3,2,0,1:T(8,128)(2,1)} %bitcast.101), channel_id=1, source_target_pairs={{0,2},{1,3},{2,0},{3,1},{4,6},{5,7},{6,4},{7,5},{8,10},{9,11},{10,... | collective-permute-start | bytes 2654216 | tf_op jit(solution)/shard_map/ppermute | solution.py:337
  206.6 14.7 %copy-start.4 = (bf16[4,1,2,48,1152]{4,3,2,1,0:T(8,128)(2,1)S(1)}, bf16[4,1,2,48,1152]{4,3,2,1,0:T(8,128)(2,1)}, u32[]{:S(2)}) copy-start(bf16[4,1,2,48,1152]{4,3,2,1,0:T(8,128)(2,1)} %get-tuple-element.31) | copy-start | bytes 2654212
  208.1 22.7 %collective-permute-start.4 = (bf16[4,48,1152]{2,1,0:T(8,128)(2,1)S(1)}, bf16[4,48,1152]{2,1,0:T(8,128)(2,1)S(1)}, u32[]{:S(2)}, u32[]{:S(2)}) collective-permute-start(bf16[4,48,1152]{2,1,0:T(8,128)(2,1)S(1)} %dynamic-slice_bitcast_fusion.2), channel_id=1, source_target_pairs={{0,2},{1,3},{2,0},{3,1},{4,6},{5,7},{6,4},{7,5},{8,10},{9,11},{10,... | collective-permute-start | bytes 1327112 | tf_op jit(solution)/shard_map/ppermute | solution.py:337
  223.5 10.6 %collective-permute-start.6 = (bf16[4,48,1152]{2,1,0:T(8,128)(2,1)}, bf16[4,48,1152]{2,1,0:T(8,128)(2,1)}, u32[]{:S(2)}, u32[]{:S(2)}) collective-permute-start(bf16[4,48,1152]{2,1,0:T(8,128)(2,1)} %dynamic-slice_bitcast_fusion.1), channel_id=1, source_target_pairs={{0,1},{1,0},{2,3},{3,2},{4,5},{5,4},{6,7},{7,6},{8,9},{9,8},{10,11... | collective-permute-start | bytes 1327112 | tf_op jit(solution)/shard_map/ppermute | solution.py:337
  235.3 6.1 %collective-permute-start.9 = (bf16[48,2304]{1,0:T(8,128)(2,1)S(1)}, bf16[48,2304]{1,0:T(8,128)(2,1)S(1)}, u32[]{:S(2)}, u32[]{:S(2)}) collective-permute-start(bf16[48,2304]{1,0:T(8,128)(2,1)S(1)} %get-tuple-element.35), channel_id=1, source_target_pairs={{0,12},{1,13},{2,14},{3,15},{4,0},{5,1},{6,2},{7,3},{8,4},{9,5},{1... | collective-permute-start | bytes 663560 | tf_op jit(solution)/shard_map/ppermute | solution.py:337
  236.1 15.6 %collective-permute-start.8 = (bf16[48,2304]{1,0:T(8,128)(2,1)S(1)}, bf16[48,2304]{1,0:T(8,128)(2,1)S(1)}, u32[]{:S(2)}, u32[]{:S(2)}) collective-permute-start(bf16[48,2304]{1,0:T(8,128)(2,1)S(1)} %get-tuple-element.34), channel_id=1, source_target_pairs={{0,8},{1,9},{2,10},{3,11},{4,12},{5,13},{6,14},{7,15},{8,0},{9,1},... | collective-permute-start | bytes 663560 | tf_op jit(solution)/shard_map/ppermute | solution.py:337
  237.6 18.8 %collective-permute-start.7 = (bf16[48,2304]{1,0:T(8,128)(2,1)S(1)}, bf16[48,2304]{1,0:T(8,128)(2,1)S(1)}, u32[]{:S(2)}, u32[]{:S(2)}) collective-permute-start(bf16[48,2304]{1,0:T(8,128)(2,1)S(1)} %get-tuple-element.33), channel_id=1, source_target_pairs={{0,4},{1,5},{2,6},{3,7},{4,8},{5,9},{6,10},{7,11},{8,12},{9,13},{1... | collective-permute-start | bytes 663560 | tf_op jit(solution)/shard_map/ppermute | solution.py:337
  256.6 3.4 %collective-permute-start.10 = (f32[24,2304]{1,0:T(8,128)S(1)}, f32[24,2304]{1,0:T(8,128)S(1)}, u32[]{:S(2)}, u32[]{:S(2)}) collective-permute-start(f32[24,2304]{1,0:T(8,128)S(1)} %get-tuple-element.42), channel_id=1, source_target_pairs={{0,16},{16,0},{1,17},{17,1},{2,18},{18,2},{3,19},{19,3},{4,20},{20... | collective-permute-start | bytes 663560 | tf_op jit(solution)/shard_map/ppermute | solution.py:332
Sparse Core Ops, SparseCore 0:
  15.2 86.0 all-gather.3
  157.7 54.2 all-gather.5

commit v3 on v2

--- a/solution.py
+++ b/solution.py
@@ -56,7 +56,7 @@
 
 def section_kernel(layout, backward, *refs):
     width, hidden, rows, ratio, ring_size, share, bias_count = layout
-    own_ref, x_ref, silu_ref = refs[:3]
+    own_ref, x_ref, modulation_ref = refs[:3]
     refs = refs[3:]
     if backward:
         dy_ref = refs[0]
@@ -69,14 +69,14 @@
     else:
         y_ref = refs[0]
         refs = refs[1:]
-    mod_w, att_w, out_w, up_w, down_p, bias_p, sems = refs[:7]
-    bias_s, down_w, down_s, block_s, qkv_s, att_s, u_s = refs[7:14]
+    att_w, out_w, up_w, down_p, bias_p, sems = refs[:6]
+    bias_s, down_w, down_s, block_s, qkv_s, att_s, u_s = refs[6:13]
     if backward:
-        soft_s, slope_s, da_s, dqkv_s, halves, out_sems = refs[14:]
+        soft_s, slope_s, da_s, dqkv_s, halves, out_sems = refs[13:]
 
     own = own_ref[0] == 1
-    held = (att_w, out_w, up_w, mod_w, down_p, bias_p)
-    sizes = (3 * width, width, hidden, 6 * width, hidden, 128)
+    held = (att_w, out_w, up_w, down_p, bias_p)
+    sizes = (3 * width, width, hidden, hidden, 128)
     starts = [sum(sizes[:i]) for i in range(len(sizes))]
 
     def fetches(source):
@@ -104,7 +104,7 @@
 
     x = x_ref[...].astype(jnp.float32)
     normed_one, factor_one = normalize_rows(x)
-    arrivals[5].wait()
+    arrivals[4].wait()
     bias_rows = bias_p[...].astype(jnp.float32)
     for d in range(ring_size):
         for i in range(0, bias_count, 128):
@@ -112,8 +112,7 @@
             start = d * bias_count + i
             row = d * rows + i // 128
             bias_s[:, start : start + wide] = bias_rows[row : row + 1, :wide]
-    arrivals[3].wait()
-    modulation = matmul(silu_ref[...], mod_w[...])[0:1, :] + bias(0, 6 * width)
+    modulation = modulation_ref[...] + bias(0, 6 * width)
     shift_one, scale_one, gate_one, shift_two, scale_two, gate_two = [
         modulation[:, i * width : (i + 1) * width] for i in range(6)
     ]
@@ -156,7 +155,7 @@
             slope_s[:, cut] = half_one + (0.5 * INNER) * a * (1.0 - turn * turn) * (
                 1.0 + (3.0 * CUBE) * square
             )
-    arrivals[4].wait()
+    arrivals[3].wait()
     block_s[...] = down_p[...].astype(jnp.float32)
     for d in range(ring_size):
         for j in range(ratio):
@@ -256,15 +255,12 @@
         grad_middle
         + normalize_back(normed_one, factor_one, grad_hidden_one * (1.0 + scale_one))
     )
-    grad_modulation = low(row_ref[:, : 6 * width])
-    row_ref[:, : 6 * width] = grad_modulation.astype(jnp.float32)
-    spread = jnp.broadcast_to(row_ref[:, : 6 * width], (16, 6 * width))
-    row_ref[:, sums_at + 4 * width + hidden :] = matmul_transposed(low(spread), mod_w[...])[0:1, :]
+    row_ref[:, : 6 * width] = low(row_ref[:, : 6 * width]).astype(jnp.float32)
     second_out[0].wait()
     first_out[0].wait()
 
 
-def run_section(layout, flags, x, silu, packs, dy=None):
+def run_section(layout, flags, x, modulation, packs, dy=None):
     width, hidden, rows, ratio, ring_size, share, bias_count = layout
     length = x.shape[0]
     backward = dy is not None
@@ -275,13 +271,12 @@
     shapes = [jax.ShapeDtypeStruct((length, width), bf16)]
     out_specs = [vmem]
     scratch = [
-        pltpu.VMEM((width, 6 * width), bf16),
         pltpu.VMEM((width, 3 * width), bf16),
         pltpu.VMEM((width, width), bf16),
         pltpu.VMEM((width, hidden), bf16),
         pltpu.VMEM((width, hidden), bf16),
         pltpu.VMEM((width, 128), bf16),
-        pltpu.SemaphoreType.DMA((6,)),
+        pltpu.SemaphoreType.DMA((5,)),
         pltpu.VMEM((1, bias_count * ring_size), f32),
         pltpu.VMEM((hidden, width), bf16),
         pltpu.VMEM((hidden, width), f32),
@@ -290,12 +285,12 @@
         pltpu.VMEM((length, width), bf16),
         pltpu.VMEM((length, hidden), bf16),
     ]
-    operands = [flags, x, silu]
+    operands = [flags, x, modulation]
     if backward:
         operands.append(dy)
         shapes += [
             jax.ShapeDtypeStruct((length, width), bf16),
-            jax.ShapeDtypeStruct((1, 11 * width + hidden), f32),
+            jax.ShapeDtypeStruct((1, 10 * width + hidden), f32),
             jax.ShapeDtypeStruct((width, half), bf16),
             jax.ShapeDtypeStruct((width, half), bf16),
         ]
@@ -328,13 +323,159 @@
     )(*operands, *packs)
 
 
+def pack_kernel(rows, ratio, att_ref, out_ref, up_ref, down_ref, bias_ref, packed_ref):
+    width = out_ref.shape[1]
+    at = 0
+    for ref in (att_ref, out_ref, up_ref):
+        packed_ref[:, at : at + ref.shape[1]] = ref[...]
+        at += ref.shape[1]
+    down = down_ref[...].astype(jnp.float32)
+    for j in range(ratio):
+        packed_ref[:, at : at + width] = low(down[j * rows : (j + 1) * rows])
+        at += width
+    packed_ref[:, at:] = bias_ref[...]
+
+
+def copy_all(copies):
+    for copy in copies:
+        copy.start()
+    for copy in copies:
+        copy.wait()
+
+
+def stack_kernel(high, split, place_ref, *refs):
+    pieces, (first_ref, second_ref), sems = refs[:high], refs[high:-1], refs[-1]
+    copies = []
+    for turn, piece in enumerate(pieces):
+        place = lax.rem(place_ref[0] + (high - turn), high)
+        copies += [
+            pltpu.make_async_copy(piece.at[:, :split], first_ref.at[place], sems.at[turn, 0]),
+            pltpu.make_async_copy(piece.at[:, split:], second_ref.at[place], sems.at[turn, 1]),
+        ]
+    copy_all(copies)
+
+
+def weave_kernel(split, place_ref, *refs):
+    pieces, full_ref, sems = refs[:8], refs[8], refs[9]
+    x, y = place_ref[1], place_ref[2]
+    copies = []
+    for i, piece in enumerate(pieces):
+        other_x, other_y = (i % 4) & 1, (i % 4) >> 1
+        row = x if not other_x else 1 - x
+        column = y if not other_y else 1 - y
+        lanes = pl.ds(0, split) if i < 4 else pl.ds(split, piece.shape[2])
+        copies.append(
+            pltpu.make_async_copy(piece, full_ref.at[:, row, column, :, lanes], sems.at[i])
+        )
+    copy_all(copies)
+
+
+def chip_sum_kernel(high, place_ref, *refs):
+    terms, (first_keep, first_send, second_keep, second_send) = refs[:4], refs[4:]
+    x, y = place_ref[1], place_ref[2]
+    rows, half = terms[0].shape[1:]
+    lanes = half // 2
+    for z in range(high):
+        for other in range(2):
+            for keep, target, span, chunk in (
+                (True, first_keep, slice(0, lanes), z * 4 + x * 2 + other),
+                (False, first_send, slice(0, lanes), z * 4 + (1 - x) * 2 + other),
+                (True, second_keep, slice(lanes, half), z * 4 + other * 2 + y),
+                (False, second_send, slice(lanes, half), z * 4 + other * 2 + (1 - y)),
+            ):
+                for section in range(2):
+                    mine, got = terms[2 * section : 2 * section + 2]
+                    target[z, other, section] = low(
+                        mine[chunk, :, span].astype(jnp.float32)
+                        + got[chunk, :, span].astype(jnp.float32)
+                    )
+
+
+def in_memory(kernel, shapes, operands, scalars=1, scratch=(), memory=pl.ANY, limit=24):
+    specs = [pl.BlockSpec(memory_space=pltpu.SMEM)] * scalars
+    specs += [pl.BlockSpec(memory_space=memory)] * (len(operands) - scalars)
+    moved = sum(2 * shape.size for shape in shapes)
+    return pl.pallas_call(
+        kernel,
+        out_shape=shapes,
+        in_specs=specs,
+        out_specs=[pl.BlockSpec(memory_space=memory)] * len(shapes),
+        scratch_shapes=list(scratch),
+        compiler_params=pltpu.CompilerParams(vmem_limit_bytes=limit * 1024 * 1024),
+        cost_estimate=pl.CostEstimate(flops=0, bytes_accessed=2 * moved, transcendentals=0),
+    )(*operands)
+
+
 def pair_swap(block, axis):
     return lax.ppermute(block, axis, [(0, 1), (1, 0)])
 
 
 def ring_exchange(block, size, step):
-    route = [(i, step(i)) for i in range(size)]
-    return lax.ppermute(block, RING, route)
+    return lax.ppermute(block, RING, [(i, step(i)) for i in range(size)])
+
+
+def flip(block, size, bit):
+    return ring_exchange(block, size, lambda i: i ^ (1 << bit))
+
+
+def rotate(block, size, turn):
+    return ring_exchange(block, size, lambda i: (i + 4 * turn) % size)
+
+
+def gather_compact(packed, place, size, split):
+    high = size // 4
+    rows, lanes = packed.shape
+    shards = [packed] + [rotate(packed, size, turn) for turn in range(1, high)]
+    first, second = in_memory(
+        partial(stack_kernel, high, split),
+        [
+            jax.ShapeDtypeStruct((high, rows, wide), packed.dtype)
+            for wide in (split, lanes - split)
+        ],
+        [place, *shards],
+        scratch=[pltpu.SemaphoreType.DMA((high, 2))],
+    )
+    first_x, second_y = flip(first, size, 1), flip(second, size, 0)
+    first_y, second_x = flip(first, size, 0), flip(second, size, 1)
+    first_both, second_both = flip(first_x, size, 0), flip(second_y, size, 1)
+    (full,) = in_memory(
+        partial(weave_kernel, split),
+        [jax.ShapeDtypeStruct((high, 2, 2, rows, lanes), packed.dtype)],
+        [place, first, first_x, first_y, first_both, second, second_x, second_y, second_both],
+        scratch=[pltpu.SemaphoreType.DMA((8,))],
+    )
+    return full.reshape(size * rows, lanes)
+
+
+def scatter_compact(terms, place, rank, size):
+    high = size // 4
+    rows, half = terms[0].shape[1:]
+    lanes = half // 2
+    shape = jax.ShapeDtypeStruct((high, 2, 2, rows, lanes), jnp.bfloat16)
+    first_keep, first_send, second_keep, second_send = in_memory(
+        partial(chip_sum_kernel, high),
+        [shape] * 4,
+        [place, *terms],
+        memory=pltpu.VMEM,
+        limit=32,
+    )
+    first_got, second_got = flip(first_send, size, 1), flip(second_send, size, 0)
+
+    def second_stage(keep, got, mine, bit):
+        total = low(keep.astype(jnp.float32) + got.astype(jnp.float32))
+        kept = lax.dynamic_index_in_dim(total, mine, 1, keepdims=False)
+        sent = lax.dynamic_index_in_dim(total, 1 - mine, 1, keepdims=False)
+        return low(kept.astype(jnp.float32) + flip(sent, size, bit).astype(jnp.float32))
+
+    first = second_stage(first_keep, first_got, rank & 1, 0)
+    second = second_stage(second_keep, second_got, (rank >> 1) & 1, 1)
+    block = jnp.concatenate([first, second], axis=-1)
+    place_high = rank >> 2
+    total = lax.dynamic_index_in_dim(block, place_high, 0, keepdims=False).astype(jnp.float32)
+    for turn in range(1, high):
+        sent = lax.dynamic_index_in_dim(block, (place_high + turn) % high, 0, keepdims=False)
+        total = total + rotate(sent, size, turn).astype(jnp.float32)
+    return total
 
 
 def scatter_sum(block, rank, size):
@@ -408,21 +549,39 @@
     table_rows = cond_table.shape[0]
     is_first = section_rank == 0
     layout = (width, hidden, rows, ratio, ring_size, 1.0 / sharers, bias_count)
-
+    compact = ring_size in (8, 16) and seq_size == slots == 2
+    place = jnp.stack([ring_rank >> 2, (ring_rank >> 1) & 1, ring_rank & 1]).astype(jnp.int32)
+
+    flat_ids = time_ids.reshape(-1)
+    selector = (
+        flat_ids[:, None] == jnp.arange(table_rows, dtype=jnp.int32)[None, :]
+    ).astype(jnp.bfloat16)
+    conditions = matmul(selector, cond_table)
+    silu_all = jax.nn.silu(conditions).astype(jnp.bfloat16)
+    silu_own = lax.dynamic_slice_in_dim(silu_all, ring_rank * rows, rows, 1)
+    products = jnp.repeat(matmul(silu_own, modulation_weight[0]), sharers, axis=0)
+    products = lax.all_to_all(
+        products[:, None], ("section", "dp", "seq"), 0, 0, tiled=True
+    ).reshape(sections, ring_size, 6 * width)
+    first_modulation, second_modulation = jnp.split(jnp.sum(products, axis=1), 2, axis=0)
+
+    lanes = 4 * width + 2 * hidden + 128
     bias_block = jnp.pad(biases[0], (0, bias_rows * 128 - bias_count)).reshape(bias_rows, 128)
-    packed = jnp.concatenate(
-        [
-            attention_weight[0],
-            output_weight[0],
-            expand_weight[0],
-            modulation_weight[0],
-            *[shrink_weight[0, j * rows : (j + 1) * rows] for j in range(ratio)],
-            jnp.pad(bias_block, ((0, rows - bias_rows), (0, 0))),
-        ],
-        axis=1,
-    )
-    own_pack = lax.all_gather(packed, RING, axis=0, tiled=True)
+    bias_block = jnp.pad(bias_block, ((0, rows - bias_rows), (0, 0)))
+    (packed,) = in_memory(
+        partial(pack_kernel, rows, ratio),
+        [jax.ShapeDtypeStruct((rows, lanes), jnp.bfloat16)],
+        [attention_weight[0], output_weight[0], expand_weight[0], shrink_weight[0], bias_block],
+        scalars=0,
+        memory=pltpu.VMEM,
+    )
+    if compact:
+        own_pack = gather_compact(packed, place, ring_size, (4 * width + 2 * hidden) // 2)
+    else:
+        own_pack = lax.all_gather(packed, RING, axis=0, tiled=True)
     packs = (own_pack, pair_swap(own_pack, "section"))
+    own_matrix = lax.all_gather(modulation_weight[0], RING, axis=0, tiled=True)
+    other_matrix = pair_swap(own_matrix, "section")
 
     live = (
         slot < lax.dynamic_index_in_dim(row_counts, section_rank, 0, keepdims=False)[0]
@@ -434,51 +593,82 @@
         ],
         axis=1,
     )
-    both = jnp.repeat(both, sharers, axis=0)
-    both = lax.all_to_all(both, "seq", 0, 0, tiled=True)
-    first_input = both[:, 0].reshape(length, width)
-    last_grad = both[:, 1].reshape(length, width) * live
-    flat_ids = time_ids.reshape(-1)
-    selector = (
-        flat_ids[:, None] == jnp.arange(table_rows, dtype=jnp.int32)[None, :]
-    ).astype(jnp.bfloat16)
-    conditions = matmul(selector, cond_table)
-    silu_all = jax.nn.silu(conditions).astype(jnp.bfloat16)
-    latent = section_rank * time_ids.shape[1] + data_rank * slots + slot
-    condition = lax.dynamic_slice_in_dim(conditions, latent, 1, 0)
-    silu_now = jnp.broadcast_to(lax.dynamic_slice_in_dim(silu_all, latent, 1, 0), (16, width))
+
+    def side_by_side(mine, got, axis):
+        return jnp.where(
+            seq_rank == 0,
+            jnp.concatenate([mine, got], axis=axis),
+            jnp.concatenate([got, mine], axis=axis),
+        )
+
+    if compact:
+        mine = lax.dynamic_index_in_dim(both, seq_rank, 0, keepdims=False)
+        sent = lax.dynamic_index_in_dim(both, 1 - seq_rank, 0, keepdims=False)
+        both = side_by_side(mine, pair_swap(sent, "seq"), 1)
+    else:
+        both = lax.all_to_all(jnp.repeat(both, sharers, axis=0), "seq", 0, 0, tiled=True)
+        both = jnp.swapaxes(both, 0, 1).reshape(2, length, width)
+    first_input = both[0]
+    last_grad = both[1] * live
 
     first_flags = jnp.stack([is_first, ~is_first]).astype(jnp.int32)
     second_flags = jnp.stack([~is_first, ~is_first]).astype(jnp.int32)
-    (first_low,) = run_section(layout, first_flags, first_input, silu_now, packs)
+    (first_low,) = run_section(layout, first_flags, first_input, first_modulation, packs)
     second_low, second_grad, second_row, second_keep, second_send = run_section(
-        layout, second_flags, first_low, silu_now, packs, last_grad
+        layout, second_flags, first_low, second_modulation, packs, last_grad
     )
     second_got = pair_swap(second_send, "section")
     _, first_grad, first_row, first_keep, first_send = run_section(
-        layout, first_flags, first_input, silu_now, packs, second_grad
+        layout, first_flags, first_input, first_modulation, packs, second_grad
     )
     first_got = pair_swap(first_send, "section")
 
-    def to_owners(first, second):
-        pieces = jnp.stack([first, second]).reshape(2 * seq_size, tokens, width)
+    early = jnp.stack([first_low * live, second_low * live, second_grad])
+    if compact:
+
+        def halves_of(block):
+            return block.reshape(-1, 2, tokens, width)
+
+        def to_slots(block):
+            block = halves_of(block)
+            mine = lax.dynamic_index_in_dim(block, seq_rank, 1, keepdims=True)
+            sent = lax.dynamic_index_in_dim(block, 1 - seq_rank, 1, keepdims=True)
+            return side_by_side(mine, pair_swap(sent, "seq"), 1)
+
+        early, late = to_slots(early), to_slots(first_grad)
+        per_first = jnp.stack([early[0], late[0]])
+        per_second = early[1:]
+        mine = jnp.where(is_first, per_first, per_second)
+        got = pair_swap(jnp.where(is_first, per_second, per_first), "section")
+        outputs = jnp.where(is_first, jnp.stack([mine, got], 1), jnp.stack([got, mine], 1))
+    else:
+        pieces = jnp.stack([early[0], first_grad, early[1], early[2]])
+        pieces = jnp.swapaxes(pieces.reshape(2, 2, seq_size, tokens, width), 1, 2)
+        pieces = pieces.reshape(2 * seq_size, 2, tokens, width)
         pieces = lax.all_to_all(pieces, ("section", "seq"), 0, 0, tiled=True)
-        return pieces.reshape(batches, slots, sharers, tokens, width)[:, :, 0]
-
-    activations = to_owners(first_low * live, second_low * live)
-    input_grads = to_owners(first_grad, second_grad).astype(jnp.float32)
+        pieces = pieces.reshape(batches, slots, sharers, 2, tokens, width)[:, :, 0]
+        outputs = jnp.moveaxis(pieces, 2, 0)
+    activations = outputs[0]
+    input_grads = outputs[1].astype(jnp.float32)
 
     half = first_keep.shape[1]
-
-    def chip_sum(keep, got):
-        total = keep.astype(jnp.float32) + got.astype(jnp.float32)
-        return total.astype(jnp.bfloat16).reshape(ring_size, 1, rows, half)
-
-    ring_terms = jnp.concatenate(
-        [chip_sum(first_keep, first_got), chip_sum(second_keep, second_got)], axis=1
-    )
-    owned = scatter_sum(ring_terms.reshape(ring_size, 2 * rows, half), ring_rank, ring_size)
-    owned = owned.reshape(2, rows, half)
+    if compact:
+        terms = [
+            term.reshape(ring_size, rows, half)
+            for term in (first_keep, first_got, second_keep, second_got)
+        ]
+        owned = scatter_compact(terms, place, ring_rank, ring_size)
+    else:
+
+        def chip_sum(keep, got):
+            total = keep.astype(jnp.float32) + got.astype(jnp.float32)
+            return total.astype(jnp.bfloat16).reshape(ring_size, 1, rows, half)
+
+        ring_terms = jnp.concatenate(
+            [chip_sum(first_keep, first_got), chip_sum(second_keep, second_got)], axis=1
+        )
+        owned = scatter_sum(ring_terms.reshape(ring_size, 2 * rows, half), ring_rank, ring_size)
+        owned = owned.reshape(2, rows, half)
     mine = lax.dynamic_index_in_dim(owned, section_rank, 0, keepdims=False)
     theirs = pair_swap(
         lax.dynamic_index_in_dim(owned, 1 - section_rank, 0, keepdims=False), "section"
@@ -494,19 +684,23 @@
         [full[:, edges[3] + j * width : edges[3] + (j + 1) * width] for j in range(ratio)], axis=0
     )
 
-    per_row = 10 * width + hidden
-    _, silu_back = jax.vjp(jax.nn.silu, condition)
-    grad_condition = silu_back(first_row[:, per_row:] + second_row[:, per_row:])[0]
-    row = jnp.concatenate([first_row[:, :per_row], second_row[:, :per_row], grad_condition], axis=1)
+    row = jnp.concatenate([first_row, second_row], axis=1)
+    per_row = first_row.shape[1]
     every = lax.all_gather(row, ("section", "dp", "seq"), axis=0, tiled=True)[::sharers]
-    section_rows = jnp.where(is_first, every[:, :per_row], every[:, per_row : 2 * per_row])
-    bias_total = jnp.sum(section_rows, axis=0)
+    first_rows, second_rows = every[:, :per_row], every[:, per_row:]
+    own_rows = jnp.where(is_first, first_rows, second_rows)
+    other_rows = jnp.where(is_first, second_rows, first_rows)[:, : 6 * width]
+    bias_total = jnp.sum(own_rows, axis=0)
     bias_grad = lax.dynamic_slice_in_dim(bias_total, ring_rank * bias_count, bias_count, 0)
-    silu_own = lax.dynamic_slice_in_dim(silu_all, ring_rank * rows, rows, 1)
-    modulation_grad = outer_sum(silu_own, section_rows[:, : 6 * width].astype(jnp.bfloat16))
+    own_rows = low(own_rows[:, : 6 * width])
+    modulation_grad = outer_sum(silu_own, own_rows)
+    _, silu_back = jax.vjp(jax.nn.silu, conditions)
+    grad_conditions = silu_back(
+        matmul_transposed(own_rows, own_matrix) + matmul_transposed(low(other_rows), other_matrix)
+    )[0]
     table_grad = lax.dot_general(
         selector.astype(jnp.float32),
-        every[:, 2 * per_row :],
+        grad_conditions,
         (((0,), (0,)), ((), ())),
         precision=lax.Precision.HIGHEST,
         preferred_element_type=jnp.float32,

time: 274 us -> 244 us (0.89)
  waiting for transfers between devices: 152 us -> 128 us
  local copies, waits for them, and re-layouts: 25.3 us -> 14.2 us
  Pallas kernels: 36.8 us -> 43.1 us
  other arithmetic: 14.1 us -> 9.54 us
  starting transfers between devices: 24.2 us -> 27.7 us
  matrix products: 3.46 us -> 6.28 us
    all_gather x1, waiting for transfers between devices: 86.3 us -> 0.01 us  [per_device(): own_matrix = lax.all_gather(modulation_weight[0], RING, axis=0, tiled=True)]
    ppermute x7 -> x16, waiting for transfers between devices: 35 us -> 79 us  [ring_exchange(): return lax.ppermute(block, RING, [(i, step(i)) for i in range(size)])]
    all_to_all x3 -> x1, waiting for transfers between devices: 29.8 us -> 0.01 us  [per_device(): lax.all_to_all(products[:, None], ('section', 'dp', 'seq'), 0, 0, tiled=T...]
    all_gather x1, waiting for transfers between devices: 0.01 us -> 27.9 us  [per_device(): lax.all_gather(row, ('section', 'dp', 'seq'), axis=0, tiled=True)[::sharers]]
    ppermute x4 -> x9, waiting for transfers between devices: 1.25 us -> 20.8 us  [pair_swap(): return lax.ppermute(block, axis, [(0, 1), (1, 0)])]
    all_to_all x3 -> x1, starting transfers between devices: 12.3 us -> 2.83 us  [per_device(): lax.all_to_all(products[:, None], ('section', 'dp', 'seq'), 0, 0, tiled=T...]
    ppermute x7 -> x16, starting transfers between devices: 7.8 us -> 16.6 us  [ring_exchange(): return lax.ppermute(block, RING, [(i, step(i)) for i in range(size)])]
    pallas_call x0 -> x4, Pallas kernels: none -> 7.17 us  [in_memory(): pl.pallas_call(kernel, out_shape=shapes, in_specs=specs, out_specs=[pl.Bl...]
  transfers between devices with their start and end apart: 16 -> 28, of which waited for: 10 -> 16; matrix products, arithmetic and copies ran while one was open for 9% -> 8% of each run, Pallas kernels for 6% -> 16%
where the time goes in v3:
time: 244 us
  waiting for transfers between devices  128 us (52%)
  Pallas kernels  43.1 us (18%)
  starting transfers between devices  27.7 us (11%)
  between operations  15.2 us (6%)
  local copies, waits for them, and re-layouts  14.2 us (6%)
  other arithmetic  9.54 us (4%)
  matrix products  6.28 us (3%)
    ppermute x16, waiting for transfers between devices, ring_exchange(): return lax.ppermute(block, RING, [(i, step(i)) for i in range(size)])  79 us
    pallas_call x3, Pallas kernels, run_section(): pl.pallas_call(partial(section_kernel, layout, backward), out_shape=shape...  35.9 us
    all_gather x1, waiting for transfers between devices, per_device(): lax.all_gather(row, ('section', 'dp', 'seq'), axis=0, tiled=True)[::sharers]  27.9 us
    ppermute x9, waiting for transfers between devices, pair_swap(): return lax.ppermute(block, axis, [(0, 1), (1, 0)])  20.8 us
    ppermute x16, starting transfers between devices, ring_exchange(): return lax.ppermute(block, RING, [(i, step(i)) for i in range(size)])  16.6 us
    ppermute x9, starting transfers between devices, pair_swap(): return lax.ppermute(block, axis, [(0, 1), (1, 0)])  8.17 us
    unnamed x40, local copies, waits for them, and re-layouts  7.25 us
    pallas_call x4, Pallas kernels, in_memory(): pl.pallas_call(kernel, out_shape=shapes, in_specs=specs, out_specs=[pl.Bl...  7.17 us
  transfers between devices with their start and end apart: 28, of which 16 were waited for; matrix products, arithmetic and copies ran while one was open for 8% of the time, Pallas kernels for 16%

profile of v3, /device:TPU:9, one launch (start us, length us, event | category | flops | bytes accessed | tf_op | source)
XLA Modules:
  0.0 243.8 jit_solution(15263232876859415774)
XLA Ops:
  11.3 1.3 collective-permute-start.1
  13.8 1.4 collective-permute-start.3
  15.2 2.6 %collective-permute-done.1.refs_1_ = bf16[24,4736]{1,0:T(8,128)(2,1)S(1)} collective-permute-done((bf16[24,4736]{1,0:T(8,128)(2,1)S(1)}, bf16[24,4736]{1,0:T(8,128)(2,1)S(1)}, u32[]{:S(2)}, u32[]{:S(2)}) %collective-permute-start.1) | collective-permute-done | bytes 227360 | tf_op jit(solution)/shard_map/ppermute | solution.py:414
  17.8 13.7 %collective-permute-done.2.refs_2_ = bf16[24,4736]{1,0:T(8,128)(2,1)S(1)} collective-permute-done((bf16[24,4736]{1,0:T(8,128)(2,1)S(1)}, bf16[24,4736]{1,0:T(8,128)(2,1)S(1)}, u32[]{:S(2)}, u32[]{:S(2)}) %collective-permute-start.2) | collective-permute-done | bytes 227360 | tf_op jit(solution)/shard_map/ppermute | solution.py:414
  31.5 2.8 %collective-permute-done.3.refs_3_ = bf16[24,4736]{1,0:T(8,128)(2,1)S(1)} collective-permute-done((bf16[24,4736]{1,0:T(8,128)(2,1)S(1)}, bf16[24,4736]{1,0:T(8,128)(2,1)S(1)}, u32[]{:S(2)}, u32[]{:S(2)}) %collective-permute-start.3) | collective-permute-done | bytes 227360 | tf_op jit(solution)/shard_map/ppermute | solution.py:414
  35.4 1.3 collective-permute-start.8
  38.2 9.1 %collective-permute-done.8.refs_6_ = bf16[4,24,2432]{2,1,0:T(8,128)(2,1)S(1)} collective-permute-done((bf16[4,24,2432]{2,1,0:T(8,128)(2,1)S(1)}, bf16[4,24,2432]{2,1,0:T(8,128)(2,1)S(1)}, u32[]{:S(2)}, u32[]{:S(2)}) %collective-permute-start.8) | collective-permute-done | bytes 466976 | tf_op jit(solution)/shard_map/ppermute | solution.py:414
  49.9 8.6 %collective-permute-done.5.refs_2_ = bf16[4,24,2304]{2,1,0:T(8,128)(2,1)S(1)} collective-permute-done((bf16[4,24,2304]{2,1,0:T(8,128)(2,1)S(1)}, bf16[4,24,2304]{2,1,0:T(8,128)(2,1)S(1)}, u32[]{:S(2)}, u32[]{:S(2)}) %collective-permute-start.5) | collective-permute-done | bytes 442400 | tf_op jit(solution)/shard_map/ppermute | solution.py:414
  58.5 9.5 %collective-permute-done.6.refs_3_ = bf16[4,24,2304]{2,1,0:T(8,128)(2,1)S(1)} collective-permute-done((bf16[4,24,2304]{2,1,0:T(8,128)(2,1)S(1)}, bf16[4,24,2304]{2,1,0:T(8,128)(2,1)S(1)}, u32[]{:S(2)}, u32[]{:S(2)}) %collective-permute-start.6) | collective-permute-done | bytes 442400 | tf_op jit(solution)/shard_map/ppermute | solution.py:414
  68.0 2.4 %shard_map.180 = bf16[4,2,2,24,4736]{4,3,2,1,0:T(8,128)(2,1)} custom-call(s32[3]{0:T(128)S(1)} %pad_add_fusion.place_ref, bf16[4,24,2304]{2,1,0:T(8,128)(2,1)S(1)} %get-tuple-element.24.refs_0_, bf16[4,24,2304]{2,1,0:T(8,128)(2,1)S(1)} %collective-permute-done.4.refs_1_, bf16[4,24,2304]{2,1,0:T(8,128)(2,1)S(1)} %collective-permute-done.5.refs_2_, ...), custom_call_target="tpu_custom_call" | custom-call | bytes 7274496 | tf_op jit(solution)/shard_map/pallas_call | solution.py:398
  70.4 2.6 %collective-permute-start.10 = (bf16[384,4736]{1,0:T(8,128)(2,1)}, bf16[384,4736]{1,0:T(8,128)(2,1)}, u32[]{:S(2)}, u32[]{:S(2)}) collective-permute-start(bf16[384,4736]{1,0:T(8,128)(2,1)} %bitcast.17.refs_3_.refs_4_), channel_id=1, source_target_pairs={{0,16},{16,0},{1,17},{17,1},{2,18},{18,2},{3,19},{19,3},{4,20},{20... | collective-permute-start | bytes 10911752 | tf_op jit(solution)/shard_map/ppermute | solution.py:410
  75.3 2.8 %all-to-all-start = ((f32[32,1,2304]{2,1,0:T(1,128)}), f32[32,1,2304]{2,1,0:T(1,128)S(1)}, u32[]{:S(2)}, u32[]{:S(2)}) async-start(f32[32,1,2304]{2,1,0:T(1,128)} %copy.22), calls=%async_computation | async-start | bytes 589824 | tf_op jit(solution)/shard_map/all_to_all | solution.py:563
  78.4 1.2 collective-permute-start
  81.0 6.8 %collective-permute-done = bf16[2,128,384]{2,1,0:T(8,128)(2,1)S(1)} collective-permute-done((bf16[2,128,384]{2,1,0:T(8,128)(2,1)S(1)}, bf16[2,128,384]{2,1,0:T(8,128)(2,1)S(1)}, u32[]{:S(2)}, u32[]{:S(2)}) %collective-permute-start) | collective-permute-done | bytes 196640 | tf_op jit(solution)/shard_map/ppermute | solution.py:410
  88.2 6.7 %shard_map.181.refs_1_ = bf16[256,384]{1,0:T(8,128)(2,1)S(1)} custom-call(s32[2]{0:T(128)S(1)} %get-tuple-element.69.refs_0_, bf16[256,384]{1,0:T(8,128)(2,1)S(1)} %get-tuple-element.60.refs_1_, f32[1,2304]{1,0:T(1,128)S(1)} %get-tuple-element.66.refs_2_, bf16[384,4736]{1,0:T(8,128)(2,1)} %bitcast.17.refs_3_.refs_4_, ...), custom_call_target="tpu_custom_call" | custom-call | flops 1006632960 | bytes 5308416 | tf_op jit(solution)/shard_map/pallas_call | solution.py:309
  94.9 14.2 %shard_map.182 = (bf16[256,384]{1,0:T(8,128)(2,1)S(1)}, bf16[256,384]{1,0:T(8,128)(2,1)S(1)}, f32[1,5376]{1,0:T(1,128)S(1)}, bf16[384,2304]{1,0:T(8,128)(2,1)S(1)}, bf16[384,2304]{1,0:T(8,128)(2,1)}) custom-call(s32[2]{0:T(128)S(1)} %get-tuple-element.70.refs_0_, bf16[256,384]{1,0:T(8,128)(2,1)S(1)} %shard_map.181.refs_1_, ...), custom_call_target="tpu_custom_call" | custom-call | flops 3019898880 | bytes 10616832 | tf_op jit(solution)/shard_map/pallas_call | solution.py:309
  109.1 15.0 %shard_map.183 = (bf16[256,384]{1,0:T(8,128)(2,1)}, bf16[256,384]{1,0:T(8,128)(2,1)S(1)}, f32[1,5376]{1,0:T(1,128)S(1)}, bf16[384,2304]{1,0:T(8,128)(2,1)S(1)}, bf16[384,2304]{1,0:T(8,128)(2,1)}) custom-call(s32[2]{0:T(128)S(1)} %get-tuple-element.69.refs_0_, bf16[256,384]{1,0:T(8,128)(2,1)S(1)} %get-tuple-element.60.refs_1_, ...), custom_call_target="tpu_custom_call" | custom-call | flops 3019898880 | bytes 10616832 | tf_op jit(solution)/shard_map/pallas_call | solution.py:309
  128.5 3.6 %collective-permute-done.12 = bf16[1,1,128,384]{3,2,1,0:T(8,128)(2,1)} collective-permute-done((bf16[1,1,128,384]{3,2,1,0:T(8,128)(2,1)}, bf16[1,1,128,384]{3,2,1,0:T(8,128)(2,1)}, u32[]{:S(2)}, u32[]{:S(2)}) %collective-permute-start.12) | collective-permute-done | bytes 98336 | tf_op jit(solution)/shard_map/ppermute | solution.py:410
  133.1 9.1 %collective-permute-done.11 = bf16[3,1,128,384]{3,2,1,0:T(8,128)(2,1)S(1)} collective-permute-done((bf16[3,1,128,384]{3,2,1,0:T(8,128)(2,1)}, bf16[3,1,128,384]{3,2,1,0:T(8,128)(2,1)S(1)}, u32[]{:S(2)}, u32[]{:S(2)}) %collective-permute-start.11) | collective-permute-done | bytes 294944 | tf_op jit(solution)/shard_map/ppermute | solution.py:410
  142.3 3.7 %shard_map.184 = (bf16[4,2,2,24,1152]{4,3,2,1,0:T(8,128)(2,1)S(1)}, bf16[4,2,2,24,1152]{4,3,2,1,0:T(8,128)(2,1)S(1)}, bf16[4,2,2,24,1152]{4,3,2,1,0:T(8,128)(2,1)S(1)}, bf16[4,2,2,24,1152]{4,3,2,1,0:T(8,128)(2,1)}) custom-call(s32[3]{0:T(128)S(1)} %pad_add_fusion.place_ref, bf16[16,24,2304]{2,1,0:T(8,128)(2,1)S(1)} %bitcast.90, ...), custom_call_target="tpu_custom_call" | custom-call | bytes 7077888 | tf_op jit(solution)/shard_map/pallas_call | solution.py:398
  149.3 1.3 collective-permute-done.13
  151.9 1.3 collective-permute-start.17
  154.3 14.9 %collective-permute-done.19 = bf16[4,2,2,24,1152]{4,3,2,1,0:T(8,128)(2,1)} collective-permute-done((bf16[4,2,2,24,1152]{4,3,2,1,0:T(8,128)(2,1)}, bf16[4,2,2,24,1152]{4,3,2,1,0:T(8,128)(2,1)}, u32[]{:S(2)}, u32[]{:S(2)}) %collective-permute-start.19) | collective-permute-done | bytes 884768 | tf_op jit(solution)/shard_map/ppermute | solution.py:414
  169.2 1.5 add_convert_fusion
  171.9 1.3 collective-permute-done.17
  175.4 27.9 %all-gather.7.cloned.1.call-done = f32[32,1,10752]{2,1,0:T(1,128)} async-done(((f32[1,1,10752]{2,1,0:T(1,128)}), f32[32,1,10752]{2,1,0:T(1,128)}) %all-gather.7.cloned.1.call-update) | async-done | bytes 1376272 | tf_op jit(solution)/shard_map/all_gather | solution.py:689
  203.3 1.4 copy.29
  209.3 2.5 %collective-permute-start.22 = (bf16[2,24,2304]{2,1,0:T(8,128)(2,1)S(1)}, bf16[2,24,2304]{2,1,0:T(8,128)(2,1)S(1)}, u32[]{:S(2)}, u32[]{:S(2)}) collective-permute-start(bf16[2,24,2304]{2,1,0:T(8,128)(2,1)S(1)} %get-tuple-element.46), channel_id=1, source_target_pairs={{0,8},{1,9},{2,10},{3,11},{4,12},{5,13},{6,14},{7,15},{8,0},{9,1},... | collective-permute-start | bytes 663560 | tf_op jit(solution)/shard_map/ppermute | solution.py:414
  212.0 2.1 convolution_add_fusion
  215.3 12.8 %collective-permute-done.22 = bf16[2,24,2304]{2,1,0:T(8,128)(2,1)S(1)} collective-permute-done((bf16[2,24,2304]{2,1,0:T(8,128)(2,1)S(1)}, bf16[2,24,2304]{2,1,0:T(8,128)(2,1)S(1)}, u32[]{:S(2)}, u32[]{:S(2)}) %collective-permute-start.22) | collective-permute-done | bytes 221216 | tf_op jit(solution)/shard_map/ppermute | solution.py:414
  228.1 2.6 %collective-permute-done.23 = bf16[2,24,2304]{2,1,0:T(8,128)(2,1)S(1)} collective-permute-done((bf16[2,24,2304]{2,1,0:T(8,128)(2,1)S(1)}, bf16[2,24,2304]{2,1,0:T(8,128)(2,1)S(1)}, u32[]{:S(2)}, u32[]{:S(2)}) %collective-permute-start.23) | collective-permute-done | bytes 221216 | tf_op jit(solution)/shard_map/ppermute | solution.py:414
  232.1 2.2 fusion.20
  (125 shorter events, 38.3 us)
Async XLA Ops:
  7.2 66.0 %copy-start = (bf16[1000,384]{1,0:T(8,128)(2,1)S(1)}, bf16[1000,384]{1,0:T(8,128)(2,1)}, u32[]{:S(2)}) copy-start(bf16[1000,384]{1,0:T(8,128)(2,1)} %param.15) | copy-start | bytes 2304004
  11.3 6.5 %collective-permute-start.1 = (bf16[24,4736]{1,0:T(8,128)(2,1)S(1)}, bf16[24,4736]{1,0:T(8,128)(2,1)S(1)}, u32[]{:S(2)}, u32[]{:S(2)}) collective-permute-start(bf16[24,4736]{1,0:T(8,128)(2,1)S(1)} %shard_map.178.refs_0_), channel_id=1, source_target_pairs={{0,4},{1,5},{2,6},{3,7},{4,8},{5,9},{6,10},{7,11},{8,12},{9,13},{1... | collective-permute-start | bytes 681992 | tf_op jit(solution)/shard_map/ppermute | solution.py:414
  12.7 18.8 %collective-permute-start.2 = (bf16[24,4736]{1,0:T(8,128)(2,1)S(1)}, bf16[24,4736]{1,0:T(8,128)(2,1)S(1)}, u32[]{:S(2)}, u32[]{:S(2)}) collective-permute-start(bf16[24,4736]{1,0:T(8,128)(2,1)S(1)} %shard_map.178.refs_0_), channel_id=1, source_target_pairs={{0,8},{1,9},{2,10},{3,11},{4,12},{5,13},{6,14},{7,15},{8,0},{9,1},... | collective-permute-start | bytes 681992 | tf_op jit(solution)/shard_map/ppermute | solution.py:414
  13.8 20.6 %collective-permute-start.3 = (bf16[24,4736]{1,0:T(8,128)(2,1)S(1)}, bf16[24,4736]{1,0:T(8,128)(2,1)S(1)}, u32[]{:S(2)}, u32[]{:S(2)}) collective-permute-start(bf16[24,4736]{1,0:T(8,128)(2,1)S(1)} %shard_map.178.refs_0_), channel_id=1, source_target_pairs={{0,12},{1,13},{2,14},{3,15},{4,0},{5,1},{6,2},{7,3},{8,4},{9,5},{1... | collective-permute-start | bytes 681992 | tf_op jit(solution)/shard_map/ppermute | solution.py:414
  35.4 11.8 %collective-permute-start.8 = (bf16[4,24,2432]{2,1,0:T(8,128)(2,1)S(1)}, bf16[4,24,2432]{2,1,0:T(8,128)(2,1)S(1)}, u32[]{:S(2)}, u32[]{:S(2)}) collective-permute-start(bf16[4,24,2432]{2,1,0:T(8,128)(2,1)S(1)} %get-tuple-element.25.refs_4_), channel_id=1, source_target_pairs={{0,1},{1,0},{2,3},{3,2},{4,5},{5,4},{6,7},{7,6},{8,9},{9,8},{10,11... | collective-permute-start | bytes 1400840 | tf_op jit(solution)/shard_map/ppermute | solution.py:414
  36.7 36.4 %copy-start.17 = (s32[2,16]{1,0:T(2,128)S(1)}, s32[2,16]{1,0:T(2,128)}, u32[]{:S(2)}) copy-start(s32[2,16]{1,0:T(2,128)} %param.13) | copy-start | bytes 388
  36.7 37.4 %copy-start.12 = (bf16[1,24,2304]{2,1,0:T(8,128)(2,1)S(1)}, bf16[1,24,2304]{2,1,0:T(8,128)(2,1)}, u32[]{:S(2)}) copy-start(bf16[1,24,2304]{2,1,0:T(8,128)(2,1)} %param.16) | copy-start | bytes 331780
  36.7 13.0 %collective-permute-start.4 = (bf16[4,24,2304]{2,1,0:T(8,128)(2,1)S(1)}, bf16[4,24,2304]{2,1,0:T(8,128)(2,1)S(1)}, u32[]{:S(2)}, u32[]{:S(2)}) collective-permute-start(bf16[4,24,2304]{2,1,0:T(8,128)(2,1)S(1)} %get-tuple-element.24.refs_0_), channel_id=1, source_target_pairs={{0,2},{1,3},{2,0},{3,1},{4,6},{5,7},{6,4},{7,5},{8,10},{9,11},{10,... | collective-permute-start | bytes 1327112 | tf_op jit(solution)/shard_map/ppermute | solution.py:414
  37.9 20.6 %collective-permute-start.7 = (bf16[4,24,2432]{2,1,0:T(8,128)(2,1)S(1)}, bf16[4,24,2432]{2,1,0:T(8,128)(2,1)S(1)}, u32[]{:S(2)}, u32[]{:S(2)}) collective-permute-start(bf16[4,24,2432]{2,1,0:T(8,128)(2,1)S(1)} %get-tuple-element.25.refs_4_), channel_id=1, source_target_pairs={{0,2},{1,3},{2,0},{3,1},{4,6},{5,7},{6,4},{7,5},{8,10},{9,11},{10,... | collective-permute-start | bytes 1400840 | tf_op jit(solution)/shard_map/ppermute | solution.py:414
  47.2 20.7 %collective-permute-start.9 = (bf16[4,24,2432]{2,1,0:T(8,128)(2,1)S(1)}, bf16[4,24,2432]{2,1,0:T(8,128)(2,1)S(1)}, u32[]{:S(2)}, u32[]{:S(2)}) collective-permute-start(bf16[4,24,2432]{2,1,0:T(8,128)(2,1)S(1)} %collective-permute-done.8.refs_6_), channel_id=1, source_target_pairs={{0,2},{1,3},{2,0},{3,1},{4,6},{5,7},{6,4},{7,5},{8,10},{9,11},{10,... | collective-permute-start | bytes 1400840 | tf_op jit(solution)/shard_map/ppermute | solution.py:414
  48.4 10.0 %collective-permute-start.5 = (bf16[4,24,2304]{2,1,0:T(8,128)(2,1)S(1)}, bf16[4,24,2304]{2,1,0:T(8,128)(2,1)S(1)}, u32[]{:S(2)}, u32[]{:S(2)}) collective-permute-start(bf16[4,24,2304]{2,1,0:T(8,128)(2,1)S(1)} %get-tuple-element.24.refs_0_), channel_id=1, source_target_pairs={{0,1},{1,0},{2,3},{3,2},{4,5},{5,4},{6,7},{7,6},{8,9},{9,8},{10,11... | collective-permute-start | bytes 1327112 | tf_op jit(solution)/shard_map/ppermute | solution.py:414
  49.7 18.3 %collective-permute-start.6 = (bf16[4,24,2304]{2,1,0:T(8,128)(2,1)S(1)}, bf16[4,24,2304]{2,1,0:T(8,128)(2,1)S(1)}, u32[]{:S(2)}, u32[]{:S(2)}) collective-permute-start(bf16[4,24,2304]{2,1,0:T(8,128)(2,1)S(1)} %collective-permute-done.4.refs_1_), channel_id=1, source_target_pairs={{0,1},{1,0},{2,3},{3,2},{4,5},{5,4},{6,7},{7,6},{8,9},{9,8},{10,11... | collective-permute-start | bytes 1327112 | tf_op jit(solution)/shard_map/ppermute | solution.py:414
  70.4 17.7 %collective-permute-start.10 = (bf16[384,4736]{1,0:T(8,128)(2,1)}, bf16[384,4736]{1,0:T(8,128)(2,1)}, u32[]{:S(2)}, u32[]{:S(2)}) collective-permute-start(bf16[384,4736]{1,0:T(8,128)(2,1)} %bitcast.17.refs_3_.refs_4_), channel_id=1, source_target_pairs={{0,16},{16,0},{1,17},{17,1},{2,18},{18,2},{3,19},{19,3},{4,20},{20... | collective-permute-start | bytes 10911752 | tf_op jit(solution)/shard_map/ppermute | solution.py:410
  75.3 12.7 %all-to-all-start = ((f32[32,1,2304]{2,1,0:T(1,128)}), f32[32,1,2304]{2,1,0:T(1,128)S(1)}, u32[]{:S(2)}, u32[]{:S(2)}) async-start(f32[32,1,2304]{2,1,0:T(1,128)} %copy.22), calls=%async_computation | async-start | bytes 589824 | tf_op jit(solution)/shard_map/all_to_all | solution.py:563
  78.2 70.9 %all-gather.5.cloned.1.call-start = ((), (), s32[]{:S(2)}) async-start(), calls=%async_computation.1 | async-start | bytes 1880064 | tf_op jit(solution)/shard_map/all_gather | solution.py:583
  78.4 9.5 %collective-permute-start = (bf16[2,128,384]{2,1,0:T(8,128)(2,1)S(1)}, bf16[2,128,384]{2,1,0:T(8,128)(2,1)S(1)}, u32[]{:S(2)}, u32[]{:S(2)}) collective-permute-start(bf16[2,128,384]{2,1,0:T(8,128)(2,1)S(1)} %get-tuple-element.62), channel_id=1, source_target_pairs={{0,1},{1,0},{2,3},{3,2},{4,5},{5,4},{6,7},{7,6},{8,9},{9,8},{10,11... | collective-permute-start | bytes 589832 | tf_op jit(solution)/shard_map/ppermute | solution.py:410
  79.6 123.7 %all-gather.7.cloned.1.call-start = ((), (), s32[]{:S(2)}) async-start(), calls=%async_computation.2 | async-start | bytes 1419264 | tf_op jit(solution)/shard_map/all_gather | solution.py:689
  124.1 18.2 %collective-permute-start.15 = (bf16[384,2304]{1,0:T(8,128)(2,1)}, bf16[384,2304]{1,0:T(8,128)(2,1)}, u32[]{:S(2)}, u32[]{:S(2)}) collective-permute-start(bf16[384,2304]{1,0:T(8,128)(2,1)} %get-tuple-element.32), channel_id=1, source_target_pairs={{0,16},{16,0},{1,17},{17,1},{2,18},{18,2},{3,19},{19,3},{4,20},{20... | collective-permute-start | bytes 5308424 | tf_op jit(solution)/shard_map/ppermute | solution.py:410
  124.2 18.1 %collective-permute-start.16 = (bf16[384,2304]{1,0:T(8,128)(2,1)}, bf16[384,2304]{1,0:T(8,128)(2,1)}, u32[]{:S(2)}, u32[]{:S(2)}) collective-permute-start(bf16[384,2304]{1,0:T(8,128)(2,1)} %get-tuple-element.34), channel_id=1, source_target_pairs={{0,16},{16,0},{1,17},{17,1},{2,18},{18,2},{3,19},{19,3},{4,20},{20... | collective-permute-start | bytes 5308424 | tf_op jit(solution)/shard_map/ppermute | solution.py:410
  125.4 6.7 %collective-permute-start.12 = (bf16[1,1,128,384]{3,2,1,0:T(8,128)(2,1)}, bf16[1,1,128,384]{3,2,1,0:T(8,128)(2,1)}, u32[]{:S(2)}, u32[]{:S(2)}) collective-permute-start(bf16[1,1,128,384]{3,2,1,0:T(8,128)(2,1)} %get-tuple-element.64), channel_id=1, source_target_pairs={{0,1},{1,0},{2,3},{3,2},{4,5},{5,4},{6,7},{7,6},{8,9},{9,8},{10,11... | collective-permute-start | bytes 294920 | tf_op jit(solution)/shard_map/ppermute | solution.py:410
  127.1 15.1 %collective-permute-start.11 = (bf16[3,1,128,384]{3,2,1,0:T(8,128)(2,1)}, bf16[3,1,128,384]{3,2,1,0:T(8,128)(2,1)S(1)}, u32[]{:S(2)}, u32[]{:S(2)}) collective-permute-start(bf16[3,1,128,384]{3,2,1,0:T(8,128)(2,1)} %get-tuple-element.51), channel_id=1, source_target_pairs={{0,1},{1,0},{2,3},{3,2},{4,5},{5,4},{6,7},{7,6},{8,9},{9,8},{10,11... | collective-permute-start | bytes 884744 | tf_op jit(solution)/shard_map/ppermute | solution.py:410
  147.9 21.3 %collective-permute-start.19 = (bf16[4,2,2,24,1152]{4,3,2,1,0:T(8,128)(2,1)}, bf16[4,2,2,24,1152]{4,3,2,1,0:T(8,128)(2,1)}, u32[]{:S(2)}, u32[]{:S(2)}) collective-permute-start(bf16[4,2,2,24,1152]{4,3,2,1,0:T(8,128)(2,1)} %get-tuple-element.38), channel_id=1, source_target_pairs={{0,1},{1,0},{2,3},{3,2},{4,5},{5,4},{6,7},{7,6},{8,9},{9,8},{10,11... | collective-permute-start | bytes 2654216 | tf_op jit(solution)/shard_map/ppermute | solution.py:414
  148.2 2.4 collective-permute-start.13
  149.1 62.9 %collective-permute-start.14 = (bf16[384,2304]{1,0:T(8,128)(2,1)}, bf16[384,2304]{1,0:T(8,128)(2,1)}, u32[]{:S(2)}, u32[]{:S(2)}) collective-permute-start(bf16[384,2304]{1,0:T(8,128)(2,1)} %bitcast.99), channel_id=1, source_target_pairs={{0,16},{16,0},{1,17},{17,1},{2,18},{18,2},{3,19},{19,3},{4,20},{20... | collective-permute-start | bytes 5308424 | tf_op jit(solution)/shard_map/ppermute | solution.py:410
  151.9 21.2 %collective-permute-start.17 = (bf16[4,2,2,24,1152]{4,3,2,0,1:T(8,128)(2,1)S(1)}, bf16[4,2,2,24,1152]{4,3,2,0,1:T(8,128)(2,1)S(1)}, u32[]{:S(2)}, u32[]{:S(2)}) collective-permute-start(bf16[4,2,2,24,1152]{4,3,2,0,1:T(8,128)(2,1)S(1)} %copy.24), channel_id=1, source_target_pairs={{0,2},{1,3},{2,0},{3,1},{4,6},{5,7},{6,4},{7,5},{8,10},{9,11},{10,... | collective-permute-start | bytes 2654216 | tf_op jit(solution)/shard_map/ppermute | solution.py:414
  170.7 36.4 %collective-permute-start.20 = (bf16[4,2,24,1152]{3,2,1,0:T(8,128)(2,1)S(1)}, bf16[4,2,24,1152]{3,2,1,0:T(8,128)(2,1)S(1)}, u32[]{:S(2)}, u32[]{:S(2)}) collective-permute-start(bf16[4,2,24,1152]{3,2,1,0:T(8,128)(2,1)S(1)} %dynamic-slice_bitcast_fusion), channel_id=1, source_target_pairs={{0,2},{1,3},{2,0},{3,1},{4,6},{5,7},{6,4},{7,5},{8,10},{9,11},{10,... | collective-permute-start | bytes 1327112 | tf_op jit(solution)/shard_map/ppermute | solution.py:414
  174.2 33.1 %collective-permute-start.18 = (bf16[4,2,24,1152]{3,2,1,0:T(8,128)(2,1)}, bf16[4,2,24,1152]{3,2,1,0:T(8,128)(2,1)}, u32[]{:S(2)}, u32[]{:S(2)}) collective-permute-start(bf16[4,2,24,1152]{3,2,1,0:T(8,128)(2,1)} %dynamic-slice_bitcast_fusion.1), channel_id=1, source_target_pairs={{0,1},{1,0},{2,3},{3,2},{4,5},{5,4},{6,7},{7,6},{8,9},{9,8},{10,11... | collective-permute-start | bytes 1327112 | tf_op jit(solution)/shard_map/ppermute | solution.py:414
  208.5 6.8 %collective-permute-start.21 = (bf16[2,24,2304]{2,1,0:T(8,128)(2,1)S(1)}, bf16[2,24,2304]{2,1,0:T(8,128)(2,1)S(1)}, u32[]{:S(2)}, u32[]{:S(2)}) collective-permute-start(bf16[2,24,2304]{2,1,0:T(8,128)(2,1)S(1)} %get-tuple-element.45), channel_id=1, source_target_pairs={{0,4},{1,5},{2,6},{3,7},{4,8},{5,9},{6,10},{7,11},{8,12},{9,13},{1... | collective-permute-start | bytes 663560 | tf_op jit(solution)/shard_map/ppermute | solution.py:414
  209.3 18.8 %collective-permute-start.22 = (bf16[2,24,2304]{2,1,0:T(8,128)(2,1)S(1)}, bf16[2,24,2304]{2,1,0:T(8,128)(2,1)S(1)}, u32[]{:S(2)}, u32[]{:S(2)}) collective-permute-start(bf16[2,24,2304]{2,1,0:T(8,128)(2,1)S(1)} %get-tuple-element.46), channel_id=1, source_target_pairs={{0,8},{1,9},{2,10},{3,11},{4,12},{5,13},{6,14},{7,15},{8,0},{9,1},... | collective-permute-start | bytes 663560 | tf_op jit(solution)/shard_map/ppermute | solution.py:414
  211.8 18.9 %collective-permute-start.23 = (bf16[2,24,2304]{2,1,0:T(8,128)(2,1)S(1)}, bf16[2,24,2304]{2,1,0:T(8,128)(2,1)S(1)}, u32[]{:S(2)}, u32[]{:S(2)}) collective-permute-start(bf16[2,24,2304]{2,1,0:T(8,128)(2,1)S(1)} %get-tuple-element.47), channel_id=1, source_target_pairs={{0,12},{1,13},{2,14},{3,15},{4,0},{5,1},{6,2},{7,3},{8,4},{9,5},{1... | collective-permute-start | bytes 663560 | tf_op jit(solution)/shard_map/ppermute | solution.py:414
  214.1 18.0 %copy-start.14 = (f32[32,384]{1,0:T(8,128)S(1)}, f32[32,384]{1,0:T(8,128)}, u32[]{:S(2)}) copy-start(f32[32,384]{1,0:T(8,128)} %copy-done.13) | copy-start | bytes 147460
  230.9 3.4 %collective-permute-start.24 = (f32[24,2304]{1,0:T(8,128)S(1)}, f32[24,2304]{1,0:T(8,128)S(1)}, u32[]{:S(2)}, u32[]{:S(2)}) collective-permute-start(f32[24,2304]{1,0:T(8,128)S(1)} %get-tuple-element.58), channel_id=1, source_target_pairs={{0,16},{16,0},{1,17},{17,1},{2,18},{18,2},{3,19},{19,3},{4,20},{20... | collective-permute-start | bytes 663560 | tf_op jit(solution)/shard_map/ppermute | solution.py:410
  (15 other events, 67.5 us)
Sparse Core Ops, SparseCore 0:
  81.8 63.4 all-gather.4
  148.7 54.5 all-gather.6

commit v4 on v2

--- a/solution.py
+++ b/solution.py
@@ -54,66 +54,62 @@
     return jnp.sum(values.astype(jnp.float32), axis=0, keepdims=True)
 
 
-def section_kernel(layout, backward, *refs):
+def section_kernel(layout, backward, after, *refs):
     width, hidden, rows, ratio, ring_size, share, bias_count = layout
-    own_ref, x_ref, silu_ref = refs[:3]
-    refs = refs[3:]
+    rank_ref, x_ref, modulation_ref, bias_ref = refs[:4]
+    refs = refs[4:]
     if backward:
         dy_ref = refs[0]
         refs = refs[1:]
-    pack_refs = refs[:2]
-    refs = refs[2:]
+    mine_ref, theirs_ref = refs[:2]
+    refs = refs[2 + after :]
     if backward:
         y_ref, dx_ref, row_ref, keep_ref, send_ref = refs[:5]
         refs = refs[5:]
     else:
         y_ref = refs[0]
         refs = refs[1:]
-    mod_w, att_w, out_w, up_w, down_p, bias_p, sems = refs[:7]
-    bias_s, down_w, down_s, block_s, qkv_s, att_s, u_s = refs[7:14]
+    att_w, out_w, up_w, down_p, sems = refs[:5]
+    bias_s, down_w, down_s, block_s, qkv_s, att_s, u_s = refs[5:12]
     if backward:
-        soft_s, slope_s, da_s, dqkv_s, halves, out_sems = refs[14:]
-
-    own = own_ref[0] == 1
-    held = (att_w, out_w, up_w, mod_w, down_p, bias_p)
-    sizes = (3 * width, width, hidden, 6 * width, hidden, 128)
-    starts = [sum(sizes[:i]) for i in range(len(sizes))]
-
-    def fetches(source):
+        soft_s, slope_s, da_s, dqkv_s, halves, out_sems = refs[12:]
+
+    rank = rank_ref[0]
+    split = hidden - 2 * width
+
+    def fetches(first, second):
+        moves = (
+            (first.at[:, : 3 * width], att_w),
+            (first.at[:, 3 * width : 4 * width], out_w),
+            (first.at[:, 4 * width :], up_w.at[:, :split]),
+            (second.at[:, : hidden - split], up_w.at[:, split:]),
+            (second.at[:, hidden - split :], down_p),
+        )
         return [
-            pltpu.make_async_copy(
-                pack_refs[source].at[:, start : start + size], target, sems.at[i]
-            )
-            for i, (target, start, size) in enumerate(zip(held, starts, sizes))
+            pltpu.make_async_copy(source, target, sems.at[i])
+            for i, (source, target) in enumerate(moves)
         ]
 
-    @pl.when(own)
+    @pl.when(rank == 0)
     def _():
-        for copy in fetches(0):
+        for copy in fetches(mine_ref, theirs_ref):
             copy.start()
 
-    @pl.when(jnp.logical_not(own))
+    @pl.when(rank != 0)
     def _():
-        for copy in fetches(1):
+        for copy in fetches(theirs_ref, mine_ref):
             copy.start()
 
-    arrivals = fetches(0)
+    arrivals = fetches(mine_ref, theirs_ref)
 
     def bias(a, b):
         return bias_s[:, a:b]
 
     x = x_ref[...].astype(jnp.float32)
     normed_one, factor_one = normalize_rows(x)
-    arrivals[5].wait()
-    bias_rows = bias_p[...].astype(jnp.float32)
     for d in range(ring_size):
-        for i in range(0, bias_count, 128):
-            wide = min(128, bias_count - i)
-            start = d * bias_count + i
-            row = d * rows + i // 128
-            bias_s[:, start : start + wide] = bias_rows[row : row + 1, :wide]
-    arrivals[3].wait()
-    modulation = matmul(silu_ref[...], mod_w[...])[0:1, :] + bias(0, 6 * width)
+        bias_s[:, d * bias_count : (d + 1) * bias_count] = bias_ref[d : d + 1, :]
+    modulation = modulation_ref[...] + bias(0, 6 * width)
     shift_one, scale_one, gate_one, shift_two, scale_two, gate_two = [
         modulation[:, i * width : (i + 1) * width] for i in range(6)
     ]
@@ -144,6 +140,7 @@
     normed_two, factor_two = normalize_rows(middle)
     hidden_two = low(normed_two * (1.0 + scale_two) + shift_two)
     arrivals[2].wait()
+    arrivals[3].wait()
     at += 3 * width
     for j in range(ratio):
         cut = slice(j * width, (j + 1) * width)
@@ -183,7 +180,6 @@
         row_ref[:, sums_at + (3 + j) * width : sums_at + (4 + j) * width] = column_sum(
             grad_expanded
         )
-    split = (4 * width + 2 * hidden) // 2 - 4 * width
     up_first = low(outer_sum(hidden_two, da_s[:, :split]) * share)
     halves[0, :, 4 * width :] = up_first
     halves[1, :, : hidden - split] = low(outer_sum(hidden_two, da_s[:, split:]) * share)
@@ -194,7 +190,6 @@
                 (d * ratio + j) * rows : (d * ratio + j + 1) * rows, :
             ]
     halves[1, :, hidden - split :] = low(block_s[...])
-    rank = own_ref[1]
     second_out = [
         pltpu.make_async_copy(halves.at[1], keep_ref, out_sems.at[1]),
         pltpu.make_async_copy(halves.at[1], send_ref, out_sems.at[1]),
@@ -256,15 +251,12 @@
         grad_middle
         + normalize_back(normed_one, factor_one, grad_hidden_one * (1.0 + scale_one))
     )
-    grad_modulation = low(row_ref[:, : 6 * width])
-    row_ref[:, : 6 * width] = grad_modulation.astype(jnp.float32)
-    spread = jnp.broadcast_to(row_ref[:, : 6 * width], (16, 6 * width))
-    row_ref[:, sums_at + 4 * width + hidden :] = matmul_transposed(low(spread), mod_w[...])[0:1, :]
+    row_ref[:, : 6 * width] = low(row_ref[:, : 6 * width]).astype(jnp.float32)
     second_out[0].wait()
     first_out[0].wait()
 
 
-def run_section(layout, flags, x, silu, packs, dy=None):
+def run_section(layout, rank, x, modulation, bias, halves, dy=None, after=()):
     width, hidden, rows, ratio, ring_size, share, bias_count = layout
     length = x.shape[0]
     backward = dy is not None
@@ -275,13 +267,11 @@
     shapes = [jax.ShapeDtypeStruct((length, width), bf16)]
     out_specs = [vmem]
     scratch = [
-        pltpu.VMEM((width, 6 * width), bf16),
         pltpu.VMEM((width, 3 * width), bf16),
         pltpu.VMEM((width, width), bf16),
         pltpu.VMEM((width, hidden), bf16),
         pltpu.VMEM((width, hidden), bf16),
-        pltpu.VMEM((width, 128), bf16),
-        pltpu.SemaphoreType.DMA((6,)),
+        pltpu.SemaphoreType.DMA((5,)),
         pltpu.VMEM((1, bias_count * ring_size), f32),
         pltpu.VMEM((hidden, width), bf16),
         pltpu.VMEM((hidden, width), f32),
@@ -290,12 +280,12 @@
         pltpu.VMEM((length, width), bf16),
         pltpu.VMEM((length, hidden), bf16),
     ]
-    operands = [flags, x, silu]
+    operands = [rank, x, modulation, bias]
     if backward:
         operands.append(dy)
         shapes += [
             jax.ShapeDtypeStruct((length, width), bf16),
-            jax.ShapeDtypeStruct((1, 11 * width + hidden), f32),
+            jax.ShapeDtypeStruct((1, 10 * width + hidden), f32),
             jax.ShapeDtypeStruct((width, half), bf16),
             jax.ShapeDtypeStruct((width, half), bf16),
         ]
@@ -308,11 +298,11 @@
             pltpu.VMEM((2, width, half), bf16),
             pltpu.SemaphoreType.DMA((2,)),
         ]
-    specs = [pl.BlockSpec(memory_space=pltpu.SMEM)] + [vmem] * (len(operands) - 1) + [hbm] * 2
+    specs = [pl.BlockSpec(memory_space=pltpu.SMEM)] + [vmem] * (len(operands) - 1) + [hbm] * (2 + len(after))
     work = 2 * length * width * (4 * width + 2 * hidden + 2 * length)
     moved = 2 * width * (10 * width + 2 * hidden)
     return pl.pallas_call(
-        partial(section_kernel, layout, backward),
+        partial(section_kernel, layout, backward, len(after)),
         out_shape=shapes,
         in_specs=specs,
         out_specs=out_specs,
@@ -325,7 +315,157 @@
             bytes_accessed=(2 if backward else 1) * moved,
             transcendentals=HEADS * length * length + length * hidden,
         ),
-    )(*operands, *packs)
+    )(*operands, *halves, *after)
+
+
+def copy_all(copies):
+    for copy in copies:
+        copy.start()
+    for copy in copies:
+        copy.wait()
+
+
+def pack_kernel(rank_ref, att_ref, out_ref, up_ref, down_ref, keep_ref, send_ref, sems):
+    ratio, rows, width = down_ref.shape
+    split = (ratio - 2) * width
+
+    def copies(first, second):
+        moves = [
+            (att_ref, first.at[:, : 3 * width]),
+            (out_ref, first.at[:, 3 * width : 4 * width]),
+            (up_ref.at[:, :split], first.at[:, 4 * width :]),
+            (up_ref.at[:, split:], second.at[:, : 2 * width]),
+        ]
+        for j in range(ratio):
+            moves.append((down_ref.at[j], second.at[:, (2 + j) * width : (3 + j) * width]))
+        return [
+            pltpu.make_async_copy(source, target, sems.at[i])
+            for i, (source, target) in enumerate(moves)
+        ]
+
+    @pl.when(rank_ref[0] == 0)
+    def _():
+        copy_all(copies(keep_ref, send_ref))
+
+    @pl.when(rank_ref[0] != 0)
+    def _():
+        copy_all(copies(send_ref, keep_ref))
+
+
+def stack_kernel(high, split, place_ref, *refs):
+    pieces, sems = refs[:high], refs[-1]
+    targets = refs[-1 - (2 if split else 1) : -1]
+    copies = []
+    for turn, piece in enumerate(pieces):
+        place = lax.rem(place_ref[0] + (high - turn), high)
+        parts = (piece.at[:, :split], piece.at[:, split:]) if split else (piece,)
+        for i, (part, target) in enumerate(zip(parts, targets)):
+            copies.append(pltpu.make_async_copy(part, target.at[place], sems.at[turn, i]))
+    copy_all(copies)
+
+
+def weave_kernel(split, place_ref, *refs):
+    pieces, full_ref, sems = refs[:-2], refs[-2], refs[-1]
+    x, y = place_ref[1], place_ref[2]
+    copies = []
+    for i, piece in enumerate(pieces):
+        other_x, other_y = (i % 4) & 1, (i % 4) >> 1
+        row = x if not other_x else 1 - x
+        column = y if not other_y else 1 - y
+        target = full_ref.at[:, row, column]
+        if split:
+            target = full_ref.at[:, row, column, :, pl.ds((i // 4) * split, split)]
+        copies.append(pltpu.make_async_copy(piece, target, sems.at[i]))
+    copy_all(copies)
+
+
+def added(former, latter):
+    return former.astype(jnp.float32) + latter.astype(jnp.float32)
+
+
+def chip_sum_kernel(high, place_ref, mine, got, first_keep, first_send, second_keep, second_send):
+    x, y = place_ref[1], place_ref[2]
+    half = mine.shape[2]
+    lanes = half // 2
+    for z in range(high):
+        for other in range(2):
+            for target, span, chunk in (
+                (first_keep, slice(0, lanes), z * 4 + x * 2 + other),
+                (first_send, slice(0, lanes), z * 4 + (1 - x) * 2 + other),
+                (second_keep, slice(lanes, half), z * 4 + other * 2 + y),
+                (second_send, slice(lanes, half), z * 4 + other * 2 + (1 - y)),
+            ):
+                target[z, other] = low(added(mine[chunk, :, span], got[chunk, :, span]))
+
+
+def turn_kernel(high, place_ref, *refs):
+    for part, own in ((0, place_ref[2]), (1, place_ref[1])):
+        kept, got = refs[2 * part : 2 * part + 2]
+        keep, send = refs[4 + 2 * part : 6 + 2 * part]
+        for z in range(high):
+            keep[z] = low(added(kept[z, own], got[z, own]))
+            send[z] = low(added(kept[z, 1 - own], got[z, 1 - own]))
+
+
+def rise_kernel(high, place_ref, *refs):
+    targets = refs[4:]
+    lanes = refs[0].shape[2]
+    for turn in range(high):
+        chunk = lax.rem(place_ref[0] + turn, high)
+        for part in range(2):
+            kept, got = refs[2 * part : 2 * part + 2]
+            total = added(kept[chunk], got[chunk])
+            span = slice(part * lanes, (part + 1) * lanes)
+            targets[turn][:, span] = total.astype(targets[turn].dtype)
+
+
+def close_kernel(high, rank_ref, *refs):
+    keep, send = refs[-2:]
+    totals = []
+    for section in range(2):
+        pieces = refs[section * high : (section + 1) * high]
+        total = pieces[0][...].astype(jnp.float32)
+        for piece in pieces[1:]:
+            total = total + piece[...].astype(jnp.float32)
+        totals.append(total)
+    first = rank_ref[0] == 0
+    keep[...] = jnp.where(first, totals[0], totals[1])
+    send[...] = jnp.where(first, totals[1], totals[0])
+
+
+def spread_kernel(rank_ref, mine, got, att_ref, out_ref, up_ref, down_ref):
+    rows, width = out_ref.shape
+    split = up_ref.shape[1] - 2 * width
+    first = rank_ref[0] == 0
+    lower = jnp.where(first, mine[...], got[...])
+    upper = jnp.where(first, got[...], mine[...])
+    att_ref[...] = lower[:, : 3 * width]
+    out_ref[...] = lower[:, 3 * width : 4 * width]
+    up_ref[:, :split] = lower[:, 4 * width :]
+    up_ref[:, split:] = upper[:, : 2 * width]
+    for j in range(down_ref.shape[0] // rows):
+        down_ref[j * rows : (j + 1) * rows, :] = upper[:, (2 + j) * width : (3 + j) * width]
+
+
+def in_memory(kernel, shapes, operands, scratch=(), memory=pltpu.VMEM, after=(), limit=32):
+    specs = [pl.BlockSpec(memory_space=pltpu.SMEM)]
+    specs += [pl.BlockSpec(memory_space=memory)] * (len(operands) - 1)
+    specs += [pl.BlockSpec(memory_space=pl.ANY)] * len(after)
+    count = len(operands)
+
+    def body(*refs):
+        kernel(*refs[:count], *refs[count + len(after) :])
+
+    moved = sum(shape.size * shape.dtype.itemsize for shape in shapes)
+    return pl.pallas_call(
+        body,
+        out_shape=shapes,
+        in_specs=specs,
+        out_specs=[pl.BlockSpec(memory_space=memory)] * len(shapes),
+        scratch_shapes=list(scratch),
+        compiler_params=pltpu.CompilerParams(vmem_limit_bytes=limit * 1024 * 1024),
+        cost_estimate=pl.CostEstimate(flops=0, bytes_accessed=3 * moved, transcendentals=0),
+    )(*operands, *after)
 
 
 def pair_swap(block, axis):
@@ -333,8 +473,94 @@
 
 
 def ring_exchange(block, size, step):
-    route = [(i, step(i)) for i in range(size)]
-    return lax.ppermute(block, RING, route)
+    return lax.ppermute(block, RING, [(i, step(i)) for i in range(size)])
+
+
+def flip(block, size, mask):
+    return ring_exchange(block, size, lambda i: i ^ mask)
+
+
+def rotate(block, size, turn):
+    return ring_exchange(block, size, lambda i: (i + 4 * turn) % size)
+
+
+def rotations(block, size):
+    return [block] + [rotate(block, size, turn) for turn in range(1, size // 4)]
+
+
+def gather_along_z(shard, place, size, after=()):
+    high = size // 4
+    rows, lanes = shard.shape
+    return in_memory(
+        partial(stack_kernel, high, lanes // 2),
+        [jax.ShapeDtypeStruct((high, rows, lanes // 2), shard.dtype)] * 2,
+        [place, *rotations(shard, size)],
+        scratch=[pltpu.SemaphoreType.DMA((high, 2))],
+        memory=pl.ANY,
+        after=after,
+    )
+
+
+def gather_across(first, second, place, size):
+    high, rows, lanes = first.shape
+    first_x, second_y = flip(first, size, 2), flip(second, size, 1)
+    first_y, second_x = flip(first, size, 1), flip(second, size, 2)
+    first_both, second_both = flip(first_x, size, 1), flip(second_y, size, 2)
+    (full,) = in_memory(
+        partial(weave_kernel, lanes),
+        [jax.ShapeDtypeStruct((high, 2, 2, rows, 2 * lanes), first.dtype)],
+        [place, first, first_x, first_y, first_both, second, second_x, second_y, second_both],
+        scratch=[pltpu.SemaphoreType.DMA((8,))],
+        memory=pl.ANY,
+    )
+    return full.reshape(size * rows, 2 * lanes)
+
+
+def gather_rows(block, place, size):
+    high = size // 4
+    (stacked,) = in_memory(
+        partial(stack_kernel, high, 0),
+        [jax.ShapeDtypeStruct((high, *block.shape), block.dtype)],
+        [place, *rotations(block, size)],
+        scratch=[pltpu.SemaphoreType.DMA((high, 1))],
+        memory=pl.ANY,
+    )
+    (full,) = in_memory(
+        partial(weave_kernel, 0),
+        [jax.ShapeDtypeStruct((high, 2, 2, *block.shape), block.dtype)],
+        [place, stacked, *[flip(stacked, size, mask) for mask in (2, 1, 3)]],
+        scratch=[pltpu.SemaphoreType.DMA((4,))],
+        memory=pl.ANY,
+    )
+    return full.reshape(size, *block.shape)
+
+
+def scatter_first(mine, got, place, size):
+    rows, half = mine.shape[1:]
+    shape = jax.ShapeDtypeStruct((size // 4, 2, rows, half // 2), jnp.bfloat16)
+    return in_memory(partial(chip_sum_kernel, size // 4), [shape] * 4, [place, mine, got])
+
+
+def scatter_flips(sorted_terms, size):
+    first_keep, first_send, second_keep, second_send = sorted_terms
+    return first_keep, flip(first_send, size, 2), second_keep, flip(second_send, size, 1)
+
+
+def scatter_rest(received, place, size):
+    high, _, rows, lanes = received[0].shape
+    shape = jax.ShapeDtypeStruct((high, rows, lanes), jnp.bfloat16)
+    first_keep, first_send, second_keep, second_send = in_memory(
+        partial(turn_kernel, high), [shape] * 4, [place, *received]
+    )
+    first_got, second_got = flip(first_send, size, 1), flip(second_send, size, 2)
+    chunk = (rows, 2 * lanes)
+    own, *sent = in_memory(
+        partial(rise_kernel, high),
+        [jax.ShapeDtypeStruct(chunk, jnp.float32)]
+        + [jax.ShapeDtypeStruct(chunk, jnp.bfloat16)] * (high - 1),
+        [place, first_keep, first_got, second_keep, second_got],
+    )
+    return [own] + [rotate(block, size, turn + 1) for turn, block in enumerate(sent)]
 
 
 def scatter_sum(block, rank, size):
@@ -403,26 +629,31 @@
     ratio = shrink_weight.shape[1] // rows
     hidden = ratio * width
     bias_count = biases.shape[1]
-    bias_rows = -(-bias_count // 128)
-    assert bias_rows <= rows and hidden == expand_weight.shape[2]
+    half = 2 * width + hidden
+    assert hidden == expand_weight.shape[2] and ratio >= 2
     table_rows = cond_table.shape[0]
     is_first = section_rank == 0
     layout = (width, hidden, rows, ratio, ring_size, 1.0 / sharers, bias_count)
-
-    bias_block = jnp.pad(biases[0], (0, bias_rows * 128 - bias_count)).reshape(bias_rows, 128)
-    packed = jnp.concatenate(
+    compact = ring_size in (8, 16) and seq_size == slots == 2
+    rank = section_rank.astype(jnp.int32).reshape(1)
+    place = jnp.stack([ring_rank >> 2, (ring_rank >> 1) & 1, ring_rank & 1]).astype(jnp.int32)
+
+    keep, send = in_memory(
+        pack_kernel,
+        [jax.ShapeDtypeStruct((rows, half), jnp.bfloat16)] * 2,
         [
+            rank,
             attention_weight[0],
             output_weight[0],
             expand_weight[0],
-            modulation_weight[0],
-            *[shrink_weight[0, j * rows : (j + 1) * rows] for j in range(ratio)],
-            jnp.pad(bias_block, ((0, rows - bias_rows), (0, 0))),
+            shrink_weight[0].reshape(ratio, rows, width),
         ],
-        axis=1,
-    )
-    own_pack = lax.all_gather(packed, RING, axis=0, tiled=True)
-    packs = (own_pack, pair_swap(own_pack, "section"))
+        scratch=[pltpu.SemaphoreType.DMA((4 + ratio,))],
+        memory=pl.ANY,
+    )
+    got = pair_swap(send, "section")
+    first_shard = jnp.where(is_first, keep, got)
+    second_shard = jnp.where(is_first, got, keep)
 
     live = (
         slot < lax.dynamic_index_in_dim(row_counts, section_rank, 0, keepdims=False)[0]
@@ -434,79 +665,158 @@
         ],
         axis=1,
     )
-    both = jnp.repeat(both, sharers, axis=0)
-    both = lax.all_to_all(both, "seq", 0, 0, tiled=True)
-    first_input = both[:, 0].reshape(length, width)
-    last_grad = both[:, 1].reshape(length, width) * live
+
+    def side_by_side(mine, got, axis):
+        return jnp.where(
+            seq_rank == 0,
+            jnp.concatenate([mine, got], axis=axis),
+            jnp.concatenate([got, mine], axis=axis),
+        )
+
+    if compact:
+        mine = lax.dynamic_index_in_dim(both, seq_rank, 0, keepdims=False)
+        sent = lax.dynamic_index_in_dim(both, 1 - seq_rank, 0, keepdims=False)
+        both = side_by_side(mine, pair_swap(sent, "seq"), 1)
+    else:
+        both = lax.all_to_all(jnp.repeat(both, sharers, axis=0), "seq", 0, 0, tiled=True)
+        both = jnp.swapaxes(both, 0, 1).reshape(2, length, width)
+    first_input = both[0]
+    last_grad = both[1] * live
+
     flat_ids = time_ids.reshape(-1)
     selector = (
         flat_ids[:, None] == jnp.arange(table_rows, dtype=jnp.int32)[None, :]
     ).astype(jnp.bfloat16)
     conditions = matmul(selector, cond_table)
     silu_all = jax.nn.silu(conditions).astype(jnp.bfloat16)
-    latent = section_rank * time_ids.shape[1] + data_rank * slots + slot
-    condition = lax.dynamic_slice_in_dim(conditions, latent, 1, 0)
-    silu_now = jnp.broadcast_to(lax.dynamic_slice_in_dim(silu_all, latent, 1, 0), (16, width))
-
-    first_flags = jnp.stack([is_first, ~is_first]).astype(jnp.int32)
-    second_flags = jnp.stack([~is_first, ~is_first]).astype(jnp.int32)
-    (first_low,) = run_section(layout, first_flags, first_input, silu_now, packs)
+    silu_own = lax.dynamic_slice_in_dim(silu_all, ring_rank * rows, rows, 1)
+    products = matmul(silu_own, modulation_weight[0])
+    own_bias = jnp.broadcast_to(biases.astype(jnp.float32), (products.shape[0], bias_count))
+    products = jnp.repeat(jnp.concatenate([products, own_bias], axis=1), sharers, axis=0)
+    products = lax.all_to_all(
+        products[:, None], ("section", "dp", "seq"), 0, 0, tiled=True
+    ).reshape(sections, ring_size, 6 * width + bias_count)
+    first_modulation, second_modulation = jnp.split(
+        jnp.sum(products[:, :, : 6 * width], axis=1), 2, axis=0
+    )
+    first_bias, second_bias = products[0, :, 6 * width :], products[1, :, 6 * width :]
+
+    if compact:
+        first_parts = gather_along_z(first_shard, place, ring_size, after=(products, both))
+        second_parts = gather_along_z(second_shard, place, ring_size)
+        first_pack = gather_across(*first_parts, place, ring_size)
+        second_pack = gather_across(*second_parts, place, ring_size)
+    else:
+        first_pack = lax.all_gather(first_shard, RING, axis=0, tiled=True)
+        second_pack = lax.all_gather(second_shard, RING, axis=0, tiled=True)
+    first_halves = (first_pack, pair_swap(first_pack, "section"))
+    second_halves = (second_pack, pair_swap(second_pack, "section"))
+    own_matrix = lax.all_gather(modulation_weight[0], RING, axis=0, tiled=True)
+
+    first = (first_input, first_modulation, first_bias, first_halves)
+    (first_low,) = run_section(layout, rank, *first)
     second_low, second_grad, second_row, second_keep, second_send = run_section(
-        layout, second_flags, first_low, silu_now, packs, last_grad
+        layout, rank, first_low, second_modulation, second_bias, second_halves, last_grad
     )
     second_got = pair_swap(second_send, "section")
+
+    def ring_terms(term):
+        return term.reshape(ring_size, rows, half)
+
+    after = ()
+    if compact:
+        second_sorted = scatter_first(
+            ring_terms(second_keep), ring_terms(second_got), place, ring_size
+        )
+        after = (second_sorted[0],)
+        second_received = scatter_flips(second_sorted, ring_size)
     _, first_grad, first_row, first_keep, first_send = run_section(
-        layout, first_flags, first_input, silu_now, packs, second_grad
+        layout, rank, *first, second_grad, after
     )
     first_got = pair_swap(first_send, "section")
 
-    def to_owners(first, second):
-        pieces = jnp.stack([first, second]).reshape(2 * seq_size, tokens, width)
+    shard = jax.ShapeDtypeStruct((rows, half), jnp.float32)
+    if compact:
+        second_pieces = scatter_rest(second_received, place, ring_size)
+        first_sorted = scatter_first(
+            ring_terms(first_keep), ring_terms(first_got), place, ring_size
+        )
+        first_pieces = scatter_rest(scatter_flips(first_sorted, ring_size), place, ring_size)
+    else:
+
+        def chip_sum(keep, got):
+            return ring_terms(low(added(keep, got)))
+
+        first_pieces, second_pieces = [
+            [scatter_sum(chip_sum(keep, got), ring_rank, ring_size)]
+            for keep, got in ((first_keep, first_got), (second_keep, second_got))
+        ]
+    mine, send = in_memory(
+        partial(close_kernel, len(first_pieces)),
+        [shard, shard],
+        [rank, *first_pieces, *second_pieces],
+    )
+    att, out, up, down = in_memory(
+        spread_kernel,
+        [
+            jax.ShapeDtypeStruct(extent, jnp.float32)
+            for extent in (
+                (rows, 3 * width),
+                (rows, width),
+                (rows, hidden),
+                (rows * ratio, width),
+            )
+        ],
+        [rank, mine, pair_swap(send, "section")],
+    )
+
+    early = jnp.stack([first_low * live, second_low * live, second_grad])
+    if compact:
+
+        def to_slots(block):
+            block = block.reshape(-1, 2, tokens, width)
+            mine = lax.dynamic_index_in_dim(block, seq_rank, 1, keepdims=True)
+            sent = lax.dynamic_index_in_dim(block, 1 - seq_rank, 1, keepdims=True)
+            return side_by_side(mine, pair_swap(sent, "seq"), 1)
+
+        early, late = to_slots(early), to_slots(first_grad)
+        per_first = jnp.stack([early[0], late[0]])
+        per_second = early[1:]
+        mine = jnp.where(is_first, per_first, per_second)
+        got = pair_swap(jnp.where(is_first, per_second, per_first), "section")
+        outputs = jnp.where(is_first, jnp.stack([mine, got], 1), jnp.stack([got, mine], 1))
+    else:
+        pieces = jnp.stack([early[0], first_grad, early[1], early[2]])
+        pieces = jnp.swapaxes(pieces.reshape(2, 2, seq_size, tokens, width), 1, 2)
+        pieces = pieces.reshape(2 * seq_size, 2, tokens, width)
         pieces = lax.all_to_all(pieces, ("section", "seq"), 0, 0, tiled=True)
-        return pieces.reshape(batches, slots, sharers, tokens, width)[:, :, 0]
-
-    activations = to_owners(first_low * live, second_low * live)
-    input_grads = to_owners(first_grad, second_grad).astype(jnp.float32)
-
-    half = first_keep.shape[1]
-
-    def chip_sum(keep, got):
-        total = keep.astype(jnp.float32) + got.astype(jnp.float32)
-        return total.astype(jnp.bfloat16).reshape(ring_size, 1, rows, half)
-
-    ring_terms = jnp.concatenate(
-        [chip_sum(first_keep, first_got), chip_sum(second_keep, second_got)], axis=1
-    )
-    owned = scatter_sum(ring_terms.reshape(ring_size, 2 * rows, half), ring_rank, ring_size)
-    owned = owned.reshape(2, rows, half)
-    mine = lax.dynamic_index_in_dim(owned, section_rank, 0, keepdims=False)
-    theirs = pair_swap(
-        lax.dynamic_index_in_dim(owned, 1 - section_rank, 0, keepdims=False), "section"
-    )
-    full = jnp.where(
+        pieces = pieces.reshape(batches, slots, sharers, 2, tokens, width)[:, :, 0]
+        outputs = jnp.moveaxis(pieces, 2, 0)
+    activations = outputs[0]
+    input_grads = outputs[1].astype(jnp.float32)
+
+    own_row = jnp.where(is_first, first_row, second_row)
+    other_row = pair_swap(low(jnp.where(is_first, second_row, first_row)), "section")
+    pair = jnp.where(
         is_first,
-        jnp.concatenate([mine, theirs], axis=1),
-        jnp.concatenate([theirs, mine], axis=1),
-    )
-    edges = [0, 3 * width, 4 * width, 4 * width + hidden]
-    att, out, up = [full[:, a:b] for a, b in zip(edges[:-1], edges[1:])]
-    down = jnp.concatenate(
-        [full[:, edges[3] + j * width : edges[3] + (j + 1) * width] for j in range(ratio)], axis=0
-    )
-
-    per_row = 10 * width + hidden
-    _, silu_back = jax.vjp(jax.nn.silu, condition)
-    grad_condition = silu_back(first_row[:, per_row:] + second_row[:, per_row:])[0]
-    row = jnp.concatenate([first_row[:, :per_row], second_row[:, :per_row], grad_condition], axis=1)
-    every = lax.all_gather(row, ("section", "dp", "seq"), axis=0, tiled=True)[::sharers]
-    section_rows = jnp.where(is_first, every[:, :per_row], every[:, per_row : 2 * per_row])
-    bias_total = jnp.sum(section_rows, axis=0)
+        jnp.concatenate([low(own_row), other_row]),
+        jnp.concatenate([other_row, low(own_row)]),
+    )
+    if compact:
+        every = gather_rows(pair, place, ring_size)
+    else:
+        every = lax.all_gather(pair, RING, axis=0)[::sharers]
+    every = jnp.swapaxes(every, 0, 1).reshape(-1, pair.shape[1])
+    bias_total = jnp.sum(every.astype(jnp.float32), axis=0)
     bias_grad = lax.dynamic_slice_in_dim(bias_total, ring_rank * bias_count, bias_count, 0)
-    silu_own = lax.dynamic_slice_in_dim(silu_all, ring_rank * rows, rows, 1)
-    modulation_grad = outer_sum(silu_own, section_rows[:, : 6 * width].astype(jnp.bfloat16))
+    modulation_rows = every[:, : 6 * width]
+    modulation_grad = outer_sum(silu_own, modulation_rows)
+    products_back = matmul_transposed(modulation_rows, own_matrix)
+    products_back = products_back + pair_swap(products_back, "section")
+    _, silu_back = jax.vjp(jax.nn.silu, conditions)
     table_grad = lax.dot_general(
         selector.astype(jnp.float32),
-        every[:, 2 * per_row :],
+        silu_back(products_back)[0],
         (((0,), (0,)), ((), ())),
         precision=lax.Precision.HIGHEST,
         preferred_element_type=jnp.float32,

time: 274 us -> 229 us (0.84)
  waiting for transfers between devices: 152 us -> 73.9 us
  starting transfers between devices: 24.2 us -> 58.7 us
  Pallas kernels: 36.8 us -> 58.8 us
  local copies, waits for them, and re-layouts: 25.3 us -> 10.1 us
  other arithmetic: 14.1 us -> 4.32 us
  matrix products: 3.46 us -> 6.7 us
    all_gather x2 -> x1, waiting for transfers between devices: 86.3 us -> 2.26 us  [per_device(): own_matrix = lax.all_gather(modulation_weight[0], RING, axis=0, tiled=True)]
    all_to_all x3 -> x1, waiting for transfers between devices: 29.8 us -> 0.01 us  [per_device(): lax.all_to_all(products[:, None], ('section', 'dp', 'seq'), 0, 0, tiled=T...]
    ppermute x7 -> x38, starting transfers between devices: 7.8 us -> 36.2 us  [ring_exchange(): return lax.ppermute(block, RING, [(i, step(i)) for i in range(size)])]
    pallas_call x3 -> x18, Pallas kernels: 36.8 us -> 58.8 us  [the longest x3 31.3 us: run_section(): pl.pallas_call(partial(section_kernel, layout, backward, len(after)), out...]
    ppermute x7 -> x38, waiting for transfers between devices: 35 us -> 55.9 us  [ring_exchange(): return lax.ppermute(block, RING, [(i, step(i)) for i in range(size)])]
    ppermute x4 -> x12, waiting for transfers between devices: 1.25 us -> 15.7 us  [pair_swap(): return lax.ppermute(block, axis, [(0, 1), (1, 0)])]
    ppermute x4 -> x12, starting transfers between devices: 3.99 us -> 17.4 us  [pair_swap(): return lax.ppermute(block, axis, [(0, 1), (1, 0)])]
    unnamed x26 -> x35, local copies, waits for them, and re-layouts: 14 us -> 5.79 us
  transfers between devices with their start and end apart: 16 -> 52, of which waited for: 10 -> 23; matrix products, arithmetic and copies ran while one was open for 9% -> 7% of each run, Pallas kernels for 6% -> 20%
where the time goes in v4:
time: 229 us; the launch traced here: 228 us
  waiting for transfers between devices  73.9 us (32%)
  Pallas kernels  58.8 us (26%)
  starting transfers between devices  58.7 us (26%)
  between operations  15.2 us (7%)
  local copies, waits for them, and re-layouts  10.1 us (4%)
  matrix products  6.7 us (3%)
  other arithmetic  4.32 us (2%)
    ppermute x38, waiting for transfers between devices, ring_exchange(): return lax.ppermute(block, RING, [(i, step(i)) for i in range(size)])  55.9 us
    ppermute x38, starting transfers between devices, ring_exchange(): return lax.ppermute(block, RING, [(i, step(i)) for i in range(size)])  36.2 us
    pallas_call x3, Pallas kernels, run_section(): pl.pallas_call(partial(section_kernel, layout, backward, len(after)), out...  31.3 us
    pallas_call x15, Pallas kernels, in_memory(): pl.pallas_call(body, out_shape=shapes, in_specs=specs, out_specs=[pl.Bloc...  27.5 us
    ppermute x12, starting transfers between devices, pair_swap(): return lax.ppermute(block, axis, [(0, 1), (1, 0)])  17.4 us
    ppermute x12, waiting for transfers between devices, pair_swap(): return lax.ppermute(block, axis, [(0, 1), (1, 0)])  15.7 us
    unnamed x35, local copies, waits for them, and re-layouts  5.79 us
    all_to_all x1, starting transfers between devices, per_device(): lax.all_to_all(products[:, None], ('section', 'dp', 'seq'), 0, 0, tiled=T...  5.03 us
  transfers between devices with their start and end apart: 52, of which 23 were waited for; matrix products, arithmetic and copies ran while one was open for 7% of the time, Pallas kernels for 20%

profile of v4, /device:TPU:9, one launch (start us, length us, event | category | flops | bytes accessed | tf_op | source)
XLA Modules:
  0.0 227.8 jit_solution(678217756060334625)
XLA Ops:
  16.2 5.0 %all-to-all-start = ((f32[32,1,2640]{2,1,0:T(1,128)}), f32[32,1,2640]{2,1,0:T(1,128)S(1)}, u32[]{:S(2)}, u32[]{:S(2)}) async-start(f32[32,1,2640]{2,1,0:T(1,128)} %copy.21), calls=%async_computation | async-start | bytes 688128 | tf_op jit(solution)/shard_map/all_to_all | solution.py:696
  25.1 3.2 %collective-permute-start.3 = (bf16[24,2304]{1,0:T(8,128)(2,1)S(1)}, bf16[24,2304]{1,0:T(8,128)(2,1)S(1)}, u32[]{:S(2)}, u32[]{:S(2)}) collective-permute-start(bf16[24,2304]{1,0:T(8,128)(2,1)S(1)} %get-tuple-element.112.refs_1_), channel_id=1, source_target_pairs={{0,8},{1,9},{2,10},{3,11},{4,12},{5,13},{6,14},{7,15},{8,0},{9,1},... | collective-permute-start | bytes 331784 | tf_op jit(solution)/shard_map/ppermute | solution.py:476
  28.3 7.7 %collective-permute-done.12.refs_2_ = bf16[24,2304]{1,0:T(8,128)(2,1)S(1)} collective-permute-done((bf16[24,2304]{1,0:T(8,128)(2,1)S(1)}, bf16[24,2304]{1,0:T(8,128)(2,1)S(1)}, u32[]{:S(2)}, u32[]{:S(2)}) %collective-permute-start.12) | collective-permute-done | bytes 110624 | tf_op jit(solution)/shard_map/ppermute | solution.py:476
  36.1 7.0 %collective-permute-done.13.refs_3_ = bf16[24,2304]{1,0:T(8,128)(2,1)S(1)} collective-permute-done((bf16[24,2304]{1,0:T(8,128)(2,1)S(1)}, bf16[24,2304]{1,0:T(8,128)(2,1)S(1)}, u32[]{:S(2)}, u32[]{:S(2)}) %collective-permute-start.13) | collective-permute-done | bytes 110624 | tf_op jit(solution)/shard_map/ppermute | solution.py:476
  54.6 1.9 collective-permute-done.9.refs_7_
  59.0 2.4 %collective-permute-done.19.refs_7_ = bf16[4,24,1152]{2,1,0:T(8,128)(2,1)S(1)} collective-permute-done((bf16[4,24,1152]{2,1,0:T(8,128)(2,1)}, bf16[4,24,1152]{2,1,0:T(8,128)(2,1)S(1)}, u32[]{:S(2)}, u32[]{:S(2)}) %collective-permute-start.19) | collective-permute-done | bytes 221216 | tf_op jit(solution)/shard_map/ppermute | solution.py:476
  62.5 3.6 %collective-permute-done.6.refs_3_ = bf16[4,24,1152]{2,1,0:T(8,128)(2,1)S(1)} collective-permute-done((bf16[4,24,1152]{2,1,0:T(8,128)(2,1)S(1)}, bf16[4,24,1152]{2,1,0:T(8,128)(2,1)S(1)}, u32[]{:S(2)}, u32[]{:S(2)}) %collective-permute-start.6) | collective-permute-done | bytes 221216 | tf_op jit(solution)/shard_map/ppermute | solution.py:476
  68.7 2.1 collective-permute-done.7.refs_4_
  71.7 3.2 %collective-permute-start.11 = (bf16[384,2304]{1,0:T(8,128)(2,1)S(1)}, bf16[384,2304]{1,0:T(8,128)(2,1)}, u32[]{:S(2)}, u32[]{:S(2)}) collective-permute-start(bf16[384,2304]{1,0:T(8,128)(2,1)S(1)} %bitcast.61), channel_id=1, source_target_pairs={{0,16},{16,0},{1,17},{17,1},{2,18},{18,2},{3,19},{19,3},{4,20},{20... | collective-permute-start | bytes 5308424 | tf_op jit(solution)/shard_map/ppermute | solution.py:472
  75.5 4.7 %collective-permute-done.17.refs_4_ = bf16[4,24,1152]{2,1,0:T(8,128)(2,1)S(1)} collective-permute-done((bf16[4,24,1152]{2,1,0:T(8,128)(2,1)}, bf16[4,24,1152]{2,1,0:T(8,128)(2,1)S(1)}, u32[]{:S(2)}, u32[]{:S(2)}) %collective-permute-start.17) | collective-permute-done | bytes 221216 | tf_op jit(solution)/shard_map/ppermute | solution.py:476
  80.3 15.1 %shard_map.183 = bf16[4,2,2,24,2304]{4,3,2,1,0:T(8,128)(2,1)} custom-call(s32[3]{0:T(128)S(1)} %pad_add_fusion.refs_0_, bf16[4,24,1152]{2,1,0:T(8,128)(2,1)S(1)} %get-tuple-element.58.refs_1_, bf16[4,24,1152]{2,1,0:T(8,128)(2,1)} %collective-permute-done.15.refs_2_, bf16[4,24,1152]{2,1,0:T(8,128)(2,1)S(1)} %collective-permute-done.16.refs_3_, ...), custom_call_target="tpu_custom_call" | custom-call | bytes 5308416 | tf_op jit(solution)/shard_map/pallas_call | solution.py:460
  95.4 1.8 collective-permute-start.21
  98.7 5.2 %shard_map.181.refs_1_ = bf16[256,384]{1,0:T(8,128)(2,1)S(1)} custom-call(s32[1]{0:T(128)} %bitcast.refs_0_, bf16[256,384]{1,0:T(8,128)(2,1)S(1)} %get-tuple-element.106.refs_1_, f32[1,2304]{1,0:T(1,128)S(1)} %get-tuple-element.118.refs_2_, f32[16,336]{1,0:T(8,128)S(1)} %get-tuple-element.110.refs_3_, bf16[384,2304]{1,0:T(8,128)(2,1)S(1)} %bitcast.62, ...), custom_call_target="tpu_custom_call" | custom-call | flops 1006632960 | bytes 5308416 | tf_op jit(solution)/shard_map/pallas_call | solution.py:304
  103.9 12.9 %shard_map.184 = (bf16[256,384]{1,0:T(8,128)(2,1)S(1)}, bf16[256,384]{1,0:T(8,128)(2,1)S(1)}, f32[1,5376]{1,0:T(1,128)S(1)}, bf16[384,2304]{1,0:T(8,128)(2,1)S(1)}, bf16[384,2304]{1,0:T(8,128)(2,1)}) custom-call(s32[1]{0:T(128)} %bitcast.refs_0_, bf16[256,384]{1,0:T(8,128)(2,1)S(1)} %shard_map.181.refs_1_, f32[1,2304]{1,0:T(1,128)S(1)} %get-tuple-element.117.refs_2_, ...), custom_call_target="tpu_custom_call" | custom-call | flops 3019898880 | bytes 10616832 | tf_op jit(solution)/shard_map/pallas_call | solution.py:304
  118.2 3.8 %collective-permute-done.23 = bf16[384,2304]{1,0:T(8,128)(2,1)} collective-permute-done((bf16[384,2304]{1,0:T(8,128)(2,1)}, bf16[384,2304]{1,0:T(8,128)(2,1)}, u32[]{:S(2)}, u32[]{:S(2)}) %collective-permute-start.23) | collective-permute-done | bytes 1769504 | tf_op jit(solution)/shard_map/ppermute | solution.py:472
  122.0 1.9 shard_map.185
  123.9 13.3 %shard_map.186 = (bf16[256,384]{1,0:T(8,128)(2,1)}, bf16[256,384]{1,0:T(8,128)(2,1)S(1)}, f32[1,5376]{1,0:T(1,128)S(1)}, bf16[384,2304]{1,0:T(8,128)(2,1)S(1)}, bf16[384,2304]{1,0:T(8,128)(2,1)S(1)}) custom-call(s32[1]{0:T(128)} %bitcast.refs_0_, bf16[256,384]{1,0:T(8,128)(2,1)S(1)} %get-tuple-element.106.refs_1_, f32[1,2304]{1,0:T(1,128)S(1)} %get-tuple-element.118.refs_2_, ...), custom_call_target="tpu_custom_call" | custom-call | flops 3019898880 | bytes 10616832 | tf_op jit(solution)/shard_map/pallas_call | solution.py:304
  142.5 5.0 %collective-permute-done.22 = bf16[3,1,128,384]{3,2,1,0:T(8,128)(2,1)S(1)} collective-permute-done((bf16[3,1,128,384]{3,2,1,0:T(8,128)(2,1)S(1)}, bf16[3,1,128,384]{3,2,1,0:T(8,128)(2,1)S(1)}, u32[]{:S(2)}, u32[]{:S(2)}) %collective-permute-start.22) | collective-permute-done | bytes 294944 | tf_op jit(solution)/shard_map/ppermute | solution.py:472
  147.6 1.9 collective-permute-start.43
  149.7 2.9 %collective-permute-done.29.refs_4_ = bf16[2,5376]{1,0:T(2,128)(2,1)S(1)} collective-permute-done((bf16[2,5376]{1,0:T(2,128)(2,1)S(1)}, bf16[2,5376]{1,0:T(2,128)(2,1)S(1)}, u32[]{:S(2)}, u32[]{:S(2)}) %collective-permute-start.29) | collective-permute-done | bytes 21536 | tf_op jit(solution)/shard_map/ppermute | solution.py:476
  154.6 6.2 %collective-permute-done.24 = bf16[1,1,128,384]{3,2,1,0:T(8,128)(2,1)S(1)} collective-permute-done((bf16[1,1,128,384]{3,2,1,0:T(8,128)(2,1)S(1)}, bf16[1,1,128,384]{3,2,1,0:T(8,128)(2,1)S(1)}, u32[]{:S(2)}, u32[]{:S(2)}) %collective-permute-start.24) | collective-permute-done | bytes 98336 | tf_op jit(solution)/shard_map/ppermute | solution.py:472
  165.0 5.0 %collective-permute-start.25 = (bf16[2,2,128,384]{3,2,1,0:T(8,128)(2,1)}, bf16[2,2,128,384]{3,2,1,0:T(8,128)(2,1)}, u32[]{:S(2)}, u32[]{:S(2)}) collective-permute-start(bf16[2,2,128,384]{3,2,1,0:T(8,128)(2,1)} %get-tuple-element.100), channel_id=1, source_target_pairs={{0,16},{16,0},{1,17},{17,1},{2,18},{18,2},{3,19},{19,3},{4,20},{20... | collective-permute-start | bytes 1179656 | tf_op jit(solution)/shard_map/ppermute | solution.py:472
  178.1 2.3 all-gather.3.cloned.1.call-done
  180.3 2.2 fusion
  187.7 5.4 %collective-permute-done.45.refs_4_ = bf16[4,24,1152]{2,1,0:T(8,128)(2,1)S(1)} collective-permute-done((bf16[4,24,1152]{2,1,0:T(8,128)(2,1)S(1)}, bf16[4,24,1152]{2,1,0:T(8,128)(2,1)S(1)}, u32[]{:S(2)}, u32[]{:S(2)}) %collective-permute-start.45) | collective-permute-done | bytes 221216 | tf_op jit(solution)/shard_map/ppermute | solution.py:476
  196.1 2.2 fusion.7
  198.3 2.2 collective-permute-done.37.refs_2_
  202.6 2.0 collective-permute-start.40
  205.9 5.7 %collective-permute-done.48.refs_8_ = bf16[24,2304]{1,0:T(8,128)(2,1)S(1)} collective-permute-done((bf16[24,2304]{1,0:T(8,128)(2,1)S(1)}, bf16[24,2304]{1,0:T(8,128)(2,1)S(1)}, u32[]{:S(2)}, u32[]{:S(2)}) %collective-permute-start.48) | collective-permute-done | bytes 110624 | tf_op jit(solution)/shard_map/ppermute | solution.py:476
  211.6 3.0 %collective-permute-done.40.refs_3_ = bf16[24,2304]{1,0:T(8,128)(2,1)S(1)} collective-permute-done((bf16[24,2304]{1,0:T(8,128)(2,1)S(1)}, bf16[24,2304]{1,0:T(8,128)(2,1)S(1)}, u32[]{:S(2)}, u32[]{:S(2)}) %collective-permute-start.40) | collective-permute-done | bytes 110624 | tf_op jit(solution)/shard_map/ppermute | solution.py:476
  214.6 2.3 %collective-permute-done.41.refs_4_ = bf16[24,2304]{1,0:T(8,128)(2,1)S(1)} collective-permute-done((bf16[24,2304]{1,0:T(8,128)(2,1)S(1)}, bf16[24,2304]{1,0:T(8,128)(2,1)S(1)}, u32[]{:S(2)}, u32[]{:S(2)}) %collective-permute-start.41) | collective-permute-done | bytes 110624 | tf_op jit(solution)/shard_map/ppermute | solution.py:476
  217.1 2.0 collective-permute-start.49
  (164 shorter events, 67.4 us)
Async XLA Ops:
  10.8 10.5 %collective-permute-start.1 = (bf16[24,2304]{1,0:T(8,128)(2,1)S(1)}, bf16[24,2304]{1,0:T(8,128)(2,1)S(1)}, u32[]{:S(2)}, u32[]{:S(2)}) collective-permute-start(bf16[24,2304]{1,0:T(8,128)(2,1)S(1)} %get-tuple-element.55), channel_id=1, source_target_pairs={{0,16},{16,0},{1,17},{17,1},{2,18},{18,2},{3,19},{19,3},{4,20},{20... | collective-permute-start | bytes 331784 | tf_op jit(solution)/shard_map/ppermute | solution.py:472
  12.6 12.4 %collective-permute-start = (bf16[2,128,384]{2,1,0:T(8,128)(2,1)S(1)}, bf16[2,128,384]{2,1,0:T(8,128)(2,1)S(1)}, u32[]{:S(2)}, u32[]{:S(2)}) collective-permute-start(bf16[2,128,384]{2,1,0:T(8,128)(2,1)S(1)} %get-tuple-element.108), channel_id=1, source_target_pairs={{0,1},{1,0},{2,3},{3,2},{4,5},{5,4},{6,7},{7,6},{8,9},{9,8},{10,11... | collective-permute-start | bytes 589832 | tf_op jit(solution)/shard_map/ppermute | solution.py:472
  16.2 31.3 %all-to-all-start = ((f32[32,1,2640]{2,1,0:T(1,128)}), f32[32,1,2640]{2,1,0:T(1,128)S(1)}, u32[]{:S(2)}, u32[]{:S(2)}) async-start(f32[32,1,2640]{2,1,0:T(1,128)} %copy.21), calls=%async_computation | async-start | bytes 688128 | tf_op jit(solution)/shard_map/all_to_all | solution.py:696
  21.2 159.1 %all-gather.3.cloned.1.call-start = ((), (), s32[]{:S(2)}) async-start(), calls=%async_computation.1 | async-start | bytes 1880064 | tf_op jit(solution)/shard_map/all_gather | solution.py:714
  21.3 14.7 %collective-permute-start.12 = (bf16[24,2304]{1,0:T(8,128)(2,1)S(1)}, bf16[24,2304]{1,0:T(8,128)(2,1)S(1)}, u32[]{:S(2)}, u32[]{:S(2)}) collective-permute-start(bf16[24,2304]{1,0:T(8,128)(2,1)S(1)} %get-tuple-element.111.refs_1_), channel_id=1, source_target_pairs={{0,4},{1,5},{2,6},{3,7},{4,8},{5,9},{6,10},{7,11},{8,12},{9,13},{1... | collective-permute-start | bytes 331784 | tf_op jit(solution)/shard_map/ppermute | solution.py:476
  22.6 20.5 %collective-permute-start.13 = (bf16[24,2304]{1,0:T(8,128)(2,1)S(1)}, bf16[24,2304]{1,0:T(8,128)(2,1)S(1)}, u32[]{:S(2)}, u32[]{:S(2)}) collective-permute-start(bf16[24,2304]{1,0:T(8,128)(2,1)S(1)} %get-tuple-element.111.refs_1_), channel_id=1, source_target_pairs={{0,8},{1,9},{2,10},{3,11},{4,12},{5,13},{6,14},{7,15},{8,0},{9,1},... | collective-permute-start | bytes 331784 | tf_op jit(solution)/shard_map/ppermute | solution.py:476
  23.6 21.3 %collective-permute-start.14 = (bf16[24,2304]{1,0:T(8,128)(2,1)S(1)}, bf16[24,2304]{1,0:T(8,128)(2,1)S(1)}, u32[]{:S(2)}, u32[]{:S(2)}) collective-permute-start(bf16[24,2304]{1,0:T(8,128)(2,1)S(1)} %get-tuple-element.111.refs_1_), channel_id=1, source_target_pairs={{0,12},{1,13},{2,14},{3,15},{4,0},{5,1},{6,2},{7,3},{8,4},{9,5},{1... | collective-permute-start | bytes 331784 | tf_op jit(solution)/shard_map/ppermute | solution.py:476
  25.0 22.4 %collective-permute-start.2 = (bf16[24,2304]{1,0:T(8,128)(2,1)S(1)}, bf16[24,2304]{1,0:T(8,128)(2,1)S(1)}, u32[]{:S(2)}, u32[]{:S(2)}) collective-permute-start(bf16[24,2304]{1,0:T(8,128)(2,1)S(1)} %get-tuple-element.112.refs_1_), channel_id=1, source_target_pairs={{0,4},{1,5},{2,6},{3,7},{4,8},{5,9},{6,10},{7,11},{8,12},{9,13},{1... | collective-permute-start | bytes 331784 | tf_op jit(solution)/shard_map/ppermute | solution.py:476
  25.1 22.8 %collective-permute-start.3 = (bf16[24,2304]{1,0:T(8,128)(2,1)S(1)}, bf16[24,2304]{1,0:T(8,128)(2,1)S(1)}, u32[]{:S(2)}, u32[]{:S(2)}) collective-permute-start(bf16[24,2304]{1,0:T(8,128)(2,1)S(1)} %get-tuple-element.112.refs_1_), channel_id=1, source_target_pairs={{0,8},{1,9},{2,10},{3,11},{4,12},{5,13},{6,14},{7,15},{8,0},{9,1},... | collective-permute-start | bytes 331784 | tf_op jit(solution)/shard_map/ppermute | solution.py:476
  36.0 13.7 %collective-permute-start.4 = (bf16[24,2304]{1,0:T(8,128)(2,1)S(1)}, bf16[24,2304]{1,0:T(8,128)(2,1)S(1)}, u32[]{:S(2)}, u32[]{:S(2)}) collective-permute-start(bf16[24,2304]{1,0:T(8,128)(2,1)S(1)} %get-tuple-element.112.refs_1_), channel_id=1, source_target_pairs={{0,12},{1,13},{2,14},{3,15},{4,0},{5,1},{6,2},{7,3},{8,4},{9,5},{1... | collective-permute-start | bytes 331784 | tf_op jit(solution)/shard_map/ppermute | solution.py:476
  53.1 12.9 %collective-permute-start.6 = (bf16[4,24,1152]{2,1,0:T(8,128)(2,1)S(1)}, bf16[4,24,1152]{2,1,0:T(8,128)(2,1)S(1)}, u32[]{:S(2)}, u32[]{:S(2)}) collective-permute-start(bf16[4,24,1152]{2,1,0:T(8,128)(2,1)S(1)} %get-tuple-element.56.refs_1_), channel_id=1, source_target_pairs={{0,1},{1,0},{2,3},{3,2},{4,5},{5,4},{6,7},{7,6},{8,9},{9,8},{10,11... | collective-permute-start | bytes 663560 | tf_op jit(solution)/shard_map/ppermute | solution.py:476
  54.4 12.9 %collective-permute-start.8 = (bf16[4,24,1152]{2,1,0:T(8,128)(2,1)S(1)}, bf16[4,24,1152]{2,1,0:T(8,128)(2,1)S(1)}, u32[]{:S(2)}, u32[]{:S(2)}) collective-permute-start(bf16[4,24,1152]{2,1,0:T(8,128)(2,1)S(1)} %get-tuple-element.57.refs_5_), channel_id=1, source_target_pairs={{0,2},{1,3},{2,0},{3,1},{4,6},{5,7},{6,4},{7,5},{8,10},{9,11},{10,... | collective-permute-start | bytes 663560 | tf_op jit(solution)/shard_map/ppermute | solution.py:476
  56.6 11.9 %collective-permute-start.10 = (bf16[4,24,1152]{2,1,0:T(8,128)(2,1)S(1)}, bf16[4,24,1152]{2,1,0:T(8,128)(2,1)S(1)}, u32[]{:S(2)}, u32[]{:S(2)}) collective-permute-start(bf16[4,24,1152]{2,1,0:T(8,128)(2,1)S(1)} %collective-permute-done.9.refs_7_), channel_id=1, source_target_pairs={{0,2},{1,3},{2,0},{3,1},{4,6},{5,7},{6,4},{7,5},{8,10},{9,11},{10,... | collective-permute-start | bytes 663560 | tf_op jit(solution)/shard_map/ppermute | solution.py:476
  57.7 13.1 %collective-permute-start.7 = (bf16[4,24,1152]{2,1,0:T(8,128)(2,1)S(1)}, bf16[4,24,1152]{2,1,0:T(8,128)(2,1)S(1)}, u32[]{:S(2)}, u32[]{:S(2)}) collective-permute-start(bf16[4,24,1152]{2,1,0:T(8,128)(2,1)S(1)} %collective-permute-done.5.refs_2_), channel_id=1, source_target_pairs={{0,1},{1,0},{2,3},{3,2},{4,5},{5,4},{6,7},{7,6},{8,9},{9,8},{10,11... | collective-permute-start | bytes 663560 | tf_op jit(solution)/shard_map/ppermute | solution.py:476
  61.3 14.2 %collective-permute-start.16 = (bf16[4,24,1152]{2,1,0:T(8,128)(2,1)S(1)}, bf16[4,24,1152]{2,1,0:T(8,128)(2,1)S(1)}, u32[]{:S(2)}, u32[]{:S(2)}) collective-permute-start(bf16[4,24,1152]{2,1,0:T(8,128)(2,1)S(1)} %get-tuple-element.58.refs_1_), channel_id=1, source_target_pairs={{0,1},{1,0},{2,3},{3,2},{4,5},{5,4},{6,7},{7,6},{8,9},{9,8},{10,11... | collective-permute-start | bytes 663560 | tf_op jit(solution)/shard_map/ppermute | solution.py:476
  67.2 13.1 %collective-permute-start.17 = (bf16[4,24,1152]{2,1,0:T(8,128)(2,1)}, bf16[4,24,1152]{2,1,0:T(8,128)(2,1)S(1)}, u32[]{:S(2)}, u32[]{:S(2)}) collective-permute-start(bf16[4,24,1152]{2,1,0:T(8,128)(2,1)} %collective-permute-done.15.refs_2_), channel_id=1, source_target_pairs={{0,1},{1,0},{2,3},{3,2},{4,5},{5,4},{6,7},{7,6},{8,9},{9,8},{10,11... | collective-permute-start | bytes 663560 | tf_op jit(solution)/shard_map/ppermute | solution.py:476
  68.5 11.8 %collective-permute-start.20 = (bf16[4,24,1152]{2,1,0:T(8,128)(2,1)S(1)}, bf16[4,24,1152]{2,1,0:T(8,128)(2,1)S(1)}, u32[]{:S(2)}, u32[]{:S(2)}) collective-permute-start(bf16[4,24,1152]{2,1,0:T(8,128)(2,1)S(1)} %collective-permute-done.19.refs_7_), channel_id=1, source_target_pairs={{0,2},{1,3},{2,0},{3,1},{4,6},{5,7},{6,4},{7,5},{8,10},{9,11},{10,... | collective-permute-start | bytes 663560 | tf_op jit(solution)/shard_map/ppermute | solution.py:476
  71.7 27.0 %collective-permute-start.11 = (bf16[384,2304]{1,0:T(8,128)(2,1)S(1)}, bf16[384,2304]{1,0:T(8,128)(2,1)}, u32[]{:S(2)}, u32[]{:S(2)}) collective-permute-start(bf16[384,2304]{1,0:T(8,128)(2,1)S(1)} %bitcast.61), channel_id=1, source_target_pairs={{0,16},{16,0},{1,17},{17,1},{2,18},{18,2},{3,19},{19,3},{4,20},{20... | collective-permute-start | bytes 5308424 | tf_op jit(solution)/shard_map/ppermute | solution.py:472
  137.2 37.9 %collective-permute-start.34 = (bf16[384,2304]{1,0:T(8,128)(2,1)S(1)}, bf16[384,2304]{1,0:T(8,128)(2,1)S(1)}, u32[]{:S(2)}, u32[]{:S(2)}) collective-permute-start(bf16[384,2304]{1,0:T(8,128)(2,1)S(1)} %get-tuple-element.69), channel_id=1, source_target_pairs={{0,16},{16,0},{1,17},{17,1},{2,18},{18,2},{3,19},{19,3},{4,20},{20... | collective-permute-start | bytes 5308424 | tf_op jit(solution)/shard_map/ppermute | solution.py:472
  139.2 32.4 %collective-permute-start.42 = (bf16[4,2,24,1152]{3,2,1,0:T(8,128)(2,1)S(1)}, bf16[4,2,24,1152]{3,2,1,0:T(8,128)(2,1)S(1)}, u32[]{:S(2)}, u32[]{:S(2)}) collective-permute-start(bf16[4,2,24,1152]{3,2,1,0:T(8,128)(2,1)S(1)} %get-tuple-element.82), channel_id=1, source_target_pairs={{0,2},{1,3},{2,0},{3,1},{4,6},{5,7},{6,4},{7,5},{8,10},{9,11},{10,... | collective-permute-start | bytes 1327112 | tf_op jit(solution)/shard_map/ppermute | solution.py:476
  147.6 24.0 %collective-permute-start.43 = (bf16[4,2,24,1152]{3,2,1,0:T(8,128)(2,1)S(1)}, bf16[4,2,24,1152]{3,2,1,0:T(8,128)(2,1)S(1)}, u32[]{:S(2)}, u32[]{:S(2)}) collective-permute-start(bf16[4,2,24,1152]{3,2,1,0:T(8,128)(2,1)S(1)} %get-tuple-element.84), channel_id=1, source_target_pairs={{0,1},{1,0},{2,3},{3,2},{4,5},{5,4},{6,7},{7,6},{8,9},{9,8},{10,11... | collective-permute-start | bytes 1327112 | tf_op jit(solution)/shard_map/ppermute | solution.py:476
  149.5 11.3 %collective-permute-start.24 = (bf16[1,1,128,384]{3,2,1,0:T(8,128)(2,1)S(1)}, bf16[1,1,128,384]{3,2,1,0:T(8,128)(2,1)S(1)}, u32[]{:S(2)}, u32[]{:S(2)}) collective-permute-start(bf16[1,1,128,384]{3,2,1,0:T(8,128)(2,1)S(1)} %get-tuple-element.114), channel_id=1, source_target_pairs={{0,1},{1,0},{2,3},{3,2},{4,5},{5,4},{6,7},{7,6},{8,9},{9,8},{10,11... | collective-permute-start | bytes 294920 | tf_op jit(solution)/shard_map/ppermute | solution.py:472
  165.0 37.6 %collective-permute-start.25 = (bf16[2,2,128,384]{3,2,1,0:T(8,128)(2,1)}, bf16[2,2,128,384]{3,2,1,0:T(8,128)(2,1)}, u32[]{:S(2)}, u32[]{:S(2)}) collective-permute-start(bf16[2,2,128,384]{3,2,1,0:T(8,128)(2,1)} %get-tuple-element.100), channel_id=1, source_target_pairs={{0,16},{16,0},{1,17},{17,1},{2,18},{18,2},{3,19},{19,3},{4,20},{20... | collective-permute-start | bytes 1179656 | tf_op jit(solution)/shard_map/ppermute | solution.py:472
  173.5 10.3 %collective-permute-start.44 = (bf16[4,24,1152]{2,1,0:T(8,128)(2,1)}, bf16[4,24,1152]{2,1,0:T(8,128)(2,1)S(1)}, u32[]{:S(2)}, u32[]{:S(2)}) collective-permute-start(bf16[4,24,1152]{2,1,0:T(8,128)(2,1)} %get-tuple-element.86), channel_id=1, source_target_pairs={{0,1},{1,0},{2,3},{3,2},{4,5},{5,4},{6,7},{7,6},{8,9},{9,8},{10,11... | collective-permute-start | bytes 663560 | tf_op jit(solution)/shard_map/ppermute | solution.py:476
  176.8 17.1 %collective-permute-start.35 = (bf16[4,2,24,1152]{3,2,1,0:T(8,128)(2,1)}, bf16[4,2,24,1152]{3,2,1,0:T(8,128)(2,1)S(1)}, u32[]{:S(2)}, u32[]{:S(2)}) collective-permute-start(bf16[4,2,24,1152]{3,2,1,0:T(8,128)(2,1)} %get-tuple-element.71), channel_id=1, source_target_pairs={{0,2},{1,3},{2,0},{3,1},{4,6},{5,7},{6,4},{7,5},{8,10},{9,11},{10,... | collective-permute-start | bytes 1327112 | tf_op jit(solution)/shard_map/ppermute | solution.py:476
  178.1 15.8 %collective-permute-start.36 = (bf16[4,2,24,1152]{3,2,1,0:T(8,128)(2,1)}, bf16[4,2,24,1152]{3,2,1,0:T(8,128)(2,1)S(1)}, u32[]{:S(2)}, u32[]{:S(2)}) collective-permute-start(bf16[4,2,24,1152]{3,2,1,0:T(8,128)(2,1)} %get-tuple-element.73), channel_id=1, source_target_pairs={{0,1},{1,0},{2,3},{3,2},{4,5},{5,4},{6,7},{7,6},{8,9},{9,8},{10,11... | collective-permute-start | bytes 1327112 | tf_op jit(solution)/shard_map/ppermute | solution.py:476
  182.6 10.5 %collective-permute-start.45 = (bf16[4,24,1152]{2,1,0:T(8,128)(2,1)S(1)}, bf16[4,24,1152]{2,1,0:T(8,128)(2,1)S(1)}, u32[]{:S(2)}, u32[]{:S(2)}) collective-permute-start(bf16[4,24,1152]{2,1,0:T(8,128)(2,1)S(1)} %copy-done.8), channel_id=1, source_target_pairs={{0,2},{1,3},{2,0},{3,1},{4,6},{5,7},{6,4},{7,5},{8,10},{9,11},{10,... | collective-permute-start | bytes 663560 | tf_op jit(solution)/shard_map/ppermute | solution.py:476
  183.9 12.2 %collective-permute-start.33 = (f32[32,384]{1,0:T(8,128)S(1)}, f32[32,384]{1,0:T(8,128)S(1)}, u32[]{:S(2)}, u32[]{:S(2)}) collective-permute-start(f32[32,384]{1,0:T(8,128)S(1)} %fusion), channel_id=1, source_target_pairs={{0,16},{16,0},{1,17},{17,1},{2,18},{18,2},{3,19},{19,3},{4,20},{20... | collective-permute-start | bytes 147464 | tf_op jit(solution)/shard_map/ppermute | solution.py:472
  193.8 10.9 %collective-permute-start.46 = (bf16[24,2304]{1,0:T(8,128)(2,1)S(1)}, bf16[24,2304]{1,0:T(8,128)(2,1)S(1)}, u32[]{:S(2)}, u32[]{:S(2)}) collective-permute-start(bf16[24,2304]{1,0:T(8,128)(2,1)S(1)} %get-tuple-element.90), channel_id=1, source_target_pairs={{0,4},{1,5},{2,6},{3,7},{4,8},{5,9},{6,10},{7,11},{8,12},{9,13},{1... | collective-permute-start | bytes 331784 | tf_op jit(solution)/shard_map/ppermute | solution.py:476
  200.4 11.2 %collective-permute-start.48 = (bf16[24,2304]{1,0:T(8,128)(2,1)S(1)}, bf16[24,2304]{1,0:T(8,128)(2,1)S(1)}, u32[]{:S(2)}, u32[]{:S(2)}) collective-permute-start(bf16[24,2304]{1,0:T(8,128)(2,1)S(1)} %get-tuple-element.92), channel_id=1, source_target_pairs={{0,12},{1,13},{2,14},{3,15},{4,0},{5,1},{6,2},{7,3},{8,4},{9,5},{1... | collective-permute-start | bytes 331784 | tf_op jit(solution)/shard_map/ppermute | solution.py:476
  202.6 12.0 %collective-permute-start.40 = (bf16[24,2304]{1,0:T(8,128)(2,1)S(1)}, bf16[24,2304]{1,0:T(8,128)(2,1)S(1)}, u32[]{:S(2)}, u32[]{:S(2)}) collective-permute-start(bf16[24,2304]{1,0:T(8,128)(2,1)S(1)} %get-tuple-element.80), channel_id=1, source_target_pairs={{0,8},{1,9},{2,10},{3,11},{4,12},{5,13},{6,14},{7,15},{8,0},{9,1},... | collective-permute-start | bytes 331784 | tf_op jit(solution)/shard_map/ppermute | solution.py:476
  204.6 12.3 %collective-permute-start.41 = (bf16[24,2304]{1,0:T(8,128)(2,1)S(1)}, bf16[24,2304]{1,0:T(8,128)(2,1)S(1)}, u32[]{:S(2)}, u32[]{:S(2)}) collective-permute-start(bf16[24,2304]{1,0:T(8,128)(2,1)S(1)} %get-tuple-element.81), channel_id=1, source_target_pairs={{0,12},{1,13},{2,14},{3,15},{4,0},{5,1},{6,2},{7,3},{8,4},{9,5},{1... | collective-permute-start | bytes 331784 | tf_op jit(solution)/shard_map/ppermute | solution.py:476
  (37 other events, 237.9 us)
Sparse Core Ops, SparseCore 0:
  118.1 62.1 all-gather.2

commit v5 on v4

--- a/solution.py
+++ b/solution.py
@@ -54,37 +54,67 @@
     return jnp.sum(values.astype(jnp.float32), axis=0, keepdims=True)
 
 
-def section_kernel(layout, backward, after, *refs):
+def saved_shapes(layout, length):
+    width, hidden = layout[:2]
+    bf16, f32 = jnp.bfloat16, jnp.float32
+    return [
+        ((1, 6 * width), f32),
+        ((length, 3 * width), bf16),
+        ((length, width), bf16),
+        ((length, hidden), bf16),
+        ((HEADS, length, length), f32),
+        ((length, hidden), f32),
+        ((length, width), f32),
+        ((length, width), f32),
+        ((hidden, width), bf16),
+    ]
+
+
+def section_kernel(layout, forward, backward, after, *refs):
     width, hidden, rows, ratio, ring_size, share, bias_count = layout
-    rank_ref, x_ref, modulation_ref, bias_ref = refs[:4]
-    refs = refs[4:]
+    refs = list(refs)
+
+    def take(count):
+        taken = refs[:count]
+        del refs[:count]
+        return taken
+
+    rank_ref, x_ref = take(2)
+    if forward:
+        modulation_ref, bias_ref = take(2)
+    else:
+        saved = take(9)
     if backward:
-        dy_ref = refs[0]
-        refs = refs[1:]
-    mine_ref, theirs_ref = refs[:2]
-    refs = refs[2 + after :]
+        (dy_ref,) = take(1)
+    mine_ref, theirs_ref = take(2)
+    take(after)
+    if forward:
+        (y_ref,) = take(1)
     if backward:
-        y_ref, dx_ref, row_ref, keep_ref, send_ref = refs[:5]
-        refs = refs[5:]
-    else:
-        y_ref = refs[0]
-        refs = refs[1:]
-    att_w, out_w, up_w, down_p, sems = refs[:5]
-    bias_s, down_w, down_s, block_s, qkv_s, att_s, u_s = refs[5:12]
+        dx_ref, dmod_ref, sums_ref, keep_ref, send_ref = take(5)
+    elif forward:
+        saved = take(9)
+    att_w, out_w, up_w, sems, down_s, block_s = take(6)
+    if forward:
+        down_p, bias_s = take(2)
     if backward:
-        soft_s, slope_s, da_s, dqkv_s, halves, out_sems = refs[12:]
+        da_s, dqkv_s, row_ref, halves, out_sems = take(5)
+    if forward and backward:
+        saved = take(9)
+    mod_s, qkv_s, att_s, u_s, soft_s, slope_s, one_s, two_s, down_w = saved
 
     rank = rank_ref[0]
     split = hidden - 2 * width
 
     def fetches(first, second):
-        moves = (
+        moves = [
             (first.at[:, : 3 * width], att_w),
             (first.at[:, 3 * width : 4 * width], out_w),
             (first.at[:, 4 * width :], up_w.at[:, :split]),
             (second.at[:, : hidden - split], up_w.at[:, split:]),
-            (second.at[:, hidden - split :], down_p),
-        )
+        ]
+        if forward:
+            moves.append((second.at[:, hidden - split :], down_p))
         return [
             pltpu.make_async_copy(source, target, sems.at[i])
             for i, (source, target) in enumerate(moves)
@@ -102,74 +132,76 @@
 
     arrivals = fetches(mine_ref, theirs_ref)
 
-    def bias(a, b):
-        return bias_s[:, a:b]
-
-    x = x_ref[...].astype(jnp.float32)
-    normed_one, factor_one = normalize_rows(x)
-    for d in range(ring_size):
-        bias_s[:, d * bias_count : (d + 1) * bias_count] = bias_ref[d : d + 1, :]
-    modulation = modulation_ref[...] + bias(0, 6 * width)
-    shift_one, scale_one, gate_one, shift_two, scale_two, gate_two = [
-        modulation[:, i * width : (i + 1) * width] for i in range(6)
-    ]
-    hidden_one = low(normed_one * (1.0 + scale_one) + shift_one)
-    at = 6 * width
-    arrivals[0].wait()
-    qkv_s[:, :width] = low(matmul(hidden_one, att_w[:, :width]) + bias(at, at + width))
-    qkv_s[:, width : 2 * width] = low(matmul(hidden_one, att_w[:, width : 2 * width]))
-    qkv_s[:, 2 * width :] = low(
-        matmul(hidden_one, att_w[:, 2 * width :]) + bias(at + width, at + 2 * width)
-    )
-
     def part(ref, member, head):
         start = member * width + head * HEAD
         return ref[:, start : start + HEAD]
 
-    for head in range(HEADS):
-        scores = matmul_transposed(part(qkv_s, 0, head), part(qkv_s, 1, head)) * SCALE
-        raised = jnp.exp(scores - jnp.max(scores, axis=-1, keepdims=True))
-        soft = raised * (1.0 / jnp.sum(raised, axis=-1, keepdims=True))
-        if backward:
+    x = x_ref[...].astype(jnp.float32)
+    normed_one, factor_one = normalize_rows(x)
+    if forward:
+        for d in range(ring_size):
+            bias_s[:, d * bias_count : (d + 1) * bias_count] = bias_ref[d : d + 1, :]
+        mod_s[...] = modulation_ref[...] + bias_s[:, : 6 * width]
+    shift_one, scale_one, gate_one, shift_two, scale_two, gate_two = [
+        mod_s[:, i * width : (i + 1) * width] for i in range(6)
+    ]
+    hidden_one = low(normed_one * (1.0 + scale_one) + shift_one)
+    if forward:
+
+        def bias(a, b):
+            return bias_s[:, a:b]
+
+        at = 6 * width
+        arrivals[0].wait()
+        qkv_s[:, :width] = low(matmul(hidden_one, att_w[:, :width]) + bias(at, at + width))
+        qkv_s[:, width : 2 * width] = low(matmul(hidden_one, att_w[:, width : 2 * width]))
+        qkv_s[:, 2 * width :] = low(
+            matmul(hidden_one, att_w[:, 2 * width :]) + bias(at + width, at + 2 * width)
+        )
+        for head in range(HEADS):
+            scores = matmul_transposed(part(qkv_s, 0, head), part(qkv_s, 1, head)) * SCALE
+            raised = jnp.exp(scores - jnp.max(scores, axis=-1, keepdims=True))
+            soft = raised * (1.0 / jnp.sum(raised, axis=-1, keepdims=True))
             soft_s[head] = soft
-        attended = matmul(low(soft), part(qkv_s, 2, head))
-        att_s[:, head * HEAD : (head + 1) * HEAD] = low(attended)
-    arrivals[1].wait()
-    branch_one = matmul(att_s[...], out_w[...]) + bias(at + 2 * width, at + 3 * width)
+            attended = matmul(low(soft), part(qkv_s, 2, head))
+            att_s[:, head * HEAD : (head + 1) * HEAD] = low(attended)
+        arrivals[1].wait()
+        one_s[...] = matmul(att_s[...], out_w[...]) + bias(at + 2 * width, at + 3 * width)
+    branch_one = one_s[...]
     middle = x + gate_one * branch_one
     normed_two, factor_two = normalize_rows(middle)
     hidden_two = low(normed_two * (1.0 + scale_two) + shift_two)
-    arrivals[2].wait()
-    arrivals[3].wait()
-    at += 3 * width
-    for j in range(ratio):
-        cut = slice(j * width, (j + 1) * width)
-        a = matmul(hidden_two, up_w[:, cut]) + bias(at + j * width, at + (j + 1) * width)
-        square = a * a
-        turn = jnp.tanh(INNER * (a + CUBE * (a * square)))
-        half_one = 0.5 * (1.0 + turn)
-        u_s[:, cut] = low(a * half_one)
-        if backward:
+    if forward:
+        arrivals[2].wait()
+        arrivals[3].wait()
+        at += 3 * width
+        for j in range(ratio):
+            cut = slice(j * width, (j + 1) * width)
+            a = matmul(hidden_two, up_w[:, cut]) + bias(at + j * width, at + (j + 1) * width)
+            square = a * a
+            turn = jnp.tanh(INNER * (a + CUBE * (a * square)))
+            half_one = 0.5 * (1.0 + turn)
+            u_s[:, cut] = low(a * half_one)
             slope_s[:, cut] = half_one + (0.5 * INNER) * a * (1.0 - turn * turn) * (
                 1.0 + (3.0 * CUBE) * square
             )
-    arrivals[4].wait()
-    block_s[...] = down_p[...].astype(jnp.float32)
-    for d in range(ring_size):
-        for j in range(ratio):
-            down_s[(d * ratio + j) * rows : (d * ratio + j + 1) * rows, :] = block_s[
-                d * rows : (d + 1) * rows, j * width : (j + 1) * width
-            ]
-    down_w[...] = low(down_s[...])
-    branch_two = matmul(u_s[...], down_w[...]) + bias(at + hidden, at + hidden + width)
-    y_ref[...] = low(middle + gate_two * branch_two)
+        arrivals[4].wait()
+        block_s[...] = down_p[...].astype(jnp.float32)
+        for d in range(ring_size):
+            for j in range(ratio):
+                down_s[(d * ratio + j) * rows : (d * ratio + j + 1) * rows, :] = block_s[
+                    d * rows : (d + 1) * rows, j * width : (j + 1) * width
+                ]
+        down_w[...] = low(down_s[...])
+        two_s[...] = matmul(u_s[...], down_w[...]) + bias(at + hidden, at + hidden + width)
+        y_ref[...] = low(middle + gate_two * two_s[...])
     if not backward:
         return
 
     grad_out = dy_ref[...].astype(jnp.float32)
     grad_branch = low(gate_two * grad_out)
     sums_at = 6 * width
-    row_ref[:, 5 * width : 6 * width] = column_sum(grad_out * branch_two)
+    row_ref[:, 5 * width : 6 * width] = column_sum(grad_out * two_s[...])
     row_ref[:, sums_at + 3 * width + hidden : sums_at + 4 * width + hidden] = column_sum(
         grad_branch
     )
@@ -180,8 +212,7 @@
         row_ref[:, sums_at + (3 + j) * width : sums_at + (4 + j) * width] = column_sum(
             grad_expanded
         )
-    up_first = low(outer_sum(hidden_two, da_s[:, :split]) * share)
-    halves[0, :, 4 * width :] = up_first
+    halves[0, :, 4 * width :] = low(outer_sum(hidden_two, da_s[:, :split]) * share)
     halves[1, :, : hidden - split] = low(outer_sum(hidden_two, da_s[:, split:]) * share)
     down_s[...] = outer_sum(u_s[...], grad_branch) * share
     for d in range(ring_size):
@@ -203,6 +234,9 @@
     def _():
         second_out[1].start()
 
+    if not forward:
+        arrivals[2].wait()
+        arrivals[3].wait()
     grad_hidden_two = matmul_transposed(da_s[...], up_w[...])
     row_ref[:, 3 * width : 4 * width] = column_sum(grad_hidden_two)
     row_ref[:, 4 * width : 5 * width] = column_sum(grad_hidden_two * normed_two)
@@ -213,6 +247,8 @@
     grad_attention = low(gate_one * grad_middle)
     row_ref[:, sums_at + 2 * width : sums_at + 3 * width] = column_sum(grad_attention)
     halves[0, :, 3 * width : 4 * width] = low(outer_sum(att_s[...], grad_attention) * share)
+    if not forward:
+        arrivals[1].wait()
     grad_attended = low(matmul_transposed(grad_attention, out_w[...]))
     for head in range(HEADS):
         soft = soft_s[head]
@@ -244,6 +280,8 @@
     def _():
         first_out[1].start()
 
+    if not forward:
+        arrivals[0].wait()
     grad_hidden_one = matmul_transposed(dqkv_s[...], att_w[...])
     row_ref[:, :width] = column_sum(grad_hidden_one)
     row_ref[:, width : 2 * width] = column_sum(grad_hidden_one * normed_one)
@@ -252,57 +290,67 @@
         + normalize_back(normed_one, factor_one, grad_hidden_one * (1.0 + scale_one))
     )
     row_ref[:, : 6 * width] = low(row_ref[:, : 6 * width]).astype(jnp.float32)
+    dmod_ref[...] = row_ref[:, : 6 * width]
+    for d in range(ring_size):
+        sums_ref[d : d + 1, :] = row_ref[:, d * bias_count : (d + 1) * bias_count]
     second_out[0].wait()
     first_out[0].wait()
 
 
-def run_section(layout, rank, x, modulation, bias, halves, dy=None, after=()):
+def run_section(layout, rank, x, halves, start=None, saved=None, dy=None, after=()):
     width, hidden, rows, ratio, ring_size, share, bias_count = layout
     length = x.shape[0]
-    backward = dy is not None
+    forward, backward = start is not None, dy is not None
     vmem = pl.BlockSpec(memory_space=pltpu.VMEM)
     hbm = pl.BlockSpec(memory_space=pl.ANY)
     bf16, f32 = jnp.bfloat16, jnp.float32
     half = 2 * width + hidden
-    shapes = [jax.ShapeDtypeStruct((length, width), bf16)]
-    out_specs = [vmem]
+    kept = saved_shapes(layout, length)
+    operands = [rank, x, *(start if forward else saved)]
+    shapes, out_specs = [], []
     scratch = [
         pltpu.VMEM((width, 3 * width), bf16),
         pltpu.VMEM((width, width), bf16),
         pltpu.VMEM((width, hidden), bf16),
-        pltpu.VMEM((width, hidden), bf16),
         pltpu.SemaphoreType.DMA((5,)),
-        pltpu.VMEM((1, bias_count * ring_size), f32),
-        pltpu.VMEM((hidden, width), bf16),
         pltpu.VMEM((hidden, width), f32),
         pltpu.VMEM((width, hidden), f32),
-        pltpu.VMEM((length, 3 * width), bf16),
-        pltpu.VMEM((length, width), bf16),
-        pltpu.VMEM((length, hidden), bf16),
     ]
-    operands = [rank, x, modulation, bias]
+    if forward:
+        shapes.append(jax.ShapeDtypeStruct((length, width), bf16))
+        scratch += [
+            pltpu.VMEM((width, hidden), bf16),
+            pltpu.VMEM((1, bias_count * ring_size), f32),
+        ]
     if backward:
         operands.append(dy)
         shapes += [
             jax.ShapeDtypeStruct((length, width), bf16),
-            jax.ShapeDtypeStruct((1, 10 * width + hidden), f32),
+            jax.ShapeDtypeStruct((1, 6 * width), f32),
+            jax.ShapeDtypeStruct((ring_size, bias_count), f32),
             jax.ShapeDtypeStruct((width, half), bf16),
             jax.ShapeDtypeStruct((width, half), bf16),
         ]
-        out_specs += [vmem, vmem, hbm, hbm]
         scratch += [
-            pltpu.VMEM((HEADS, length, length), f32),
-            pltpu.VMEM((length, hidden), f32),
             pltpu.VMEM((length, hidden), bf16),
             pltpu.VMEM((length, 3 * width), bf16),
+            pltpu.VMEM((1, 10 * width + hidden), f32),
             pltpu.VMEM((2, width, half), bf16),
             pltpu.SemaphoreType.DMA((2,)),
         ]
-    specs = [pl.BlockSpec(memory_space=pltpu.SMEM)] + [vmem] * (len(operands) - 1) + [hbm] * (2 + len(after))
+        if forward:
+            scratch += [pltpu.VMEM(extent, kind) for extent, kind in kept]
+    else:
+        shapes += [jax.ShapeDtypeStruct(extent, kind) for extent, kind in kept]
+    out_specs = [vmem] * len(shapes)
+    if backward:
+        out_specs[-2:] = [hbm, hbm]
+    specs = [pl.BlockSpec(memory_space=pltpu.SMEM)] + [vmem] * (len(operands) - 1)
+    specs += [hbm] * (2 + len(after))
     work = 2 * length * width * (4 * width + 2 * hidden + 2 * length)
     moved = 2 * width * (10 * width + 2 * hidden)
     return pl.pallas_call(
-        partial(section_kernel, layout, backward, len(after)),
+        partial(section_kernel, layout, forward, backward, len(after)),
         out_shape=shapes,
         in_specs=specs,
         out_specs=out_specs,
@@ -311,8 +359,8 @@
             vmem_limit_bytes=(36 if length <= 256 else 56) * 1024 * 1024
         ),
         cost_estimate=pl.CostEstimate(
-            flops=(3 if backward else 1) * work,
-            bytes_accessed=(2 if backward else 1) * moved,
+            flops=(forward + 2 * backward) * work,
+            bytes_accessed=(1 + backward) * moved,
             transcendentals=HEADS * length * length + length * hidden,
         ),
     )(*operands, *halves, *after)
@@ -356,6 +404,9 @@
     pieces, sems = refs[:high], refs[-1]
     targets = refs[-1 - (2 if split else 1) : -1]
     copies = []
+    if len(refs) > high + 1 + len(targets):
+        targets = refs[high + 1 : -1]
+        copies.append(pltpu.make_async_copy(refs[high], targets[-1], sems.at[high, 0]))
     for turn, piece in enumerate(pieces):
         place = lax.rem(place_ref[0] + (high - turn), high)
         parts = (piece.at[:, :split], piece.at[:, split:]) if split else (piece,)
@@ -461,7 +512,7 @@
         body,
         out_shape=shapes,
         in_specs=specs,
-        out_specs=[pl.BlockSpec(memory_space=memory)] * len(shapes),
+        out_specs=[pl.BlockSpec(memory_space=pltpu.VMEM)] * len(shapes),
         scratch_shapes=list(scratch),
         compiler_params=pltpu.CompilerParams(vmem_limit_bytes=limit * 1024 * 1024),
         cost_estimate=pl.CostEstimate(flops=0, bytes_accessed=3 * moved, transcendentals=0),
@@ -488,22 +539,25 @@
     return [block] + [rotate(block, size, turn) for turn in range(1, size // 4)]
 
 
-def gather_along_z(shard, place, size, after=()):
+def gather_along_z(shard, place, size, handed=(), after=()):
     high = size // 4
     rows, lanes = shard.shape
     return in_memory(
         partial(stack_kernel, high, lanes // 2),
-        [jax.ShapeDtypeStruct((high, rows, lanes // 2), shard.dtype)] * 2,
-        [place, *rotations(shard, size)],
-        scratch=[pltpu.SemaphoreType.DMA((high, 2))],
-        memory=pl.ANY,
+        [jax.ShapeDtypeStruct((high, rows, lanes // 2), shard.dtype)] * 2
+        + [jax.ShapeDtypeStruct(block.shape, block.dtype) for block in handed],
+        [place, *rotations(shard, size), *handed],
+        scratch=[pltpu.SemaphoreType.DMA((high + 1, 2))],
         after=after,
     )
 
 
-def gather_across(first, second, place, size):
+def first_flips(first, second, size):
+    return flip(first, size, 2), flip(second, size, 1)
+
+
+def gather_across(first, second, first_x, second_y, place, size):
     high, rows, lanes = first.shape
-    first_x, second_y = flip(first, size, 2), flip(second, size, 1)
     first_y, second_x = flip(first, size, 1), flip(second, size, 2)
     first_both, second_both = flip(first_x, size, 1), flip(second_y, size, 2)
     (full,) = in_memory(
@@ -511,34 +565,16 @@
         [jax.ShapeDtypeStruct((high, 2, 2, rows, 2 * lanes), first.dtype)],
         [place, first, first_x, first_y, first_both, second, second_x, second_y, second_both],
         scratch=[pltpu.SemaphoreType.DMA((8,))],
-        memory=pl.ANY,
     )
     return full.reshape(size * rows, 2 * lanes)
 
 
-def gather_rows(block, place, size):
-    high = size // 4
-    (stacked,) = in_memory(
-        partial(stack_kernel, high, 0),
-        [jax.ShapeDtypeStruct((high, *block.shape), block.dtype)],
-        [place, *rotations(block, size)],
-        scratch=[pltpu.SemaphoreType.DMA((high, 1))],
-        memory=pl.ANY,
-    )
-    (full,) = in_memory(
-        partial(weave_kernel, 0),
-        [jax.ShapeDtypeStruct((high, 2, 2, *block.shape), block.dtype)],
-        [place, stacked, *[flip(stacked, size, mask) for mask in (2, 1, 3)]],
-        scratch=[pltpu.SemaphoreType.DMA((4,))],
-        memory=pl.ANY,
-    )
-    return full.reshape(size, *block.shape)
-
-
-def scatter_first(mine, got, place, size):
+def scatter_first(mine, got, place, size, after=()):
     rows, half = mine.shape[1:]
     shape = jax.ShapeDtypeStruct((size // 4, 2, rows, half // 2), jnp.bfloat16)
-    return in_memory(partial(chip_sum_kernel, size // 4), [shape] * 4, [place, mine, got])
+    return in_memory(
+        partial(chip_sum_kernel, size // 4), [shape] * 4, [place, mine, got], after=after
+    )
 
 
 def scatter_flips(sorted_terms, size):
@@ -546,12 +582,17 @@
     return first_keep, flip(first_send, size, 2), second_keep, flip(second_send, size, 1)
 
 
-def scatter_rest(received, place, size):
+def scatter_second(received, place, size, after=()):
     high, _, rows, lanes = received[0].shape
     shape = jax.ShapeDtypeStruct((high, rows, lanes), jnp.bfloat16)
-    first_keep, first_send, second_keep, second_send = in_memory(
-        partial(turn_kernel, high), [shape] * 4, [place, *received]
-    )
+    return in_memory(
+        partial(turn_kernel, high), [shape] * 4, [place, *received], after=after
+    )
+
+
+def scatter_rest(turned, place, size):
+    high, rows, lanes = turned[0].shape
+    first_keep, first_send, second_keep, second_send = turned
     first_got, second_got = flip(first_send, size, 1), flip(second_send, size, 2)
     chunk = (rows, 2 * lanes)
     own, *sent = in_memory(
@@ -650,6 +691,7 @@
         ],
         scratch=[pltpu.SemaphoreType.DMA((4 + ratio,))],
         memory=pl.ANY,
+        limit=56,
     )
     got = pair_swap(send, "section")
     first_shard = jnp.where(is_first, keep, got)
@@ -702,8 +744,14 @@
     first_bias, second_bias = products[0, :, 6 * width :], products[1, :, 6 * width :]
 
     if compact:
-        first_parts = gather_along_z(first_shard, place, ring_size, after=(products, both))
-        second_parts = gather_along_z(second_shard, place, ring_size)
+        *first_parts, second_shard = gather_along_z(
+            first_shard, place, ring_size, handed=(second_shard,)
+        )
+        first_parts += first_flips(*first_parts, ring_size)
+        second_parts = gather_along_z(
+            second_shard, place, ring_size, after=(products, both, *first_parts[2:])
+        )
+        second_parts += first_flips(*second_parts, ring_size)
         first_pack = gather_across(*first_parts, place, ring_size)
         second_pack = gather_across(*second_parts, place, ring_size)
     else:
@@ -713,35 +761,66 @@
     second_halves = (second_pack, pair_swap(second_pack, "section"))
     own_matrix = lax.all_gather(modulation_weight[0], RING, axis=0, tiled=True)
 
-    first = (first_input, first_modulation, first_bias, first_halves)
-    (first_low,) = run_section(layout, rank, *first)
-    second_low, second_grad, second_row, second_keep, second_send = run_section(
-        layout, rank, first_low, second_modulation, second_bias, second_halves, last_grad
+    first_low, *first_saved = run_section(
+        layout, rank, first_input, first_halves, (first_modulation, first_bias)
+    )
+    second_low, second_grad, second_dmod, second_sums, second_keep, second_send = run_section(
+        layout, rank, first_low, second_halves, (second_modulation, second_bias), dy=last_grad
     )
     second_got = pair_swap(second_send, "section")
 
     def ring_terms(term):
         return term.reshape(ring_size, rows, half)
 
-    after = ()
+    early = jnp.stack([first_low * live, second_low * live, second_grad])
+
+    def to_slots(block):
+        block = block.reshape(-1, 2, tokens, width)
+        mine = lax.dynamic_index_in_dim(block, seq_rank, 1, keepdims=True)
+        sent = lax.dynamic_index_in_dim(block, 1 - seq_rank, 1, keepdims=True)
+        return mine, pair_swap(sent, "seq")
+
+    if compact:
+        early = to_slots(early)
+    first_grad, first_dmod, first_sums, first_keep, first_send = run_section(
+        layout, rank, first_input, first_halves, saved=first_saved, dy=second_grad
+    )
+    first_got = pair_swap(first_send, "section")
+
+    if compact:
+        early_full, late = side_by_side(*early, 1), side_by_side(*to_slots(first_grad), 1)
+        per_first = jnp.stack([early_full[0], late[0]])
+        per_second = early_full[1:]
+        mine = jnp.where(is_first, per_first, per_second)
+        got = pair_swap(jnp.where(is_first, per_second, per_first), "section")
+        outputs = jnp.where(is_first, jnp.stack([mine, got], 1), jnp.stack([got, mine], 1))
+    else:
+        pieces = jnp.stack([early[0], first_grad, early[1], early[2]])
+        pieces = jnp.swapaxes(pieces.reshape(2, 2, seq_size, tokens, width), 1, 2)
+        pieces = pieces.reshape(2 * seq_size, 2, tokens, width)
+        pieces = lax.all_to_all(pieces, ("section", "seq"), 0, 0, tiled=True)
+        pieces = pieces.reshape(batches, slots, sharers, 2, tokens, width)[:, :, 0]
+        outputs = jnp.moveaxis(pieces, 2, 0)
+    activations = outputs[0]
+    input_grads = outputs[1].astype(jnp.float32)
+
+    shard = jax.ShapeDtypeStruct((rows, half), jnp.float32)
     if compact:
         second_sorted = scatter_first(
             ring_terms(second_keep), ring_terms(second_got), place, ring_size
         )
-        after = (second_sorted[0],)
         second_received = scatter_flips(second_sorted, ring_size)
-    _, first_grad, first_row, first_keep, first_send = run_section(
-        layout, rank, *first, second_grad, after
-    )
-    first_got = pair_swap(first_send, "section")
-
-    shard = jax.ShapeDtypeStruct((rows, half), jnp.float32)
-    if compact:
-        second_pieces = scatter_rest(second_received, place, ring_size)
+        second_turned = scatter_second(second_received, place, ring_size, (early[1],))
         first_sorted = scatter_first(
-            ring_terms(first_keep), ring_terms(first_got), place, ring_size
+            ring_terms(first_keep),
+            ring_terms(first_got),
+            place,
+            ring_size,
+            (second_sorted[0],),
         )
-        first_pieces = scatter_rest(scatter_flips(first_sorted, ring_size), place, ring_size)
+        first_turned = scatter_second(scatter_flips(first_sorted, ring_size), place, ring_size)
+        second_pieces = scatter_rest(second_turned, place, ring_size)
+        first_pieces = scatter_rest(first_turned, place, ring_size)
     else:
 
         def chip_sum(keep, got):
@@ -770,46 +849,18 @@
         [rank, mine, pair_swap(send, "section")],
     )
 
-    early = jnp.stack([first_low * live, second_low * live, second_grad])
-    if compact:
-
-        def to_slots(block):
-            block = block.reshape(-1, 2, tokens, width)
-            mine = lax.dynamic_index_in_dim(block, seq_rank, 1, keepdims=True)
-            sent = lax.dynamic_index_in_dim(block, 1 - seq_rank, 1, keepdims=True)
-            return side_by_side(mine, pair_swap(sent, "seq"), 1)
-
-        early, late = to_slots(early), to_slots(first_grad)
-        per_first = jnp.stack([early[0], late[0]])
-        per_second = early[1:]
-        mine = jnp.where(is_first, per_first, per_second)
-        got = pair_swap(jnp.where(is_first, per_second, per_first), "section")
-        outputs = jnp.where(is_first, jnp.stack([mine, got], 1), jnp.stack([got, mine], 1))
-    else:
-        pieces = jnp.stack([early[0], first_grad, early[1], early[2]])
-        pieces = jnp.swapaxes(pieces.reshape(2, 2, seq_size, tokens, width), 1, 2)
-        pieces = pieces.reshape(2 * seq_size, 2, tokens, width)
-        pieces = lax.all_to_all(pieces, ("section", "seq"), 0, 0, tiled=True)
-        pieces = pieces.reshape(batches, slots, sharers, 2, tokens, width)[:, :, 0]
-        outputs = jnp.moveaxis(pieces, 2, 0)
-    activations = outputs[0]
-    input_grads = outputs[1].astype(jnp.float32)
-
-    own_row = jnp.where(is_first, first_row, second_row)
-    other_row = pair_swap(low(jnp.where(is_first, second_row, first_row)), "section")
-    pair = jnp.where(
-        is_first,
-        jnp.concatenate([low(own_row), other_row]),
-        jnp.concatenate([other_row, low(own_row)]),
-    )
-    if compact:
-        every = gather_rows(pair, place, ring_size)
-    else:
-        every = lax.all_gather(pair, RING, axis=0)[::sharers]
-    every = jnp.swapaxes(every, 0, 1).reshape(-1, pair.shape[1])
-    bias_total = jnp.sum(every.astype(jnp.float32), axis=0)
-    bias_grad = lax.dynamic_slice_in_dim(bias_total, ring_rank * bias_count, bias_count, 0)
-    modulation_rows = every[:, : 6 * width]
+    rows_back = jnp.concatenate(
+        [
+            jnp.concatenate(
+                [jnp.broadcast_to(dmod, (ring_size, 6 * width)), sums], axis=1
+            )
+            for dmod, sums in ((first_dmod, first_sums), (second_dmod, second_sums))
+        ]
+    )
+    every = lax.all_to_all(rows_back[:, None], ("section", "dp", "seq"), 0, 0, tiled=True)
+    every = every[::sharers, 0]
+    bias_grad = jnp.sum(every[:, 6 * width :], axis=0)
+    modulation_rows = low(every[:, : 6 * width])
     modulation_grad = outer_sum(silu_own, modulation_rows)
     products_back = matmul_transposed(modulation_rows, own_matrix)
     products_back = products_back + pair_swap(products_back, "section")

time: 229 us -> 196 us (0.86)
  waiting for transfers between devices: 73.9 us -> 44 us
  Pallas kernels: 58.8 us -> 42.4 us
  starting transfers between devices: 58.7 us -> 65.2 us
  local copies, waits for them, and re-layouts: 10.1 us -> 15.7 us
    ppermute x38 -> x32, waiting for transfers between devices: 55.9 us -> 38.1 us  [ring_exchange(): return lax.ppermute(block, RING, [(i, step(i)) for i in range(size)])]
    pallas_call x15 -> x13, Pallas kernels: 27.5 us -> 16.3 us  [in_memory(): pl.pallas_call(body, out_shape=shapes, in_specs=specs, out_specs=[pl.Bloc...]
    ppermute x12 -> x11, waiting for transfers between devices: 15.7 us -> 5.87 us  [pair_swap(): return lax.ppermute(block, axis, [(0, 1), (1, 0)])]
    pallas_call x3, Pallas kernels: 31.3 us -> 26.1 us  [run_section(): pl.pallas_call(partial(section_kernel, layout, forward, backward, len(aft...]
    all_to_all x0 -> x1, starting transfers between devices: none -> 4.69 us  [per_device(): lax.all_to_all(rows_back[:, None], ('section', 'dp', 'seq'), 0, 0, tiled=...]
    unnamed x35 -> x60, local copies, waits for them, and re-layouts: 5.79 us -> 10.4 us
    ppermute x38 -> x32, starting transfers between devices: 36.2 us -> 37.1 us  [ring_exchange(): return lax.ppermute(block, RING, [(i, step(i)) for i in range(size)])]
    ppermute x12 -> x11, starting transfers between devices: 17.4 us -> 18.3 us  [pair_swap(): return lax.ppermute(block, axis, [(0, 1), (1, 0)])]
  transfers between devices with their start and end apart: 52 -> 46, of which waited for: 23 -> 14; matrix products, arithmetic and copies ran while one was open for 7% -> 10% of each run, Pallas kernels for 20% -> 21%
where the time goes in v5:
time: 196 us; the launch traced here: 195 us
  starting transfers between devices  65.2 us (33%)
  waiting for transfers between devices  44 us (22%)
  Pallas kernels  42.4 us (22%)
  local copies, waits for them, and re-layouts  15.7 us (8%)
  between operations  15.3 us (8%)
  other arithmetic  6.26 us (3%)
  matrix products  5.81 us (3%)
    ppermute x32, waiting for transfers between devices, ring_exchange(): return lax.ppermute(block, RING, [(i, step(i)) for i in range(size)])  38.1 us
    ppermute x32, starting transfers between devices, ring_exchange(): return lax.ppermute(block, RING, [(i, step(i)) for i in range(size)])  37.1 us
    pallas_call x3, Pallas kernels, run_section(): pl.pallas_call(partial(section_kernel, layout, forward, backward, len(aft...  26.1 us
    ppermute x11, starting transfers between devices, pair_swap(): return lax.ppermute(block, axis, [(0, 1), (1, 0)])  18.3 us
    pallas_call x13, Pallas kernels, in_memory(): pl.pallas_call(body, out_shape=shapes, in_specs=specs, out_specs=[pl.Bloc...  16.3 us
    unnamed x60, local copies, waits for them, and re-layouts  10.4 us
    ppermute x11, waiting for transfers between devices, pair_swap(): return lax.ppermute(block, axis, [(0, 1), (1, 0)])  5.87 us
    all_to_all x1, starting transfers between devices, per_device(): lax.all_to_all(products[:, None], ('section', 'dp', 'seq'), 0, 0, tiled=T...  5.03 us
  transfers between devices with their start and end apart: 46, of which 14 were waited for; matrix products, arithmetic and copies ran while one was open for 10% of the time, Pallas kernels for 21%

profile of v5, /device:TPU:9, one launch (start us, length us, event | category | flops | bytes accessed | tf_op | source)
XLA Modules:
  0.0 194.7 jit_solution(17751215410447113403)
XLA Ops:
  7.2 1.7 shard_map.178
  13.9 5.0 %all-to-all-start = ((f32[32,1,2640]{2,1,0:T(1,128)}), f32[32,1,2640]{2,1,0:T(1,128)S(1)}, u32[]{:S(2)}, u32[]{:S(2)}) async-start(f32[32,1,2640]{2,1,0:T(1,128)} %copy.22), calls=%async_computation | async-start | bytes 688128 | tf_op jit(solution)/shard_map/all_to_all | solution.py:738
  22.8 10.9 %collective-permute-done.2.refs_2_ = bf16[24,2304]{1,0:T(8,128)(2,1)S(1)} collective-permute-done((bf16[24,2304]{1,0:T(8,128)(2,1)S(1)}, bf16[24,2304]{1,0:T(8,128)(2,1)S(1)}, u32[]{:S(2)}, u32[]{:S(2)}) %collective-permute-start.2) | collective-permute-done | bytes 110624 | tf_op jit(solution)/shard_map/ppermute | solution.py:527
  33.7 2.4 %collective-permute-done.3.refs_3_ = bf16[24,2304]{1,0:T(8,128)(2,1)S(1)} collective-permute-done((bf16[24,2304]{1,0:T(8,128)(2,1)S(1)}, bf16[24,2304]{1,0:T(8,128)(2,1)S(1)}, u32[]{:S(2)}, u32[]{:S(2)}) %collective-permute-start.3) | collective-permute-done | bytes 110624 | tf_op jit(solution)/shard_map/ppermute | solution.py:527
  36.1 1.8 collective-permute-done.4.refs_4_
  47.4 3.7 %collective-permute-done.14.refs_4_ = bf16[24,2304]{1,0:T(8,128)(2,1)S(1)} collective-permute-done((bf16[24,2304]{1,0:T(8,128)(2,1)S(1)}, bf16[24,2304]{1,0:T(8,128)(2,1)S(1)}, u32[]{:S(2)}, u32[]{:S(2)}) %collective-permute-start.14) | collective-permute-done | bytes 110624 | tf_op jit(solution)/shard_map/ppermute | solution.py:527
  52.3 2.1 %collective-permute-start.19 = (bf16[4,24,1152]{2,1,0:T(8,128)(2,1)S(1)}, bf16[4,24,1152]{2,1,0:T(8,128)(2,1)S(1)}, u32[]{:S(2)}, u32[]{:S(2)}) collective-permute-start(bf16[4,24,1152]{2,1,0:T(8,128)(2,1)S(1)} %get-tuple-element.74.refs_5_), channel_id=1, source_target_pairs={{0,1},{1,0},{2,3},{3,2},{4,5},{5,4},{6,7},{7,6},{8,9},{9,8},{10,11... | collective-permute-start | bytes 663560 | tf_op jit(solution)/shard_map/ppermute | solution.py:527
  56.6 2.8 %collective-permute-done.15.refs_2_ = bf16[4,24,1152]{2,1,0:T(8,128)(2,1)S(1)} collective-permute-done((bf16[4,24,1152]{2,1,0:T(8,128)(2,1)S(1)}, bf16[4,24,1152]{2,1,0:T(8,128)(2,1)S(1)}, u32[]{:S(2)}, u32[]{:S(2)}) %collective-permute-start.15) | collective-permute-done | bytes 221216 | tf_op jit(solution)/shard_map/ppermute | solution.py:527
  67.8 5.4 %collective-permute-start.11 = (bf16[384,2304]{1,0:T(8,128)(2,1)S(1)}, bf16[384,2304]{1,0:T(8,128)(2,1)}, u32[]{:S(2)}, u32[]{:S(2)}) collective-permute-start(bf16[384,2304]{1,0:T(8,128)(2,1)S(1)} %bitcast.66), channel_id=1, source_target_pairs={{0,16},{16,0},{1,17},{17,1},{2,18},{18,2},{3,19},{19,3},{4,20},{20... | collective-permute-start | bytes 5308424 | tf_op jit(solution)/shard_map/ppermute | solution.py:523
  73.2 2.1 %shard_map.183 = bf16[4,2,2,24,2304]{4,3,2,1,0:T(8,128)(2,1)} custom-call(s32[3]{0:T(128)S(1)} %pad_add_fusion.refs_0_, bf16[4,24,1152]{2,1,0:T(8,128)(2,1)S(1)} %get-tuple-element.73.refs_1_, bf16[4,24,1152]{2,1,0:T(8,128)(2,1)S(1)} %collective-permute-done.15.refs_2_, bf16[4,24,1152]{2,1,0:T(8,128)(2,1)S(1)} %collective-permute-done.16.refs_3_, ...), custom_call_target="tpu_custom_call" | custom-call | bytes 5308416 | tf_op jit(solution)/shard_map/pallas_call | solution.py:511
  75.3 1.8 collective-permute-start.21
  78.6 5.6 %shard_map.181 = (bf16[256,384]{1,0:T(8,128)(2,1)S(1)}, f32[1,2304]{1,0:T(1,128)S(1)}, bf16[256,1152]{1,0:T(8,128)(2,1)S(1)}, bf16[256,384]{1,0:T(8,128)(2,1)S(1...) custom-call(s32[1]{0:T(128)} %bitcast.refs_0_, ...), custom_call_target="tpu_custom_call" | custom-call | flops 1006632960 | bytes 5308416 | tf_op jit(solution)/shard_map/pallas_call | solution.py:352
  84.2 12.9 %shard_map.184 = (bf16[256,384]{1,0:T(8,128)(2,1)S(1)}, bf16[256,384]{1,0:T(8,128)(2,1)S(1)}, f32[1,2304]{1,0:T(1,128)S(1)}, f32[16,336]{1,0:T(8,128)S(1)}, bf16...) custom-call(s32[1]{0:T(128)} %bitcast.refs_0_, bf16[256,384]{1,0:T(8,128)(2,1)S(1)} %get-tuple-element.71.refs_1_, ...), custom_call_target="tpu_custom_call" | custom-call | flops 3019898880 | bytes 10616832 | tf_op jit(solution)/shard_map/pallas_call | solution.py:352
  98.5 7.6 %shard_map.185 = (bf16[256,384]{1,0:T(8,128)(2,1)S(1)}, f32[1,2304]{1,0:T(1,128)S(1)}, f32[16,336]{1,0:T(8,128)S(1)}, bf16[384,2304]{1,0:T(8,128)(2,1)S(1)}, bf16[384,2304]{1,0:T(8,128)(2,1)}) custom-call(s32[1]{0:T(128)} %bitcast.refs_0_, bf16[256,384]{1,0:T(8,128)(2,1)S(1)} %get-tuple-element.150.refs_1_, f32[1,2304]{1,0:T(1,128)S(1)} %get-tuple-element.77.refs_2_, ...), custom_call_target="tpu_custom_call" | custom-call | flops 2013265920 | bytes 10616832 | tf_op jit(solution)/shard_map/pallas_call | solution.py:352
  111.0 4.7 %all-to-all-start.1 = ((f32[32,1,2640]{2,1,0:T(1,128)}), f32[32,1,2640]{2,1,0:T(1,128)}, u32[]{:S(2)}, u32[]{:S(2)}) async-start(f32[32,1,2640]{2,1,0:T(1,128)} %broadcast_in_dim.58), calls=%async_computation.1 | async-start | bytes 688128 | tf_op jit(solution)/shard_map/all_to_all | solution.py:860
  117.0 5.8 %collective-permute-done.23 = bf16[1,1,128,384]{3,2,1,0:T(8,128)(2,1)S(1)} collective-permute-done((bf16[1,1,128,384]{3,2,1,0:T(8,128)(2,1)S(1)}, bf16[1,1,128,384]{3,2,1,0:T(8,128)(2,1)S(1)}, u32[]{:S(2)}, u32[]{:S(2)}) %collective-permute-start.23) | collective-permute-done | bytes 98336 | tf_op jit(solution)/shard_map/ppermute | solution.py:523
  124.1 2.8 %shard_map.186 = (bf16[4,2,24,1152]{3,2,1,0:T(8,128)(2,1)S(1)}, bf16[4,2,24,1152]{3,2,1,0:T(8,128)(2,1)}, bf16[4,2,24,1152]{3,2,1,0:T(8,128)(2,1)S(1)}, bf16[4,2,24,1152]{3,2,1,0:T(8,128)(2,1)}) custom-call(s32[3]{0:T(128)S(1)} %pad_add_fusion.refs_0_, bf16[16,24,2304]{2,1,0:T(8,128)(2,1)S(1)} %bitcast.73, bf16[16,24,2304]{2,1,0:T(8,128)(2,1)} %bitcast.34.refs_2_), custom_call_target="tpu_custom_call" | custom-call | bytes 5308416 | tf_op jit(solution)/shard_map/pallas_call | solution.py:511
  130.4 2.7 %shard_map.187 = (bf16[4,2,24,1152]{3,2,1,0:T(8,128)(2,1)S(1)}, bf16[4,2,24,1152]{3,2,1,0:T(8,128)(2,1)}, bf16[4,2,24,1152]{3,2,1,0:T(8,128)(2,1)S(1)}, bf16[4,2,24,1152]{3,2,1,0:T(8,128)(2,1)}) custom-call(s32[3]{0:T(128)S(1)} %pad_add_fusion.refs_0_, bf16[16,24,2304]{2,1,0:T(8,128)(2,1)S(1)} %bitcast.72, bf16[16,24,2304]{2,1,0:T(8,128)(2,1)} %bitcast.32.refs_2_, ...), custom_call_target="tpu_custom_call" | custom-call | bytes 5308416 | tf_op jit(solution)/shard_map/pallas_call | solution.py:511
  136.4 1.9 collective-permute-start.24
  138.3 1.7 copy.28
  140.0 2.2 %fusion = f32[32,384]{1,0:T(8,128)S(1)} fusion(bf16[1,384,2304]{2,1,0:T(8,128)(2,1)} %all-gather.3.cloned.1.call-done, f32[32,2640]{1,0:T(8,128)} %bitcast.76), kind=kOutput, calls=%fused_computation.1 | convolution fusion | flops 56623104 | bytes 1966080 | tf_op jit(solution)/shard_map/dot_general | solution.py:24
  147.3 1.9 collective-permute-done.29.refs_4_
  150.5 2.4 %collective-permute-start.30 = (bf16[4,24,1152]{2,1,0:T(8,128)(2,1)S(1)}, bf16[4,24,1152]{2,1,0:T(8,128)(2,1)S(1)}, u32[]{:S(2)}, u32[]{:S(2)}) collective-permute-start(bf16[4,24,1152]{2,1,0:T(8,128)(2,1)S(1)} %get-tuple-element.101), channel_id=1, source_target_pairs={{0,1},{1,0},{2,3},{3,2},{4,5},{5,4},{6,7},{7,6},{8,9},{9,8},{10,11... | collective-permute-start | bytes 663560 | tf_op jit(solution)/shard_map/ppermute | solution.py:527
  155.0 3.4 %collective-permute-start.25 = (f32[32,384]{1,0:T(8,128)S(1)}, f32[32,384]{1,0:T(8,128)S(1)}, u32[]{:S(2)}, u32[]{:S(2)}) collective-permute-start(f32[32,384]{1,0:T(8,128)S(1)} %fusion), channel_id=1, source_target_pairs={{0,16},{16,0},{1,17},{17,1},{2,18},{18,2},{3,19},{19,3},{4,20},{20... | collective-permute-start | bytes 147464 | tf_op jit(solution)/shard_map/ppermute | solution.py:523
  159.0 1.9 collective-permute-start.39
  160.9 3.9 %collective-permute-start.40 = (bf16[24,2304]{1,0:T(8,128)(2,1)S(1)}, bf16[24,2304]{1,0:T(8,128)(2,1)S(1)}, u32[]{:S(2)}, u32[]{:S(2)}) collective-permute-start(bf16[24,2304]{1,0:T(8,128)(2,1)S(1)} %get-tuple-element.117), channel_id=1, source_target_pairs={{0,8},{1,9},{2,10},{3,11},{4,12},{5,13},{6,14},{7,15},{8,0},{9,1},... | collective-permute-start | bytes 331784 | tf_op jit(solution)/shard_map/ppermute | solution.py:527
  168.3 1.8 collective-permute-start.33
  170.1 2.1 %collective-permute-done.40.refs_7_ = bf16[24,2304]{1,0:T(8,128)(2,1)S(1)} collective-permute-done((bf16[24,2304]{1,0:T(8,128)(2,1)S(1)}, bf16[24,2304]{1,0:T(8,128)(2,1)S(1)}, u32[]{:S(2)}, u32[]{:S(2)}) %collective-permute-start.40) | collective-permute-done | bytes 110624 | tf_op jit(solution)/shard_map/ppermute | solution.py:527
  174.3 4.8 %collective-permute-done.41.refs_8_ = bf16[24,2304]{1,0:T(8,128)(2,1)S(1)} collective-permute-done((bf16[24,2304]{1,0:T(8,128)(2,1)S(1)}, bf16[24,2304]{1,0:T(8,128)(2,1)S(1)}, u32[]{:S(2)}, u32[]{:S(2)}) %collective-permute-start.41) | collective-permute-done | bytes 110624 | tf_op jit(solution)/shard_map/ppermute | solution.py:527
  179.1 2.6 %collective-permute-done.33.refs_3_ = bf16[24,2304]{1,0:T(8,128)(2,1)S(1)} collective-permute-done((bf16[24,2304]{1,0:T(8,128)(2,1)S(1)}, bf16[24,2304]{1,0:T(8,128)(2,1)S(1)}, u32[]{:S(2)}, u32[]{:S(2)}) %collective-permute-start.33) | collective-permute-done | bytes 110624 | tf_op jit(solution)/shard_map/ppermute | solution.py:527
  181.7 2.1 %collective-permute-done.34.refs_4_ = bf16[24,2304]{1,0:T(8,128)(2,1)S(1)} collective-permute-done((bf16[24,2304]{1,0:T(8,128)(2,1)S(1)}, bf16[24,2304]{1,0:T(8,128)(2,1)S(1)}, u32[]{:S(2)}, u32[]{:S(2)}) %collective-permute-start.34) | collective-permute-done | bytes 110624 | tf_op jit(solution)/shard_map/ppermute | solution.py:527
  184.8 2.2 %fusion.8 = f32[1000,384]{1,0:T(8,128)} fusion(s32[32]{0:T(128)S(1)} %eq.25, f32[32,384]{1,0:T(8,128)S(1)} %get-tuple-element.162, f32[32,384]{1,0:T(8,128)S(1)} %fusion, f32[32,384]{1,0:T(8,128)S(1)} %collective-permute-done.25), kind=kOutput, calls=%fused_computation.33 | convolution fusion | flops 147610880 | bytes 1683584 | tf_op jit(solution)/shard_map/dot_general | solution.py:868
  (178 shorter events, 62.5 us)
Async XLA Ops:
  10.8 32.0 %collective-permute-start = (bf16[2,128,384]{2,1,0:T(8,128)(2,1)S(1)}, bf16[2,128,384]{2,1,0:T(8,128)(2,1)S(1)}, u32[]{:S(2)}, u32[]{:S(2)}) collective-permute-start(bf16[2,128,384]{2,1,0:T(8,128)(2,1)S(1)} %get-tuple-element.152), channel_id=1, source_target_pairs={{0,1},{1,0},{2,3},{3,2},{4,5},{5,4},{6,7},{7,6},{8,9},{9,8},{10,11... | collective-permute-start | bytes 589832 | tf_op jit(solution)/shard_map/ppermute | solution.py:523
  13.9 31.8 %all-to-all-start = ((f32[32,1,2640]{2,1,0:T(1,128)}), f32[32,1,2640]{2,1,0:T(1,128)S(1)}, u32[]{:S(2)}, u32[]{:S(2)}) async-start(f32[32,1,2640]{2,1,0:T(1,128)} %copy.22), calls=%async_computation | async-start | bytes 688128 | tf_op jit(solution)/shard_map/all_to_all | solution.py:738
  18.9 121.1 %all-gather.3.cloned.1.call-start = ((), (), s32[]{:S(2)}) async-start(), calls=%async_computation.2 | async-start | bytes 1880064 | tf_op jit(solution)/shard_map/all_gather | solution.py:762
  19.0 14.7 %collective-permute-start.2 = (bf16[24,2304]{1,0:T(8,128)(2,1)S(1)}, bf16[24,2304]{1,0:T(8,128)(2,1)S(1)}, u32[]{:S(2)}, u32[]{:S(2)}) collective-permute-start(bf16[24,2304]{1,0:T(8,128)(2,1)S(1)} %get-tuple-element.156.refs_1_), channel_id=1, source_target_pairs={{0,4},{1,5},{2,6},{3,7},{4,8},{5,9},{6,10},{7,11},{8,12},{9,13},{1... | collective-permute-start | bytes 331784 | tf_op jit(solution)/shard_map/ppermute | solution.py:527
  20.3 15.8 %collective-permute-start.3 = (bf16[24,2304]{1,0:T(8,128)(2,1)S(1)}, bf16[24,2304]{1,0:T(8,128)(2,1)S(1)}, u32[]{:S(2)}, u32[]{:S(2)}) collective-permute-start(bf16[24,2304]{1,0:T(8,128)(2,1)S(1)} %get-tuple-element.156.refs_1_), channel_id=1, source_target_pairs={{0,8},{1,9},{2,10},{3,11},{4,12},{5,13},{6,14},{7,15},{8,0},{9,1},... | collective-permute-start | bytes 331784 | tf_op jit(solution)/shard_map/ppermute | solution.py:527
  21.3 16.5 %collective-permute-start.4 = (bf16[24,2304]{1,0:T(8,128)(2,1)S(1)}, bf16[24,2304]{1,0:T(8,128)(2,1)S(1)}, u32[]{:S(2)}, u32[]{:S(2)}) collective-permute-start(bf16[24,2304]{1,0:T(8,128)(2,1)S(1)} %get-tuple-element.156.refs_1_), channel_id=1, source_target_pairs={{0,12},{1,13},{2,14},{3,15},{4,0},{5,1},{6,2},{7,3},{8,4},{9,5},{1... | collective-permute-start | bytes 331784 | tf_op jit(solution)/shard_map/ppermute | solution.py:527
  40.2 10.9 %collective-permute-start.5 = (bf16[4,24,1152]{2,1,0:T(8,128)(2,1)S(1)}, bf16[4,24,1152]{2,1,0:T(8,128)(2,1)S(1)}, u32[]{:S(2)}, u32[]{:S(2)}) collective-permute-start(bf16[4,24,1152]{2,1,0:T(8,128)(2,1)S(1)} %get-tuple-element.69.refs_1_), channel_id=1, source_target_pairs={{0,2},{1,3},{2,0},{3,1},{4,6},{5,7},{6,4},{7,5},{8,10},{9,11},{10,... | collective-permute-start | bytes 663560 | tf_op jit(solution)/shard_map/ppermute | solution.py:527
  46.3 10.3 %collective-permute-start.10 = (bf16[4,24,1152]{2,1,0:T(8,128)(2,1)S(1)}, bf16[4,24,1152]{2,1,0:T(8,128)(2,1)S(1)}, u32[]{:S(2)}, u32[]{:S(2)}) collective-permute-start(bf16[4,24,1152]{2,1,0:T(8,128)(2,1)S(1)} %collective-permute-done.9.refs_7_.refs_8_), channel_id=1, source_target_pairs={{0,2},{1,3},{2,0},{3,1},{4,6},{5,7},{6,4},{7,5},{8,10},{9,11},{10,... | collective-permute-start | bytes 663560 | tf_op jit(solution)/shard_map/ppermute | solution.py:527
  55.1 18.1 %collective-permute-start.16 = (bf16[4,24,1152]{2,1,0:T(8,128)(2,1)S(1)}, bf16[4,24,1152]{2,1,0:T(8,128)(2,1)S(1)}, u32[]{:S(2)}, u32[]{:S(2)}) collective-permute-start(bf16[4,24,1152]{2,1,0:T(8,128)(2,1)S(1)} %get-tuple-element.73.refs_1_), channel_id=1, source_target_pairs={{0,1},{1,0},{2,3},{3,2},{4,5},{5,4},{6,7},{7,6},{8,9},{9,8},{10,11... | collective-permute-start | bytes 663560 | tf_op jit(solution)/shard_map/ppermute | solution.py:527
  56.5 16.7 %collective-permute-start.18 = (bf16[4,24,1152]{2,1,0:T(8,128)(2,1)S(1)}, bf16[4,24,1152]{2,1,0:T(8,128)(2,1)S(1)}, u32[]{:S(2)}, u32[]{:S(2)}) collective-permute-start(bf16[4,24,1152]{2,1,0:T(8,128)(2,1)S(1)} %get-tuple-element.74.refs_5_), channel_id=1, source_target_pairs={{0,2},{1,3},{2,0},{3,1},{4,6},{5,7},{6,4},{7,5},{8,10},{9,11},{10,... | collective-permute-start | bytes 663560 | tf_op jit(solution)/shard_map/ppermute | solution.py:527
  59.4 13.8 %collective-permute-start.17 = (bf16[4,24,1152]{2,1,0:T(8,128)(2,1)S(1)}, bf16[4,24,1152]{2,1,0:T(8,128)(2,1)S(1)}, u32[]{:S(2)}, u32[]{:S(2)}) collective-permute-start(bf16[4,24,1152]{2,1,0:T(8,128)(2,1)S(1)} %collective-permute-done.15.refs_2_), channel_id=1, source_target_pairs={{0,1},{1,0},{2,3},{3,2},{4,5},{5,4},{6,7},{7,6},{8,9},{9,8},{10,11... | collective-permute-start | bytes 663560 | tf_op jit(solution)/shard_map/ppermute | solution.py:527
  60.4 12.8 %collective-permute-start.20 = (bf16[4,24,1152]{2,1,0:T(8,128)(2,1)S(1)}, bf16[4,24,1152]{2,1,0:T(8,128)(2,1)S(1)}, u32[]{:S(2)}, u32[]{:S(2)}) collective-permute-start(bf16[4,24,1152]{2,1,0:T(8,128)(2,1)S(1)} %collective-permute-done.19.refs_7_), channel_id=1, source_target_pairs={{0,2},{1,3},{2,0},{3,1},{4,6},{5,7},{6,4},{7,5},{8,10},{9,11},{10,... | collective-permute-start | bytes 663560 | tf_op jit(solution)/shard_map/ppermute | solution.py:527
  67.8 10.8 %collective-permute-start.11 = (bf16[384,2304]{1,0:T(8,128)(2,1)S(1)}, bf16[384,2304]{1,0:T(8,128)(2,1)}, u32[]{:S(2)}, u32[]{:S(2)}) collective-permute-start(bf16[384,2304]{1,0:T(8,128)(2,1)S(1)} %bitcast.66), channel_id=1, source_target_pairs={{0,16},{16,0},{1,17},{17,1},{2,18},{18,2},{3,19},{19,3},{4,20},{20... | collective-permute-start | bytes 5308424 | tf_op jit(solution)/shard_map/ppermute | solution.py:523
  98.5 25.6 %collective-permute-start.27 = (bf16[384,2304]{1,0:T(8,128)(2,1)}, bf16[384,2304]{1,0:T(8,128)(2,1)}, u32[]{:S(2)}, u32[]{:S(2)}) collective-permute-start(bf16[384,2304]{1,0:T(8,128)(2,1)} %get-tuple-element.94), channel_id=1, source_target_pairs={{0,16},{16,0},{1,17},{17,1},{2,18},{18,2},{3,19},{19,3},{4,20},{20... | collective-permute-start | bytes 5308424 | tf_op jit(solution)/shard_map/ppermute | solution.py:523
  107.3 23.1 %collective-permute-start.26 = (bf16[384,2304]{1,0:T(8,128)(2,1)}, bf16[384,2304]{1,0:T(8,128)(2,1)}, u32[]{:S(2)}, u32[]{:S(2)}) collective-permute-start(bf16[384,2304]{1,0:T(8,128)(2,1)} %get-tuple-element.92), channel_id=1, source_target_pairs={{0,16},{16,0},{1,17},{17,1},{2,18},{18,2},{3,19},{19,3},{4,20},{20... | collective-permute-start | bytes 5308424 | tf_op jit(solution)/shard_map/ppermute | solution.py:523
  108.4 14.5 %collective-permute-start.22 = (bf16[3,1,128,384]{3,2,1,0:T(8,128)(2,1)}, bf16[3,1,128,384]{3,2,1,0:T(8,128)(2,1)S(1)}, u32[]{:S(2)}, u32[]{:S(2)}) collective-permute-start(bf16[3,1,128,384]{3,2,1,0:T(8,128)(2,1)} %get-tuple-element.148), channel_id=1, source_target_pairs={{0,1},{1,0},{2,3},{3,2},{4,5},{5,4},{6,7},{7,6},{8,9},{9,8},{10,11... | collective-permute-start | bytes 884744 | tf_op jit(solution)/shard_map/ppermute | solution.py:523
  111.0 27.3 %all-to-all-start.1 = ((f32[32,1,2640]{2,1,0:T(1,128)}), f32[32,1,2640]{2,1,0:T(1,128)}, u32[]{:S(2)}, u32[]{:S(2)}) async-start(f32[32,1,2640]{2,1,0:T(1,128)} %broadcast_in_dim.58), calls=%async_computation.1 | async-start | bytes 688128 | tf_op jit(solution)/shard_map/all_to_all | solution.py:860
  127.7 14.6 %collective-permute-start.35 = (bf16[4,2,24,1152]{3,2,1,0:T(8,128)(2,1)}, bf16[4,2,24,1152]{3,2,1,0:T(8,128)(2,1)S(1)}, u32[]{:S(2)}, u32[]{:S(2)}) collective-permute-start(bf16[4,2,24,1152]{3,2,1,0:T(8,128)(2,1)} %get-tuple-element.108), channel_id=1, source_target_pairs={{0,2},{1,3},{2,0},{3,1},{4,6},{5,7},{6,4},{7,5},{8,10},{9,11},{10,... | collective-permute-start | bytes 1327112 | tf_op jit(solution)/shard_map/ppermute | solution.py:527
  129.1 13.2 %collective-permute-start.36 = (bf16[4,2,24,1152]{3,2,1,0:T(8,128)(2,1)}, bf16[4,2,24,1152]{3,2,1,0:T(8,128)(2,1)S(1)}, u32[]{:S(2)}, u32[]{:S(2)}) collective-permute-start(bf16[4,2,24,1152]{3,2,1,0:T(8,128)(2,1)} %get-tuple-element.110), channel_id=1, source_target_pairs={{0,1},{1,0},{2,3},{3,2},{4,5},{5,4},{6,7},{7,6},{8,9},{9,8},{10,11... | collective-permute-start | bytes 1327112 | tf_op jit(solution)/shard_map/ppermute | solution.py:527
  133.9 13.4 %collective-permute-start.28 = (bf16[4,2,24,1152]{3,2,1,0:T(8,128)(2,1)}, bf16[4,2,24,1152]{3,2,1,0:T(8,128)(2,1)}, u32[]{:S(2)}, u32[]{:S(2)}) collective-permute-start(bf16[4,2,24,1152]{3,2,1,0:T(8,128)(2,1)} %get-tuple-element.97), channel_id=1, source_target_pairs={{0,2},{1,3},{2,0},{3,1},{4,6},{5,7},{6,4},{7,5},{8,10},{9,11},{10,... | collective-permute-start | bytes 1327112 | tf_op jit(solution)/shard_map/ppermute | solution.py:527
  135.4 13.8 %collective-permute-start.29 = (bf16[4,2,24,1152]{3,2,1,0:T(8,128)(2,1)}, bf16[4,2,24,1152]{3,2,1,0:T(8,128)(2,1)}, u32[]{:S(2)}, u32[]{:S(2)}) collective-permute-start(bf16[4,2,24,1152]{3,2,1,0:T(8,128)(2,1)} %get-tuple-element.99), channel_id=1, source_target_pairs={{0,1},{1,0},{2,3},{3,2},{4,5},{5,4},{6,7},{7,6},{8,9},{9,8},{10,11... | collective-permute-start | bytes 1327112 | tf_op jit(solution)/shard_map/ppermute | solution.py:527
  136.4 24.5 %collective-permute-start.24 = (bf16[2,2,128,384]{3,2,1,0:T(8,128)(2,1)}, bf16[2,2,128,384]{3,2,1,0:T(8,128)(2,1)}, u32[]{:S(2)}, u32[]{:S(2)}) collective-permute-start(bf16[2,2,128,384]{3,2,1,0:T(8,128)(2,1)} %get-tuple-element.144), channel_id=1, source_target_pairs={{0,16},{16,0},{1,17},{17,1},{2,18},{18,2},{3,19},{19,3},{4,20},{20... | collective-permute-start | bytes 1179656 | tf_op jit(solution)/shard_map/ppermute | solution.py:523
  143.1 11.8 %collective-permute-start.37 = (bf16[4,24,1152]{2,1,0:T(8,128)(2,1)S(1)}, bf16[4,24,1152]{2,1,0:T(8,128)(2,1)S(1)}, u32[]{:S(2)}, u32[]{:S(2)}) collective-permute-start(bf16[4,24,1152]{2,1,0:T(8,128)(2,1)S(1)} %get-tuple-element.112), channel_id=1, source_target_pairs={{0,1},{1,0},{2,3},{3,2},{4,5},{5,4},{6,7},{7,6},{8,9},{9,8},{10,11... | collective-permute-start | bytes 663560 | tf_op jit(solution)/shard_map/ppermute | solution.py:527
  144.3 14.1 %collective-permute-start.38 = (bf16[4,24,1152]{2,1,0:T(8,128)(2,1)S(1)}, bf16[4,24,1152]{2,1,0:T(8,128)(2,1)S(1)}, u32[]{:S(2)}, u32[]{:S(2)}) collective-permute-start(bf16[4,24,1152]{2,1,0:T(8,128)(2,1)S(1)} %get-tuple-element.114), channel_id=1, source_target_pairs={{0,2},{1,3},{2,0},{3,1},{4,6},{5,7},{6,4},{7,5},{8,10},{9,11},{10,... | collective-permute-start | bytes 663560 | tf_op jit(solution)/shard_map/ppermute | solution.py:527
  150.5 15.6 %collective-permute-start.30 = (bf16[4,24,1152]{2,1,0:T(8,128)(2,1)S(1)}, bf16[4,24,1152]{2,1,0:T(8,128)(2,1)S(1)}, u32[]{:S(2)}, u32[]{:S(2)}) collective-permute-start(bf16[4,24,1152]{2,1,0:T(8,128)(2,1)S(1)} %get-tuple-element.101), channel_id=1, source_target_pairs={{0,1},{1,0},{2,3},{3,2},{4,5},{5,4},{6,7},{7,6},{8,9},{9,8},{10,11... | collective-permute-start | bytes 663560 | tf_op jit(solution)/shard_map/ppermute | solution.py:527
  152.9 13.3 %collective-permute-start.31 = (bf16[4,24,1152]{2,1,0:T(8,128)(2,1)S(1)}, bf16[4,24,1152]{2,1,0:T(8,128)(2,1)S(1)}, u32[]{:S(2)}, u32[]{:S(2)}) collective-permute-start(bf16[4,24,1152]{2,1,0:T(8,128)(2,1)S(1)} %get-tuple-element.103), channel_id=1, source_target_pairs={{0,2},{1,3},{2,0},{3,1},{4,6},{5,7},{6,4},{7,5},{8,10},{9,11},{10,... | collective-permute-start | bytes 663560 | tf_op jit(solution)/shard_map/ppermute | solution.py:527
  155.0 29.9 %collective-permute-start.25 = (f32[32,384]{1,0:T(8,128)S(1)}, f32[32,384]{1,0:T(8,128)S(1)}, u32[]{:S(2)}, u32[]{:S(2)}) collective-permute-start(f32[32,384]{1,0:T(8,128)S(1)} %fusion), channel_id=1, source_target_pairs={{0,16},{16,0},{1,17},{17,1},{2,18},{18,2},{3,19},{19,3},{4,20},{20... | collective-permute-start | bytes 147464 | tf_op jit(solution)/shard_map/ppermute | solution.py:523
  160.9 11.3 %collective-permute-start.40 = (bf16[24,2304]{1,0:T(8,128)(2,1)S(1)}, bf16[24,2304]{1,0:T(8,128)(2,1)S(1)}, u32[]{:S(2)}, u32[]{:S(2)}) collective-permute-start(bf16[24,2304]{1,0:T(8,128)(2,1)S(1)} %get-tuple-element.117), channel_id=1, source_target_pairs={{0,8},{1,9},{2,10},{3,11},{4,12},{5,13},{6,14},{7,15},{8,0},{9,1},... | collective-permute-start | bytes 331784 | tf_op jit(solution)/shard_map/ppermute | solution.py:527
  166.1 13.0 %collective-permute-start.41 = (bf16[24,2304]{1,0:T(8,128)(2,1)S(1)}, bf16[24,2304]{1,0:T(8,128)(2,1)S(1)}, u32[]{:S(2)}, u32[]{:S(2)}) collective-permute-start(bf16[24,2304]{1,0:T(8,128)(2,1)S(1)} %get-tuple-element.118), channel_id=1, source_target_pairs={{0,12},{1,13},{2,14},{3,15},{4,0},{5,1},{6,2},{7,3},{8,4},{9,5},{1... | collective-permute-start | bytes 331784 | tf_op jit(solution)/shard_map/ppermute | solution.py:527
  166.8 12.2 %collective-permute-start.32 = (bf16[24,2304]{1,0:T(8,128)(2,1)S(1)}, bf16[24,2304]{1,0:T(8,128)(2,1)S(1)}, u32[]{:S(2)}, u32[]{:S(2)}) collective-permute-start(bf16[24,2304]{1,0:T(8,128)(2,1)S(1)} %get-tuple-element.105), channel_id=1, source_target_pairs={{0,4},{1,5},{2,6},{3,7},{4,8},{5,9},{6,10},{7,11},{8,12},{9,13},{1... | collective-permute-start | bytes 331784 | tf_op jit(solution)/shard_map/ppermute | solution.py:527
  168.3 13.3 %collective-permute-start.33 = (bf16[24,2304]{1,0:T(8,128)(2,1)S(1)}, bf16[24,2304]{1,0:T(8,128)(2,1)S(1)}, u32[]{:S(2)}, u32[]{:S(2)}) collective-permute-start(bf16[24,2304]{1,0:T(8,128)(2,1)S(1)} %get-tuple-element.106), channel_id=1, source_target_pairs={{0,8},{1,9},{2,10},{3,11},{4,12},{5,13},{6,14},{7,15},{8,0},{9,1},... | collective-permute-start | bytes 331784 | tf_op jit(solution)/shard_map/ppermute | solution.py:527
  172.2 11.6 %collective-permute-start.34 = (bf16[24,2304]{1,0:T(8,128)(2,1)S(1)}, bf16[24,2304]{1,0:T(8,128)(2,1)S(1)}, u32[]{:S(2)}, u32[]{:S(2)}) collective-permute-start(bf16[24,2304]{1,0:T(8,128)(2,1)S(1)} %get-tuple-element.107), channel_id=1, source_target_pairs={{0,12},{1,13},{2,14},{3,15},{4,0},{5,1},{6,2},{7,3},{8,4},{9,5},{1... | collective-permute-start | bytes 331784 | tf_op jit(solution)/shard_map/ppermute | solution.py:527
  (44 other events, 330.7 us)
Sparse Core Ops, SparseCore 0:
  77.3 59.6 all-gather.2

commit v6 on v5

--- a/solution.py
+++ b/solution.py
@@ -402,14 +402,15 @@
 
 def stack_kernel(high, split, place_ref, *refs):
     pieces, sems = refs[:high], refs[-1]
-    targets = refs[-1 - (2 if split else 1) : -1]
-    copies = []
-    if len(refs) > high + 1 + len(targets):
-        targets = refs[high + 1 : -1]
-        copies.append(pltpu.make_async_copy(refs[high], targets[-1], sems.at[high, 0]))
+    count = (len(refs) - high - 3) // 2
+    handed, targets = refs[high : high + count], refs[high + count : -1]
+    copies = [
+        pltpu.make_async_copy(former, latter, sems.at[high + i, 0])
+        for i, (former, latter) in enumerate(zip(handed, targets[2:]))
+    ]
     for turn, piece in enumerate(pieces):
         place = lax.rem(place_ref[0] + (high - turn), high)
-        parts = (piece.at[:, :split], piece.at[:, split:]) if split else (piece,)
+        parts = (piece.at[:, :split], piece.at[:, split:])
         for i, (part, target) in enumerate(zip(parts, targets)):
             copies.append(pltpu.make_async_copy(part, target.at[place], sems.at[turn, i]))
     copy_all(copies)
@@ -423,9 +424,7 @@
         other_x, other_y = (i % 4) & 1, (i % 4) >> 1
         row = x if not other_x else 1 - x
         column = y if not other_y else 1 - y
-        target = full_ref.at[:, row, column]
-        if split:
-            target = full_ref.at[:, row, column, :, pl.ds((i // 4) * split, split)]
+        target = full_ref.at[:, row, column, :, pl.ds((i // 4) * split, split)]
         copies.append(pltpu.make_async_copy(piece, target, sems.at[i]))
     copy_all(copies)
 
@@ -434,7 +433,11 @@
     return former.astype(jnp.float32) + latter.astype(jnp.float32)
 
 
-def chip_sum_kernel(high, place_ref, mine, got, first_keep, first_send, second_keep, second_send):
+def chip_sum_kernel(high, place_ref, mine, got, *refs):
+    count = (len(refs) - 4) // 2
+    first_keep, first_send, second_keep, second_send = refs[count : count + 4]
+    for former, latter in zip(refs[:count], refs[count + 4 :]):
+        latter[...] = former[...]
     x, y = place_ref[1], place_ref[2]
     half = mine.shape[2]
     lanes = half // 2
@@ -547,7 +550,7 @@
         [jax.ShapeDtypeStruct((high, rows, lanes // 2), shard.dtype)] * 2
         + [jax.ShapeDtypeStruct(block.shape, block.dtype) for block in handed],
         [place, *rotations(shard, size), *handed],
-        scratch=[pltpu.SemaphoreType.DMA((high + 1, 2))],
+        scratch=[pltpu.SemaphoreType.DMA((high + len(handed), 2))],
         after=after,
     )
 
@@ -569,11 +572,14 @@
     return full.reshape(size * rows, 2 * lanes)
 
 
-def scatter_first(mine, got, place, size, after=()):
+def scatter_first(mine, got, place, size, handed=(), after=()):
     rows, half = mine.shape[1:]
     shape = jax.ShapeDtypeStruct((size // 4, 2, rows, half // 2), jnp.bfloat16)
     return in_memory(
-        partial(chip_sum_kernel, size // 4), [shape] * 4, [place, mine, got], after=after
+        partial(chip_sum_kernel, size // 4),
+        [shape] * 4 + [jax.ShapeDtypeStruct(block.shape, block.dtype) for block in handed],
+        [place, mine, got, *handed],
+        after=after,
     )
 
 
@@ -732,7 +738,25 @@
     conditions = matmul(selector, cond_table)
     silu_all = jax.nn.silu(conditions).astype(jnp.bfloat16)
     silu_own = lax.dynamic_slice_in_dim(silu_all, ring_rank * rows, rows, 1)
-    products = matmul(silu_own, modulation_weight[0])
+    if compact:
+        *first_parts, second_shard, silu_late = gather_along_z(
+            first_shard, place, ring_size, handed=(second_shard, silu_own)
+        )
+        first_parts += first_flips(*first_parts, ring_size)
+        second_parts = gather_along_z(
+            second_shard, place, ring_size, after=(both, *first_parts[2:])
+        )
+        second_parts += first_flips(*second_parts, ring_size)
+        first_pack = gather_across(*first_parts, place, ring_size)
+        second_pack = gather_across(*second_parts, place, ring_size)
+    else:
+        silu_late = silu_own
+        first_pack = lax.all_gather(first_shard, RING, axis=0, tiled=True)
+        second_pack = lax.all_gather(second_shard, RING, axis=0, tiled=True)
+    first_halves = (first_pack, pair_swap(first_pack, "section"))
+    second_halves = (second_pack, pair_swap(second_pack, "section"))
+
+    products = matmul(silu_late, modulation_weight[0])
     own_bias = jnp.broadcast_to(biases.astype(jnp.float32), (products.shape[0], bias_count))
     products = jnp.repeat(jnp.concatenate([products, own_bias], axis=1), sharers, axis=0)
     products = lax.all_to_all(
@@ -743,23 +767,6 @@
     )
     first_bias, second_bias = products[0, :, 6 * width :], products[1, :, 6 * width :]
 
-    if compact:
-        *first_parts, second_shard = gather_along_z(
-            first_shard, place, ring_size, handed=(second_shard,)
-        )
-        first_parts += first_flips(*first_parts, ring_size)
-        second_parts = gather_along_z(
-            second_shard, place, ring_size, after=(products, both, *first_parts[2:])
-        )
-        second_parts += first_flips(*second_parts, ring_size)
-        first_pack = gather_across(*first_parts, place, ring_size)
-        second_pack = gather_across(*second_parts, place, ring_size)
-    else:
-        first_pack = lax.all_gather(first_shard, RING, axis=0, tiled=True)
-        second_pack = lax.all_gather(second_shard, RING, axis=0, tiled=True)
-    first_halves = (first_pack, pair_swap(first_pack, "section"))
-    second_halves = (second_pack, pair_swap(second_pack, "section"))
-    own_matrix = lax.all_gather(modulation_weight[0], RING, axis=0, tiled=True)
 
     first_low, *first_saved = run_section(
         layout, rank, first_input, first_halves, (first_modulation, first_bias)
@@ -787,6 +794,37 @@
     )
     first_got = pair_swap(first_send, "section")
 
+    shard = jax.ShapeDtypeStruct((rows, half), jnp.float32)
+    if compact:
+        second_sorted = scatter_first(
+            ring_terms(second_keep),
+            ring_terms(second_got),
+            place,
+            ring_size,
+            after=(early[1],),
+        )
+        second_received = scatter_flips(second_sorted, ring_size)
+        second_turned = scatter_second(second_received, place, ring_size)
+        *first_sorted, first_grad, first_dmod, first_sums = scatter_first(
+            ring_terms(first_keep),
+            ring_terms(first_got),
+            place,
+            ring_size,
+            handed=(first_grad, first_dmod, first_sums),
+            after=(second_sorted[0],),
+        )
+        first_turned = scatter_second(scatter_flips(first_sorted, ring_size), place, ring_size)
+        second_pieces = scatter_rest(second_turned, place, ring_size)
+        first_pieces = scatter_rest(first_turned, place, ring_size)
+    else:
+
+        def chip_sum(keep, got):
+            return ring_terms(low(added(keep, got)))
+
+        first_pieces, second_pieces = [
+            [scatter_sum(chip_sum(keep, got), ring_rank, ring_size)]
+            for keep, got in ((first_keep, first_got), (second_keep, second_got))
+        ]
     if compact:
         early_full, late = side_by_side(*early, 1), side_by_side(*to_slots(first_grad), 1)
         per_first = jnp.stack([early_full[0], late[0]])
@@ -804,32 +842,6 @@
     activations = outputs[0]
     input_grads = outputs[1].astype(jnp.float32)
 
-    shard = jax.ShapeDtypeStruct((rows, half), jnp.float32)
-    if compact:
-        second_sorted = scatter_first(
-            ring_terms(second_keep), ring_terms(second_got), place, ring_size
-        )
-        second_received = scatter_flips(second_sorted, ring_size)
-        second_turned = scatter_second(second_received, place, ring_size, (early[1],))
-        first_sorted = scatter_first(
-            ring_terms(first_keep),
-            ring_terms(first_got),
-            place,
-            ring_size,
-            (second_sorted[0],),
-        )
-        first_turned = scatter_second(scatter_flips(first_sorted, ring_size), place, ring_size)
-        second_pieces = scatter_rest(second_turned, place, ring_size)
-        first_pieces = scatter_rest(first_turned, place, ring_size)
-    else:
-
-        def chip_sum(keep, got):
-            return ring_terms(low(added(keep, got)))
-
-        first_pieces, second_pieces = [
-            [scatter_sum(chip_sum(keep, got), ring_rank, ring_size)]
-            for keep, got in ((first_keep, first_got), (second_keep, second_got))
-        ]
     mine, send = in_memory(
         partial(close_kernel, len(first_pieces)),
         [shard, shard],
@@ -862,8 +874,11 @@
     bias_grad = jnp.sum(every[:, 6 * width :], axis=0)
     modulation_rows = low(every[:, : 6 * width])
     modulation_grad = outer_sum(silu_own, modulation_rows)
-    products_back = matmul_transposed(modulation_rows, own_matrix)
-    products_back = products_back + pair_swap(products_back, "section")
+    columns = matmul_transposed(modulation_rows, modulation_weight[0])
+    columns = jnp.broadcast_to(columns.reshape(1, 1, -1), (sections * ring_size, 1, columns.size))
+    columns = lax.all_to_all(columns, ("section", "dp", "seq"), 0, 0, tiled=True)
+    columns = jnp.sum(columns.reshape(sections, ring_size, -1, rows), axis=0)
+    products_back = jnp.swapaxes(columns, 0, 1).reshape(-1, width)
     _, silu_back = jax.vjp(jax.nn.silu, conditions)
     table_grad = lax.dot_general(
         selector.astype(jnp.float32),

time: 196 us -> 186 us (0.949)
  waiting for transfers between devices: 44 us -> 60.6 us
  between operations: 15.3 us -> 1.95 us
  starting transfers between devices: 65.2 us -> 55.5 us
  matrix products: 5.81 us -> 3.71 us
    ppermute x32, waiting for transfers between devices: 38.1 us -> 48.5 us  [ring_exchange(): return lax.ppermute(block, RING, [(i, step(i)) for i in range(size)])]
    ppermute x32, starting transfers between devices: 37.1 us -> 27.2 us  [ring_exchange(): return lax.ppermute(block, RING, [(i, step(i)) for i in range(size)])]
    all_to_all x0 -> x1, starting transfers between devices: none -> 8.06 us  [per_device(): lax.all_to_all(columns, ('section', 'dp', 'seq'), 0, 0, tiled=True)]
    ppermute x11 -> x10, starting transfers between devices: 18.3 us -> 10.7 us  [pair_swap(): return lax.ppermute(block, axis, [(0, 1), (1, 0)])]
    all_to_all x1, waiting for transfers between devices: 0.01 us -> 5.31 us  [per_device(): lax.all_to_all(products[:, None], ('section', 'dp', 'seq'), 0, 0, tiled=T...]
    unnamed x60 -> x64, local copies, waits for them, and re-layouts: 10.4 us -> 7.39 us
    dot_general x1, matrix products: 2.24 us -> 0.15 us  [matmul_transposed(): lax.dot_general(former, latter, (((1,), (1,)), ((), ())), preferred_eleme...]
    select_n x3, other arithmetic: 2.3 us -> 0.25 us  [side_by_side(): jnp.where(seq_rank == 0, jnp.concatenate([mine, got], axis=axis), jnp.con...]
  transfers between devices with their start and end apart: 46 -> 45, of which waited for: 14 -> 15; matrix products, arithmetic and copies ran while one was open for 10% -> 10% of each run, Pallas kernels for 21% -> 14%
where the time goes in v6:
time: 186 us; the launch traced here: 185 us
  waiting for transfers between devices  60.6 us (33%)
  starting transfers between devices  55.5 us (30%)
  Pallas kernels  43.4 us (23%)
  local copies, waits for them, and re-layouts  14.1 us (8%)
  other arithmetic  5.83 us (3%)
  matrix products  3.71 us (2%)
  between operations  1.95 us (1%)
    ppermute x32, waiting for transfers between devices, ring_exchange(): return lax.ppermute(block, RING, [(i, step(i)) for i in range(size)])  48.5 us
    ppermute x32, starting transfers between devices, ring_exchange(): return lax.ppermute(block, RING, [(i, step(i)) for i in range(size)])  27.2 us
    pallas_call x3, Pallas kernels, run_section(): pl.pallas_call(partial(section_kernel, layout, forward, backward, len(aft...  26.1 us
    pallas_call x13, Pallas kernels, in_memory(): pl.pallas_call(body, out_shape=shapes, in_specs=specs, out_specs=[pl.Bloc...  17.3 us
    ppermute x10, starting transfers between devices, pair_swap(): return lax.ppermute(block, axis, [(0, 1), (1, 0)])  10.7 us
    all_to_all x1, starting transfers between devices, per_device(): lax.all_to_all(columns, ('section', 'dp', 'seq'), 0, 0, tiled=True)  8.06 us
    unnamed x64, local copies, waits for them, and re-layouts  7.39 us
    ppermute x10, waiting for transfers between devices, pair_swap(): return lax.ppermute(block, axis, [(0, 1), (1, 0)])  6.75 us
  transfers between devices with their start and end apart: 45, of which 15 were waited for; matrix products, arithmetic and copies ran while one was open for 10% of the time, Pallas kernels for 14%

profile of v6, /device:TPU:9, one launch (start us, length us, event | category | flops | bytes accessed | tf_op | source)
XLA Modules:
  0.0 185.1 jit_solution(15240829308511113628)
XLA Ops:
  0.7 1.7 shard_map.178
  6.1 1.3 collective-permute-start.2
  8.5 1.4 collective-permute-start.4
  10.5 6.2 %collective-permute-done.3.refs_3_ = bf16[24,2304]{1,0:T(8,128)(2,1)S(1)} collective-permute-done((bf16[24,2304]{1,0:T(8,128)(2,1)S(1)}, bf16[24,2304]{1,0:T(8,128)(2,1)S(1)}, u32[]{:S(2)}, u32[]{:S(2)}) %collective-permute-start.3) | collective-permute-done | bytes 110624 | tf_op jit(solution)/shard_map/ppermute | solution.py:530
  16.7 2.4 %collective-permute-done.4.refs_4_ = bf16[24,2304]{1,0:T(8,128)(2,1)S(1)} collective-permute-done((bf16[24,2304]{1,0:T(8,128)(2,1)S(1)}, bf16[24,2304]{1,0:T(8,128)(2,1)S(1)}, u32[]{:S(2)}, u32[]{:S(2)}) %collective-permute-start.4) | collective-permute-done | bytes 110624 | tf_op jit(solution)/shard_map/ppermute | solution.py:530
  23.8 2.9 %collective-permute-done.12.refs_2_ = bf16[24,2304]{1,0:T(8,128)(2,1)S(1)} collective-permute-done((bf16[24,2304]{1,0:T(8,128)(2,1)S(1)}, bf16[24,2304]{1,0:T(8,128)(2,1)S(1)}, u32[]{:S(2)}, u32[]{:S(2)}) %collective-permute-start.12) | collective-permute-done | bytes 110624 | tf_op jit(solution)/shard_map/ppermute | solution.py:530
  28.7 5.9 %collective-permute-done.14.refs_4_ = bf16[24,2304]{1,0:T(8,128)(2,1)S(1)} collective-permute-done((bf16[24,2304]{1,0:T(8,128)(2,1)S(1)}, bf16[24,2304]{1,0:T(8,128)(2,1)S(1)}, u32[]{:S(2)}, u32[]{:S(2)}) %collective-permute-start.14) | collective-permute-done | bytes 110624 | tf_op jit(solution)/shard_map/ppermute | solution.py:530
  38.9 7.7 %collective-permute-done.10.refs_8_ = bf16[4,24,1152]{2,1,0:T(8,128)(2,1)S(1)} collective-permute-done((bf16[4,24,1152]{2,1,0:T(8,128)(2,1)S(1)}, bf16[4,24,1152]{2,1,0:T(8,128)(2,1)S(1)}, u32[]{:S(2)}, u32[]{:S(2)}) %collective-permute-start.10) | collective-permute-done | bytes 221216 | tf_op jit(solution)/shard_map/ppermute | solution.py:530
  47.7 3.0 %collective-permute-start.11 = (bf16[384,2304]{1,0:T(8,128)(2,1)S(1)}, bf16[384,2304]{1,0:T(8,128)(2,1)}, u32[]{:S(2)}, u32[]{:S(2)}) collective-permute-start(bf16[384,2304]{1,0:T(8,128)(2,1)S(1)} %bitcast.66), channel_id=1, source_target_pairs={{0,16},{16,0},{1,17},{17,1},{2,18},{18,2},{3,19},{19,3},{4,20},{20... | collective-permute-start | bytes 5308424 | tf_op jit(solution)/shard_map/ppermute | solution.py:526
  53.2 5.1 %all-to-all-start = ((f32[32,1,2640]{2,1,0:T(1,128)}), f32[32,1,2640]{2,1,0:T(1,128)}, u32[]{:S(2)}, u32[]{:S(2)}) async-start(f32[32,1,2640]{2,1,0:T(1,128)} %copy.25), calls=%async_computation | async-start | bytes 688128 | tf_op jit(solution)/shard_map/all_to_all | solution.py:762
  58.4 2.9 %shard_map.183 = bf16[4,2,2,24,2304]{4,3,2,1,0:T(8,128)(2,1)} custom-call(s32[3]{0:T(128)S(1)} %pad_add_fusion.refs_0_, bf16[4,24,1152]{2,1,0:T(8,128)(2,1)S(1)} %get-tuple-element.78.refs_1_, bf16[4,24,1152]{2,1,0:T(8,128)(2,1)} %collective-permute-done.15.refs_2_, bf16[4,24,1152]{2,1,0:T(8,128)(2,1)} %collective-permute-done.16.refs_3_, ...), custom_call_target="tpu_custom_call" | custom-call | bytes 5308416 | tf_op jit(solution)/shard_map/pallas_call | solution.py:514
  63.5 5.3 %all-to-all-done = f32[32,1,2640]{2,1,0:T(1,128)} async-done(((f32[32,1,2640]{2,1,0:T(1,128)}), f32[32,1,2640]{2,1,0:T(1,128)}, u32[]{:S(2)}, u32[]{:S(2)}) %all-to-all-start) | async-done | bytes 337952 | tf_op jit(solution)/shard_map/all_to_all | solution.py:762
  69.9 5.6 %shard_map.181 = (bf16[256,384]{1,0:T(8,128)(2,1)S(1)}, f32[1,2304]{1,0:T(1,128)S(1)}, bf16[256,1152]{1,0:T(8,128)(2,1)S(1)}, bf16[256,384]{1,0:T(8,128)(2,1)S(1...) custom-call(s32[1]{0:T(128)} %bitcast.refs_0_, ...), custom_call_target="tpu_custom_call" | custom-call | flops 1006632960 | bytes 5308416 | tf_op jit(solution)/shard_map/pallas_call | solution.py:352
  75.6 12.9 %shard_map.184 = (bf16[256,384]{1,0:T(8,128)(2,1)S(1)}, bf16[256,384]{1,0:T(8,128)(2,1)S(1)}, f32[1,2304]{1,0:T(1,128)S(1)}, f32[16,336]{1,0:T(8,128)S(1)}, bf16...) custom-call(s32[1]{0:T(128)} %bitcast.refs_0_, bf16[256,384]{1,0:T(8,128)(2,1)S(1)} %get-tuple-element.76.refs_1_, ...), custom_call_target="tpu_custom_call" | custom-call | flops 3019898880 | bytes 10616832 | tf_op jit(solution)/shard_map/pallas_call | solution.py:352
  90.3 7.5 %shard_map.185 = (bf16[256,384]{1,0:T(8,128)(2,1)S(1)}, f32[1,2304]{1,0:T(1,128)S(1)}, f32[16,336]{1,0:T(8,128)S(1)}, bf16[384,2304]{1,0:T(8,128)(2,1)S(1)}, bf16[384,2304]{1,0:T(8,128)(2,1)}) custom-call(s32[1]{0:T(128)} %bitcast.refs_0_, bf16[256,384]{1,0:T(8,128)(2,1)S(1)} %get-tuple-element.167.refs_1_, f32[1,2304]{1,0:T(1,128)S(1)} %get-tuple-element.82.refs_2_, ...), custom_call_target="tpu_custom_call" | custom-call | flops 2013265920 | bytes 10616832 | tf_op jit(solution)/shard_map/pallas_call | solution.py:352
  101.3 6.7 %collective-permute-done.22.refs_3_ = bf16[3,1,128,384]{3,2,1,0:T(8,128)(2,1)S(1)} collective-permute-done((bf16[3,1,128,384]{3,2,1,0:T(8,128)(2,1)S(1)}, bf16[3,1,128,384]{3,2,1,0:T(8,128)(2,1)S(1)}, u32[]{:S(2)}, u32[]{:S(2)}) %collective-permute-start.22) | collective-permute-done | bytes 294944 | tf_op jit(solution)/shard_map/ppermute | solution.py:526
  108.1 1.5 copy-done.4
  109.6 2.7 %shard_map.186 = (bf16[4,2,24,1152]{3,2,1,0:T(8,128)(2,1)S(1)}, bf16[4,2,24,1152]{3,2,1,0:T(8,128)(2,1)}, bf16[4,2,24,1152]{3,2,1,0:T(8,128)(2,1)S(1)}, bf16[4,2,24,1152]{3,2,1,0:T(8,128)(2,1)}) custom-call(s32[3]{0:T(128)S(1)} %pad_add_fusion.refs_0_, bf16[16,24,2304]{2,1,0:T(8,128)(2,1)S(1)} %bitcast.71, bf16[16,24,2304]{2,1,0:T(8,128)(2,1)} %bitcast.27.refs_2_, ...), custom_call_target="tpu_custom_call" | custom-call | bytes 5308416 | tf_op jit(solution)/shard_map/pallas_call | solution.py:514
  113.1 1.7 shard_map.187
  120.5 2.8 %collective-permute-start.26 = (bf16[2,2,128,384]{3,2,1,0:T(8,128)(2,1)}, bf16[2,2,128,384]{3,2,1,0:T(8,128)(2,1)}, u32[]{:S(2)}, u32[]{:S(2)}) collective-permute-start(bf16[2,2,128,384]{3,2,1,0:T(8,128)(2,1)} %get-tuple-element.161), channel_id=1, source_target_pairs={{0,16},{16,0},{1,17},{17,1},{2,18},{18,2},{3,19},{19,3},{4,20},{20... | collective-permute-start | bytes 1179656 | tf_op jit(solution)/shard_map/ppermute | solution.py:526
  124.4 4.4 %all-to-all-start.1 = ((f32[32,1,2640]{2,1,0:T(1,128)}), f32[32,1,2640]{2,1,0:T(1,128)}, u32[]{:S(2)}, u32[]{:S(2)}) async-start(f32[32,1,2640]{2,1,0:T(1,128)} %broadcast_in_dim.65), calls=%async_computation.1 | async-start | bytes 688128 | tf_op jit(solution)/shard_map/all_to_all | solution.py:872
  128.8 2.1 %shard_map.190 = (bf16[4,24,1152]{2,1,0:T(8,128)(2,1)S(1)}, bf16[4,24,1152]{2,1,0:T(8,128)(2,1)}, bf16[4,24,1152]{2,1,0:T(8,128)(2,1)S(1)}, bf16[4,24,1152]{2,1,0:T(8,128)(2,1)}) custom-call(s32[3]{0:T(128)S(1)} %pad_add_fusion.refs_0_, bf16[4,2,24,1152]{3,2,1,0:T(8,128)(2,1)S(1)} %get-tuple-element.98.refs_6_.refs_1_, ...), custom_call_target="tpu_custom_call" | custom-call | bytes 2654208 | tf_op jit(solution)/shard_map/pallas_call | solution.py:514
  133.3 4.7 %collective-permute-done.27.refs_2_ = bf16[4,2,24,1152]{3,2,1,0:T(8,128)(2,1)S(1)} collective-permute-done((bf16[4,2,24,1152]{3,2,1,0:T(8,128)(2,1)}, bf16[4,2,24,1152]{3,2,1,0:T(8,128)(2,1)S(1)}, u32[]{:S(2)}, u32[]{:S(2)}) %collective-permute-start.27) | collective-permute-done | bytes 442400 | tf_op jit(solution)/shard_map/ppermute | solution.py:530
  138.0 2.8 %collective-permute-done.28.refs_4_ = bf16[4,2,24,1152]{3,2,1,0:T(8,128)(2,1)S(1)} collective-permute-done((bf16[4,2,24,1152]{3,2,1,0:T(8,128)(2,1)}, bf16[4,2,24,1152]{3,2,1,0:T(8,128)(2,1)S(1)}, u32[]{:S(2)}, u32[]{:S(2)}) %collective-permute-start.28) | collective-permute-done | bytes 442400 | tf_op jit(solution)/shard_map/ppermute | solution.py:530
  140.9 1.4 shard_map.188
  148.4 8.1 %all-to-all-start.2 = ((f32[32,1,768]{2,1,0:T(1,128)}), f32[32,1,768]{2,1,0:T(1,128)S(1)}, u32[]{:S(2)}, u32[]{:S(2)}) async-start(f32[32,1,768]{2,1,0:T(1,128)} %broadcast_in_dim.67), calls=%async_computation.2 | async-start | bytes 196608 | tf_op jit(solution)/shard_map/all_to_all | solution.py:879
  160.0 1.5 collective-permute-start.40
  162.2 3.2 %collective-permute-start.32 = (bf16[24,2304]{1,0:T(8,128)(2,1)S(1)}, bf16[24,2304]{1,0:T(8,128)(2,1)S(1)}, u32[]{:S(2)}, u32[]{:S(2)}) collective-permute-start(bf16[24,2304]{1,0:T(8,128)(2,1)S(1)} %get-tuple-element.114), channel_id=1, source_target_pairs={{0,8},{1,9},{2,10},{3,11},{4,12},{5,13},{6,14},{7,15},{8,0},{9,1},... | collective-permute-start | bytes 331784 | tf_op jit(solution)/shard_map/ppermute | solution.py:530
  167.2 8.5 %collective-permute-done.40.refs_8_ = bf16[24,2304]{1,0:T(8,128)(2,1)S(1)} collective-permute-done((bf16[24,2304]{1,0:T(8,128)(2,1)S(1)}, bf16[24,2304]{1,0:T(8,128)(2,1)S(1)}, u32[]{:S(2)}, u32[]{:S(2)}) %collective-permute-start.40) | collective-permute-done | bytes 110624 | tf_op jit(solution)/shard_map/ppermute | solution.py:530
  175.7 1.4 collective-permute-done.32.refs_3_
  177.1 3.3 %collective-permute-done.33.refs_4_ = bf16[24,2304]{1,0:T(8,128)(2,1)S(1)} collective-permute-done((bf16[24,2304]{1,0:T(8,128)(2,1)S(1)}, bf16[24,2304]{1,0:T(8,128)(2,1)S(1)}, u32[]{:S(2)}, u32[]{:S(2)}) %collective-permute-start.33) | collective-permute-done | bytes 110624 | tf_op jit(solution)/shard_map/ppermute | solution.py:530
  182.1 2.2 %fusion.6 = f32[1000,384]{1,0:T(8,128)} fusion(s32[32]{0:T(128)S(1)} %eq.25, f32[32,384]{1,0:T(8,128)S(1)} %copy-done.25, f32[32,384]{1,0:T(8,128)S(1)} %reshape.130), kind=kOutput, calls=%fused_computation.31 | convolution fusion | flops 147598592 | bytes 1634432 | tf_op jit(solution)/shard_map/dot_general | solution.py:883
  (185 shorter events, 52.4 us)
Async XLA Ops:
  4.2 18.6 %collective-permute-start = (bf16[2,128,384]{2,1,0:T(8,128)(2,1)S(1)}, bf16[2,128,384]{2,1,0:T(8,128)(2,1)S(1)}, u32[]{:S(2)}, u32[]{:S(2)}) collective-permute-start(bf16[2,128,384]{2,1,0:T(8,128)(2,1)S(1)} %get-tuple-element.169), channel_id=1, source_target_pairs={{0,1},{1,0},{2,3},{3,2},{4,5},{5,4},{6,7},{7,6},{8,9},{9,8},{10,11... | collective-permute-start | bytes 589832 | tf_op jit(solution)/shard_map/ppermute | solution.py:526
  8.5 10.6 %collective-permute-start.4 = (bf16[24,2304]{1,0:T(8,128)(2,1)S(1)}, bf16[24,2304]{1,0:T(8,128)(2,1)S(1)}, u32[]{:S(2)}, u32[]{:S(2)}) collective-permute-start(bf16[24,2304]{1,0:T(8,128)(2,1)S(1)} %get-tuple-element.173.refs_1_), channel_id=1, source_target_pairs={{0,12},{1,13},{2,14},{3,15},{4,0},{5,1},{6,2},{7,3},{8,4},{9,5},{1... | collective-permute-start | bytes 331784 | tf_op jit(solution)/shard_map/ppermute | solution.py:530
  20.1 14.5 %collective-permute-start.5 = (bf16[4,24,1152]{2,1,0:T(8,128)(2,1)S(1)}, bf16[4,24,1152]{2,1,0:T(8,128)(2,1)S(1)}, u32[]{:S(2)}, u32[]{:S(2)}) collective-permute-start(bf16[4,24,1152]{2,1,0:T(8,128)(2,1)S(1)} %get-tuple-element.74.refs_1_), channel_id=1, source_target_pairs={{0,2},{1,3},{2,0},{3,1},{4,6},{5,7},{6,4},{7,5},{8,10},{9,11},{10,... | collective-permute-start | bytes 663560 | tf_op jit(solution)/shard_map/ppermute | solution.py:530
  21.4 15.8 %collective-permute-start.6 = (bf16[4,24,1152]{2,1,0:T(8,128)(2,1)S(1)}, bf16[4,24,1152]{2,1,0:T(8,128)(2,1)S(1)}, u32[]{:S(2)}, u32[]{:S(2)}) collective-permute-start(bf16[4,24,1152]{2,1,0:T(8,128)(2,1)S(1)} %get-tuple-element.74.refs_1_), channel_id=1, source_target_pairs={{0,1},{1,0},{2,3},{3,2},{4,5},{5,4},{6,7},{7,6},{8,9},{9,8},{10,11... | collective-permute-start | bytes 663560 | tf_op jit(solution)/shard_map/ppermute | solution.py:530
  21.6 13.0 %collective-permute-start.9 = (bf16[4,24,1152]{2,1,0:T(8,128)(2,1)S(1)}, bf16[4,24,1152]{2,1,0:T(8,128)(2,1)S(1)}, u32[]{:S(2)}, u32[]{:S(2)}) collective-permute-start(bf16[4,24,1152]{2,1,0:T(8,128)(2,1)S(1)} %get-tuple-element.75.refs_5_), channel_id=1, source_target_pairs={{0,1},{1,0},{2,3},{3,2},{4,5},{5,4},{6,7},{7,6},{8,9},{9,8},{10,11... | collective-permute-start | bytes 663560 | tf_op jit(solution)/shard_map/ppermute | solution.py:530
  28.4 10.2 %collective-permute-start.8 = (bf16[4,24,1152]{2,1,0:T(8,128)(2,1)S(1)}, bf16[4,24,1152]{2,1,0:T(8,128)(2,1)S(1)}, u32[]{:S(2)}, u32[]{:S(2)}) collective-permute-start(bf16[4,24,1152]{2,1,0:T(8,128)(2,1)S(1)} %get-tuple-element.75.refs_5_), channel_id=1, source_target_pairs={{0,2},{1,3},{2,0},{3,1},{4,6},{5,7},{6,4},{7,5},{8,10},{9,11},{10,... | collective-permute-start | bytes 663560 | tf_op jit(solution)/shard_map/ppermute | solution.py:530
  35.4 15.2 %collective-permute-start.15 = (bf16[4,24,1152]{2,1,0:T(8,128)(2,1)S(1)}, bf16[4,24,1152]{2,1,0:T(8,128)(2,1)}, u32[]{:S(2)}, u32[]{:S(2)}) collective-permute-start(bf16[4,24,1152]{2,1,0:T(8,128)(2,1)S(1)} %get-tuple-element.78.refs_1_), channel_id=1, source_target_pairs={{0,2},{1,3},{2,0},{3,1},{4,6},{5,7},{6,4},{7,5},{8,10},{9,11},{10,... | collective-permute-start | bytes 663560 | tf_op jit(solution)/shard_map/ppermute | solution.py:530
  35.7 15.2 %collective-permute-start.19 = (bf16[4,24,1152]{2,1,0:T(8,128)(2,1)S(1)}, bf16[4,24,1152]{2,1,0:T(8,128)(2,1)}, u32[]{:S(2)}, u32[]{:S(2)}) collective-permute-start(bf16[4,24,1152]{2,1,0:T(8,128)(2,1)S(1)} %get-tuple-element.79.refs_5_), channel_id=1, source_target_pairs={{0,1},{1,0},{2,3},{3,2},{4,5},{5,4},{6,7},{7,6},{8,9},{9,8},{10,11... | collective-permute-start | bytes 663560 | tf_op jit(solution)/shard_map/ppermute | solution.py:530
  36.0 10.6 %collective-permute-start.10 = (bf16[4,24,1152]{2,1,0:T(8,128)(2,1)S(1)}, bf16[4,24,1152]{2,1,0:T(8,128)(2,1)S(1)}, u32[]{:S(2)}, u32[]{:S(2)}) collective-permute-start(bf16[4,24,1152]{2,1,0:T(8,128)(2,1)S(1)} %collective-permute-done.9.refs_7_), channel_id=1, source_target_pairs={{0,2},{1,3},{2,0},{3,1},{4,6},{5,7},{6,4},{7,5},{8,10},{9,11},{10,... | collective-permute-start | bytes 663560 | tf_op jit(solution)/shard_map/ppermute | solution.py:530
  37.2 9.6 %collective-permute-start.7 = (bf16[4,24,1152]{2,1,0:T(8,128)(2,1)S(1)}, bf16[4,24,1152]{2,1,0:T(8,128)(2,1)S(1)}, u32[]{:S(2)}, u32[]{:S(2)}) collective-permute-start(bf16[4,24,1152]{2,1,0:T(8,128)(2,1)S(1)} %collective-permute-done.5.refs_2_.refs_6_), channel_id=1, source_target_pairs={{0,1},{1,0},{2,3},{3,2},{4,5},{5,4},{6,7},{7,6},{8,9},{9,8},{10,11... | collective-permute-start | bytes 663560 | tf_op jit(solution)/shard_map/ppermute | solution.py:530
  38.6 19.8 %collective-permute-start.16 = (bf16[4,24,1152]{2,1,0:T(8,128)(2,1)S(1)}, bf16[4,24,1152]{2,1,0:T(8,128)(2,1)}, u32[]{:S(2)}, u32[]{:S(2)}) collective-permute-start(bf16[4,24,1152]{2,1,0:T(8,128)(2,1)S(1)} %get-tuple-element.78.refs_1_), channel_id=1, source_target_pairs={{0,1},{1,0},{2,3},{3,2},{4,5},{5,4},{6,7},{7,6},{8,9},{9,8},{10,11... | collective-permute-start | bytes 663560 | tf_op jit(solution)/shard_map/ppermute | solution.py:530
  46.5 11.8 %collective-permute-start.18 = (bf16[4,24,1152]{2,1,0:T(8,128)(2,1)S(1)}, bf16[4,24,1152]{2,1,0:T(8,128)(2,1)}, u32[]{:S(2)}, u32[]{:S(2)}) collective-permute-start(bf16[4,24,1152]{2,1,0:T(8,128)(2,1)S(1)} %get-tuple-element.79.refs_5_), channel_id=1, source_target_pairs={{0,2},{1,3},{2,0},{3,1},{4,6},{5,7},{6,4},{7,5},{8,10},{9,11},{10,... | collective-permute-start | bytes 663560 | tf_op jit(solution)/shard_map/ppermute | solution.py:530
  47.7 22.3 %collective-permute-start.11 = (bf16[384,2304]{1,0:T(8,128)(2,1)S(1)}, bf16[384,2304]{1,0:T(8,128)(2,1)}, u32[]{:S(2)}, u32[]{:S(2)}) collective-permute-start(bf16[384,2304]{1,0:T(8,128)(2,1)S(1)} %bitcast.66), channel_id=1, source_target_pairs={{0,16},{16,0},{1,17},{17,1},{2,18},{18,2},{3,19},{19,3},{4,20},{20... | collective-permute-start | bytes 5308424 | tf_op jit(solution)/shard_map/ppermute | solution.py:526
  53.2 15.6 %all-to-all-start = ((f32[32,1,2640]{2,1,0:T(1,128)}), f32[32,1,2640]{2,1,0:T(1,128)}, u32[]{:S(2)}, u32[]{:S(2)}) async-start(f32[32,1,2640]{2,1,0:T(1,128)} %copy.25), calls=%async_computation | async-start | bytes 688128 | tf_op jit(solution)/shard_map/all_to_all | solution.py:762
  61.3 14.3 %collective-permute-start.21 = (bf16[384,2304]{1,0:T(8,128)(2,1)}, bf16[384,2304]{1,0:T(8,128)(2,1)}, u32[]{:S(2)}, u32[]{:S(2)}) collective-permute-start(bf16[384,2304]{1,0:T(8,128)(2,1)} %bitcast.21.refs_5_), channel_id=1, source_target_pairs={{0,16},{16,0},{1,17},{17,1},{2,18},{18,2},{3,19},{19,3},{4,20},{20... | collective-permute-start | bytes 5308424 | tf_op jit(solution)/shard_map/ppermute | solution.py:526
  89.7 18.4 %collective-permute-start.24 = (bf16[384,2304]{1,0:T(8,128)(2,1)}, bf16[384,2304]{1,0:T(8,128)(2,1)}, u32[]{:S(2)}, u32[]{:S(2)}) collective-permute-start(bf16[384,2304]{1,0:T(8,128)(2,1)} %get-tuple-element.97), channel_id=1, source_target_pairs={{0,16},{16,0},{1,17},{17,1},{2,18},{18,2},{3,19},{19,3},{4,20},{20... | collective-permute-start | bytes 5308424 | tf_op jit(solution)/shard_map/ppermute | solution.py:526
  99.1 14.0 %collective-permute-start.23 = (bf16[384,2304]{1,0:T(8,128)(2,1)}, bf16[384,2304]{1,0:T(8,128)(2,1)S(1)}, u32[]{:S(2)}, u32[]{:S(2)}) collective-permute-start(bf16[384,2304]{1,0:T(8,128)(2,1)} %get-tuple-element.92), channel_id=1, source_target_pairs={{0,16},{16,0},{1,17},{17,1},{2,18},{18,2},{3,19},{19,3},{4,20},{20... | collective-permute-start | bytes 5308424 | tf_op jit(solution)/shard_map/ppermute | solution.py:526
  115.7 13.1 %collective-permute-start.34 = (bf16[4,2,24,1152]{3,2,1,0:T(8,128)(2,1)}, bf16[4,2,24,1152]{3,2,1,0:T(8,128)(2,1)}, u32[]{:S(2)}, u32[]{:S(2)}) collective-permute-start(bf16[4,2,24,1152]{3,2,1,0:T(8,128)(2,1)} %get-tuple-element.116), channel_id=1, source_target_pairs={{0,2},{1,3},{2,0},{3,1},{4,6},{5,7},{6,4},{7,5},{8,10},{9,11},{10,... | collective-permute-start | bytes 1327112 | tf_op jit(solution)/shard_map/ppermute | solution.py:530
  116.8 12.0 %collective-permute-start.35 = (bf16[4,2,24,1152]{3,2,1,0:T(8,128)(2,1)}, bf16[4,2,24,1152]{3,2,1,0:T(8,128)(2,1)}, u32[]{:S(2)}, u32[]{:S(2)}) collective-permute-start(bf16[4,2,24,1152]{3,2,1,0:T(8,128)(2,1)} %get-tuple-element.118), channel_id=1, source_target_pairs={{0,1},{1,0},{2,3},{3,2},{4,5},{5,4},{6,7},{7,6},{8,9},{9,8},{10,11... | collective-permute-start | bytes 1327112 | tf_op jit(solution)/shard_map/ppermute | solution.py:530
  117.7 20.3 %collective-permute-start.27 = (bf16[4,2,24,1152]{3,2,1,0:T(8,128)(2,1)}, bf16[4,2,24,1152]{3,2,1,0:T(8,128)(2,1)S(1)}, u32[]{:S(2)}, u32[]{:S(2)}) collective-permute-start(bf16[4,2,24,1152]{3,2,1,0:T(8,128)(2,1)} %get-tuple-element.105), channel_id=1, source_target_pairs={{0,2},{1,3},{2,0},{3,1},{4,6},{5,7},{6,4},{7,5},{8,10},{9,11},{10,... | collective-permute-start | bytes 1327112 | tf_op jit(solution)/shard_map/ppermute | solution.py:530
  118.0 22.8 %collective-permute-start.28 = (bf16[4,2,24,1152]{3,2,1,0:T(8,128)(2,1)}, bf16[4,2,24,1152]{3,2,1,0:T(8,128)(2,1)S(1)}, u32[]{:S(2)}, u32[]{:S(2)}) collective-permute-start(bf16[4,2,24,1152]{3,2,1,0:T(8,128)(2,1)} %get-tuple-element.107), channel_id=1, source_target_pairs={{0,1},{1,0},{2,3},{3,2},{4,5},{5,4},{6,7},{7,6},{8,9},{9,8},{10,11... | collective-permute-start | bytes 1327112 | tf_op jit(solution)/shard_map/ppermute | solution.py:530
  120.5 23.4 %collective-permute-start.26 = (bf16[2,2,128,384]{3,2,1,0:T(8,128)(2,1)}, bf16[2,2,128,384]{3,2,1,0:T(8,128)(2,1)}, u32[]{:S(2)}, u32[]{:S(2)}) collective-permute-start(bf16[2,2,128,384]{3,2,1,0:T(8,128)(2,1)} %get-tuple-element.161), channel_id=1, source_target_pairs={{0,16},{16,0},{1,17},{17,1},{2,18},{18,2},{3,19},{19,3},{4,20},{20... | collective-permute-start | bytes 1179656 | tf_op jit(solution)/shard_map/ppermute | solution.py:526
  124.4 22.0 %all-to-all-start.1 = ((f32[32,1,2640]{2,1,0:T(1,128)}), f32[32,1,2640]{2,1,0:T(1,128)}, u32[]{:S(2)}, u32[]{:S(2)}) async-start(f32[32,1,2640]{2,1,0:T(1,128)} %broadcast_in_dim.65), calls=%async_computation.1 | async-start | bytes 688128 | tf_op jit(solution)/shard_map/all_to_all | solution.py:872
  130.9 25.5 %collective-permute-start.36 = (bf16[4,24,1152]{2,1,0:T(8,128)(2,1)}, bf16[4,24,1152]{2,1,0:T(8,128)(2,1)S(1)}, u32[]{:S(2)}, u32[]{:S(2)}) collective-permute-start(bf16[4,24,1152]{2,1,0:T(8,128)(2,1)} %get-tuple-element.120), channel_id=1, source_target_pairs={{0,1},{1,0},{2,3},{3,2},{4,5},{5,4},{6,7},{7,6},{8,9},{9,8},{10,11... | collective-permute-start | bytes 663560 | tf_op jit(solution)/shard_map/ppermute | solution.py:530
  132.1 24.3 %collective-permute-start.37 = (bf16[4,24,1152]{2,1,0:T(8,128)(2,1)}, bf16[4,24,1152]{2,1,0:T(8,128)(2,1)S(1)}, u32[]{:S(2)}, u32[]{:S(2)}) collective-permute-start(bf16[4,24,1152]{2,1,0:T(8,128)(2,1)} %get-tuple-element.122), channel_id=1, source_target_pairs={{0,2},{1,3},{2,0},{3,1},{4,6},{5,7},{6,4},{7,5},{8,10},{9,11},{10,... | collective-permute-start | bytes 663560 | tf_op jit(solution)/shard_map/ppermute | solution.py:530
  142.2 19.2 %collective-permute-start.29 = (bf16[4,24,1152]{2,1,0:T(8,128)(2,1)}, bf16[4,24,1152]{2,1,0:T(8,128)(2,1)S(1)}, u32[]{:S(2)}, u32[]{:S(2)}) collective-permute-start(bf16[4,24,1152]{2,1,0:T(8,128)(2,1)} %get-tuple-element.109), channel_id=1, source_target_pairs={{0,1},{1,0},{2,3},{3,2},{4,5},{5,4},{6,7},{7,6},{8,9},{9,8},{10,11... | collective-permute-start | bytes 663560 | tf_op jit(solution)/shard_map/ppermute | solution.py:530
  142.6 18.9 %collective-permute-start.30 = (bf16[4,24,1152]{2,1,0:T(8,128)(2,1)}, bf16[4,24,1152]{2,1,0:T(8,128)(2,1)S(1)}, u32[]{:S(2)}, u32[]{:S(2)}) collective-permute-start(bf16[4,24,1152]{2,1,0:T(8,128)(2,1)} %get-tuple-element.111), channel_id=1, source_target_pairs={{0,2},{1,3},{2,0},{3,1},{4,6},{5,7},{6,4},{7,5},{8,10},{9,11},{10,... | collective-permute-start | bytes 663560 | tf_op jit(solution)/shard_map/ppermute | solution.py:530
  148.4 32.7 %all-to-all-start.2 = ((f32[32,1,768]{2,1,0:T(1,128)}), f32[32,1,768]{2,1,0:T(1,128)S(1)}, u32[]{:S(2)}, u32[]{:S(2)}) async-start(f32[32,1,768]{2,1,0:T(1,128)} %broadcast_in_dim.67), calls=%async_computation.2 | async-start | bytes 196608 | tf_op jit(solution)/shard_map/all_to_all | solution.py:879
  160.0 15.7 %collective-permute-start.40 = (bf16[24,2304]{1,0:T(8,128)(2,1)S(1)}, bf16[24,2304]{1,0:T(8,128)(2,1)S(1)}, u32[]{:S(2)}, u32[]{:S(2)}) collective-permute-start(bf16[24,2304]{1,0:T(8,128)(2,1)S(1)} %get-tuple-element.126), channel_id=1, source_target_pairs={{0,12},{1,13},{2,14},{3,15},{4,0},{5,1},{6,2},{7,3},{8,4},{9,5},{1... | collective-permute-start | bytes 331784 | tf_op jit(solution)/shard_map/ppermute | solution.py:530
  162.1 13.6 %collective-permute-start.31 = (bf16[24,2304]{1,0:T(8,128)(2,1)S(1)}, bf16[24,2304]{1,0:T(8,128)(2,1)S(1)}, u32[]{:S(2)}, u32[]{:S(2)}) collective-permute-start(bf16[24,2304]{1,0:T(8,128)(2,1)S(1)} %get-tuple-element.113), channel_id=1, source_target_pairs={{0,4},{1,5},{2,6},{3,7},{4,8},{5,9},{6,10},{7,11},{8,12},{9,13},{1... | collective-permute-start | bytes 331784 | tf_op jit(solution)/shard_map/ppermute | solution.py:530
  162.2 14.9 %collective-permute-start.32 = (bf16[24,2304]{1,0:T(8,128)(2,1)S(1)}, bf16[24,2304]{1,0:T(8,128)(2,1)S(1)}, u32[]{:S(2)}, u32[]{:S(2)}) collective-permute-start(bf16[24,2304]{1,0:T(8,128)(2,1)S(1)} %get-tuple-element.114), channel_id=1, source_target_pairs={{0,8},{1,9},{2,10},{3,11},{4,12},{5,13},{6,14},{7,15},{8,0},{9,1},... | collective-permute-start | bytes 331784 | tf_op jit(solution)/shard_map/ppermute | solution.py:530
  165.4 15.1 %collective-permute-start.33 = (bf16[24,2304]{1,0:T(8,128)(2,1)S(1)}, bf16[24,2304]{1,0:T(8,128)(2,1)S(1)}, u32[]{:S(2)}, u32[]{:S(2)}) collective-permute-start(bf16[24,2304]{1,0:T(8,128)(2,1)S(1)} %get-tuple-element.115), channel_id=1, source_target_pairs={{0,12},{1,13},{2,14},{3,15},{4,0},{5,1},{6,2},{7,3},{8,4},{9,5},{1... | collective-permute-start | bytes 331784 | tf_op jit(solution)/shard_map/ppermute | solution.py:530
  (44 other events, 326.7 us)

commit v7 on v6

--- a/solution.py
+++ b/solution.py
@@ -356,7 +356,7 @@
         out_specs=out_specs,
         scratch_shapes=scratch,
         compiler_params=pltpu.CompilerParams(
-            vmem_limit_bytes=(36 if length <= 256 else 56) * 1024 * 1024
+            vmem_limit_bytes=(26 if length <= 256 else 56) * 1024 * 1024
         ),
         cost_estimate=pl.CostEstimate(
             flops=(forward + 2 * backward) * work,
@@ -400,62 +400,80 @@
         copy_all(copies(send_ref, keep_ref))
 
 
-def stack_kernel(high, split, place_ref, *refs):
+def stack_kernel(high, place_ref, *refs):
     pieces, sems = refs[:high], refs[-1]
-    count = (len(refs) - high - 3) // 2
-    handed, targets = refs[high : high + count], refs[high + count : -1]
+    count = (len(refs) - high - 2) // 2
+    handed, block = refs[high : high + count], refs[high + count]
+    lanes = block.shape[3]
     copies = [
         pltpu.make_async_copy(former, latter, sems.at[high + i, 0])
-        for i, (former, latter) in enumerate(zip(handed, targets[2:]))
+        for i, (former, latter) in enumerate(zip(handed, refs[high + count + 1 : -1]))
     ]
     for turn, piece in enumerate(pieces):
         place = lax.rem(place_ref[0] + (high - turn), high)
-        parts = (piece.at[:, :split], piece.at[:, split:])
-        for i, (part, target) in enumerate(zip(parts, targets)):
-            copies.append(pltpu.make_async_copy(part, target.at[place], sems.at[turn, i]))
+        for part in range(2):
+            source = piece.at[:, pl.ds(part * lanes, lanes)]
+            copies.append(
+                pltpu.make_async_copy(source, block.at[part, place], sems.at[turn, part])
+            )
     copy_all(copies)
 
 
-def weave_kernel(split, place_ref, *refs):
-    pieces, full_ref, sems = refs[:-2], refs[-2], refs[-1]
+def weave_kernel(place_ref, own, from_x, from_y, first_both, second_both, full_ref, sems):
     x, y = place_ref[1], place_ref[2]
-    copies = []
-    for i, piece in enumerate(pieces):
-        other_x, other_y = (i % 4) & 1, (i % 4) >> 1
-        row = x if not other_x else 1 - x
-        column = y if not other_y else 1 - y
-        target = full_ref.at[:, row, column, :, pl.ds((i // 4) * split, split)]
-        copies.append(pltpu.make_async_copy(piece, target, sems.at[i]))
-    copy_all(copies)
+    lanes = own.shape[3]
+    moves = []
+    for part, both in ((0, first_both), (1, second_both)):
+        for source, row, column in (
+            (own.at[part], x, y),
+            (from_x.at[part], 1 - x, y),
+            (from_y.at[part], x, 1 - y),
+            (both, 1 - x, 1 - y),
+        ):
+            moves.append((source, full_ref.at[:, row, column, :, pl.ds(part * lanes, lanes)]))
+    copy_all(
+        [
+            pltpu.make_async_copy(source, target, sems.at[i])
+            for i, (source, target) in enumerate(moves)
+        ]
+    )
 
 
 def added(former, latter):
     return former.astype(jnp.float32) + latter.astype(jnp.float32)
 
 
-def chip_sum_kernel(high, place_ref, mine, got, *refs):
-    count = (len(refs) - 4) // 2
-    first_keep, first_send, second_keep, second_send = refs[count : count + 4]
-    for former, latter in zip(refs[:count], refs[count + 4 :]):
-        latter[...] = former[...]
+def chip_sum_kernel(rank_ref, mine, got, total):
+    total[...] = low(added(mine[...], got[...]))
+
+
+def sort_kernel(high, place_ref, *refs):
+    count = (len(refs) - 7) // 2
+    mine, got, done = refs[:3]
+    handed = refs[3 : 3 + count]
+    first_keep, first_send, second_keep, second_send = refs[3 + count : 7 + count]
     x, y = place_ref[1], place_ref[2]
     half = mine.shape[2]
     lanes = half // 2
     for z in range(high):
         for other in range(2):
             for target, span, chunk in (
+                (first_send, slice(0, lanes), z * 4 + (1 - x) * 2 + other),
+                (second_send, slice(lanes, half), z * 4 + other * 2 + (1 - y)),
                 (first_keep, slice(0, lanes), z * 4 + x * 2 + other),
-                (first_send, slice(0, lanes), z * 4 + (1 - x) * 2 + other),
                 (second_keep, slice(lanes, half), z * 4 + other * 2 + y),
-                (second_send, slice(lanes, half), z * 4 + other * 2 + (1 - y)),
             ):
-                target[z, other] = low(added(mine[chunk, :, span], got[chunk, :, span]))
+                target[z, other, 0] = low(added(mine[chunk, :, span], got[chunk, :, span]))
+                target[z, other, 1] = done[chunk, :, span]
+    for former, latter in zip(handed, refs[7 + count :]):
+        latter[...] = former[...]
 
 
 def turn_kernel(high, place_ref, *refs):
+    refs[-1][...] = refs[4][...]
     for part, own in ((0, place_ref[2]), (1, place_ref[1])):
         kept, got = refs[2 * part : 2 * part + 2]
-        keep, send = refs[4 + 2 * part : 6 + 2 * part]
+        keep, send = refs[5 + 2 * part : 7 + 2 * part]
         for z in range(high):
             keep[z] = low(added(kept[z, own], got[z, own]))
             send[z] = low(added(kept[z, 1 - own], got[z, 1 - own]))
@@ -463,28 +481,24 @@
 
 def rise_kernel(high, place_ref, *refs):
     targets = refs[4:]
-    lanes = refs[0].shape[2]
+    lanes = refs[0].shape[3]
     for turn in range(high):
         chunk = lax.rem(place_ref[0] + turn, high)
         for part in range(2):
             kept, got = refs[2 * part : 2 * part + 2]
             total = added(kept[chunk], got[chunk])
             span = slice(part * lanes, (part + 1) * lanes)
-            targets[turn][:, span] = total.astype(targets[turn].dtype)
-
-
-def close_kernel(high, rank_ref, *refs):
-    keep, send = refs[-2:]
-    totals = []
-    for section in range(2):
-        pieces = refs[section * high : (section + 1) * high]
-        total = pieces[0][...].astype(jnp.float32)
+            targets[turn][:, :, span] = total.astype(targets[turn].dtype)
+
+
+def close_kernel(rank_ref, *refs):
+    pieces, (keep, send) = refs[:-2], refs[-2:]
+    own = rank_ref[0]
+    for target, section in ((keep, own), (send, 1 - own)):
+        total = pieces[0][section].astype(jnp.float32)
         for piece in pieces[1:]:
-            total = total + piece[...].astype(jnp.float32)
-        totals.append(total)
-    first = rank_ref[0] == 0
-    keep[...] = jnp.where(first, totals[0], totals[1])
-    send[...] = jnp.where(first, totals[1], totals[0])
+            total = total + piece[section].astype(jnp.float32)
+        target[...] = total
 
 
 def spread_kernel(rank_ref, mine, got, att_ref, out_ref, up_ref, down_ref):
@@ -546,8 +560,8 @@
     high = size // 4
     rows, lanes = shard.shape
     return in_memory(
-        partial(stack_kernel, high, lanes // 2),
-        [jax.ShapeDtypeStruct((high, rows, lanes // 2), shard.dtype)] * 2
+        partial(stack_kernel, high),
+        [jax.ShapeDtypeStruct((2, high, rows, lanes // 2), shard.dtype)]
         + [jax.ShapeDtypeStruct(block.shape, block.dtype) for block in handed],
         [place, *rotations(shard, size), *handed],
         scratch=[pltpu.SemaphoreType.DMA((high + len(handed), 2))],
@@ -555,59 +569,47 @@
     )
 
 
-def first_flips(first, second, size):
-    return flip(first, size, 2), flip(second, size, 1)
-
-
-def gather_across(first, second, first_x, second_y, place, size):
-    high, rows, lanes = first.shape
-    first_y, second_x = flip(first, size, 1), flip(second, size, 2)
-    first_both, second_both = flip(first_x, size, 1), flip(second_y, size, 2)
+def gather_across(block, from_x, from_y, place, size):
+    _, high, rows, lanes = block.shape
+    first_both, second_both = flip(from_x[0], size, 1), flip(from_y[1], size, 2)
     (full,) = in_memory(
-        partial(weave_kernel, lanes),
-        [jax.ShapeDtypeStruct((high, 2, 2, rows, 2 * lanes), first.dtype)],
-        [place, first, first_x, first_y, first_both, second, second_x, second_y, second_both],
+        weave_kernel,
+        [jax.ShapeDtypeStruct((high, 2, 2, rows, 2 * lanes), block.dtype)],
+        [place, block, from_x, from_y, first_both, second_both],
         scratch=[pltpu.SemaphoreType.DMA((8,))],
     )
     return full.reshape(size * rows, 2 * lanes)
 
 
-def scatter_first(mine, got, place, size, handed=(), after=()):
-    rows, half = mine.shape[1:]
-    shape = jax.ShapeDtypeStruct((size // 4, 2, rows, half // 2), jnp.bfloat16)
-    return in_memory(
-        partial(chip_sum_kernel, size // 4),
-        [shape] * 4 + [jax.ShapeDtypeStruct(block.shape, block.dtype) for block in handed],
-        [place, mine, got, *handed],
-        after=after,
-    )
-
-
-def scatter_flips(sorted_terms, size):
-    first_keep, first_send, second_keep, second_send = sorted_terms
-    return first_keep, flip(first_send, size, 2), second_keep, flip(second_send, size, 1)
-
-
-def scatter_second(received, place, size, after=()):
-    high, _, rows, lanes = received[0].shape
-    shape = jax.ShapeDtypeStruct((high, rows, lanes), jnp.bfloat16)
-    return in_memory(
-        partial(turn_kernel, high), [shape] * 4, [place, *received], after=after
-    )
-
-
-def scatter_rest(turned, place, size):
-    high, rows, lanes = turned[0].shape
-    first_keep, first_send, second_keep, second_send = turned
+def scatter_along(terms, place, size, handed, later):
+    high = size // 4
+    rows, half = terms[0].shape[1:]
+    lanes = half // 2
+    low_type = jnp.bfloat16
+    first_keep, first_send, second_keep, second_send, *handed = in_memory(
+        partial(sort_kernel, high),
+        [jax.ShapeDtypeStruct((high, 2, 2, rows, lanes), low_type)] * 4
+        + [jax.ShapeDtypeStruct(block.shape, block.dtype) for block in handed],
+        [place, *terms, *handed],
+    )
+    first_got, second_got = flip(first_send, size, 2), flip(second_send, size, 1)
+    first_keep, first_send, second_keep, second_send, later = in_memory(
+        partial(turn_kernel, high),
+        [jax.ShapeDtypeStruct((high, 2, rows, lanes), low_type)] * 4
+        + [jax.ShapeDtypeStruct(later.shape, later.dtype)],
+        [place, first_keep, first_got, second_keep, second_got, later],
+    )
     first_got, second_got = flip(first_send, size, 1), flip(second_send, size, 2)
-    chunk = (rows, 2 * lanes)
     own, *sent = in_memory(
         partial(rise_kernel, high),
-        [jax.ShapeDtypeStruct(chunk, jnp.float32)]
-        + [jax.ShapeDtypeStruct(chunk, jnp.bfloat16)] * (high - 1),
+        [
+            jax.ShapeDtypeStruct((2, rows, half), kind)
+            for kind in (jnp.float32, *[low_type] * (high - 1))
+        ],
         [place, first_keep, first_got, second_keep, second_got],
     )
-    return [own] + [rotate(block, size, turn + 1) for turn, block in enumerate(sent)]
+    received = [rotate(block, size, turn + 1) for turn, block in enumerate(sent)]
+    return [own, *received], handed, later
 
 
 def scatter_sum(block, rank, size):
@@ -739,22 +741,12 @@
     silu_all = jax.nn.silu(conditions).astype(jnp.bfloat16)
     silu_own = lax.dynamic_slice_in_dim(silu_all, ring_rank * rows, rows, 1)
     if compact:
-        *first_parts, second_shard, silu_late = gather_along_z(
+        first_block, second_shard, silu_late = gather_along_z(
             first_shard, place, ring_size, handed=(second_shard, silu_own)
         )
-        first_parts += first_flips(*first_parts, ring_size)
-        second_parts = gather_along_z(
-            second_shard, place, ring_size, after=(both, *first_parts[2:])
-        )
-        second_parts += first_flips(*second_parts, ring_size)
-        first_pack = gather_across(*first_parts, place, ring_size)
-        second_pack = gather_across(*second_parts, place, ring_size)
+        first_blocks = (first_block, flip(first_block, ring_size, 2), flip(first_block, ring_size, 1))
     else:
         silu_late = silu_own
-        first_pack = lax.all_gather(first_shard, RING, axis=0, tiled=True)
-        second_pack = lax.all_gather(second_shard, RING, axis=0, tiled=True)
-    first_halves = (first_pack, pair_swap(first_pack, "section"))
-    second_halves = (second_pack, pair_swap(second_pack, "section"))
 
     products = matmul(silu_late, modulation_weight[0])
     own_bias = jnp.broadcast_to(biases.astype(jnp.float32), (products.shape[0], bias_count))
@@ -768,18 +760,29 @@
     first_bias, second_bias = products[0, :, 6 * width :], products[1, :, 6 * width :]
 
 
+    if compact:
+        (second_block,) = gather_along_z(
+            second_shard, place, ring_size, after=(products, both, *first_blocks[1:])
+        )
+        second_blocks = (
+            second_block,
+            flip(second_block, ring_size, 2),
+            flip(second_block, ring_size, 1),
+        )
+        first_pack = gather_across(*first_blocks, place, ring_size)
+        second_pack = gather_across(*second_blocks, place, ring_size)
+    else:
+        first_pack = lax.all_gather(first_shard, RING, axis=0, tiled=True)
+        second_pack = lax.all_gather(second_shard, RING, axis=0, tiled=True)
+    first_halves = (first_pack, pair_swap(first_pack, "section"))
+    second_halves = (second_pack, pair_swap(second_pack, "section"))
+
     first_low, *first_saved = run_section(
         layout, rank, first_input, first_halves, (first_modulation, first_bias)
     )
-    second_low, second_grad, second_dmod, second_sums, second_keep, second_send = run_section(
-        layout, rank, first_low, second_halves, (second_modulation, second_bias), dy=last_grad
-    )
-    second_got = pair_swap(second_send, "section")
-
-    def ring_terms(term):
-        return term.reshape(ring_size, rows, half)
-
-    early = jnp.stack([first_low * live, second_low * live, second_grad])
+    second_low, *second_saved = run_section(
+        layout, rank, first_low, second_halves, (second_modulation, second_bias)
+    )
 
     def to_slots(block):
         block = block.reshape(-1, 2, tokens, width)
@@ -787,66 +790,69 @@
         sent = lax.dynamic_index_in_dim(block, 1 - seq_rank, 1, keepdims=True)
         return mine, pair_swap(sent, "seq")
 
+    early = jnp.stack([first_low * live, second_low * live])
+    after = ()
     if compact:
         early = to_slots(early)
+        after = (early[1],)
+    second_grad, second_dmod, second_sums, second_keep, second_send = run_section(
+        layout, rank, first_low, second_halves, saved=second_saved, dy=last_grad
+    )
+    second_got = pair_swap(second_send, "section")
     first_grad, first_dmod, first_sums, first_keep, first_send = run_section(
-        layout, rank, first_input, first_halves, saved=first_saved, dy=second_grad
+        layout, rank, first_input, first_halves, saved=first_saved, dy=second_grad, after=after
     )
     first_got = pair_swap(first_send, "section")
+
+    def ring_terms(term):
+        return term.reshape(ring_size, rows, half)
 
     shard = jax.ShapeDtypeStruct((rows, half), jnp.float32)
     if compact:
-        second_sorted = scatter_first(
-            ring_terms(second_keep),
-            ring_terms(second_got),
+        second_term = ring_terms(second_keep)
+        (second_total,) = in_memory(
+            chip_sum_kernel,
+            [jax.ShapeDtypeStruct(second_term.shape, second_term.dtype)],
+            [rank, second_term, ring_terms(second_got)],
+        )
+        pieces, (first_dmod, first_sums), first_grad = scatter_along(
+            [ring_terms(first_keep), ring_terms(first_got), second_total],
             place,
             ring_size,
-            after=(early[1],),
+            (first_dmod, first_sums),
+            first_grad,
         )
-        second_received = scatter_flips(second_sorted, ring_size)
-        second_turned = scatter_second(second_received, place, ring_size)
-        *first_sorted, first_grad, first_dmod, first_sums = scatter_first(
-            ring_terms(first_keep),
-            ring_terms(first_got),
-            place,
-            ring_size,
-            handed=(first_grad, first_dmod, first_sums),
-            after=(second_sorted[0],),
-        )
-        first_turned = scatter_second(scatter_flips(first_sorted, ring_size), place, ring_size)
-        second_pieces = scatter_rest(second_turned, place, ring_size)
-        first_pieces = scatter_rest(first_turned, place, ring_size)
     else:
 
         def chip_sum(keep, got):
             return ring_terms(low(added(keep, got)))
 
-        first_pieces, second_pieces = [
-            [scatter_sum(chip_sum(keep, got), ring_rank, ring_size)]
-            for keep, got in ((first_keep, first_got), (second_keep, second_got))
+        pieces = [
+            jnp.stack(
+                [
+                    scatter_sum(chip_sum(keep, got), ring_rank, ring_size)
+                    for keep, got in ((first_keep, first_got), (second_keep, second_got))
+                ]
+            )
         ]
     if compact:
-        early_full, late = side_by_side(*early, 1), side_by_side(*to_slots(first_grad), 1)
-        per_first = jnp.stack([early_full[0], late[0]])
-        per_second = early_full[1:]
+        late = to_slots(jnp.stack([first_grad, second_grad]))
+        per_section = jnp.stack([side_by_side(*early, 1), side_by_side(*late, 1)], axis=1)
+        per_first, per_second = per_section
         mine = jnp.where(is_first, per_first, per_second)
         got = pair_swap(jnp.where(is_first, per_second, per_first), "section")
         outputs = jnp.where(is_first, jnp.stack([mine, got], 1), jnp.stack([got, mine], 1))
     else:
-        pieces = jnp.stack([early[0], first_grad, early[1], early[2]])
-        pieces = jnp.swapaxes(pieces.reshape(2, 2, seq_size, tokens, width), 1, 2)
-        pieces = pieces.reshape(2 * seq_size, 2, tokens, width)
-        pieces = lax.all_to_all(pieces, ("section", "seq"), 0, 0, tiled=True)
-        pieces = pieces.reshape(batches, slots, sharers, 2, tokens, width)[:, :, 0]
-        outputs = jnp.moveaxis(pieces, 2, 0)
+        blocks = jnp.stack([early[0], first_grad, early[1], second_grad])
+        blocks = jnp.swapaxes(blocks.reshape(2, 2, seq_size, tokens, width), 1, 2)
+        blocks = blocks.reshape(2 * seq_size, 2, tokens, width)
+        blocks = lax.all_to_all(blocks, ("section", "seq"), 0, 0, tiled=True)
+        blocks = blocks.reshape(batches, slots, sharers, 2, tokens, width)[:, :, 0]
+        outputs = jnp.moveaxis(blocks, 2, 0)
     activations = outputs[0]
     input_grads = outputs[1].astype(jnp.float32)
 
-    mine, send = in_memory(
-        partial(close_kernel, len(first_pieces)),
-        [shard, shard],
-        [rank, *first_pieces, *second_pieces],
-    )
+    mine, send = in_memory(close_kernel, [shard, shard], [rank, *pieces])
     att, out, up, down = in_memory(
         spread_kernel,
         [

time: 186 us -> 206 us (1.11)
  waiting for transfers between devices: 60.6 us -> 73.6 us
  starting transfers between devices: 55.5 us -> 43.7 us
  local copies, waits for them, and re-layouts: 14.1 us -> 25.2 us
  other arithmetic: 5.83 us -> 13.6 us
  Pallas kernels: 43.4 us -> 41.3 us
    all_to_all x1, waiting for transfers between devices: 0.01 us -> 17.4 us  [per_device(): lax.all_to_all(rows_back[:, None], ('section', 'dp', 'seq'), 0, 0, tiled=...]
    unnamed x64 -> x82, local copies, waits for them, and re-layouts: 7.39 us -> 14.5 us
    ppermute x10, waiting for transfers between devices: 6.75 us -> 1.04 us  [pair_swap(): return lax.ppermute(block, axis, [(0, 1), (1, 0)])]
    select_n x3, other arithmetic: 0.25 us -> 4.45 us  [side_by_side(): jnp.where(seq_rank == 0, jnp.concatenate([mine, got], axis=axis), jnp.con...]
    all_to_all x1, starting transfers between devices: 8.06 us -> 3.9 us  [per_device(): lax.all_to_all(columns, ('section', 'dp', 'seq'), 0, 0, tiled=True)]
    pallas_call x13 -> x11, Pallas kernels: 17.3 us -> 14.1 us  [in_memory(): pl.pallas_call(body, out_shape=shapes, in_specs=specs, out_specs=[pl.Bloc...]
    ppermute x32 -> x21, starting transfers between devices: 27.2 us -> 23.9 us  [ring_exchange(): return lax.ppermute(block, RING, [(i, step(i)) for i in range(size)])]
    ppermute x10, starting transfers between devices: 10.7 us -> 8.42 us  [pair_swap(): return lax.ppermute(block, axis, [(0, 1), (1, 0)])]
  transfers between devices with their start and end apart: 45 -> 34, of which waited for: 15 -> 16; matrix products, arithmetic and copies ran while one was open for 10% -> 14% of each run, Pallas kernels for 14% -> 15%
where the time goes in v7:
time: 206 us; the launch traced here: 205 us
  waiting for transfers between devices  73.6 us (36%)
  starting transfers between devices  43.7 us (21%)
  Pallas kernels  41.3 us (20%)
  local copies, waits for them, and re-layouts  25.2 us (12%)
  other arithmetic  13.6 us (7%)
  matrix products  5.53 us (3%)
    ppermute x21, waiting for transfers between devices, ring_exchange(): return lax.ppermute(block, RING, [(i, step(i)) for i in range(size)])  48.1 us
    pallas_call x4, Pallas kernels, run_section(): pl.pallas_call(partial(section_kernel, layout, forward, backward, len(aft...  27.3 us
    ppermute x21, starting transfers between devices, ring_exchange(): return lax.ppermute(block, RING, [(i, step(i)) for i in range(size)])  23.9 us
    all_to_all x1, waiting for transfers between devices, per_device(): lax.all_to_all(rows_back[:, None], ('section', 'dp', 'seq'), 0, 0, tiled=...  17.4 us
    unnamed x82, local copies, waits for them, and re-layouts  14.5 us
    pallas_call x11, Pallas kernels, in_memory(): pl.pallas_call(body, out_shape=shapes, in_specs=specs, out_specs=[pl.Bloc...  14.1 us
    ppermute x10, starting transfers between devices, pair_swap(): return lax.ppermute(block, axis, [(0, 1), (1, 0)])  8.42 us
    all_to_all x1, waiting for transfers between devices, per_device(): lax.all_to_all(products[:, None], ('section', 'dp', 'seq'), 0, 0, tiled=T...  7.08 us
  transfers between devices with their start and end apart: 34, of which 16 were waited for; matrix products, arithmetic and copies ran while one was open for 14% of the time, Pallas kernels for 15%

profile of v7, /device:TPU:9, one launch (start us, length us, event | category | flops | bytes accessed | tf_op | source)
XLA Modules:
  0.0 204.9 jit_solution(12847603682066940963)
XLA Ops:
  3.2 1.6 shard_map.178
  7.9 1.3 collective-permute-start.2
  10.4 1.4 collective-permute-start.4
  12.3 6.2 %collective-permute-done.3.refs_3_ = bf16[24,2304]{1,0:T(8,128)(2,1)S(1)} collective-permute-done((bf16[24,2304]{1,0:T(8,128)(2,1)S(1)}, bf16[24,2304]{1,0:T(8,128)(2,1)S(1)}, u32[]{:S(2)}, u32[]{:S(2)}) %collective-permute-start.3) | collective-permute-done | bytes 110624 | tf_op jit(solution)/shard_map/ppermute | solution.py:544
  18.5 2.4 %collective-permute-done.4.refs_4_ = bf16[24,2304]{1,0:T(8,128)(2,1)S(1)} collective-permute-done((bf16[24,2304]{1,0:T(8,128)(2,1)S(1)}, bf16[24,2304]{1,0:T(8,128)(2,1)S(1)}, u32[]{:S(2)}, u32[]{:S(2)}) %collective-permute-start.4) | collective-permute-done | bytes 110624 | tf_op jit(solution)/shard_map/ppermute | solution.py:544
  24.5 3.7 %all-to-all-start = ((f32[32,1,2640]{2,1,0:T(1,128)}), f32[32,1,2640]{2,1,0:T(1,128)}, u32[]{:S(2)}, u32[]{:S(2)}) async-start(f32[32,1,2640]{2,1,0:T(1,128)} %copy.35), calls=%async_computation | async-start | bytes 688128 | tf_op jit(solution)/shard_map/all_to_all | solution.py:754
  35.9 7.1 %all-to-all-done = f32[32,1,2640]{2,1,0:T(1,128)} async-done(((f32[32,1,2640]{2,1,0:T(1,128)}), f32[32,1,2640]{2,1,0:T(1,128)}, u32[]{:S(2)}, u32[]{:S(2)}) %all-to-all-start) | async-done | bytes 337952 | tf_op jit(solution)/shard_map/all_to_all | solution.py:754
  45.3 1.9 collective-permute-done.12.refs_4_
  51.2 12.8 %collective-permute-done.8.refs_5_ = bf16[4,24,1152]{2,1,0:T(8,128)(2,1)S(1)} collective-permute-done((bf16[4,24,1152]{2,1,0:T(8,128)(2,1)S(1)}, bf16[4,24,1152]{2,1,0:T(8,128)(2,1)S(1)}, u32[]{:S(2)}, u32[]{:S(2)}) %collective-permute-start.8) | collective-permute-done | bytes 221216 | tf_op jit(solution)/shard_map/ppermute | solution.py:544
  66.9 1.8 collective-permute-start.9
  71.3 4.5 %collective-permute-done.15.refs_4_ = bf16[4,24,1152]{2,1,0:T(8,128)(2,1)S(1)} collective-permute-done((bf16[4,24,1152]{2,1,0:T(8,128)(2,1)S(1)}, bf16[4,24,1152]{2,1,0:T(8,128)(2,1)S(1)}, u32[]{:S(2)}, u32[]{:S(2)}) %collective-permute-start.15) | collective-permute-done | bytes 221216 | tf_op jit(solution)/shard_map/ppermute | solution.py:544
  76.9 2.1 %shard_map.183 = bf16[4,2,2,24,2304]{4,3,2,1,0:T(8,128)(2,1)} custom-call(s32[3]{0:T(128)S(1)} %pad_add_fusion.refs_0_, bf16[2,4,24,1152]{3,2,1,0:T(8,128)(2,1)S(1)} %shard_map.182.refs_1_, bf16[2,4,24,1152]{3,2,1,0:T(8,128)(2,1)S(1)} %collective-permute-done.13.refs_2_, bf16[2,4,24,1152]{3,2,1,0:T(8,128)(2,1)S(1)} %collective-permute-done.14.refs_3_, ...), custom_call_target="tpu_custom_call" | custom-call | bytes 5308416 | tf_op jit(solution)/shard_map/pallas_call | solution.py:528
  81.5 5.6 %shard_map.181 = (bf16[256,384]{1,0:T(8,128)(2,1)S(1)}, f32[1,2304]{1,0:T(1,128)S(1)}, bf16[256,1152]{1,0:T(8,128)(2,1)S(1)}, bf16[256,384]{1,0:T(8,128)(2,1)S(1...) custom-call(s32[1]{0:T(128)} %bitcast.refs_0_, ...), custom_call_target="tpu_custom_call" | custom-call | flops 1006632960 | bytes 5308416 | tf_op jit(solution)/shard_map/pallas_call | solution.py:352
  87.2 5.8 %shard_map.184 = (bf16[256,384]{1,0:T(8,128)(2,1)S(1)}, f32[1,2304]{1,0:T(1,128)S(1)}, bf16[256,1152]{1,0:T(8,128)(2,1)S(1)}, bf16[256,384]{1,0:T(8,128)(2,1)S(1...) custom-call(s32[1]{0:T(128)} %bitcast.refs_0_, ...), custom_call_target="tpu_custom_call" | custom-call | flops 1006632960 | bytes 5308416 | tf_op jit(solution)/shard_map/pallas_call | solution.py:352
  94.0 8.3 %shard_map.185 = (bf16[256,384]{1,0:T(8,128)(2,1)S(1)}, f32[1,2304]{1,0:T(1,128)S(1)}, f32[16,336]{1,0:T(8,128)S(1)}, bf16[384,2304]{1,0:T(8,128)(2,1)S(1)}, bf16[384,2304]{1,0:T(8,128)(2,1)}) custom-call(s32[1]{0:T(128)} %bitcast.refs_0_, bf16[256,384]{1,0:T(8,128)(2,1)S(1)} %get-tuple-element.69.refs_1_, f32[1,2304]{1,0:T(1,128)S(1)} %get-tuple-element.81.refs_2_, ...), custom_call_target="tpu_custom_call" | custom-call | flops 2013265920 | bytes 10616832 | tf_op jit(solution)/shard_map/pallas_call | solution.py:352
  103.6 7.6 %shard_map.186 = (bf16[256,384]{1,0:T(8,128)(2,1)S(1)}, f32[1,2304]{1,0:T(1,128)S(1)}, f32[16,336]{1,0:T(8,128)S(1)}, bf16[384,2304]{1,0:T(8,128)(2,1)S(1)}, bf16[384,2304]{1,0:T(8,128)(2,1)}) custom-call(s32[1]{0:T(128)} %bitcast.refs_0_, bf16[256,384]{1,0:T(8,128)(2,1)S(1)} %get-tuple-element.155.refs_1_, f32[1,2304]{1,0:T(1,128)S(1)} %get-tuple-element.72.refs_2_, ...), custom_call_target="tpu_custom_call" | custom-call | flops 2013265920 | bytes 10616832 | tf_op jit(solution)/shard_map/pallas_call | solution.py:352
  113.2 1.5 copy-done.6
  114.7 2.0 shard_map.187.refs_3_
  117.0 2.0 shard_map.188
  123.4 3.7 %all-to-all-start.1 = ((f32[32,1,2640]{2,1,0:T(1,128)}), f32[32,1,2640]{2,1,0:T(1,128)}, u32[]{:S(2)}, u32[]{:S(2)}) async-start(f32[32,1,2640]{2,1,0:T(1,128)} %broadcast_in_dim.65), calls=%async_computation.1 | async-start | bytes 688128 | tf_op jit(solution)/shard_map/all_to_all | solution.py:878
  127.2 2.0 maximum_select_fusion.2
  129.2 17.4 %all-to-all-done.1 = f32[32,1,2640]{2,1,0:T(1,128)} async-done(((f32[32,1,2640]{2,1,0:T(1,128)}), f32[32,1,2640]{2,1,0:T(1,128)}, u32[]{:S(2)}, u32[]{:S(2)}) %all-to-all-start.1) | async-done | bytes 337952 | tf_op jit(solution)/shard_map/all_to_all | solution.py:878
  148.6 1.6 shard_map.189
  155.7 3.9 %all-to-all-start.2 = ((f32[32,1,768]{2,1,0:T(1,128)}), f32[32,1,768]{2,1,0:T(1,128)S(1)}, u32[]{:S(2)}, u32[]{:S(2)}) async-start(f32[32,1,768]{2,1,0:T(1,128)} %broadcast_in_dim.67), calls=%async_computation.2 | async-start | bytes 196608 | tf_op jit(solution)/shard_map/all_to_all | solution.py:885
  159.6 1.9 convolution_bitcast_fusion
  170.5 1.9 reduce_sum.28
  172.3 1.8 copy.42
  174.2 1.7 reshape.208
  175.9 3.1 %fusion.15 = f32[1000,384]{1,0:T(8,128)} fusion(s32[32]{0:T(128)S(1)} %eq.25, f32[32,384]{1,0:T(8,128)S(1)} %copy-done.34, f32[32,384]{1,0:T(8,128)} %reshape.208), kind=kOutput, calls=%fused_computation.53 | convolution fusion | flops 147598592 | bytes 1634432 | tf_op jit(solution)/shard_map/dot_general | solution.py:889
  184.8 2.1 %collective-permute-done.27.refs_2_ = bf16[2,24,2304]{2,1,0:T(8,128)(2,1)S(1)} collective-permute-done((bf16[2,24,2304]{2,1,0:T(8,128)(2,1)S(1)}, bf16[2,24,2304]{2,1,0:T(8,128)(2,1)S(1)}, u32[]{:S(2)}, u32[]{:S(2)}) %collective-permute-start.27) | collective-permute-done | bytes 221216 | tf_op jit(solution)/shard_map/ppermute | solution.py:544
  186.8 13.2 %collective-permute-done.28.refs_3_ = bf16[2,24,2304]{2,1,0:T(8,128)(2,1)S(1)} collective-permute-done((bf16[2,24,2304]{2,1,0:T(8,128)(2,1)S(1)}, bf16[2,24,2304]{2,1,0:T(8,128)(2,1)S(1)}, u32[]{:S(2)}, u32[]{:S(2)}) %collective-permute-start.28) | collective-permute-done | bytes 221216 | tf_op jit(solution)/shard_map/ppermute | solution.py:544
  200.1 2.2 %collective-permute-done.29.refs_4_ = bf16[2,24,2304]{2,1,0:T(8,128)(2,1)S(1)} collective-permute-done((bf16[2,24,2304]{2,1,0:T(8,128)(2,1)S(1)}, bf16[2,24,2304]{2,1,0:T(8,128)(2,1)S(1)}, u32[]{:S(2)}, u32[]{:S(2)}) %collective-permute-start.29) | collective-permute-done | bytes 221216 | tf_op jit(solution)/shard_map/ppermute | solution.py:544
  (183 shorter events, 66.8 us)
Async XLA Ops:
  1.9 26.3 %collective-permute-start = (bf16[2,128,384]{2,1,0:T(8,128)(2,1)S(1)}, bf16[2,128,384]{2,1,0:T(8,128)(2,1)S(1)}, u32[]{:S(2)}, u32[]{:S(2)}) collective-permute-start(bf16[2,128,384]{2,1,0:T(8,128)(2,1)S(1)} %get-tuple-element.157), channel_id=1, source_target_pairs={{0,1},{1,0},{2,3},{3,2},{4,5},{5,4},{6,7},{7,6},{8,9},{9,8},{10,11... | collective-permute-start | bytes 589832 | tf_op jit(solution)/shard_map/ppermute | solution.py:540
  7.9 4.3 %collective-permute-start.2 = (bf16[24,2304]{1,0:T(8,128)(2,1)S(1)}, bf16[24,2304]{1,0:T(8,128)(2,1)S(1)}, u32[]{:S(2)}, u32[]{:S(2)}) collective-permute-start(bf16[24,2304]{1,0:T(8,128)(2,1)S(1)} %get-tuple-element.161.refs_1_), channel_id=1, source_target_pairs={{0,4},{1,5},{2,6},{3,7},{4,8},{5,9},{6,10},{7,11},{8,12},{9,13},{1... | collective-permute-start | bytes 331784 | tf_op jit(solution)/shard_map/ppermute | solution.py:544
  9.3 9.2 %collective-permute-start.3 = (bf16[24,2304]{1,0:T(8,128)(2,1)S(1)}, bf16[24,2304]{1,0:T(8,128)(2,1)S(1)}, u32[]{:S(2)}, u32[]{:S(2)}) collective-permute-start(bf16[24,2304]{1,0:T(8,128)(2,1)S(1)} %get-tuple-element.161.refs_1_), channel_id=1, source_target_pairs={{0,8},{1,9},{2,10},{3,11},{4,12},{5,13},{6,14},{7,15},{8,0},{9,1},... | collective-permute-start | bytes 331784 | tf_op jit(solution)/shard_map/ppermute | solution.py:544
  10.4 10.6 %collective-permute-start.4 = (bf16[24,2304]{1,0:T(8,128)(2,1)S(1)}, bf16[24,2304]{1,0:T(8,128)(2,1)S(1)}, u32[]{:S(2)}, u32[]{:S(2)}) collective-permute-start(bf16[24,2304]{1,0:T(8,128)(2,1)S(1)} %get-tuple-element.161.refs_1_), channel_id=1, source_target_pairs={{0,12},{1,13},{2,14},{3,15},{4,0},{5,1},{6,2},{7,3},{8,4},{9,5},{1... | collective-permute-start | bytes 331784 | tf_op jit(solution)/shard_map/ppermute | solution.py:544
  21.9 13.0 %collective-permute-start.5 = (bf16[2,4,24,1152]{3,2,1,0:T(8,128)(2,1)S(1)}, bf16[2,4,24,1152]{3,2,1,0:T(8,128)(2,1)S(1)}, u32[]{:S(2)}, u32[]{:S(2)}) collective-permute-start(bf16[2,4,24,1152]{3,2,1,0:T(8,128)(2,1)S(1)} %get-tuple-element.68.refs_1_), channel_id=1, source_target_pairs={{0,2},{1,3},{2,0},{3,1},{4,6},{5,7},{6,4},{7,5},{8,10},{9,11},{10,... | collective-permute-start | bytes 1327112 | tf_op jit(solution)/shard_map/ppermute | solution.py:544
  24.5 18.5 %all-to-all-start = ((f32[32,1,2640]{2,1,0:T(1,128)}), f32[32,1,2640]{2,1,0:T(1,128)}, u32[]{:S(2)}, u32[]{:S(2)}) async-start(f32[32,1,2640]{2,1,0:T(1,128)} %copy.35), calls=%async_computation | async-start | bytes 688128 | tf_op jit(solution)/shard_map/all_to_all | solution.py:754
  30.0 17.1 %collective-permute-start.6 = (bf16[2,4,24,1152]{3,2,1,0:T(8,128)(2,1)S(1)}, bf16[2,4,24,1152]{3,2,1,0:T(8,128)(2,1)S(1)}, u32[]{:S(2)}, u32[]{:S(2)}) collective-permute-start(bf16[2,4,24,1152]{3,2,1,0:T(8,128)(2,1)S(1)} %get-tuple-element.68.refs_1_), channel_id=1, source_target_pairs={{0,1},{1,0},{2,3},{3,2},{4,5},{5,4},{6,7},{7,6},{8,9},{9,8},{10,11... | collective-permute-start | bytes 1327112 | tf_op jit(solution)/shard_map/ppermute | solution.py:544
  31.3 12.8 %collective-permute-start.10 = (bf16[24,2304]{1,0:T(8,128)(2,1)S(1)}, bf16[24,2304]{1,0:T(8,128)(2,1)S(1)}, u32[]{:S(2)}, u32[]{:S(2)}) collective-permute-start(bf16[24,2304]{1,0:T(8,128)(2,1)S(1)} %get-tuple-element.70.refs_1_), channel_id=1, source_target_pairs={{0,4},{1,5},{2,6},{3,7},{4,8},{5,9},{6,10},{7,11},{8,12},{9,13},{1... | collective-permute-start | bytes 331784 | tf_op jit(solution)/shard_map/ppermute | solution.py:544
  32.5 12.8 %collective-permute-start.11 = (bf16[24,2304]{1,0:T(8,128)(2,1)S(1)}, bf16[24,2304]{1,0:T(8,128)(2,1)S(1)}, u32[]{:S(2)}, u32[]{:S(2)}) collective-permute-start(bf16[24,2304]{1,0:T(8,128)(2,1)S(1)} %get-tuple-element.70.refs_1_), channel_id=1, source_target_pairs={{0,8},{1,9},{2,10},{3,11},{4,12},{5,13},{6,14},{7,15},{8,0},{9,1},... | collective-permute-start | bytes 331784 | tf_op jit(solution)/shard_map/ppermute | solution.py:544
  33.6 13.5 %collective-permute-start.12 = (bf16[24,2304]{1,0:T(8,128)(2,1)S(1)}, bf16[24,2304]{1,0:T(8,128)(2,1)}, u32[]{:S(2)}, u32[]{:S(2)}) collective-permute-start(bf16[24,2304]{1,0:T(8,128)(2,1)S(1)} %get-tuple-element.70.refs_1_), channel_id=1, source_target_pairs={{0,12},{1,13},{2,14},{3,15},{4,0},{5,1},{6,2},{7,3},{8,4},{9,5},{1... | collective-permute-start | bytes 331784 | tf_op jit(solution)/shard_map/ppermute | solution.py:544
  35.7 15.5 %collective-permute-start.7 = (bf16[4,24,1152]{2,1,0:T(8,128)(2,1)}, bf16[4,24,1152]{2,1,0:T(8,128)(2,1)S(1)}, u32[]{:S(2)}, u32[]{:S(2)}) collective-permute-start(bf16[4,24,1152]{2,1,0:T(8,128)(2,1)} %slice_bitcast_fusion.5), channel_id=1, source_target_pairs={{0,1},{1,0},{2,3},{3,2},{4,5},{5,4},{6,7},{7,6},{8,9},{9,8},{10,11... | collective-permute-start | bytes 663560 | tf_op jit(solution)/shard_map/ppermute | solution.py:544
  48.4 20.3 %collective-permute-start.13 = (bf16[2,4,24,1152]{3,2,1,0:T(8,128)(2,1)S(1)}, bf16[2,4,24,1152]{3,2,1,0:T(8,128)(2,1)S(1)}, u32[]{:S(2)}, u32[]{:S(2)}) collective-permute-start(bf16[2,4,24,1152]{3,2,1,0:T(8,128)(2,1)S(1)} %shard_map.182.refs_1_), channel_id=1, source_target_pairs={{0,2},{1,3},{2,0},{3,1},{4,6},{5,7},{6,4},{7,5},{8,10},{9,11},{10,... | collective-permute-start | bytes 1327112 | tf_op jit(solution)/shard_map/ppermute | solution.py:544
  49.7 14.3 %collective-permute-start.8 = (bf16[4,24,1152]{2,1,0:T(8,128)(2,1)S(1)}, bf16[4,24,1152]{2,1,0:T(8,128)(2,1)S(1)}, u32[]{:S(2)}, u32[]{:S(2)}) collective-permute-start(bf16[4,24,1152]{2,1,0:T(8,128)(2,1)S(1)} %slice_bitcast_fusion.4), channel_id=1, source_target_pairs={{0,2},{1,3},{2,0},{3,1},{4,6},{5,7},{6,4},{7,5},{8,10},{9,11},{10,... | collective-permute-start | bytes 663560 | tf_op jit(solution)/shard_map/ppermute | solution.py:544
  50.0 20.0 %collective-permute-start.14 = (bf16[2,4,24,1152]{3,2,1,0:T(8,128)(2,1)S(1)}, bf16[2,4,24,1152]{3,2,1,0:T(8,128)(2,1)S(1)}, u32[]{:S(2)}, u32[]{:S(2)}) collective-permute-start(bf16[2,4,24,1152]{3,2,1,0:T(8,128)(2,1)S(1)} %shard_map.182.refs_1_), channel_id=1, source_target_pairs={{0,1},{1,0},{2,3},{3,2},{4,5},{5,4},{6,7},{7,6},{8,9},{9,8},{10,11... | collective-permute-start | bytes 1327112 | tf_op jit(solution)/shard_map/ppermute | solution.py:544
  66.9 14.6 %collective-permute-start.9 = (bf16[384,2304]{1,0:T(8,128)(2,1)S(1)}, bf16[384,2304]{1,0:T(8,128)(2,1)}, u32[]{:S(2)}, u32[]{:S(2)}) collective-permute-start(bf16[384,2304]{1,0:T(8,128)(2,1)S(1)} %bitcast.96), channel_id=1, source_target_pairs={{0,16},{16,0},{1,17},{17,1},{2,18},{18,2},{3,19},{19,3},{4,20},{20... | collective-permute-start | bytes 5308424 | tf_op jit(solution)/shard_map/ppermute | solution.py:540
  68.8 7.1 %collective-permute-start.15 = (bf16[4,24,1152]{2,1,0:T(8,128)(2,1)S(1)}, bf16[4,24,1152]{2,1,0:T(8,128)(2,1)S(1)}, u32[]{:S(2)}, u32[]{:S(2)}) collective-permute-start(bf16[4,24,1152]{2,1,0:T(8,128)(2,1)S(1)} %slice_bitcast_fusion.3), channel_id=1, source_target_pairs={{0,1},{1,0},{2,3},{3,2},{4,5},{5,4},{6,7},{7,6},{8,9},{9,8},{10,11... | collective-permute-start | bytes 663560 | tf_op jit(solution)/shard_map/ppermute | solution.py:544
  70.1 6.8 %collective-permute-start.16 = (bf16[4,24,1152]{2,1,0:T(8,128)(2,1)S(1)}, bf16[4,24,1152]{2,1,0:T(8,128)(2,1)S(1)}, u32[]{:S(2)}, u32[]{:S(2)}) collective-permute-start(bf16[4,24,1152]{2,1,0:T(8,128)(2,1)S(1)} %slice_bitcast_fusion.2), channel_id=1, source_target_pairs={{0,2},{1,3},{2,0},{3,1},{4,6},{5,7},{6,4},{7,5},{8,10},{9,11},{10,... | collective-permute-start | bytes 663560 | tf_op jit(solution)/shard_map/ppermute | solution.py:544
  79.0 8.3 %collective-permute-start.17 = (bf16[384,2304]{1,0:T(8,128)(2,1)}, bf16[384,2304]{1,0:T(8,128)(2,1)}, u32[]{:S(2)}, u32[]{:S(2)}) collective-permute-start(bf16[384,2304]{1,0:T(8,128)(2,1)} %bitcast.24.refs_4_.refs_12_), channel_id=1, source_target_pairs={{0,16},{16,0},{1,17},{17,1},{2,18},{18,2},{3,19},{19,3},{4,20},{20... | collective-permute-start | bytes 5308424 | tf_op jit(solution)/shard_map/ppermute | solution.py:540
  93.7 9.8 %collective-permute-start.18 = (bf16[2,1,128,384]{3,2,1,0:T(8,128)(2,1)S(1)}, bf16[2,1,128,384]{3,2,1,0:T(8,128)(2,1)S(1)}, u32[]{:S(2)}, u32[]{:S(2)}) collective-permute-start(bf16[2,1,128,384]{3,2,1,0:T(8,128)(2,1)S(1)} %get-tuple-element.151), channel_id=1, source_target_pairs={{0,1},{1,0},{2,3},{3,2},{4,5},{5,4},{6,7},{7,6},{8,9},{9,8},{10,11... | collective-permute-start | bytes 589832 | tf_op jit(solution)/shard_map/ppermute | solution.py:540
  103.6 9.6 %collective-permute-start.20 = (bf16[384,2304]{1,0:T(8,128)(2,1)}, bf16[384,2304]{1,0:T(8,128)(2,1)}, u32[]{:S(2)}, u32[]{:S(2)}) collective-permute-start(bf16[384,2304]{1,0:T(8,128)(2,1)} %get-tuple-element.94), channel_id=1, source_target_pairs={{0,16},{16,0},{1,17},{17,1},{2,18},{18,2},{3,19},{19,3},{4,20},{20... | collective-permute-start | bytes 5308424 | tf_op jit(solution)/shard_map/ppermute | solution.py:540
  113.1 3.9 %collective-permute-start.19 = (bf16[384,2304]{1,0:T(8,128)(2,1)}, bf16[384,2304]{1,0:T(8,128)(2,1)S(1)}, u32[]{:S(2)}, u32[]{:S(2)}) collective-permute-start(bf16[384,2304]{1,0:T(8,128)(2,1)} %get-tuple-element.92), channel_id=1, source_target_pairs={{0,16},{16,0},{1,17},{17,1},{2,18},{18,2},{3,19},{19,3},{4,20},{20... | collective-permute-start | bytes 5308424 | tf_op jit(solution)/shard_map/ppermute | solution.py:540
  119.9 27.6 %collective-permute-start.21 = (bf16[4,2,2,24,1152]{4,3,2,1,0:T(8,128)(2,1)}, bf16[4,2,2,24,1152]{4,3,2,1,0:T(8,128)(2,1)S(1)}, u32[]{:S(2)}, u32[]{:S(2)}) collective-permute-start(bf16[4,2,2,24,1152]{4,3,2,1,0:T(8,128)(2,1)} %get-tuple-element.98), channel_id=1, source_target_pairs={{0,2},{1,3},{2,0},{3,1},{4,6},{5,7},{6,4},{7,5},{8,10},{9,11},{10,... | collective-permute-start | bytes 2654216 | tf_op jit(solution)/shard_map/ppermute | solution.py:544
  121.1 26.5 %collective-permute-start.22 = (bf16[4,2,2,24,1152]{4,3,2,1,0:T(8,128)(2,1)}, bf16[4,2,2,24,1152]{4,3,2,1,0:T(8,128)(2,1)}, u32[]{:S(2)}, u32[]{:S(2)}) collective-permute-start(bf16[4,2,2,24,1152]{4,3,2,1,0:T(8,128)(2,1)} %get-tuple-element.100), channel_id=1, source_target_pairs={{0,1},{1,0},{2,3},{3,2},{4,5},{5,4},{6,7},{7,6},{8,9},{9,8},{10,11... | collective-permute-start | bytes 2654216 | tf_op jit(solution)/shard_map/ppermute | solution.py:544
  123.4 23.1 %all-to-all-start.1 = ((f32[32,1,2640]{2,1,0:T(1,128)}), f32[32,1,2640]{2,1,0:T(1,128)}, u32[]{:S(2)}, u32[]{:S(2)}) async-start(f32[32,1,2640]{2,1,0:T(1,128)} %broadcast_in_dim.65), calls=%async_computation.1 | async-start | bytes 688128 | tf_op jit(solution)/shard_map/all_to_all | solution.py:878
  153.4 10.4 %collective-permute-start.23 = (bf16[2,1,128,384]{3,2,0,1:T(8,128)(2,1)S(1)}, bf16[2,1,128,384]{3,2,0,1:T(8,128)(2,1)S(1)}, u32[]{:S(2)}, u32[]{:S(2)}) collective-permute-start(bf16[2,1,128,384]{3,2,0,1:T(8,128)(2,1)S(1)} %get-tuple-element.153), channel_id=1, source_target_pairs={{0,1},{1,0},{2,3},{3,2},{4,5},{5,4},{6,7},{7,6},{8,9},{9,8},{10,11... | collective-permute-start | bytes 589832 | tf_op jit(solution)/shard_map/ppermute | solution.py:540
  155.7 13.3 %all-to-all-start.2 = ((f32[32,1,768]{2,1,0:T(1,128)}), f32[32,1,768]{2,1,0:T(1,128)S(1)}, u32[]{:S(2)}, u32[]{:S(2)}) async-start(f32[32,1,768]{2,1,0:T(1,128)} %broadcast_in_dim.67), calls=%async_computation.2 | async-start | bytes 196608 | tf_op jit(solution)/shard_map/all_to_all | solution.py:885
  161.5 17.5 %collective-permute-start.25 = (bf16[4,2,24,1152]{3,2,1,0:T(8,128)(2,1)S(1)}, bf16[4,2,24,1152]{3,2,1,0:T(8,128)(2,1)S(1)}, u32[]{:S(2)}, u32[]{:S(2)}) collective-permute-start(bf16[4,2,24,1152]{3,2,1,0:T(8,128)(2,1)S(1)} %copy-done.25), channel_id=1, source_target_pairs={{0,1},{1,0},{2,3},{3,2},{4,5},{5,4},{6,7},{7,6},{8,9},{9,8},{10,11... | collective-permute-start | bytes 1327112 | tf_op jit(solution)/shard_map/ppermute | solution.py:544
  162.7 16.3 %collective-permute-start.26 = (bf16[4,2,24,1152]{3,2,1,0:T(8,128)(2,1)S(1)}, bf16[4,2,24,1152]{3,2,1,0:T(8,128)(2,1)S(1)}, u32[]{:S(2)}, u32[]{:S(2)}) collective-permute-start(bf16[4,2,24,1152]{3,2,1,0:T(8,128)(2,1)S(1)} %copy-done.23), channel_id=1, source_target_pairs={{0,2},{1,3},{2,0},{3,1},{4,6},{5,7},{6,4},{7,5},{8,10},{9,11},{10,... | collective-permute-start | bytes 1327112 | tf_op jit(solution)/shard_map/ppermute | solution.py:544
  166.7 16.8 %collective-permute-start.24 = (bf16[2,2,128,384]{3,2,1,0:T(8,128)(2,1)}, bf16[2,2,128,384]{3,2,1,0:T(8,128)(2,1)}, u32[]{:S(2)}, u32[]{:S(2)}) collective-permute-start(bf16[2,2,128,384]{3,2,1,0:T(8,128)(2,1)} %fusion), channel_id=1, source_target_pairs={{0,16},{16,0},{1,17},{17,1},{2,18},{18,2},{3,19},{19,3},{4,20},{20... | collective-permute-start | bytes 1179656 | tf_op jit(solution)/shard_map/ppermute | solution.py:540
  179.7 7.1 %collective-permute-start.27 = (bf16[2,24,2304]{2,1,0:T(8,128)(2,1)S(1)}, bf16[2,24,2304]{2,1,0:T(8,128)(2,1)S(1)}, u32[]{:S(2)}, u32[]{:S(2)}) collective-permute-start(bf16[2,24,2304]{2,1,0:T(8,128)(2,1)S(1)} %get-tuple-element.112), channel_id=1, source_target_pairs={{0,4},{1,5},{2,6},{3,7},{4,8},{5,9},{6,10},{7,11},{8,12},{9,13},{1... | collective-permute-start | bytes 663560 | tf_op jit(solution)/shard_map/ppermute | solution.py:544
  181.0 19.1 %collective-permute-start.28 = (bf16[2,24,2304]{2,1,0:T(8,128)(2,1)S(1)}, bf16[2,24,2304]{2,1,0:T(8,128)(2,1)S(1)}, u32[]{:S(2)}, u32[]{:S(2)}) collective-permute-start(bf16[2,24,2304]{2,1,0:T(8,128)(2,1)S(1)} %get-tuple-element.113), channel_id=1, source_target_pairs={{0,8},{1,9},{2,10},{3,11},{4,12},{5,13},{6,14},{7,15},{8,0},{9,1},... | collective-permute-start | bytes 663560 | tf_op jit(solution)/shard_map/ppermute | solution.py:544
  182.1 20.2 %collective-permute-start.29 = (bf16[2,24,2304]{2,1,0:T(8,128)(2,1)S(1)}, bf16[2,24,2304]{2,1,0:T(8,128)(2,1)S(1)}, u32[]{:S(2)}, u32[]{:S(2)}) collective-permute-start(bf16[2,24,2304]{2,1,0:T(8,128)(2,1)S(1)} %get-tuple-element.114), channel_id=1, source_target_pairs={{0,12},{1,13},{2,14},{3,15},{4,0},{5,1},{6,2},{7,3},{8,4},{9,5},{1... | collective-permute-start | bytes 663560 | tf_op jit(solution)/shard_map/ppermute | solution.py:544
  (42 other events, 279.3 us)

commit v8 on v6

--- a/solution.py
+++ b/solution.py
@@ -356,7 +356,9 @@
         out_specs=out_specs,
         scratch_shapes=scratch,
         compiler_params=pltpu.CompilerParams(
-            vmem_limit_bytes=(36 if length <= 256 else 56) * 1024 * 1024
+            vmem_limit_bytes=(56 if length > 256 else 26 if forward and backward else 22)
+            * 1024
+            * 1024
         ),
         cost_estimate=pl.CostEstimate(
             flops=(forward + 2 * backward) * work,
@@ -453,9 +455,12 @@
 
 
 def turn_kernel(high, place_ref, *refs):
+    count = (len(refs) - 8) // 2
+    for former, latter in zip(refs[4 : 4 + count], refs[8 + count :]):
+        latter[...] = former[...]
     for part, own in ((0, place_ref[2]), (1, place_ref[1])):
         kept, got = refs[2 * part : 2 * part + 2]
-        keep, send = refs[4 + 2 * part : 6 + 2 * part]
+        keep, send = refs[4 + count + 2 * part : 6 + count + 2 * part]
         for z in range(high):
             keep[z] = low(added(kept[z, own], got[z, own]))
             send[z] = low(added(kept[z, 1 - own], got[z, 1 - own]))
@@ -501,7 +506,7 @@
         down_ref[j * rows : (j + 1) * rows, :] = upper[:, (2 + j) * width : (3 + j) * width]
 
 
-def in_memory(kernel, shapes, operands, scratch=(), memory=pltpu.VMEM, after=(), limit=32):
+def in_memory(kernel, shapes, operands, scratch=(), memory=pltpu.VMEM, after=(), limit=16):
     specs = [pl.BlockSpec(memory_space=pltpu.SMEM)]
     specs += [pl.BlockSpec(memory_space=memory)] * (len(operands) - 1)
     specs += [pl.BlockSpec(memory_space=pl.ANY)] * len(after)
@@ -588,25 +593,33 @@
     return first_keep, flip(first_send, size, 2), second_keep, flip(second_send, size, 1)
 
 
-def scatter_second(received, place, size, after=()):
+def scatter_second(received, place, size, handed=(), after=()):
     high, _, rows, lanes = received[0].shape
     shape = jax.ShapeDtypeStruct((high, rows, lanes), jnp.bfloat16)
+    first_keep, first_send, second_keep, second_send, *handed = in_memory(
+        partial(turn_kernel, high),
+        [shape] * 4 + [jax.ShapeDtypeStruct(block.shape, block.dtype) for block in handed],
+        [place, *received, *handed],
+        after=after,
+    )
+    turned = (first_keep, flip(first_send, size, 1), second_keep, flip(second_send, size, 2))
+    return turned, handed
+
+
+def scatter_third(turned, place, size, after=()):
+    high, rows, lanes = turned[0].shape
+    chunk = (rows, 2 * lanes)
     return in_memory(
-        partial(turn_kernel, high), [shape] * 4, [place, *received], after=after
-    )
-
-
-def scatter_rest(turned, place, size):
-    high, rows, lanes = turned[0].shape
-    first_keep, first_send, second_keep, second_send = turned
-    first_got, second_got = flip(first_send, size, 1), flip(second_send, size, 2)
-    chunk = (rows, 2 * lanes)
-    own, *sent = in_memory(
         partial(rise_kernel, high),
         [jax.ShapeDtypeStruct(chunk, jnp.float32)]
         + [jax.ShapeDtypeStruct(chunk, jnp.bfloat16)] * (high - 1),
-        [place, first_keep, first_got, second_keep, second_got],
-    )
+        [place, *turned],
+        after=after,
+    )
+
+
+def scatter_along_z(pieces, size):
+    own, *sent = pieces
     return [own] + [rotate(block, size, turn + 1) for turn, block in enumerate(sent)]
 
 
@@ -743,18 +756,8 @@
             first_shard, place, ring_size, handed=(second_shard, silu_own)
         )
         first_parts += first_flips(*first_parts, ring_size)
-        second_parts = gather_along_z(
-            second_shard, place, ring_size, after=(both, *first_parts[2:])
-        )
-        second_parts += first_flips(*second_parts, ring_size)
-        first_pack = gather_across(*first_parts, place, ring_size)
-        second_pack = gather_across(*second_parts, place, ring_size)
     else:
         silu_late = silu_own
-        first_pack = lax.all_gather(first_shard, RING, axis=0, tiled=True)
-        second_pack = lax.all_gather(second_shard, RING, axis=0, tiled=True)
-    first_halves = (first_pack, pair_swap(first_pack, "section"))
-    second_halves = (second_pack, pair_swap(second_pack, "section"))
 
     products = matmul(silu_late, modulation_weight[0])
     own_bias = jnp.broadcast_to(biases.astype(jnp.float32), (products.shape[0], bias_count))
@@ -767,6 +770,18 @@
     )
     first_bias, second_bias = products[0, :, 6 * width :], products[1, :, 6 * width :]
 
+    if compact:
+        second_parts = gather_along_z(
+            second_shard, place, ring_size, after=(products, both, *first_parts[2:])
+        )
+        second_parts += first_flips(*second_parts, ring_size)
+        first_pack = gather_across(*first_parts, place, ring_size)
+        second_pack = gather_across(*second_parts, place, ring_size)
+    else:
+        first_pack = lax.all_gather(first_shard, RING, axis=0, tiled=True)
+        second_pack = lax.all_gather(second_shard, RING, axis=0, tiled=True)
+    first_halves = (first_pack, pair_swap(first_pack, "section"))
+    second_halves = (second_pack, pair_swap(second_pack, "section"))
 
     first_low, *first_saved = run_section(
         layout, rank, first_input, first_halves, (first_modulation, first_bias)
@@ -779,16 +794,6 @@
     def ring_terms(term):
         return term.reshape(ring_size, rows, half)
 
-    early = jnp.stack([first_low * live, second_low * live, second_grad])
-
-    def to_slots(block):
-        block = block.reshape(-1, 2, tokens, width)
-        mine = lax.dynamic_index_in_dim(block, seq_rank, 1, keepdims=True)
-        sent = lax.dynamic_index_in_dim(block, 1 - seq_rank, 1, keepdims=True)
-        return mine, pair_swap(sent, "seq")
-
-    if compact:
-        early = to_slots(early)
     first_grad, first_dmod, first_sums, first_keep, first_send = run_section(
         layout, rank, first_input, first_halves, saved=first_saved, dy=second_grad
     )
@@ -797,25 +802,26 @@
     shard = jax.ShapeDtypeStruct((rows, half), jnp.float32)
     if compact:
         second_sorted = scatter_first(
-            ring_terms(second_keep),
-            ring_terms(second_got),
-            place,
-            ring_size,
-            after=(early[1],),
+            ring_terms(second_keep), ring_terms(second_got), place, ring_size
         )
         second_received = scatter_flips(second_sorted, ring_size)
-        second_turned = scatter_second(second_received, place, ring_size)
-        *first_sorted, first_grad, first_dmod, first_sums = scatter_first(
+        *first_sorted, first_dmod, first_sums = scatter_first(
             ring_terms(first_keep),
             ring_terms(first_got),
             place,
             ring_size,
-            handed=(first_grad, first_dmod, first_sums),
+            handed=(first_dmod, first_sums),
             after=(second_sorted[0],),
         )
-        first_turned = scatter_second(scatter_flips(first_sorted, ring_size), place, ring_size)
-        second_pieces = scatter_rest(second_turned, place, ring_size)
-        first_pieces = scatter_rest(first_turned, place, ring_size)
+        first_received = scatter_flips(first_sorted, ring_size)
+        second_turned, _ = scatter_second(second_received, place, ring_size)
+        second_sent = scatter_third(second_turned, place, ring_size)
+        second_pieces = scatter_along_z(second_sent, ring_size)
+        first_turned, (first_grad,) = scatter_second(
+            first_received, place, ring_size, handed=(first_grad,), after=(second_sent[0],)
+        )
+        first_sent = scatter_third(first_turned, place, ring_size, tuple(second_pieces[1:]))
+        first_pieces = scatter_along_z(first_sent, ring_size)
     else:
 
         def chip_sum(keep, got):
@@ -825,15 +831,19 @@
             [scatter_sum(chip_sum(keep, got), ring_rank, ring_size)]
             for keep, got in ((first_keep, first_got), (second_keep, second_got))
         ]
+    outputs_ready = (first_low * live, second_low * live)
     if compact:
-        early_full, late = side_by_side(*early, 1), side_by_side(*to_slots(first_grad), 1)
-        per_first = jnp.stack([early_full[0], late[0]])
-        per_second = early_full[1:]
+        block = jnp.stack([outputs_ready[0], first_grad, outputs_ready[1], second_grad])
+        block = block.reshape(4, 2, tokens, width)
+        mine = lax.dynamic_index_in_dim(block, seq_rank, 1, keepdims=True)
+        sent = lax.dynamic_index_in_dim(block, 1 - seq_rank, 1, keepdims=True)
+        block = side_by_side(mine, pair_swap(sent, "seq"), 1)
+        per_first, per_second = block[:2], block[2:]
         mine = jnp.where(is_first, per_first, per_second)
         got = pair_swap(jnp.where(is_first, per_second, per_first), "section")
         outputs = jnp.where(is_first, jnp.stack([mine, got], 1), jnp.stack([got, mine], 1))
     else:
-        pieces = jnp.stack([early[0], first_grad, early[1], early[2]])
+        pieces = jnp.stack([outputs_ready[0], first_grad, outputs_ready[1], second_grad])
         pieces = jnp.swapaxes(pieces.reshape(2, 2, seq_size, tokens, width), 1, 2)
         pieces = pieces.reshape(2 * seq_size, 2, tokens, width)
         pieces = lax.all_to_all(pieces, ("section", "seq"), 0, 0, tiled=True)

time: 186 us -> 183 us (0.984)
  waiting for transfers between devices: 60.6 us -> 44.5 us
  starting transfers between devices: 55.5 us -> 65.2 us
  local copies, waits for them, and re-layouts: 14.1 us -> 18.2 us
  Pallas kernels: 43.4 us -> 39.9 us
  other arithmetic: 5.83 us -> 8.87 us
    ppermute x32, waiting for transfers between devices: 48.5 us -> 39.7 us  [ring_exchange(): return lax.ppermute(block, RING, [(i, step(i)) for i in range(size)])]
    all_to_all x1, waiting for transfers between devices: 5.31 us -> 0.01 us  [per_device(): lax.all_to_all(products[:, None], ('section', 'dp', 'seq'), 0, 0, tiled=T...]
    ppermute x32, starting transfers between devices: 27.2 us -> 31.9 us  [ring_exchange(): return lax.ppermute(block, RING, [(i, step(i)) for i in range(size)])]
    unnamed x64 -> x76, local copies, waits for them, and re-layouts: 7.39 us -> 11.9 us
    all_to_all x1, starting transfers between devices: 4.44 us -> 7.93 us  [per_device(): lax.all_to_all(rows_back[:, None], ('section', 'dp', 'seq'), 0, 0, tiled=...]
    pallas_call x13, Pallas kernels: 17.3 us -> 14 us  [in_memory(): pl.pallas_call(body, out_shape=shapes, in_specs=specs, out_specs=[pl.Bloc...]
    ppermute x10 -> x9, starting transfers between devices: 10.7 us -> 13.7 us  [pair_swap(): return lax.ppermute(block, axis, [(0, 1), (1, 0)])]
    select_n x3 -> x2, other arithmetic: 0.25 us -> 2.36 us  [side_by_side(): jnp.where(seq_rank == 0, jnp.concatenate([mine, got], axis=axis), jnp.con...]
  transfers between devices with their start and end apart: 45 -> 44, of which waited for: 15 -> 16; matrix products, arithmetic and copies ran while one was open for 10% -> 8% of each run, Pallas kernels for 14% -> 13%
where the time goes in v8:
time: 183 us; the launch traced here: 182 us
  starting transfers between devices  65.2 us (36%)
  waiting for transfers between devices  44.5 us (24%)
  Pallas kernels  39.9 us (22%)
  local copies, waits for them, and re-layouts  18.2 us (10%)
  other arithmetic  8.87 us (5%)
  matrix products  3.7 us (2%)
  between operations  1.96 us (1%)
    ppermute x32, waiting for transfers between devices, ring_exchange(): return lax.ppermute(block, RING, [(i, step(i)) for i in range(size)])  39.7 us
    ppermute x32, starting transfers between devices, ring_exchange(): return lax.ppermute(block, RING, [(i, step(i)) for i in range(size)])  31.9 us
    pallas_call x3, Pallas kernels, run_section(): pl.pallas_call(partial(section_kernel, layout, forward, backward, len(aft...  25.9 us
    pallas_call x13, Pallas kernels, in_memory(): pl.pallas_call(body, out_shape=shapes, in_specs=specs, out_specs=[pl.Bloc...  14 us
    ppermute x9, starting transfers between devices, pair_swap(): return lax.ppermute(block, axis, [(0, 1), (1, 0)])  13.7 us
    unnamed x76, local copies, waits for them, and re-layouts  11.9 us
    all_to_all x1, starting transfers between devices, per_device(): lax.all_to_all(rows_back[:, None], ('section', 'dp', 'seq'), 0, 0, tiled=...  7.93 us
    all_to_all x1, starting transfers between devices, per_device(): lax.all_to_all(columns, ('section', 'dp', 'seq'), 0, 0, tiled=True)  6.57 us
  transfers between devices with their start and end apart: 44, of which 16 were waited for; matrix products, arithmetic and copies ran while one was open for 8% of the time, Pallas kernels for 13%

profile of v8, /device:TPU:9, one launch (start us, length us, event | category | flops | bytes accessed | tf_op | source)
XLA Modules:
  0.0 182.4 jit_solution(4532548886882748014)
XLA Ops:
  0.7 1.7 shard_map.178
  6.0 1.3 collective-permute-start.2
  8.4 1.4 collective-permute-start.4
  10.7 6.2 %collective-permute-done.3.refs_3_ = bf16[24,2304]{1,0:T(8,128)(2,1)S(1)} collective-permute-done((bf16[24,2304]{1,0:T(8,128)(2,1)S(1)}, bf16[24,2304]{1,0:T(8,128)(2,1)S(1)}, u32[]{:S(2)}, u32[]{:S(2)}) %collective-permute-start.3) | collective-permute-done | bytes 110624 | tf_op jit(solution)/shard_map/ppermute | solution.py:535
  16.9 2.1 %collective-permute-done.4.refs_4_ = bf16[24,2304]{1,0:T(8,128)(2,1)S(1)} collective-permute-done((bf16[24,2304]{1,0:T(8,128)(2,1)S(1)}, bf16[24,2304]{1,0:T(8,128)(2,1)S(1)}, u32[]{:S(2)}, u32[]{:S(2)}) %collective-permute-start.4) | collective-permute-done | bytes 110624 | tf_op jit(solution)/shard_map/ppermute | solution.py:535
  21.4 5.2 %all-to-all-start = ((f32[32,1,2640]{2,1,0:T(1,128)}), f32[32,1,2640]{2,1,0:T(1,128)S(1)}, u32[]{:S(2)}, u32[]{:S(2)}) async-start(f32[32,1,2640]{2,1,0:T(1,128)} %copy.21), calls=%async_computation | async-start | bytes 688128 | tf_op jit(solution)/shard_map/all_to_all | solution.py:765
  31.8 4.8 %collective-permute-done = bf16[2,128,384]{2,1,0:T(8,128)(2,1)} collective-permute-done((bf16[2,128,384]{2,1,0:T(8,128)(2,1)S(1)}, bf16[2,128,384]{2,1,0:T(8,128)(2,1)}, u32[]{:S(2)}, u32[]{:S(2)}) %collective-permute-start) | collective-permute-done | bytes 196640 | tf_op jit(solution)/shard_map/ppermute | solution.py:531
  36.5 2.4 %collective-permute-done.12.refs_2_ = bf16[24,2304]{1,0:T(8,128)(2,1)S(1)} collective-permute-done((bf16[24,2304]{1,0:T(8,128)(2,1)S(1)}, bf16[24,2304]{1,0:T(8,128)(2,1)S(1)}, u32[]{:S(2)}, u32[]{:S(2)}) %collective-permute-start.12) | collective-permute-done | bytes 110624 | tf_op jit(solution)/shard_map/ppermute | solution.py:535
  41.4 2.1 %collective-permute-done.13.refs_3_ = bf16[24,2304]{1,0:T(8,128)(2,1)S(1)} collective-permute-done((bf16[24,2304]{1,0:T(8,128)(2,1)S(1)}, bf16[24,2304]{1,0:T(8,128)(2,1)S(1)}, u32[]{:S(2)}, u32[]{:S(2)}) %collective-permute-start.13) | collective-permute-done | bytes 110624 | tf_op jit(solution)/shard_map/ppermute | solution.py:535
  43.5 1.6 collective-permute-start.8
  51.4 3.4 %collective-permute-done.10.refs_8_ = bf16[4,24,1152]{2,1,0:T(8,128)(2,1)S(1)} collective-permute-done((bf16[4,24,1152]{2,1,0:T(8,128)(2,1)S(1)}, bf16[4,24,1152]{2,1,0:T(8,128)(2,1)S(1)}, u32[]{:S(2)}, u32[]{:S(2)}) %collective-permute-start.10) | collective-permute-done | bytes 221216 | tf_op jit(solution)/shard_map/ppermute | solution.py:535
  54.8 1.6 collective-permute-start.18
  56.4 3.2 %collective-permute-done.15.refs_2_ = bf16[4,24,1152]{2,1,0:T(8,128)(2,1)S(1)} collective-permute-done((bf16[4,24,1152]{2,1,0:T(8,128)(2,1)S(1)}, bf16[4,24,1152]{2,1,0:T(8,128)(2,1)S(1)}, u32[]{:S(2)}, u32[]{:S(2)}) %collective-permute-start.15) | collective-permute-done | bytes 221216 | tf_op jit(solution)/shard_map/ppermute | solution.py:535
  64.8 3.1 %collective-permute-start.11 = (bf16[384,2304]{1,0:T(8,128)(2,1)S(1)}, bf16[384,2304]{1,0:T(8,128)(2,1)}, u32[]{:S(2)}, u32[]{:S(2)}) collective-permute-start(bf16[384,2304]{1,0:T(8,128)(2,1)S(1)} %bitcast.59), channel_id=1, source_target_pairs={{0,16},{16,0},{1,17},{17,1},{2,18},{18,2},{3,19},{19,3},{4,20},{20... | collective-permute-start | bytes 5308424 | tf_op jit(solution)/shard_map/ppermute | solution.py:531
  68.5 2.0 %shard_map.183 = bf16[4,2,2,24,2304]{4,3,2,1,0:T(8,128)(2,1)} custom-call(s32[3]{0:T(128)S(1)} %pad_add_fusion.refs_0_, bf16[4,24,1152]{2,1,0:T(8,128)(2,1)S(1)} %get-tuple-element.87.refs_1_, bf16[4,24,1152]{2,1,0:T(8,128)(2,1)S(1)} %collective-permute-done.15.refs_2_, bf16[4,24,1152]{2,1,0:T(8,128)(2,1)S(1)} %collective-permute-done.16.refs_3_, ...), custom_call_target="tpu_custom_call" | custom-call | bytes 5308416 | tf_op jit(solution)/shard_map/pallas_call | solution.py:519
  70.5 2.0 %collective-permute-start.21 = (bf16[384,2304]{1,0:T(8,128)(2,1)}, bf16[384,2304]{1,0:T(8,128)(2,1)}, u32[]{:S(2)}, u32[]{:S(2)}) collective-permute-start(bf16[384,2304]{1,0:T(8,128)(2,1)} %bitcast.21.refs_5_), channel_id=1, source_target_pairs={{0,16},{16,0},{1,17},{17,1},{2,18},{18,2},{3,19},{19,3},{4,20},{20... | collective-permute-start | bytes 5308424 | tf_op jit(solution)/shard_map/ppermute | solution.py:531
  74.0 5.6 %shard_map.181 = (bf16[256,384]{1,0:T(8,128)(2,1)S(1)}, f32[1,2304]{1,0:T(1,128)S(1)}, bf16[256,1152]{1,0:T(8,128)(2,1)S(1)}, bf16[256,384]{1,0:T(8,128)(2,1)S(1...) custom-call(s32[1]{0:T(128)} %bitcast.refs_0_, ...), custom_call_target="tpu_custom_call" | custom-call | flops 1006632960 | bytes 5308416 | tf_op jit(solution)/shard_map/pallas_call | solution.py:352
  79.6 12.7 %shard_map.184 = (bf16[256,384]{1,0:T(8,128)(2,1)S(1)}, bf16[256,384]{1,0:T(8,128)(2,1)S(1)}, f32[1,2304]{1,0:T(1,128)S(1)}, f32[16,336]{1,0:T(8,128)S(1)}, bf16...) custom-call(s32[1]{0:T(128)} %bitcast.refs_0_, bf16[256,384]{1,0:T(8,128)(2,1)S(1)} %get-tuple-element.76.refs_1_, ...), custom_call_target="tpu_custom_call" | custom-call | flops 3019898880 | bytes 10616832 | tf_op jit(solution)/shard_map/pallas_call | solution.py:352
  92.4 7.6 %shard_map.185 = (bf16[256,384]{1,0:T(8,128)(2,1)S(1)}, f32[1,2304]{1,0:T(1,128)S(1)}, f32[16,336]{1,0:T(8,128)S(1)}, bf16[384,2304]{1,0:T(8,128)(2,1)S(1)}, bf16[384,2304]{1,0:T(8,128)(2,1)}) custom-call(s32[1]{0:T(128)} %bitcast.refs_0_, bf16[256,384]{1,0:T(8,128)(2,1)S(1)} %get-tuple-element.140.refs_1_, f32[1,2304]{1,0:T(1,128)S(1)} %get-tuple-element.77.refs_2_, ...), custom_call_target="tpu_custom_call" | custom-call | flops 2013265920 | bytes 10616832 | tf_op jit(solution)/shard_map/pallas_call | solution.py:352
  100.1 1.7 shard_map.186
  102.6 1.5 collective-permute-start.26
  105.9 1.5 copy-done.2
  107.3 1.7 shard_map.187
  112.2 7.9 %all-to-all-start.1 = ((f32[32,1,2640]{2,1,0:T(1,128)}), f32[32,1,2640]{2,1,0:T(1,128)}, u32[]{:S(2)}, u32[]{:S(2)}) async-start(f32[32,1,2640]{2,1,0:T(1,128)} %broadcast_in_dim.65), calls=%async_computation.1 | async-start | bytes 688128 | tf_op jit(solution)/shard_map/all_to_all | solution.py:882
  121.2 1.4 shard_map.188
  125.1 8.1 %collective-permute-done.28.refs_2_ = bf16[4,24,1152]{2,1,0:T(8,128)(2,1)S(1)} collective-permute-done((bf16[4,24,1152]{2,1,0:T(8,128)(2,1)S(1)}, bf16[4,24,1152]{2,1,0:T(8,128)(2,1)S(1)}, u32[]{:S(2)}, u32[]{:S(2)}) %collective-permute-start.28) | collective-permute-done | bytes 221216 | tf_op jit(solution)/shard_map/ppermute | solution.py:535
  142.0 6.6 %all-to-all-start.2 = ((f32[32,1,768]{2,1,0:T(1,128)}), f32[32,1,768]{2,1,0:T(1,128)S(1)}, u32[]{:S(2)}, u32[]{:S(2)}) async-start(f32[32,1,768]{2,1,0:T(1,128)} %broadcast_in_dim.67), calls=%async_computation.2 | async-start | bytes 196608 | tf_op jit(solution)/shard_map/all_to_all | solution.py:889
  156.8 4.7 %collective-permute-start.31 = (bf16[2,2,128,384]{3,2,1,0:T(8,128)(2,1)}, bf16[2,2,128,384]{3,2,1,0:T(8,128)(2,1)}, u32[]{:S(2)}, u32[]{:S(2)}) collective-permute-start(bf16[2,2,128,384]{3,2,1,0:T(8,128)(2,1)} %get-tuple-element.136), channel_id=1, source_target_pairs={{0,16},{16,0},{1,17},{17,1},{2,18},{18,2},{3,19},{19,3},{4,20},{20... | collective-permute-start | bytes 1179656 | tf_op jit(solution)/shard_map/ppermute | solution.py:531
  162.0 2.0 %collective-permute-done.36.refs_7_.refs_8_ = bf16[24,2304]{1,0:T(8,128)(2,1)S(1)} collective-permute-done((bf16[24,2304]{1,0:T(8,128)(2,1)S(1)}, bf16[24,2304]{1,0:T(8,128)(2,1)S(1)}, u32[]{:S(2)}, u32[]{:S(2)}) %collective-permute-start.36) | collective-permute-done | bytes 110624 | tf_op jit(solution)/shard_map/ppermute | solution.py:535
  168.9 5.7 %collective-permute-done.38.refs_3_ = bf16[24,2304]{1,0:T(8,128)(2,1)S(1)} collective-permute-done((bf16[24,2304]{1,0:T(8,128)(2,1)S(1)}, bf16[24,2304]{1,0:T(8,128)(2,1)S(1)}, u32[]{:S(2)}, u32[]{:S(2)}) %collective-permute-start.38) | collective-permute-done | bytes 110624 | tf_op jit(solution)/shard_map/ppermute | solution.py:535
  174.6 1.7 collective-permute-done.39.refs_4_
  177.0 2.2 %fusion.5 = f32[1000,384]{1,0:T(8,128)} fusion(s32[32]{0:T(128)S(1)} %eq.24, f32[32,384]{1,0:T(8,128)S(1)} %copy-done.33, f32[32,384]{1,0:T(8,128)S(1)} %reshape.76), kind=kOutput, calls=%fused_computation.27 | convolution fusion | flops 147598592 | bytes 1634432 | tf_op jit(solution)/shard_map/dot_general | solution.py:893
  (192 shorter events, 63.9 us)
Async XLA Ops:
  7.4 9.6 %collective-permute-start.3 = (bf16[24,2304]{1,0:T(8,128)(2,1)S(1)}, bf16[24,2304]{1,0:T(8,128)(2,1)S(1)}, u32[]{:S(2)}, u32[]{:S(2)}) collective-permute-start(bf16[24,2304]{1,0:T(8,128)(2,1)S(1)} %get-tuple-element.146.refs_1_), channel_id=1, source_target_pairs={{0,8},{1,9},{2,10},{3,11},{4,12},{5,13},{6,14},{7,15},{8,0},{9,1},... | collective-permute-start | bytes 331784 | tf_op jit(solution)/shard_map/ppermute | solution.py:535
  8.4 10.6 %collective-permute-start.4 = (bf16[24,2304]{1,0:T(8,128)(2,1)S(1)}, bf16[24,2304]{1,0:T(8,128)(2,1)S(1)}, u32[]{:S(2)}, u32[]{:S(2)}) collective-permute-start(bf16[24,2304]{1,0:T(8,128)(2,1)S(1)} %get-tuple-element.146.refs_1_), channel_id=1, source_target_pairs={{0,12},{1,13},{2,14},{3,15},{4,0},{5,1},{6,2},{7,3},{8,4},{9,5},{1... | collective-permute-start | bytes 331784 | tf_op jit(solution)/shard_map/ppermute | solution.py:535
  21.4 20.0 %all-to-all-start = ((f32[32,1,2640]{2,1,0:T(1,128)}), f32[32,1,2640]{2,1,0:T(1,128)S(1)}, u32[]{:S(2)}, u32[]{:S(2)}) async-start(f32[32,1,2640]{2,1,0:T(1,128)} %copy.21), calls=%async_computation | async-start | bytes 688128 | tf_op jit(solution)/shard_map/all_to_all | solution.py:765
  26.7 9.8 %collective-permute-start = (bf16[2,128,384]{2,1,0:T(8,128)(2,1)S(1)}, bf16[2,128,384]{2,1,0:T(8,128)(2,1)}, u32[]{:S(2)}, u32[]{:S(2)}) collective-permute-start(bf16[2,128,384]{2,1,0:T(8,128)(2,1)S(1)} %get-tuple-element.142), channel_id=1, source_target_pairs={{0,1},{1,0},{2,3},{3,2},{4,5},{5,4},{6,7},{7,6},{8,9},{9,8},{10,11... | collective-permute-start | bytes 589832 | tf_op jit(solution)/shard_map/ppermute | solution.py:531
  28.0 11.0 %collective-permute-start.12 = (bf16[24,2304]{1,0:T(8,128)(2,1)S(1)}, bf16[24,2304]{1,0:T(8,128)(2,1)S(1)}, u32[]{:S(2)}, u32[]{:S(2)}) collective-permute-start(bf16[24,2304]{1,0:T(8,128)(2,1)S(1)} %get-tuple-element.86.refs_1_), channel_id=1, source_target_pairs={{0,4},{1,5},{2,6},{3,7},{4,8},{5,9},{6,10},{7,11},{8,12},{9,13},{1... | collective-permute-start | bytes 331784 | tf_op jit(solution)/shard_map/ppermute | solution.py:535
  29.2 16.0 %collective-permute-start.9 = (bf16[4,24,1152]{2,1,0:T(8,128)(2,1)S(1)}, bf16[4,24,1152]{2,1,0:T(8,128)(2,1)S(1)}, u32[]{:S(2)}, u32[]{:S(2)}) collective-permute-start(bf16[4,24,1152]{2,1,0:T(8,128)(2,1)S(1)} %get-tuple-element.75.refs_5_), channel_id=1, source_target_pairs={{0,1},{1,0},{2,3},{3,2},{4,5},{5,4},{6,7},{7,6},{8,9},{9,8},{10,11... | collective-permute-start | bytes 663560 | tf_op jit(solution)/shard_map/ppermute | solution.py:535
  29.4 16.0 %collective-permute-start.5 = (bf16[4,24,1152]{2,1,0:T(8,128)(2,1)S(1)}, bf16[4,24,1152]{2,1,0:T(8,128)(2,1)S(1)}, u32[]{:S(2)}, u32[]{:S(2)}) collective-permute-start(bf16[4,24,1152]{2,1,0:T(8,128)(2,1)S(1)} %get-tuple-element.74.refs_1_), channel_id=1, source_target_pairs={{0,2},{1,3},{2,0},{3,1},{4,6},{5,7},{6,4},{7,5},{8,10},{9,11},{10,... | collective-permute-start | bytes 663560 | tf_op jit(solution)/shard_map/ppermute | solution.py:535
  30.6 12.9 %collective-permute-start.13 = (bf16[24,2304]{1,0:T(8,128)(2,1)S(1)}, bf16[24,2304]{1,0:T(8,128)(2,1)S(1)}, u32[]{:S(2)}, u32[]{:S(2)}) collective-permute-start(bf16[24,2304]{1,0:T(8,128)(2,1)S(1)} %get-tuple-element.86.refs_1_), channel_id=1, source_target_pairs={{0,8},{1,9},{2,10},{3,11},{4,12},{5,13},{6,14},{7,15},{8,0},{9,1},... | collective-permute-start | bytes 331784 | tf_op jit(solution)/shard_map/ppermute | solution.py:535
  39.0 9.8 %collective-permute-start.6 = (bf16[4,24,1152]{2,1,0:T(8,128)(2,1)S(1)}, bf16[4,24,1152]{2,1,0:T(8,128)(2,1)S(1)}, u32[]{:S(2)}, u32[]{:S(2)}) collective-permute-start(bf16[4,24,1152]{2,1,0:T(8,128)(2,1)S(1)} %get-tuple-element.74.refs_1_), channel_id=1, source_target_pairs={{0,1},{1,0},{2,3},{3,2},{4,5},{5,4},{6,7},{7,6},{8,9},{9,8},{10,11... | collective-permute-start | bytes 663560 | tf_op jit(solution)/shard_map/ppermute | solution.py:535
  45.1 9.7 %collective-permute-start.10 = (bf16[4,24,1152]{2,1,0:T(8,128)(2,1)S(1)}, bf16[4,24,1152]{2,1,0:T(8,128)(2,1)S(1)}, u32[]{:S(2)}, u32[]{:S(2)}) collective-permute-start(bf16[4,24,1152]{2,1,0:T(8,128)(2,1)S(1)} %collective-permute-done.9.refs_7_.refs_8_), channel_id=1, source_target_pairs={{0,2},{1,3},{2,0},{3,1},{4,6},{5,7},{6,4},{7,5},{8,10},{9,11},{10,... | collective-permute-start | bytes 663560 | tf_op jit(solution)/shard_map/ppermute | solution.py:535
  46.3 13.3 %collective-permute-start.15 = (bf16[4,24,1152]{2,1,0:T(8,128)(2,1)S(1)}, bf16[4,24,1152]{2,1,0:T(8,128)(2,1)S(1)}, u32[]{:S(2)}, u32[]{:S(2)}) collective-permute-start(bf16[4,24,1152]{2,1,0:T(8,128)(2,1)S(1)} %get-tuple-element.87.refs_1_), channel_id=1, source_target_pairs={{0,2},{1,3},{2,0},{3,1},{4,6},{5,7},{6,4},{7,5},{8,10},{9,11},{10,... | collective-permute-start | bytes 663560 | tf_op jit(solution)/shard_map/ppermute | solution.py:535
  47.5 13.3 %collective-permute-start.19 = (bf16[4,24,1152]{2,1,0:T(8,128)(2,1)S(1)}, bf16[4,24,1152]{2,1,0:T(8,128)(2,1)S(1)}, u32[]{:S(2)}, u32[]{:S(2)}) collective-permute-start(bf16[4,24,1152]{2,1,0:T(8,128)(2,1)S(1)} %get-tuple-element.88.refs_5_), channel_id=1, source_target_pairs={{0,1},{1,0},{2,3},{3,2},{4,5},{5,4},{6,7},{7,6},{8,9},{9,8},{10,11... | collective-permute-start | bytes 663560 | tf_op jit(solution)/shard_map/ppermute | solution.py:535
  49.4 12.6 %collective-permute-start.7 = (bf16[4,24,1152]{2,1,0:T(8,128)(2,1)S(1)}, bf16[4,24,1152]{2,1,0:T(8,128)(2,1)S(1)}, u32[]{:S(2)}, u32[]{:S(2)}) collective-permute-start(bf16[4,24,1152]{2,1,0:T(8,128)(2,1)S(1)} %collective-permute-done.5.refs_2_.refs_7_), channel_id=1, source_target_pairs={{0,1},{1,0},{2,3},{3,2},{4,5},{5,4},{6,7},{7,6},{8,9},{9,8},{10,11... | collective-permute-start | bytes 663560 | tf_op jit(solution)/shard_map/ppermute | solution.py:535
  50.1 17.9 %collective-permute-start.16 = (bf16[4,24,1152]{2,1,0:T(8,128)(2,1)S(1)}, bf16[4,24,1152]{2,1,0:T(8,128)(2,1)S(1)}, u32[]{:S(2)}, u32[]{:S(2)}) collective-permute-start(bf16[4,24,1152]{2,1,0:T(8,128)(2,1)S(1)} %get-tuple-element.87.refs_1_), channel_id=1, source_target_pairs={{0,1},{1,0},{2,3},{3,2},{4,5},{5,4},{6,7},{7,6},{8,9},{9,8},{10,11... | collective-permute-start | bytes 663560 | tf_op jit(solution)/shard_map/ppermute | solution.py:535
  54.8 13.1 %collective-permute-start.18 = (bf16[4,24,1152]{2,1,0:T(8,128)(2,1)S(1)}, bf16[4,24,1152]{2,1,0:T(8,128)(2,1)S(1)}, u32[]{:S(2)}, u32[]{:S(2)}) collective-permute-start(bf16[4,24,1152]{2,1,0:T(8,128)(2,1)S(1)} %get-tuple-element.88.refs_5_), channel_id=1, source_target_pairs={{0,2},{1,3},{2,0},{3,1},{4,6},{5,7},{6,4},{7,5},{8,10},{9,11},{10,... | collective-permute-start | bytes 663560 | tf_op jit(solution)/shard_map/ppermute | solution.py:535
  64.8 9.1 %collective-permute-start.11 = (bf16[384,2304]{1,0:T(8,128)(2,1)S(1)}, bf16[384,2304]{1,0:T(8,128)(2,1)}, u32[]{:S(2)}, u32[]{:S(2)}) collective-permute-start(bf16[384,2304]{1,0:T(8,128)(2,1)S(1)} %bitcast.59), channel_id=1, source_target_pairs={{0,16},{16,0},{1,17},{17,1},{2,18},{18,2},{3,19},{19,3},{4,20},{20... | collective-permute-start | bytes 5308424 | tf_op jit(solution)/shard_map/ppermute | solution.py:531
  102.6 17.6 %collective-permute-start.26 = (bf16[4,2,24,1152]{3,2,1,0:T(8,128)(2,1)}, bf16[4,2,24,1152]{3,2,1,0:T(8,128)(2,1)}, u32[]{:S(2)}, u32[]{:S(2)}) collective-permute-start(bf16[4,2,24,1152]{3,2,1,0:T(8,128)(2,1)} %get-tuple-element.102), channel_id=1, source_target_pairs={{0,2},{1,3},{2,0},{3,1},{4,6},{5,7},{6,4},{7,5},{8,10},{9,11},{10,... | collective-permute-start | bytes 1327112 | tf_op jit(solution)/shard_map/ppermute | solution.py:535
  104.0 16.2 %collective-permute-start.27 = (bf16[4,2,24,1152]{3,2,1,0:T(8,128)(2,1)}, bf16[4,2,24,1152]{3,2,1,0:T(8,128)(2,1)}, u32[]{:S(2)}, u32[]{:S(2)}) collective-permute-start(bf16[4,2,24,1152]{3,2,1,0:T(8,128)(2,1)} %get-tuple-element.104), channel_id=1, source_target_pairs={{0,1},{1,0},{2,3},{3,2},{4,5},{5,4},{6,7},{7,6},{8,9},{9,8},{10,11... | collective-permute-start | bytes 1327112 | tf_op jit(solution)/shard_map/ppermute | solution.py:535
  110.5 25.2 %collective-permute-start.24 = (bf16[4,2,24,1152]{3,2,1,0:T(8,128)(2,1)}, bf16[4,2,24,1152]{3,2,1,0:T(8,128)(2,1)S(1)}, u32[]{:S(2)}, u32[]{:S(2)}) collective-permute-start(bf16[4,2,24,1152]{3,2,1,0:T(8,128)(2,1)} %get-tuple-element.98), channel_id=1, source_target_pairs={{0,2},{1,3},{2,0},{3,1},{4,6},{5,7},{6,4},{7,5},{8,10},{9,11},{10,... | collective-permute-start | bytes 1327112 | tf_op jit(solution)/shard_map/ppermute | solution.py:535
  110.8 24.9 %collective-permute-start.25 = (bf16[4,2,24,1152]{3,2,1,0:T(8,128)(2,1)}, bf16[4,2,24,1152]{3,2,1,0:T(8,128)(2,1)S(1)}, u32[]{:S(2)}, u32[]{:S(2)}) collective-permute-start(bf16[4,2,24,1152]{3,2,1,0:T(8,128)(2,1)} %get-tuple-element.100), channel_id=1, source_target_pairs={{0,1},{1,0},{2,3},{3,2},{4,5},{5,4},{6,7},{7,6},{8,9},{9,8},{10,11... | collective-permute-start | bytes 1327112 | tf_op jit(solution)/shard_map/ppermute | solution.py:535
  112.2 27.8 %all-to-all-start.1 = ((f32[32,1,2640]{2,1,0:T(1,128)}), f32[32,1,2640]{2,1,0:T(1,128)}, u32[]{:S(2)}, u32[]{:S(2)}) async-start(f32[32,1,2640]{2,1,0:T(1,128)} %broadcast_in_dim.65), calls=%async_computation.1 | async-start | bytes 688128 | tf_op jit(solution)/shard_map/all_to_all | solution.py:882
  122.6 10.5 %collective-permute-start.28 = (bf16[4,24,1152]{2,1,0:T(8,128)(2,1)S(1)}, bf16[4,24,1152]{2,1,0:T(8,128)(2,1)S(1)}, u32[]{:S(2)}, u32[]{:S(2)}) collective-permute-start(bf16[4,24,1152]{2,1,0:T(8,128)(2,1)S(1)} %get-tuple-element.106), channel_id=1, source_target_pairs={{0,1},{1,0},{2,3},{3,2},{4,5},{5,4},{6,7},{7,6},{8,9},{9,8},{10,11... | collective-permute-start | bytes 663560 | tf_op jit(solution)/shard_map/ppermute | solution.py:535
  123.9 9.3 %collective-permute-start.29 = (bf16[4,24,1152]{2,1,0:T(8,128)(2,1)S(1)}, bf16[4,24,1152]{2,1,0:T(8,128)(2,1)S(1)}, u32[]{:S(2)}, u32[]{:S(2)}) collective-permute-start(bf16[4,24,1152]{2,1,0:T(8,128)(2,1)S(1)} %get-tuple-element.108), channel_id=1, source_target_pairs={{0,2},{1,3},{2,0},{3,1},{4,6},{5,7},{6,4},{7,5},{8,10},{9,11},{10,... | collective-permute-start | bytes 663560 | tf_op jit(solution)/shard_map/ppermute | solution.py:535
  139.0 14.4 %collective-permute-start.30 = (bf16[4,1,128,384]{3,2,1,0:T(8,128)(2,1)}, bf16[4,1,128,384]{3,2,1,0:T(8,128)(2,1)}, u32[]{:S(2)}, u32[]{:S(2)}) collective-permute-start(bf16[4,1,128,384]{3,2,1,0:T(8,128)(2,1)} %get-tuple-element.138), channel_id=1, source_target_pairs={{0,1},{1,0},{2,3},{3,2},{4,5},{5,4},{6,7},{7,6},{8,9},{9,8},{10,11... | collective-permute-start | bytes 1179656 | tf_op jit(solution)/shard_map/ppermute | solution.py:531
  142.0 25.1 %all-to-all-start.2 = ((f32[32,1,768]{2,1,0:T(1,128)}), f32[32,1,768]{2,1,0:T(1,128)S(1)}, u32[]{:S(2)}, u32[]{:S(2)}) async-start(f32[32,1,768]{2,1,0:T(1,128)} %broadcast_in_dim.67), calls=%async_computation.2 | async-start | bytes 196608 | tf_op jit(solution)/shard_map/all_to_all | solution.py:889
  148.6 15.4 %collective-permute-start.32 = (bf16[4,24,1152]{2,1,0:T(8,128)(2,1)}, bf16[4,24,1152]{2,1,0:T(8,128)(2,1)S(1)}, u32[]{:S(2)}, u32[]{:S(2)}) collective-permute-start(bf16[4,24,1152]{2,1,0:T(8,128)(2,1)} %copy-done.22), channel_id=1, source_target_pairs={{0,1},{1,0},{2,3},{3,2},{4,5},{5,4},{6,7},{7,6},{8,9},{9,8},{10,11... | collective-permute-start | bytes 663560 | tf_op jit(solution)/shard_map/ppermute | solution.py:535
  149.9 14.2 %collective-permute-start.33 = (bf16[4,24,1152]{2,1,0:T(8,128)(2,1)}, bf16[4,24,1152]{2,1,0:T(8,128)(2,1)S(1)}, u32[]{:S(2)}, u32[]{:S(2)}) collective-permute-start(bf16[4,24,1152]{2,1,0:T(8,128)(2,1)} %copy-done.21), channel_id=1, source_target_pairs={{0,2},{1,3},{2,0},{3,1},{4,6},{5,7},{6,4},{7,5},{8,10},{9,11},{10,... | collective-permute-start | bytes 663560 | tf_op jit(solution)/shard_map/ppermute | solution.py:535
  152.3 9.8 %collective-permute-start.35 = (bf16[24,2304]{1,0:T(8,128)(2,1)S(1)}, bf16[24,2304]{1,0:T(8,128)(2,1)S(1)}, u32[]{:S(2)}, u32[]{:S(2)}) collective-permute-start(bf16[24,2304]{1,0:T(8,128)(2,1)S(1)} %copy-done.26), channel_id=1, source_target_pairs={{0,8},{1,9},{2,10},{3,11},{4,12},{5,13},{6,14},{7,15},{8,0},{9,1},... | collective-permute-start | bytes 331784 | tf_op jit(solution)/shard_map/ppermute | solution.py:535
  153.4 10.6 %collective-permute-start.36 = (bf16[24,2304]{1,0:T(8,128)(2,1)S(1)}, bf16[24,2304]{1,0:T(8,128)(2,1)S(1)}, u32[]{:S(2)}, u32[]{:S(2)}) collective-permute-start(bf16[24,2304]{1,0:T(8,128)(2,1)S(1)} %copy-done.24), channel_id=1, source_target_pairs={{0,12},{1,13},{2,14},{3,15},{4,0},{5,1},{6,2},{7,3},{8,4},{9,5},{1... | collective-permute-start | bytes 331784 | tf_op jit(solution)/shard_map/ppermute | solution.py:535
  156.8 23.2 %collective-permute-start.31 = (bf16[2,2,128,384]{3,2,1,0:T(8,128)(2,1)}, bf16[2,2,128,384]{3,2,1,0:T(8,128)(2,1)}, u32[]{:S(2)}, u32[]{:S(2)}) collective-permute-start(bf16[2,2,128,384]{3,2,1,0:T(8,128)(2,1)} %get-tuple-element.136), channel_id=1, source_target_pairs={{0,16},{16,0},{1,17},{17,1},{2,18},{18,2},{3,19},{19,3},{4,20},{20... | collective-permute-start | bytes 1179656 | tf_op jit(solution)/shard_map/ppermute | solution.py:531
  165.0 9.6 %collective-permute-start.38 = (bf16[24,2304]{1,0:T(8,128)(2,1)S(1)}, bf16[24,2304]{1,0:T(8,128)(2,1)S(1)}, u32[]{:S(2)}, u32[]{:S(2)}) collective-permute-start(bf16[24,2304]{1,0:T(8,128)(2,1)S(1)} %get-tuple-element.125), channel_id=1, source_target_pairs={{0,8},{1,9},{2,10},{3,11},{4,12},{5,13},{6,14},{7,15},{8,0},{9,1},... | collective-permute-start | bytes 331784 | tf_op jit(solution)/shard_map/ppermute | solution.py:535
  165.7 10.6 %collective-permute-start.39 = (bf16[24,2304]{1,0:T(8,128)(2,1)S(1)}, bf16[24,2304]{1,0:T(8,128)(2,1)S(1)}, u32[]{:S(2)}, u32[]{:S(2)}) collective-permute-start(bf16[24,2304]{1,0:T(8,128)(2,1)S(1)} %get-tuple-element.126), channel_id=1, source_target_pairs={{0,12},{1,13},{2,14},{3,15},{4,0},{5,1},{6,2},{7,3},{8,4},{9,5},{1... | collective-permute-start | bytes 331784 | tf_op jit(solution)/shard_map/ppermute | solution.py:535
  (49 other events, 425.1 us)

commit v9 on v8

--- a/solution.py
+++ b/solution.py
@@ -467,7 +467,10 @@
 
 
 def rise_kernel(high, place_ref, *refs):
-    targets = refs[4:]
+    count = (len(refs) - 4 - high) // 2
+    for former, latter in zip(refs[4 : 4 + count], refs[4 + count + high :]):
+        latter[...] = former[...]
+    targets = refs[4 + count :]
     lanes = refs[0].shape[2]
     for turn in range(high):
         chunk = lax.rem(place_ref[0] + turn, high)
@@ -564,7 +567,7 @@
     return flip(first, size, 2), flip(second, size, 1)
 
 
-def gather_across(first, second, first_x, second_y, place, size):
+def gather_across(first, second, first_x, second_y, place, size, after=()):
     high, rows, lanes = first.shape
     first_y, second_x = flip(first, size, 1), flip(second, size, 2)
     first_both, second_both = flip(first_x, size, 1), flip(second_y, size, 2)
@@ -573,6 +576,7 @@
         [jax.ShapeDtypeStruct((high, 2, 2, rows, 2 * lanes), first.dtype)],
         [place, first, first_x, first_y, first_both, second, second_x, second_y, second_both],
         scratch=[pltpu.SemaphoreType.DMA((8,))],
+        after=after,
     )
     return full.reshape(size * rows, 2 * lanes)
 
@@ -606,14 +610,15 @@
     return turned, handed
 
 
-def scatter_third(turned, place, size, after=()):
+def scatter_third(turned, place, size, handed=(), after=()):
     high, rows, lanes = turned[0].shape
     chunk = (rows, 2 * lanes)
     return in_memory(
         partial(rise_kernel, high),
         [jax.ShapeDtypeStruct(chunk, jnp.float32)]
-        + [jax.ShapeDtypeStruct(chunk, jnp.bfloat16)] * (high - 1),
-        [place, *turned],
+        + [jax.ShapeDtypeStruct(chunk, jnp.bfloat16)] * (high - 1)
+        + [jax.ShapeDtypeStruct(block.shape, block.dtype) for block in handed],
+        [place, *turned, *handed],
         after=after,
     )
 
@@ -752,10 +757,14 @@
     silu_all = jax.nn.silu(conditions).astype(jnp.bfloat16)
     silu_own = lax.dynamic_slice_in_dim(silu_all, ring_rank * rows, rows, 1)
     if compact:
-        *first_parts, second_shard, silu_late = gather_along_z(
-            first_shard, place, ring_size, handed=(second_shard, silu_own)
+        *first_parts, second_shard = gather_along_z(
+            first_shard, place, ring_size, handed=(second_shard,)
         )
         first_parts += first_flips(*first_parts, ring_size)
+        *second_parts, silu_late = gather_along_z(
+            second_shard, place, ring_size, handed=(silu_own,), after=(both, *first_parts[2:])
+        )
+        second_parts += first_flips(*second_parts, ring_size)
     else:
         silu_late = silu_own
 
@@ -771,11 +780,7 @@
     first_bias, second_bias = products[0, :, 6 * width :], products[1, :, 6 * width :]
 
     if compact:
-        second_parts = gather_along_z(
-            second_shard, place, ring_size, after=(products, both, *first_parts[2:])
-        )
-        second_parts += first_flips(*second_parts, ring_size)
-        first_pack = gather_across(*first_parts, place, ring_size)
+        first_pack = gather_across(*first_parts, place, ring_size, after=(products,))
         second_pack = gather_across(*second_parts, place, ring_size)
     else:
         first_pack = lax.all_gather(first_shard, RING, axis=0, tiled=True)
@@ -805,22 +810,42 @@
             ring_terms(second_keep), ring_terms(second_got), place, ring_size
         )
         second_received = scatter_flips(second_sorted, ring_size)
-        *first_sorted, first_dmod, first_sums = scatter_first(
+        first_sorted = scatter_first(
             ring_terms(first_keep),
             ring_terms(first_got),
             place,
             ring_size,
-            handed=(first_dmod, first_sums),
             after=(second_sorted[0],),
         )
         first_received = scatter_flips(first_sorted, ring_size)
-        second_turned, _ = scatter_second(second_received, place, ring_size)
+        second_turned, (first_dmod, first_sums) = scatter_second(
+            second_received, place, ring_size, handed=(first_dmod, first_sums)
+        )
         second_sent = scatter_third(second_turned, place, ring_size)
         second_pieces = scatter_along_z(second_sent, ring_size)
         first_turned, (first_grad,) = scatter_second(
             first_received, place, ring_size, handed=(first_grad,), after=(second_sent[0],)
         )
-        first_sent = scatter_third(first_turned, place, ring_size, tuple(second_pieces[1:]))
+
+    rows_back = jnp.concatenate(
+        [
+            jnp.concatenate(
+                [jnp.broadcast_to(dmod, (ring_size, 6 * width)), sums], axis=1
+            )
+            for dmod, sums in ((first_dmod, first_sums), (second_dmod, second_sums))
+        ]
+    )
+    every = lax.all_to_all(rows_back[:, None], ("section", "dp", "seq"), 0, 0, tiled=True)
+    every = every[::sharers, 0]
+    bias_grad = jnp.sum(every[:, 6 * width :], axis=0)
+    modulation_rows = low(every[:, : 6 * width])
+    modulation_grad = outer_sum(silu_own, modulation_rows)
+    columns = matmul_transposed(modulation_rows, modulation_weight[0])
+
+    if compact:
+        *first_sent, columns = scatter_third(
+            first_turned, place, ring_size, handed=(columns,), after=tuple(second_pieces[1:])
+        )
         first_pieces = scatter_along_z(first_sent, ring_size)
     else:
 
@@ -871,20 +896,6 @@
         [rank, mine, pair_swap(send, "section")],
     )
 
-    rows_back = jnp.concatenate(
-        [
-            jnp.concatenate(
-                [jnp.broadcast_to(dmod, (ring_size, 6 * width)), sums], axis=1
-            )
-            for dmod, sums in ((first_dmod, first_sums), (second_dmod, second_sums))
-        ]
-    )
-    every = lax.all_to_all(rows_back[:, None], ("section", "dp", "seq"), 0, 0, tiled=True)
-    every = every[::sharers, 0]
-    bias_grad = jnp.sum(every[:, 6 * width :], axis=0)
-    modulation_rows = low(every[:, : 6 * width])
-    modulation_grad = outer_sum(silu_own, modulation_rows)
-    columns = matmul_transposed(modulation_rows, modulation_weight[0])
     columns = jnp.broadcast_to(columns.reshape(1, 1, -1), (sections * ring_size, 1, columns.size))
     columns = lax.all_to_all(columns, ("section", "dp", "seq"), 0, 0, tiled=True)
     columns = jnp.sum(columns.reshape(sections, ring_size, -1, rows), axis=0)

time: 183 us -> 194 us (1.060)
  waiting for transfers between devices: 44.5 us -> 62.4 us
  starting transfers between devices: 65.2 us -> 52.3 us
  local copies, waits for them, and re-layouts: 18.2 us -> 22 us
  Pallas kernels: 39.9 us -> 43.2 us
    ppermute x32, waiting for transfers between devices: 39.7 us -> 55.8 us  [ring_exchange(): return lax.ppermute(block, RING, [(i, step(i)) for i in range(size)])]
    ppermute x9, starting transfers between devices: 13.7 us -> 6.15 us  [pair_swap(): return lax.ppermute(block, axis, [(0, 1), (1, 0)])]
    all_to_all x1, waiting for transfers between devices: 0.01 us -> 6.48 us  [per_device(): lax.all_to_all(rows_back[:, None], ('section', 'dp', 'seq'), 0, 0, tiled=...]
    ppermute x9, waiting for transfers between devices: 4.77 us -> 0.12 us  [pair_swap(): return lax.ppermute(block, axis, [(0, 1), (1, 0)])]
    unnamed x76 -> x88, local copies, waits for them, and re-layouts: 11.9 us -> 15.3 us
    pallas_call x13, Pallas kernels: 14 us -> 17.1 us  [in_memory(): pl.pallas_call(body, out_shape=shapes, in_specs=specs, out_specs=[pl.Bloc...]
  transfers between devices with their start and end apart: 44 -> 44, of which waited for: 16 -> 17; matrix products, arithmetic and copies ran while one was open for 8% -> 7% of each run, Pallas kernels for 13% -> 13%
where the time goes in v9:
time: 194 us; the launch traced here: 193 us
  waiting for transfers between devices  62.4 us (32%)
  starting transfers between devices  52.3 us (27%)
  Pallas kernels  43.2 us (22%)
  local copies, waits for them, and re-layouts  22 us (11%)
  other arithmetic  7.95 us (4%)
  matrix products  3.7 us (2%)
    ppermute x32, waiting for transfers between devices, ring_exchange(): return lax.ppermute(block, RING, [(i, step(i)) for i in range(size)])  55.8 us
    ppermute x32, starting transfers between devices, ring_exchange(): return lax.ppermute(block, RING, [(i, step(i)) for i in range(size)])  30.3 us
    pallas_call x3, Pallas kernels, run_section(): pl.pallas_call(partial(section_kernel, layout, forward, backward, len(aft...  26.2 us
    pallas_call x13, Pallas kernels, in_memory(): pl.pallas_call(body, out_shape=shapes, in_specs=specs, out_specs=[pl.Bloc...  17.1 us
    unnamed x88, local copies, waits for them, and re-layouts  15.3 us
    all_to_all x1, waiting for transfers between devices, per_device(): lax.all_to_all(rows_back[:, None], ('section', 'dp', 'seq'), 0, 0, tiled=...  6.48 us
    all_to_all x1, starting transfers between devices, per_device(): lax.all_to_all(rows_back[:, None], ('section', 'dp', 'seq'), 0, 0, tiled=...  6.47 us
    ppermute x9, starting transfers between devices, pair_swap(): return lax.ppermute(block, axis, [(0, 1), (1, 0)])  6.15 us
  transfers between devices with their start and end apart: 44, of which 17 were waited for; matrix products, arithmetic and copies ran while one was open for 7% of the time, Pallas kernels for 13%

profile of v9, /device:TPU:9, one launch (start us, length us, event | category | flops | bytes accessed | tf_op | source)
XLA Modules:
  0.0 193.5 jit_solution(7663465678663154878)
XLA Ops:
  0.7 1.7 shard_map.178
  8.5 1.4 collective-permute-start.4
  10.4 6.2 %collective-permute-done.3.refs_3_ = bf16[24,2304]{1,0:T(8,128)(2,1)S(1)} collective-permute-done((bf16[24,2304]{1,0:T(8,128)(2,1)S(1)}, bf16[24,2304]{1,0:T(8,128)(2,1)S(1)}, u32[]{:S(2)}, u32[]{:S(2)}) %collective-permute-start.3) | collective-permute-done | bytes 110624 | tf_op jit(solution)/shard_map/ppermute | solution.py:538
  16.6 2.4 %collective-permute-done.4.refs_4_ = bf16[24,2304]{1,0:T(8,128)(2,1)S(1)} collective-permute-done((bf16[24,2304]{1,0:T(8,128)(2,1)S(1)}, bf16[24,2304]{1,0:T(8,128)(2,1)S(1)}, u32[]{:S(2)}, u32[]{:S(2)}) %collective-permute-start.4) | collective-permute-done | bytes 110624 | tf_op jit(solution)/shard_map/ppermute | solution.py:538
  23.9 1.6 collective-permute-done.5.refs_2_
  25.5 1.8 collective-permute-done.6.refs_3_
  27.3 6.2 %collective-permute-done.7.refs_4_ = bf16[24,2304]{1,0:T(8,128)(2,1)S(1)} collective-permute-done((bf16[24,2304]{1,0:T(8,128)(2,1)S(1)}, bf16[24,2304]{1,0:T(8,128)(2,1)S(1)}, u32[]{:S(2)}, u32[]{:S(2)}) %collective-permute-start.7) | collective-permute-done | bytes 110624 | tf_op jit(solution)/shard_map/ppermute | solution.py:538
  33.5 1.6 shard_map.180
  36.4 4.1 %all-to-all-start = ((f32[32,1,2640]{2,1,0:T(1,128)}), f32[32,1,2640]{2,1,0:T(1,128)S(1)}, u32[]{:S(2)}, u32[]{:S(2)}) async-start(f32[32,1,2640]{2,1,0:T(1,128)} %copy.22), calls=%async_computation | async-start | bytes 688128 | tf_op jit(solution)/shard_map/all_to_all | solution.py:774
  44.7 6.2 %collective-permute-done.10.refs_3_ = bf16[4,24,1152]{2,1,0:T(8,128)(2,1)S(1)} collective-permute-done((bf16[4,24,1152]{2,1,0:T(8,128)(2,1)S(1)}, bf16[4,24,1152]{2,1,0:T(8,128)(2,1)S(1)}, u32[]{:S(2)}, u32[]{:S(2)}) %collective-permute-start.10) | collective-permute-done | bytes 221216 | tf_op jit(solution)/shard_map/ppermute | solution.py:538
  50.8 1.6 collective-permute-start.13
  52.4 3.3 %collective-permute-done.15.refs_2_ = bf16[4,24,1152]{2,1,0:T(8,128)(2,1)} collective-permute-done((bf16[4,24,1152]{2,1,0:T(8,128)(2,1)}, bf16[4,24,1152]{2,1,0:T(8,128)(2,1)}, u32[]{:S(2)}, u32[]{:S(2)}) %collective-permute-start.15) | collective-permute-done | bytes 221216 | tf_op jit(solution)/shard_map/ppermute | solution.py:538
  57.2 3.2 %collective-permute-done.11.refs_4_ = bf16[4,24,1152]{2,1,0:T(8,128)(2,1)S(1)} collective-permute-done((bf16[4,24,1152]{2,1,0:T(8,128)(2,1)S(1)}, bf16[4,24,1152]{2,1,0:T(8,128)(2,1)S(1)}, u32[]{:S(2)}, u32[]{:S(2)}) %collective-permute-start.11) | collective-permute-done | bytes 221216 | tf_op jit(solution)/shard_map/ppermute | solution.py:538
  60.4 1.5 collective-permute-start.20
  71.2 3.1 %shard_map.183 = bf16[4,2,2,24,2304]{4,3,2,1,0:T(8,128)(2,1)} custom-call(s32[3]{0:T(128)S(1)} %pad_add_fusion.refs_0_, bf16[4,24,1152]{2,1,0:T(8,128)(2,1)} %get-tuple-element.88.refs_1_, bf16[4,24,1152]{2,1,0:T(8,128)(2,1)} %collective-permute-done.15.refs_2_, bf16[4,24,1152]{2,1,0:T(8,128)(2,1)} %collective-permute-done.16.refs_3_, ...), custom_call_target="tpu_custom_call" | custom-call | bytes 5308416 | tf_op jit(solution)/shard_map/pallas_call | solution.py:522
  75.8 5.6 %shard_map.182 = (bf16[256,384]{1,0:T(8,128)(2,1)S(1)}, f32[1,2304]{1,0:T(1,128)S(1)}, bf16[256,1152]{1,0:T(8,128)(2,1)S(1)}, bf16[256,384]{1,0:T(8,128)(2,1)S(1...) custom-call(s32[1]{0:T(128)} %bitcast.refs_0_, ...), custom_call_target="tpu_custom_call" | custom-call | flops 1006632960 | bytes 5308416 | tf_op jit(solution)/shard_map/pallas_call | solution.py:352
  81.5 12.7 %shard_map.184 = (bf16[256,384]{1,0:T(8,128)(2,1)S(1)}, bf16[256,384]{1,0:T(8,128)(2,1)S(1)}, f32[1,2304]{1,0:T(1,128)S(1)}, f32[16,336]{1,0:T(8,128)S(1)}, bf16...) custom-call(s32[1]{0:T(128)} %bitcast.refs_0_, bf16[256,384]{1,0:T(8,128)(2,1)S(1)} %get-tuple-element.78.refs_1_, ...), custom_call_target="tpu_custom_call" | custom-call | flops 3019898880 | bytes 10616832 | tf_op jit(solution)/shard_map/pallas_call | solution.py:352
  94.3 7.8 %shard_map.185 = (bf16[256,384]{1,0:T(8,128)(2,1)S(1)}, f32[1,2304]{1,0:T(1,128)S(1)}, f32[16,336]{1,0:T(8,128)S(1)}, bf16[384,2304]{1,0:T(8,128)(2,1)S(1)}, bf16[384,2304]{1,0:T(8,128)(2,1)}) custom-call(s32[1]{0:T(128)} %bitcast.refs_0_, bf16[256,384]{1,0:T(8,128)(2,1)S(1)} %get-tuple-element.142.refs_1_, f32[1,2304]{1,0:T(1,128)S(1)} %get-tuple-element.79.refs_2_, ...), custom_call_target="tpu_custom_call" | custom-call | flops 2013265920 | bytes 10616832 | tf_op jit(solution)/shard_map/pallas_call | solution.py:352
  102.3 1.7 shard_map.186
  106.1 1.5 copy-done.2
  107.6 1.7 shard_map.187
  112.3 4.0 %collective-permute-done.26.refs_2_ = bf16[4,2,24,1152]{3,2,1,0:T(8,128)(2,1)} collective-permute-done((bf16[4,2,24,1152]{3,2,1,0:T(8,128)(2,1)}, bf16[4,2,24,1152]{3,2,1,0:T(8,128)(2,1)}, u32[]{:S(2)}, u32[]{:S(2)}) %collective-permute-start.26) | collective-permute-done | bytes 442400 | tf_op jit(solution)/shard_map/ppermute | solution.py:538
  116.8 2.1 %shard_map.188 = (bf16[4,24,1152]{2,1,0:T(8,128)(2,1)S(1)}, bf16[4,24,1152]{2,1,0:T(8,128)(2,1)}, bf16[4,24,1152]{2,1,0:T(8,128)(2,1)S(1)}, bf16[4,24,1152]{2,1,...) custom-call(s32[3]{0:T(128)S(1)} %pad_add_fusion.refs_0_, ...), custom_call_target="tpu_custom_call" | custom-call | bytes 2746368 | tf_op jit(solution)/shard_map/pallas_call | solution.py:522
  121.2 9.8 %collective-permute-done.28.refs_2_ = bf16[4,24,1152]{2,1,0:T(8,128)(2,1)S(1)} collective-permute-done((bf16[4,24,1152]{2,1,0:T(8,128)(2,1)}, bf16[4,24,1152]{2,1,0:T(8,128)(2,1)S(1)}, u32[]{:S(2)}, u32[]{:S(2)}) %collective-permute-start.28) | collective-permute-done | bytes 221216 | tf_op jit(solution)/shard_map/ppermute | solution.py:538
  140.2 6.5 %all-to-all-start.1 = ((f32[32,1,2640]{2,1,0:T(1,128)}), f32[32,1,2640]{2,1,0:T(1,128)}, u32[]{:S(2)}, u32[]{:S(2)}) async-start(f32[32,1,2640]{2,1,0:T(1,128)} %broadcast_in_dim.65), calls=%async_computation.1 | async-start | bytes 688128 | tf_op jit(solution)/shard_map/all_to_all | solution.py:838
  155.0 6.5 %all-to-all-done.1 = f32[32,1,2640]{2,1,0:T(1,128)} async-done(((f32[32,1,2640]{2,1,0:T(1,128)}), f32[32,1,2640]{2,1,0:T(1,128)}, u32[]{:S(2)}, u32[]{:S(2)}) %all-to-all-start.1) | async-done | bytes 337952 | tf_op jit(solution)/shard_map/all_to_all | solution.py:838
  162.6 1.5 collective-permute-start.31
  167.0 5.3 %all-to-all-start.2 = ((f32[32,1,768]{2,1,0:T(1,128)}), f32[32,1,768]{2,1,0:T(1,128)S(1)}, u32[]{:S(2)}, u32[]{:S(2)}) async-start(f32[32,1,768]{2,1,0:T(1,128)} %broadcast_in_dim.67), calls=%async_computation.2 | async-start | bytes 196608 | tf_op jit(solution)/shard_map/all_to_all | solution.py:900
  174.6 1.4 collective-permute-start.39
  177.4 6.7 %collective-permute-done.38.refs_3_ = bf16[24,2304]{1,0:T(8,128)(2,1)S(1)} collective-permute-done((bf16[24,2304]{1,0:T(8,128)(2,1)S(1)}, bf16[24,2304]{1,0:T(8,128)(2,1)S(1)}, u32[]{:S(2)}, u32[]{:S(2)}) %collective-permute-start.38) | collective-permute-done | bytes 110624 | tf_op jit(solution)/shard_map/ppermute | solution.py:538
  184.2 2.0 %collective-permute-done.39.refs_4_ = bf16[24,2304]{1,0:T(8,128)(2,1)S(1)} collective-permute-done((bf16[24,2304]{1,0:T(8,128)(2,1)S(1)}, bf16[24,2304]{1,0:T(8,128)(2,1)S(1)}, u32[]{:S(2)}, u32[]{:S(2)}) %collective-permute-start.39) | collective-permute-done | bytes 110624 | tf_op jit(solution)/shard_map/ppermute | solution.py:538
  188.1 2.2 %fusion.5 = f32[1000,384]{1,0:T(8,128)} fusion(s32[32]{0:T(128)S(1)} %eq.24, f32[32,384]{1,0:T(8,128)S(1)} %copy-done.38, f32[32,384]{1,0:T(8,128)S(1)} %reshape.76), kind=kOutput, calls=%fused_computation.27 | convolution fusion | flops 147598592 | bytes 1634432 | tf_op jit(solution)/shard_map/dot_general | solution.py:904
  (204 shorter events, 66.9 us)
Async XLA Ops:
  4.2 18.3 %collective-permute-start = (bf16[2,128,384]{2,1,0:T(8,128)(2,1)S(1)}, bf16[2,128,384]{2,1,0:T(8,128)(2,1)S(1)}, u32[]{:S(2)}, u32[]{:S(2)}) collective-permute-start(bf16[2,128,384]{2,1,0:T(8,128)(2,1)S(1)} %get-tuple-element.144), channel_id=1, source_target_pairs={{0,1},{1,0},{2,3},{3,2},{4,5},{5,4},{6,7},{7,6},{8,9},{9,8},{10,11... | collective-permute-start | bytes 589832 | tf_op jit(solution)/shard_map/ppermute | solution.py:534
  8.5 10.6 %collective-permute-start.4 = (bf16[24,2304]{1,0:T(8,128)(2,1)S(1)}, bf16[24,2304]{1,0:T(8,128)(2,1)S(1)}, u32[]{:S(2)}, u32[]{:S(2)}) collective-permute-start(bf16[24,2304]{1,0:T(8,128)(2,1)S(1)} %get-tuple-element.148.refs_1_), channel_id=1, source_target_pairs={{0,12},{1,13},{2,14},{3,15},{4,0},{5,1},{6,2},{7,3},{8,4},{9,5},{1... | collective-permute-start | bytes 331784 | tf_op jit(solution)/shard_map/ppermute | solution.py:538
  20.0 13.5 %collective-permute-start.8 = (bf16[4,24,1152]{2,1,0:T(8,128)(2,1)S(1)}, bf16[4,24,1152]{2,1,0:T(8,128)(2,1)S(1)}, u32[]{:S(2)}, u32[]{:S(2)}) collective-permute-start(bf16[4,24,1152]{2,1,0:T(8,128)(2,1)S(1)} %get-tuple-element.75.refs_1_), channel_id=1, source_target_pairs={{0,2},{1,3},{2,0},{3,1},{4,6},{5,7},{6,4},{7,5},{8,10},{9,11},{10,... | collective-permute-start | bytes 663560 | tf_op jit(solution)/shard_map/ppermute | solution.py:538
  21.3 12.2 %collective-permute-start.9 = (bf16[4,24,1152]{2,1,0:T(8,128)(2,1)S(1)}, bf16[4,24,1152]{2,1,0:T(8,128)(2,1)S(1)}, u32[]{:S(2)}, u32[]{:S(2)}) collective-permute-start(bf16[4,24,1152]{2,1,0:T(8,128)(2,1)S(1)} %get-tuple-element.76.refs_5_), channel_id=1, source_target_pairs={{0,1},{1,0},{2,3},{3,2},{4,5},{5,4},{6,7},{7,6},{8,9},{9,8},{10,11... | collective-permute-start | bytes 663560 | tf_op jit(solution)/shard_map/ppermute | solution.py:538
  22.5 11.0 %collective-permute-start.7 = (bf16[24,2304]{1,0:T(8,128)(2,1)S(1)}, bf16[24,2304]{1,0:T(8,128)(2,1)S(1)}, u32[]{:S(2)}, u32[]{:S(2)}) collective-permute-start(bf16[24,2304]{1,0:T(8,128)(2,1)S(1)} %get-tuple-element.74.refs_1_), channel_id=1, source_target_pairs={{0,12},{1,13},{2,14},{3,15},{4,0},{5,1},{6,2},{7,3},{8,4},{9,5},{1... | collective-permute-start | bytes 331784 | tf_op jit(solution)/shard_map/ppermute | solution.py:538
  36.4 25.5 %all-to-all-start = ((f32[32,1,2640]{2,1,0:T(1,128)}), f32[32,1,2640]{2,1,0:T(1,128)S(1)}, u32[]{:S(2)}, u32[]{:S(2)}) async-start(f32[32,1,2640]{2,1,0:T(1,128)} %copy.22), calls=%async_computation | async-start | bytes 688128 | tf_op jit(solution)/shard_map/all_to_all | solution.py:774
  41.8 10.7 %collective-permute-start.12 = (bf16[4,24,1152]{2,1,0:T(8,128)(2,1)S(1)}, bf16[4,24,1152]{2,1,0:T(8,128)(2,1)S(1)}, u32[]{:S(2)}, u32[]{:S(2)}) collective-permute-start(bf16[4,24,1152]{2,1,0:T(8,128)(2,1)S(1)} %get-tuple-element.76.refs_5_), channel_id=1, source_target_pairs={{0,2},{1,3},{2,0},{3,1},{4,6},{5,7},{6,4},{7,5},{8,10},{9,11},{10,... | collective-permute-start | bytes 663560 | tf_op jit(solution)/shard_map/ppermute | solution.py:538
  42.9 12.8 %collective-permute-start.15 = (bf16[4,24,1152]{2,1,0:T(8,128)(2,1)}, bf16[4,24,1152]{2,1,0:T(8,128)(2,1)}, u32[]{:S(2)}, u32[]{:S(2)}) collective-permute-start(bf16[4,24,1152]{2,1,0:T(8,128)(2,1)} %get-tuple-element.88.refs_1_), channel_id=1, source_target_pairs={{0,2},{1,3},{2,0},{3,1},{4,6},{5,7},{6,4},{7,5},{8,10},{9,11},{10,... | collective-permute-start | bytes 663560 | tf_op jit(solution)/shard_map/ppermute | solution.py:538
  43.2 13.4 %collective-permute-start.19 = (bf16[4,24,1152]{2,1,0:T(8,128)(2,1)}, bf16[4,24,1152]{2,1,0:T(8,128)(2,1)}, u32[]{:S(2)}, u32[]{:S(2)}) collective-permute-start(bf16[4,24,1152]{2,1,0:T(8,128)(2,1)} %get-tuple-element.89.refs_5_), channel_id=1, source_target_pairs={{0,1},{1,0},{2,3},{3,2},{4,5},{5,4},{6,7},{7,6},{8,9},{9,8},{10,11... | collective-permute-start | bytes 663560 | tf_op jit(solution)/shard_map/ppermute | solution.py:538
  43.5 16.9 %collective-permute-start.11 = (bf16[4,24,1152]{2,1,0:T(8,128)(2,1)S(1)}, bf16[4,24,1152]{2,1,0:T(8,128)(2,1)S(1)}, u32[]{:S(2)}, u32[]{:S(2)}) collective-permute-start(bf16[4,24,1152]{2,1,0:T(8,128)(2,1)S(1)} %collective-permute-done.8.refs_7_.refs_2_), channel_id=1, source_target_pairs={{0,1},{1,0},{2,3},{3,2},{4,5},{5,4},{6,7},{7,6},{8,9},{9,8},{10,11... | collective-permute-start | bytes 663560 | tf_op jit(solution)/shard_map/ppermute | solution.py:538
  50.8 11.1 %collective-permute-start.13 = (bf16[4,24,1152]{2,1,0:T(8,128)(2,1)S(1)}, bf16[4,24,1152]{2,1,0:T(8,128)(2,1)S(1)}, u32[]{:S(2)}, u32[]{:S(2)}) collective-permute-start(bf16[4,24,1152]{2,1,0:T(8,128)(2,1)S(1)} %collective-permute-done.9.refs_8_.refs_7_), channel_id=1, source_target_pairs={{0,2},{1,3},{2,0},{3,1},{4,6},{5,7},{6,4},{7,5},{8,10},{9,11},{10,... | collective-permute-start | bytes 663560 | tf_op jit(solution)/shard_map/ppermute | solution.py:538
  52.4 18.8 %collective-permute-start.16 = (bf16[4,24,1152]{2,1,0:T(8,128)(2,1)}, bf16[4,24,1152]{2,1,0:T(8,128)(2,1)}, u32[]{:S(2)}, u32[]{:S(2)}) collective-permute-start(bf16[4,24,1152]{2,1,0:T(8,128)(2,1)} %get-tuple-element.88.refs_1_), channel_id=1, source_target_pairs={{0,1},{1,0},{2,3},{3,2},{4,5},{5,4},{6,7},{7,6},{8,9},{9,8},{10,11... | collective-permute-start | bytes 663560 | tf_op jit(solution)/shard_map/ppermute | solution.py:538
  55.8 15.5 %collective-permute-start.18 = (bf16[4,24,1152]{2,1,0:T(8,128)(2,1)}, bf16[4,24,1152]{2,1,0:T(8,128)(2,1)}, u32[]{:S(2)}, u32[]{:S(2)}) collective-permute-start(bf16[4,24,1152]{2,1,0:T(8,128)(2,1)} %get-tuple-element.89.refs_5_), channel_id=1, source_target_pairs={{0,2},{1,3},{2,0},{3,1},{4,6},{5,7},{6,4},{7,5},{8,10},{9,11},{10,... | collective-permute-start | bytes 663560 | tf_op jit(solution)/shard_map/ppermute | solution.py:538
  56.6 14.6 %collective-permute-start.17 = (bf16[4,24,1152]{2,1,0:T(8,128)(2,1)}, bf16[4,24,1152]{2,1,0:T(8,128)(2,1)}, u32[]{:S(2)}, u32[]{:S(2)}) collective-permute-start(bf16[4,24,1152]{2,1,0:T(8,128)(2,1)} %collective-permute-done.15.refs_2_), channel_id=1, source_target_pairs={{0,1},{1,0},{2,3},{3,2},{4,5},{5,4},{6,7},{7,6},{8,9},{9,8},{10,11... | collective-permute-start | bytes 663560 | tf_op jit(solution)/shard_map/ppermute | solution.py:538
  60.4 10.8 %collective-permute-start.20 = (bf16[4,24,1152]{2,1,0:T(8,128)(2,1)}, bf16[4,24,1152]{2,1,0:T(8,128)(2,1)}, u32[]{:S(2)}, u32[]{:S(2)}) collective-permute-start(bf16[4,24,1152]{2,1,0:T(8,128)(2,1)} %collective-permute-done.19.refs_7_), channel_id=1, source_target_pairs={{0,2},{1,3},{2,0},{3,1},{4,6},{5,7},{6,4},{7,5},{8,10},{9,11},{10,... | collective-permute-start | bytes 663560 | tf_op jit(solution)/shard_map/ppermute | solution.py:538
  104.7 11.6 %collective-permute-start.26 = (bf16[4,2,24,1152]{3,2,1,0:T(8,128)(2,1)}, bf16[4,2,24,1152]{3,2,1,0:T(8,128)(2,1)}, u32[]{:S(2)}, u32[]{:S(2)}) collective-permute-start(bf16[4,2,24,1152]{3,2,1,0:T(8,128)(2,1)} %get-tuple-element.101), channel_id=1, source_target_pairs={{0,2},{1,3},{2,0},{3,1},{4,6},{5,7},{6,4},{7,5},{8,10},{9,11},{10,... | collective-permute-start | bytes 1327112 | tf_op jit(solution)/shard_map/ppermute | solution.py:538
  105.5 11.3 %collective-permute-start.27 = (bf16[4,2,24,1152]{3,2,1,0:T(8,128)(2,1)}, bf16[4,2,24,1152]{3,2,1,0:T(8,128)(2,1)}, u32[]{:S(2)}, u32[]{:S(2)}) collective-permute-start(bf16[4,2,24,1152]{3,2,1,0:T(8,128)(2,1)} %get-tuple-element.103), channel_id=1, source_target_pairs={{0,1},{1,0},{2,3},{3,2},{4,5},{5,4},{6,7},{7,6},{8,9},{9,8},{10,11... | collective-permute-start | bytes 1327112 | tf_op jit(solution)/shard_map/ppermute | solution.py:538
  110.0 23.5 %collective-permute-start.24 = (bf16[4,2,24,1152]{3,2,1,0:T(8,128)(2,1)}, bf16[4,2,24,1152]{3,2,1,0:T(8,128)(2,1)S(1)}, u32[]{:S(2)}, u32[]{:S(2)}) collective-permute-start(bf16[4,2,24,1152]{3,2,1,0:T(8,128)(2,1)} %get-tuple-element.97), channel_id=1, source_target_pairs={{0,2},{1,3},{2,0},{3,1},{4,6},{5,7},{6,4},{7,5},{8,10},{9,11},{10,... | collective-permute-start | bytes 1327112 | tf_op jit(solution)/shard_map/ppermute | solution.py:538
  111.0 22.5 %collective-permute-start.25 = (bf16[4,2,24,1152]{3,2,1,0:T(8,128)(2,1)}, bf16[4,2,24,1152]{3,2,1,0:T(8,128)(2,1)S(1)}, u32[]{:S(2)}, u32[]{:S(2)}) collective-permute-start(bf16[4,2,24,1152]{3,2,1,0:T(8,128)(2,1)} %get-tuple-element.99), channel_id=1, source_target_pairs={{0,1},{1,0},{2,3},{3,2},{4,5},{5,4},{6,7},{7,6},{8,9},{9,8},{10,11... | collective-permute-start | bytes 1327112 | tf_op jit(solution)/shard_map/ppermute | solution.py:538
  118.9 12.0 %collective-permute-start.28 = (bf16[4,24,1152]{2,1,0:T(8,128)(2,1)}, bf16[4,24,1152]{2,1,0:T(8,128)(2,1)S(1)}, u32[]{:S(2)}, u32[]{:S(2)}) collective-permute-start(bf16[4,24,1152]{2,1,0:T(8,128)(2,1)} %get-tuple-element.107), channel_id=1, source_target_pairs={{0,1},{1,0},{2,3},{3,2},{4,5},{5,4},{6,7},{7,6},{8,9},{9,8},{10,11... | collective-permute-start | bytes 663560 | tf_op jit(solution)/shard_map/ppermute | solution.py:538
  119.3 11.6 %collective-permute-start.29 = (bf16[4,24,1152]{2,1,0:T(8,128)(2,1)}, bf16[4,24,1152]{2,1,0:T(8,128)(2,1)S(1)}, u32[]{:S(2)}, u32[]{:S(2)}) collective-permute-start(bf16[4,24,1152]{2,1,0:T(8,128)(2,1)} %get-tuple-element.109), channel_id=1, source_target_pairs={{0,2},{1,3},{2,0},{3,1},{4,6},{5,7},{6,4},{7,5},{8,10},{9,11},{10,... | collective-permute-start | bytes 663560 | tf_op jit(solution)/shard_map/ppermute | solution.py:538
  138.7 12.7 %collective-permute-start.30 = (bf16[4,1,128,384]{3,2,1,0:T(8,128)(2,1)}, bf16[4,1,128,384]{3,2,1,0:T(8,128)(2,1)}, u32[]{:S(2)}, u32[]{:S(2)}) collective-permute-start(bf16[4,1,128,384]{3,2,1,0:T(8,128)(2,1)} %get-tuple-element.140), channel_id=1, source_target_pairs={{0,1},{1,0},{2,3},{3,2},{4,5},{5,4},{6,7},{7,6},{8,9},{9,8},{10,11... | collective-permute-start | bytes 1179656 | tf_op jit(solution)/shard_map/ppermute | solution.py:534
  140.2 21.3 %all-to-all-start.1 = ((f32[32,1,2640]{2,1,0:T(1,128)}), f32[32,1,2640]{2,1,0:T(1,128)}, u32[]{:S(2)}, u32[]{:S(2)}) async-start(f32[32,1,2640]{2,1,0:T(1,128)} %broadcast_in_dim.65), calls=%async_computation.1 | async-start | bytes 688128 | tf_op jit(solution)/shard_map/all_to_all | solution.py:838
  146.7 18.9 %collective-permute-start.32 = (bf16[4,24,1152]{2,1,0:T(8,128)(2,1)}, bf16[4,24,1152]{2,1,0:T(8,128)(2,1)S(1)}, u32[]{:S(2)}, u32[]{:S(2)}) collective-permute-start(bf16[4,24,1152]{2,1,0:T(8,128)(2,1)} %get-tuple-element.114), channel_id=1, source_target_pairs={{0,1},{1,0},{2,3},{3,2},{4,5},{5,4},{6,7},{7,6},{8,9},{9,8},{10,11... | collective-permute-start | bytes 663560 | tf_op jit(solution)/shard_map/ppermute | solution.py:538
  147.9 17.6 %collective-permute-start.33 = (bf16[4,24,1152]{2,1,0:T(8,128)(2,1)S(1)}, bf16[4,24,1152]{2,1,0:T(8,128)(2,1)S(1)}, u32[]{:S(2)}, u32[]{:S(2)}) collective-permute-start(bf16[4,24,1152]{2,1,0:T(8,128)(2,1)S(1)} %get-tuple-element.116), channel_id=1, source_target_pairs={{0,2},{1,3},{2,0},{3,1},{4,6},{5,7},{6,4},{7,5},{8,10},{9,11},{10,... | collective-permute-start | bytes 663560 | tf_op jit(solution)/shard_map/ppermute | solution.py:538
  149.1 13.5 %collective-permute-start.34 = (bf16[24,2304]{1,0:T(8,128)(2,1)S(1)}, bf16[24,2304]{1,0:T(8,128)(2,1)S(1)}, u32[]{:S(2)}, u32[]{:S(2)}) collective-permute-start(bf16[24,2304]{1,0:T(8,128)(2,1)S(1)} %copy-done.32), channel_id=1, source_target_pairs={{0,4},{1,5},{2,6},{3,7},{4,8},{5,9},{6,10},{7,11},{8,12},{9,13},{1... | collective-permute-start | bytes 331784 | tf_op jit(solution)/shard_map/ppermute | solution.py:538
  150.3 13.8 %collective-permute-start.35 = (bf16[24,2304]{1,0:T(8,128)(2,1)S(1)}, bf16[24,2304]{1,0:T(8,128)(2,1)S(1)}, u32[]{:S(2)}, u32[]{:S(2)}) collective-permute-start(bf16[24,2304]{1,0:T(8,128)(2,1)S(1)} %copy-done.30), channel_id=1, source_target_pairs={{0,8},{1,9},{2,10},{3,11},{4,12},{5,13},{6,14},{7,15},{8,0},{9,1},... | collective-permute-start | bytes 331784 | tf_op jit(solution)/shard_map/ppermute | solution.py:538
  151.5 14.0 %collective-permute-start.36 = (bf16[24,2304]{1,0:T(8,128)(2,1)S(1)}, bf16[24,2304]{1,0:T(8,128)(2,1)S(1)}, u32[]{:S(2)}, u32[]{:S(2)}) collective-permute-start(bf16[24,2304]{1,0:T(8,128)(2,1)S(1)} %copy-done.28), channel_id=1, source_target_pairs={{0,12},{1,13},{2,14},{3,15},{4,0},{5,1},{6,2},{7,3},{8,4},{9,5},{1... | collective-permute-start | bytes 331784 | tf_op jit(solution)/shard_map/ppermute | solution.py:538
  162.6 28.4 %collective-permute-start.31 = (bf16[2,2,128,384]{3,2,1,0:T(8,128)(2,1)}, bf16[2,2,128,384]{3,2,1,0:T(8,128)(2,1)}, u32[]{:S(2)}, u32[]{:S(2)}) collective-permute-start(bf16[2,2,128,384]{3,2,1,0:T(8,128)(2,1)} %get-tuple-element.138), channel_id=1, source_target_pairs={{0,16},{16,0},{1,17},{17,1},{2,18},{18,2},{3,19},{19,3},{4,20},{20... | collective-permute-start | bytes 1179656 | tf_op jit(solution)/shard_map/ppermute | solution.py:534
  167.0 20.1 %all-to-all-start.2 = ((f32[32,1,768]{2,1,0:T(1,128)}), f32[32,1,768]{2,1,0:T(1,128)S(1)}, u32[]{:S(2)}, u32[]{:S(2)}) async-start(f32[32,1,768]{2,1,0:T(1,128)} %broadcast_in_dim.67), calls=%async_computation.2 | async-start | bytes 196608 | tf_op jit(solution)/shard_map/all_to_all | solution.py:900
  173.6 10.6 %collective-permute-start.38 = (bf16[24,2304]{1,0:T(8,128)(2,1)S(1)}, bf16[24,2304]{1,0:T(8,128)(2,1)S(1)}, u32[]{:S(2)}, u32[]{:S(2)}) collective-permute-start(bf16[24,2304]{1,0:T(8,128)(2,1)S(1)} %get-tuple-element.127), channel_id=1, source_target_pairs={{0,8},{1,9},{2,10},{3,11},{4,12},{5,13},{6,14},{7,15},{8,0},{9,1},... | collective-permute-start | bytes 331784 | tf_op jit(solution)/shard_map/ppermute | solution.py:538
  174.6 11.6 %collective-permute-start.39 = (bf16[24,2304]{1,0:T(8,128)(2,1)S(1)}, bf16[24,2304]{1,0:T(8,128)(2,1)S(1)}, u32[]{:S(2)}, u32[]{:S(2)}) collective-permute-start(bf16[24,2304]{1,0:T(8,128)(2,1)S(1)} %get-tuple-element.128), channel_id=1, source_target_pairs={{0,12},{1,13},{2,14},{3,15},{4,0},{5,1},{6,2},{7,3},{8,4},{9,5},{1... | collective-permute-start | bytes 331784 | tf_op jit(solution)/shard_map/ppermute | solution.py:538
  (55 other events, 380.3 us)

commit v10 on v8

--- a/solution.py
+++ b/solution.py
@@ -527,6 +527,15 @@
     )(*operands, *after)
 
 
+def hand_kernel(rank_ref, former, latter):
+    latter[...] = former[...]
+
+
+def hand_on(rank, block, after):
+    shape = jax.ShapeDtypeStruct(block.shape, block.dtype)
+    return in_memory(hand_kernel, [shape], [rank, block], after=after)[0]
+
+
 def pair_swap(block, axis):
     return lax.ppermute(block, axis, [(0, 1), (1, 0)])
 
@@ -547,15 +556,16 @@
     return [block] + [rotate(block, size, turn) for turn in range(1, size // 4)]
 
 
-def gather_along_z(shard, place, size, handed=(), after=()):
-    high = size // 4
-    rows, lanes = shard.shape
+def gather_along_z(shards, place, handed=(), after=()):
+    high = len(shards)
+    rows, lanes = shards[0].shape
     return in_memory(
         partial(stack_kernel, high, lanes // 2),
-        [jax.ShapeDtypeStruct((high, rows, lanes // 2), shard.dtype)] * 2
+        [jax.ShapeDtypeStruct((high, rows, lanes // 2), shards[0].dtype)] * 2
         + [jax.ShapeDtypeStruct(block.shape, block.dtype) for block in handed],
-        [place, *rotations(shard, size), *handed],
+        [place, *shards, *handed],
         scratch=[pltpu.SemaphoreType.DMA((high + len(handed), 2))],
+        memory=pl.ANY,
         after=after,
     )
 
@@ -573,6 +583,7 @@
         [jax.ShapeDtypeStruct((high, 2, 2, rows, 2 * lanes), first.dtype)],
         [place, first, first_x, first_y, first_both, second, second_x, second_y, second_both],
         scratch=[pltpu.SemaphoreType.DMA((8,))],
+        memory=pl.ANY,
     )
     return full.reshape(size * rows, 2 * lanes)
 
@@ -752,9 +763,9 @@
     silu_all = jax.nn.silu(conditions).astype(jnp.bfloat16)
     silu_own = lax.dynamic_slice_in_dim(silu_all, ring_rank * rows, rows, 1)
     if compact:
-        *first_parts, second_shard, silu_late = gather_along_z(
-            first_shard, place, ring_size, handed=(second_shard, silu_own)
-        )
+        first_shards = rotations(first_shard, ring_size)
+        silu_late = hand_on(rank, silu_own, (first_shards[1],))
+        *first_parts, second_shard = gather_along_z(first_shards, place, handed=(second_shard,))
         first_parts += first_flips(*first_parts, ring_size)
     else:
         silu_late = silu_own
@@ -772,7 +783,7 @@
 
     if compact:
         second_parts = gather_along_z(
-            second_shard, place, ring_size, after=(products, both, *first_parts[2:])
+            rotations(second_shard, ring_size), place, after=(products, both, *first_parts[2:])
         )
         second_parts += first_flips(*second_parts, ring_size)
         first_pack = gather_across(*first_parts, place, ring_size)
@@ -831,6 +842,25 @@
             [scatter_sum(chip_sum(keep, got), ring_rank, ring_size)]
             for keep, got in ((first_keep, first_got), (second_keep, second_got))
         ]
+    rows_back = jnp.concatenate(
+        [
+            jnp.concatenate(
+                [jnp.broadcast_to(dmod, (ring_size, 6 * width)), sums], axis=1
+            )
+            for dmod, sums in ((first_dmod, first_sums), (second_dmod, second_sums))
+        ]
+    )
+    every = lax.all_to_all(rows_back[:, None], ("section", "dp", "seq"), 0, 0, tiled=True)
+    every = every[::sharers, 0]
+    bias_grad = jnp.sum(every[:, 6 * width :], axis=0)
+    modulation_rows = low(every[:, : 6 * width])
+    modulation_grad = outer_sum(silu_own, modulation_rows)
+    columns = matmul_transposed(modulation_rows, modulation_weight[0])
+    if compact:
+        columns = hand_on(rank, columns, (second_pieces[1],))
+    columns = jnp.broadcast_to(columns.reshape(1, 1, -1), (sections * ring_size, 1, columns.size))
+    columns = lax.all_to_all(columns, ("section", "dp", "seq"), 0, 0, tiled=True)
+
     outputs_ready = (first_low * live, second_low * live)
     if compact:
         block = jnp.stack([outputs_ready[0], first_grad, outputs_ready[1], second_grad])
@@ -856,6 +886,7 @@
         partial(close_kernel, len(first_pieces)),
         [shard, shard],
         [rank, *first_pieces, *second_pieces],
+        after=(columns,),
     )
     att, out, up, down = in_memory(
         spread_kernel,
@@ -871,22 +902,6 @@
         [rank, mine, pair_swap(send, "section")],
     )
 
-    rows_back = jnp.concatenate(
-        [
-            jnp.concatenate(
-                [jnp.broadcast_to(dmod, (ring_size, 6 * width)), sums], axis=1
-            )
-            for dmod, sums in ((first_dmod, first_sums), (second_dmod, second_sums))
-        ]
-    )
-    every = lax.all_to_all(rows_back[:, None], ("section", "dp", "seq"), 0, 0, tiled=True)
-    every = every[::sharers, 0]
-    bias_grad = jnp.sum(every[:, 6 * width :], axis=0)
-    modulation_rows = low(every[:, : 6 * width])
-    modulation_grad = outer_sum(silu_own, modulation_rows)
-    columns = matmul_transposed(modulation_rows, modulation_weight[0])
-    columns = jnp.broadcast_to(columns.reshape(1, 1, -1), (sections * ring_size, 1, columns.size))
-    columns = lax.all_to_all(columns, ("section", "dp", "seq"), 0, 0, tiled=True)
     columns = jnp.sum(columns.reshape(sections, ring_size, -1, rows), axis=0)
     products_back = jnp.swapaxes(columns, 0, 1).reshape(-1, width)
     _, silu_back = jax.vjp(jax.nn.silu, conditions)

time: 183 us -> 181 us (0.989)
  waiting for transfers between devices: 44.5 us -> 39.5 us
    ppermute x9, waiting for transfers between devices: 4.77 us -> 0.02 us  [pair_swap(): return lax.ppermute(block, axis, [(0, 1), (1, 0)])]
    ppermute x32, starting transfers between devices: 31.9 us -> 34.1 us  [ring_exchange(): return lax.ppermute(block, RING, [(i, step(i)) for i in range(size)])]
    ppermute x9, starting transfers between devices: 13.7 us -> 11.6 us  [pair_swap(): return lax.ppermute(block, axis, [(0, 1), (1, 0)])]
    unnamed x76 -> x78, local copies, waits for them, and re-layouts: 11.9 us -> 12.6 us
    pallas_call x13 -> x15, Pallas kernels: 14 us -> 14 us  [in_memory(): pl.pallas_call(body, out_shape=shapes, in_specs=specs, out_specs=[pl.Bloc...]
  transfers between devices with their start and end apart: 44 -> 44, of which waited for: 16 -> 10; matrix products, arithmetic and copies ran while one was open for 8% -> 10% of each run, Pallas kernels for 13% -> 14%
where the time goes in v10:
time: 181 us; the launch traced here: 180 us
  starting transfers between devices  64.8 us (36%)
  Pallas kernels  39.9 us (22%)
  waiting for transfers between devices  39.5 us (22%)
  local copies, waits for them, and re-layouts  19.8 us (11%)
  other arithmetic  10 us (6%)
  matrix products  3.7 us (2%)
  between operations  1.99 us (1%)
    ppermute x32, waiting for transfers between devices, ring_exchange(): return lax.ppermute(block, RING, [(i, step(i)) for i in range(size)])  39.5 us
    ppermute x32, starting transfers between devices, ring_exchange(): return lax.ppermute(block, RING, [(i, step(i)) for i in range(size)])  34.1 us
    pallas_call x3, Pallas kernels, run_section(): pl.pallas_call(partial(section_kernel, layout, forward, backward, len(aft...  25.9 us
    pallas_call x15, Pallas kernels, in_memory(): pl.pallas_call(body, out_shape=shapes, in_specs=specs, out_specs=[pl.Bloc...  14 us
    unnamed x78, local copies, waits for them, and re-layouts  12.6 us
    ppermute x9, starting transfers between devices, pair_swap(): return lax.ppermute(block, axis, [(0, 1), (1, 0)])  11.6 us
    all_to_all x1, starting transfers between devices, per_device(): lax.all_to_all(products[:, None], ('section', 'dp', 'seq'), 0, 0, tiled=T...  6.5 us
    all_to_all x1, starting transfers between devices, per_device(): lax.all_to_all(columns, ('section', 'dp', 'seq'), 0, 0, tiled=True)  6.44 us
  transfers between devices with their start and end apart: 44, of which 10 were waited for; matrix products, arithmetic and copies ran while one was open for 10% of the time, Pallas kernels for 14%

profile of v10, /device:TPU:9, one launch (start us, length us, event | category | flops | bytes accessed | tf_op | source)
XLA Modules:
  0.0 179.8 jit_solution(15380548870463959594)
XLA Ops:
  0.7 1.7 shard_map.178
  7.3 3.3 %collective-permute-done.2.refs_2_ = bf16[24,2304]{1,0:T(8,128)(2,1)S(1)} collective-permute-done((bf16[24,2304]{1,0:T(8,128)(2,1)S(1)}, bf16[24,2304]{1,0:T(8,128)(2,1)S(1)}, u32[]{:S(2)}, u32[]{:S(2)}) %collective-permute-start.2) | collective-permute-done | bytes 110624 | tf_op jit(solution)/shard_map/ppermute | solution.py:544
  11.8 6.5 %all-to-all-start = ((f32[32,1,2640]{2,1,0:T(1,128)}), f32[32,1,2640]{2,1,0:T(1,128)S(1)}, u32[]{:S(2)}, u32[]{:S(2)}) async-start(f32[32,1,2640]{2,1,0:T(1,128)} %copy.22), calls=%async_computation | async-start | bytes 688128 | tf_op jit(solution)/shard_map/all_to_all | solution.py:776
  20.7 2.2 %collective-permute-start.3 = (bf16[24,2304]{1,0:T(8,128)(2,1)S(1)}, bf16[24,2304]{1,0:T(8,128)(2,1)S(1)}, u32[]{:S(2)}, u32[]{:S(2)}) collective-permute-start(bf16[24,2304]{1,0:T(8,128)(2,1)S(1)} %get-tuple-element.144.refs_1_), channel_id=1, source_target_pairs={{0,8},{1,9},{2,10},{3,11},{4,12},{5,13},{6,14},{7,15},{8,0},{9,1},... | collective-permute-start | bytes 331784 | tf_op jit(solution)/shard_map/ppermute | solution.py:544
  23.1 10.0 %collective-permute-done.3.refs_3_ = bf16[24,2304]{1,0:T(8,128)(2,1)S(1)} collective-permute-done((bf16[24,2304]{1,0:T(8,128)(2,1)S(1)}, bf16[24,2304]{1,0:T(8,128)(2,1)S(1)}, u32[]{:S(2)}, u32[]{:S(2)}) %collective-permute-start.3) | collective-permute-done | bytes 110624 | tf_op jit(solution)/shard_map/ppermute | solution.py:544
  33.1 1.8 collective-permute-done.4.refs_4_
  38.4 1.4 collective-permute-start.13
  39.8 1.4 collective-permute-start.14
  44.5 3.7 %collective-permute-done.14.refs_4_ = bf16[24,2304]{1,0:T(8,128)(2,1)S(1)} collective-permute-done((bf16[24,2304]{1,0:T(8,128)(2,1)S(1)}, bf16[24,2304]{1,0:T(8,128)(2,1)S(1)}, u32[]{:S(2)}, u32[]{:S(2)}) %collective-permute-start.14) | collective-permute-done | bytes 110624 | tf_op jit(solution)/shard_map/ppermute | solution.py:544
  49.4 2.1 %collective-permute-start.19 = (bf16[4,24,1152]{2,1,0:T(8,128)(2,1)S(1)}, bf16[4,24,1152]{2,1,0:T(8,128)(2,1)S(1)}, u32[]{:S(2)}, u32[]{:S(2)}) collective-permute-start(bf16[4,24,1152]{2,1,0:T(8,128)(2,1)S(1)} %get-tuple-element.86.refs_5_), channel_id=1, source_target_pairs={{0,1},{1,0},{2,3},{3,2},{4,5},{5,4},{6,7},{7,6},{8,9},{9,8},{10,11... | collective-permute-start | bytes 663560 | tf_op jit(solution)/shard_map/ppermute | solution.py:544
  52.1 1.4 collective-permute-start.16
  53.6 2.8 %collective-permute-done.15.refs_2_ = bf16[4,24,1152]{2,1,0:T(8,128)(2,1)S(1)} collective-permute-done((bf16[4,24,1152]{2,1,0:T(8,128)(2,1)S(1)}, bf16[4,24,1152]{2,1,0:T(8,128)(2,1)S(1)}, u32[]{:S(2)}, u32[]{:S(2)}) %collective-permute-start.15) | collective-permute-done | bytes 221216 | tf_op jit(solution)/shard_map/ppermute | solution.py:544
  57.4 1.5 collective-permute-start.20
  64.8 5.5 %collective-permute-start.11 = (bf16[384,2304]{1,0:T(8,128)(2,1)S(1)}, bf16[384,2304]{1,0:T(8,128)(2,1)}, u32[]{:S(2)}, u32[]{:S(2)}) collective-permute-start(bf16[384,2304]{1,0:T(8,128)(2,1)S(1)} %bitcast.59), channel_id=1, source_target_pairs={{0,16},{16,0},{1,17},{17,1},{2,18},{18,2},{3,19},{19,3},{4,20},{20... | collective-permute-start | bytes 5308424 | tf_op jit(solution)/shard_map/ppermute | solution.py:540
  70.3 2.1 %shard_map.184 = bf16[4,2,2,24,2304]{4,3,2,1,0:T(8,128)(2,1)} custom-call(s32[3]{0:T(128)S(1)} %pad_add_fusion.refs_0_, bf16[4,24,1152]{2,1,0:T(8,128)(2,1)S(1)} %get-tuple-element.85.refs_1_, bf16[4,24,1152]{2,1,0:T(8,128)(2,1)S(1)} %collective-permute-done.15.refs_2_, bf16[4,24,1152]{2,1,0:T(8,128)(2,1)S(1)} %collective-permute-done.16.refs_3_, ...), custom_call_target="tpu_custom_call" | custom-call | bytes 5308416 | tf_op jit(solution)/shard_map/pallas_call | solution.py:519
  72.3 1.8 collective-permute-start.21
  75.5 5.7 %shard_map.182 = (bf16[256,384]{1,0:T(8,128)(2,1)S(1)}, f32[1,2304]{1,0:T(1,128)S(1)}, bf16[256,1152]{1,0:T(8,128)(2,1)S(1)}, bf16[256,384]{1,0:T(8,128)(2,1)S(1...) custom-call(s32[1]{0:T(128)} %bitcast.refs_0_, ...), custom_call_target="tpu_custom_call" | custom-call | flops 1006632960 | bytes 5308416 | tf_op jit(solution)/shard_map/pallas_call | solution.py:352
  81.2 12.7 %shard_map.185 = (bf16[256,384]{1,0:T(8,128)(2,1)S(1)}, bf16[256,384]{1,0:T(8,128)(2,1)S(1)}, f32[1,2304]{1,0:T(1,128)S(1)}, f32[16,336]{1,0:T(8,128)S(1)}, bf16...) custom-call(s32[1]{0:T(128)} %bitcast.refs_0_, bf16[256,384]{1,0:T(8,128)(2,1)S(1)} %get-tuple-element.74.refs_1_, ...), custom_call_target="tpu_custom_call" | custom-call | flops 3019898880 | bytes 10616832 | tf_op jit(solution)/shard_map/pallas_call | solution.py:352
  94.0 7.6 %shard_map.186 = (bf16[256,384]{1,0:T(8,128)(2,1)S(1)}, f32[1,2304]{1,0:T(1,128)S(1)}, f32[16,336]{1,0:T(8,128)S(1)}, bf16[384,2304]{1,0:T(8,128)(2,1)S(1)}, bf16[384,2304]{1,0:T(8,128)(2,1)}) custom-call(s32[1]{0:T(128)} %bitcast.refs_0_, bf16[256,384]{1,0:T(8,128)(2,1)S(1)} %get-tuple-element.138.refs_1_, f32[1,2304]{1,0:T(1,128)S(1)} %get-tuple-element.75.refs_2_, ...), custom_call_target="tpu_custom_call" | custom-call | flops 2013265920 | bytes 10616832 | tf_op jit(solution)/shard_map/pallas_call | solution.py:352
  101.7 1.7 shard_map.187
  106.4 1.5 copy-done.2
  107.9 1.7 shard_map.188
  113.6 6.1 %all-to-all-start.1 = ((f32[32,1,2640]{2,1,0:T(1,128)}), f32[32,1,2640]{2,1,0:T(1,128)}, u32[]{:S(2)}, u32[]{:S(2)}) async-start(f32[32,1,2640]{2,1,0:T(1,128)} %broadcast_in_dim.65), calls=%async_computation.1 | async-start | bytes 688128 | tf_op jit(solution)/shard_map/all_to_all | solution.py:853
  124.6 9.1 %collective-permute-done.28.refs_2_ = bf16[4,24,1152]{2,1,0:T(8,128)(2,1)S(1)} collective-permute-done((bf16[4,24,1152]{2,1,0:T(8,128)(2,1)S(1)}, bf16[4,24,1152]{2,1,0:T(8,128)(2,1)S(1)}, u32[]{:S(2)}, u32[]{:S(2)}) %collective-permute-start.28) | collective-permute-done | bytes 221216 | tf_op jit(solution)/shard_map/ppermute | solution.py:544
  142.6 3.3 %collective-permute-start.35 = (bf16[24,2304]{1,0:T(8,128)(2,1)}, bf16[24,2304]{1,0:T(8,128)(2,1)S(1)}, u32[]{:S(2)}, u32[]{:S(2)}) collective-permute-start(bf16[24,2304]{1,0:T(8,128)(2,1)} %copy-done.24), channel_id=1, source_target_pairs={{0,8},{1,9},{2,10},{3,11},{4,12},{5,13},{6,14},{7,15},{8,0},{9,1},... | collective-permute-start | bytes 331784 | tf_op jit(solution)/shard_map/ppermute | solution.py:544
  145.8 2.7 %collective-permute-start.36 = (bf16[24,2304]{1,0:T(8,128)(2,1)}, bf16[24,2304]{1,0:T(8,128)(2,1)S(1)}, u32[]{:S(2)}, u32[]{:S(2)}) collective-permute-start(bf16[24,2304]{1,0:T(8,128)(2,1)} %copy-done.23), channel_id=1, source_target_pairs={{0,12},{1,13},{2,14},{3,15},{4,0},{5,1},{6,2},{7,3},{8,4},{9,5},{1... | collective-permute-start | bytes 331784 | tf_op jit(solution)/shard_map/ppermute | solution.py:544
  149.3 6.4 %all-to-all-start.2 = ((f32[32,1,768]{2,1,0:T(1,128)}), f32[32,1,768]{2,1,0:T(1,128)S(1)}, u32[]{:S(2)}, u32[]{:S(2)}) async-start(f32[32,1,768]{2,1,0:T(1,128)} %broadcast_in_dim.67), calls=%async_computation.2 | async-start | bytes 196608 | tf_op jit(solution)/shard_map/all_to_all | solution.py:862
  155.8 1.6 maximum_select_fusion
  163.1 1.4 collective-permute-start.39
  166.4 5.1 %collective-permute-done.38.refs_3_ = bf16[24,2304]{1,0:T(8,128)(2,1)S(1)} collective-permute-done((bf16[24,2304]{1,0:T(8,128)(2,1)S(1)}, bf16[24,2304]{1,0:T(8,128)(2,1)S(1)}, u32[]{:S(2)}, u32[]{:S(2)}) %collective-permute-start.38) | collective-permute-done | bytes 110624 | tf_op jit(solution)/shard_map/ppermute | solution.py:544
  171.5 2.2 %collective-permute-done.39.refs_4_ = bf16[24,2304]{1,0:T(8,128)(2,1)S(1)} collective-permute-done((bf16[24,2304]{1,0:T(8,128)(2,1)S(1)}, bf16[24,2304]{1,0:T(8,128)(2,1)S(1)}, u32[]{:S(2)}, u32[]{:S(2)}) %collective-permute-start.39) | collective-permute-done | bytes 110624 | tf_op jit(solution)/shard_map/ppermute | solution.py:544
  174.4 2.2 %fusion.5 = f32[1000,384]{1,0:T(8,128)} fusion(s32[32]{0:T(128)S(1)} %eq.24, f32[32,384]{1,0:T(8,128)S(1)} %copy-done.34, f32[32,384]{1,0:T(8,128)S(1)} %reshape.76), kind=kOutput, calls=%fused_computation.27 | convolution fusion | flops 147598592 | bytes 1634432 | tf_op jit(solution)/shard_map/dot_general | solution.py:908
  (196 shorter events, 58.0 us)
Async XLA Ops:
  11.8 30.9 %all-to-all-start = ((f32[32,1,2640]{2,1,0:T(1,128)}), f32[32,1,2640]{2,1,0:T(1,128)S(1)}, u32[]{:S(2)}, u32[]{:S(2)}) async-start(f32[32,1,2640]{2,1,0:T(1,128)} %copy.22), calls=%async_computation | async-start | bytes 688128 | tf_op jit(solution)/shard_map/all_to_all | solution.py:776
  19.4 20.4 %collective-permute-start = (bf16[2,128,384]{2,1,0:T(8,128)(2,1)S(1)}, bf16[2,128,384]{2,1,0:T(8,128)(2,1)S(1)}, u32[]{:S(2)}, u32[]{:S(2)}) collective-permute-start(bf16[2,128,384]{2,1,0:T(8,128)(2,1)S(1)} %get-tuple-element.140), channel_id=1, source_target_pairs={{0,1},{1,0},{2,3},{3,2},{4,5},{5,4},{6,7},{7,6},{8,9},{9,8},{10,11... | collective-permute-start | bytes 589832 | tf_op jit(solution)/shard_map/ppermute | solution.py:540
  20.7 12.5 %collective-permute-start.3 = (bf16[24,2304]{1,0:T(8,128)(2,1)S(1)}, bf16[24,2304]{1,0:T(8,128)(2,1)S(1)}, u32[]{:S(2)}, u32[]{:S(2)}) collective-permute-start(bf16[24,2304]{1,0:T(8,128)(2,1)S(1)} %get-tuple-element.144.refs_1_), channel_id=1, source_target_pairs={{0,8},{1,9},{2,10},{3,11},{4,12},{5,13},{6,14},{7,15},{8,0},{9,1},... | collective-permute-start | bytes 331784 | tf_op jit(solution)/shard_map/ppermute | solution.py:544
  22.8 12.1 %collective-permute-start.4 = (bf16[24,2304]{1,0:T(8,128)(2,1)S(1)}, bf16[24,2304]{1,0:T(8,128)(2,1)S(1)}, u32[]{:S(2)}, u32[]{:S(2)}) collective-permute-start(bf16[24,2304]{1,0:T(8,128)(2,1)S(1)} %get-tuple-element.144.refs_1_), channel_id=1, source_target_pairs={{0,12},{1,13},{2,14},{3,15},{4,0},{5,1},{6,2},{7,3},{8,4},{9,5},{1... | collective-permute-start | bytes 331784 | tf_op jit(solution)/shard_map/ppermute | solution.py:544
  37.2 10.9 %collective-permute-start.5 = (bf16[4,24,1152]{2,1,0:T(8,128)(2,1)S(1)}, bf16[4,24,1152]{2,1,0:T(8,128)(2,1)S(1)}, u32[]{:S(2)}, u32[]{:S(2)}) collective-permute-start(bf16[4,24,1152]{2,1,0:T(8,128)(2,1)S(1)} %get-tuple-element.72.refs_1_), channel_id=1, source_target_pairs={{0,2},{1,3},{2,0},{3,1},{4,6},{5,7},{6,4},{7,5},{8,10},{9,11},{10,... | collective-permute-start | bytes 663560 | tf_op jit(solution)/shard_map/ppermute | solution.py:544
  39.8 8.3 %collective-permute-start.14 = (bf16[24,2304]{1,0:T(8,128)(2,1)S(1)}, bf16[24,2304]{1,0:T(8,128)(2,1)S(1)}, u32[]{:S(2)}, u32[]{:S(2)}) collective-permute-start(bf16[24,2304]{1,0:T(8,128)(2,1)S(1)} %get-tuple-element.84.refs_1_), channel_id=1, source_target_pairs={{0,12},{1,13},{2,14},{3,15},{4,0},{5,1},{6,2},{7,3},{8,4},{9,5},{1... | collective-permute-start | bytes 331784 | tf_op jit(solution)/shard_map/ppermute | solution.py:544
  41.2 10.2 %collective-permute-start.6 = (bf16[4,24,1152]{2,1,0:T(8,128)(2,1)S(1)}, bf16[4,24,1152]{2,1,0:T(8,128)(2,1)S(1)}, u32[]{:S(2)}, u32[]{:S(2)}) collective-permute-start(bf16[4,24,1152]{2,1,0:T(8,128)(2,1)S(1)} %get-tuple-element.72.refs_1_), channel_id=1, source_target_pairs={{0,1},{1,0},{2,3},{3,2},{4,5},{5,4},{6,7},{7,6},{8,9},{9,8},{10,11... | collective-permute-start | bytes 663560 | tf_op jit(solution)/shard_map/ppermute | solution.py:544
  43.0 9.1 %collective-permute-start.8 = (bf16[4,24,1152]{2,1,0:T(8,128)(2,1)S(1)}, bf16[4,24,1152]{2,1,0:T(8,128)(2,1)S(1)}, u32[]{:S(2)}, u32[]{:S(2)}) collective-permute-start(bf16[4,24,1152]{2,1,0:T(8,128)(2,1)S(1)} %get-tuple-element.73.refs_5_), channel_id=1, source_target_pairs={{0,2},{1,3},{2,0},{3,1},{4,6},{5,7},{6,4},{7,5},{8,10},{9,11},{10,... | collective-permute-start | bytes 663560 | tf_op jit(solution)/shard_map/ppermute | solution.py:544
  43.3 10.3 %collective-permute-start.10 = (bf16[4,24,1152]{2,1,0:T(8,128)(2,1)S(1)}, bf16[4,24,1152]{2,1,0:T(8,128)(2,1)S(1)}, u32[]{:S(2)}, u32[]{:S(2)}) collective-permute-start(bf16[4,24,1152]{2,1,0:T(8,128)(2,1)S(1)} %collective-permute-done.9.refs_7_.refs_8_), channel_id=1, source_target_pairs={{0,2},{1,3},{2,0},{3,1},{4,6},{5,7},{6,4},{7,5},{8,10},{9,11},{10,... | collective-permute-start | bytes 663560 | tf_op jit(solution)/shard_map/ppermute | solution.py:544
  52.1 8.1 %collective-permute-start.7 = (bf16[4,24,1152]{2,1,0:T(8,128)(2,1)S(1)}, bf16[4,24,1152]{2,1,0:T(8,128)(2,1)S(1)}, u32[]{:S(2)}, u32[]{:S(2)}) collective-permute-start(bf16[4,24,1152]{2,1,0:T(8,128)(2,1)S(1)} %collective-permute-done.5.refs_2_.refs_7_), channel_id=1, source_target_pairs={{0,1},{1,0},{2,3},{3,2},{4,5},{5,4},{6,7},{7,6},{8,9},{9,8},{10,11... | collective-permute-start | bytes 663560 | tf_op jit(solution)/shard_map/ppermute | solution.py:544
  52.1 18.1 %collective-permute-start.16 = (bf16[4,24,1152]{2,1,0:T(8,128)(2,1)S(1)}, bf16[4,24,1152]{2,1,0:T(8,128)(2,1)S(1)}, u32[]{:S(2)}, u32[]{:S(2)}) collective-permute-start(bf16[4,24,1152]{2,1,0:T(8,128)(2,1)S(1)} %get-tuple-element.85.refs_1_), channel_id=1, source_target_pairs={{0,1},{1,0},{2,3},{3,2},{4,5},{5,4},{6,7},{7,6},{8,9},{9,8},{10,11... | collective-permute-start | bytes 663560 | tf_op jit(solution)/shard_map/ppermute | solution.py:544
  53.6 16.7 %collective-permute-start.18 = (bf16[4,24,1152]{2,1,0:T(8,128)(2,1)S(1)}, bf16[4,24,1152]{2,1,0:T(8,128)(2,1)S(1)}, u32[]{:S(2)}, u32[]{:S(2)}) collective-permute-start(bf16[4,24,1152]{2,1,0:T(8,128)(2,1)S(1)} %get-tuple-element.86.refs_5_), channel_id=1, source_target_pairs={{0,2},{1,3},{2,0},{3,1},{4,6},{5,7},{6,4},{7,5},{8,10},{9,11},{10,... | collective-permute-start | bytes 663560 | tf_op jit(solution)/shard_map/ppermute | solution.py:544
  56.4 13.8 %collective-permute-start.17 = (bf16[4,24,1152]{2,1,0:T(8,128)(2,1)S(1)}, bf16[4,24,1152]{2,1,0:T(8,128)(2,1)S(1)}, u32[]{:S(2)}, u32[]{:S(2)}) collective-permute-start(bf16[4,24,1152]{2,1,0:T(8,128)(2,1)S(1)} %collective-permute-done.15.refs_2_), channel_id=1, source_target_pairs={{0,1},{1,0},{2,3},{3,2},{4,5},{5,4},{6,7},{7,6},{8,9},{9,8},{10,11... | collective-permute-start | bytes 663560 | tf_op jit(solution)/shard_map/ppermute | solution.py:544
  57.4 12.9 %collective-permute-start.20 = (bf16[4,24,1152]{2,1,0:T(8,128)(2,1)S(1)}, bf16[4,24,1152]{2,1,0:T(8,128)(2,1)S(1)}, u32[]{:S(2)}, u32[]{:S(2)}) collective-permute-start(bf16[4,24,1152]{2,1,0:T(8,128)(2,1)S(1)} %collective-permute-done.19.refs_7_), channel_id=1, source_target_pairs={{0,2},{1,3},{2,0},{3,1},{4,6},{5,7},{6,4},{7,5},{8,10},{9,11},{10,... | collective-permute-start | bytes 663560 | tf_op jit(solution)/shard_map/ppermute | solution.py:544
  64.8 10.7 %collective-permute-start.11 = (bf16[384,2304]{1,0:T(8,128)(2,1)S(1)}, bf16[384,2304]{1,0:T(8,128)(2,1)}, u32[]{:S(2)}, u32[]{:S(2)}) collective-permute-start(bf16[384,2304]{1,0:T(8,128)(2,1)S(1)} %bitcast.59), channel_id=1, source_target_pairs={{0,16},{16,0},{1,17},{17,1},{2,18},{18,2},{3,19},{19,3},{4,20},{20... | collective-permute-start | bytes 5308424 | tf_op jit(solution)/shard_map/ppermute | solution.py:540
  72.3 8.8 %collective-permute-start.21 = (bf16[384,2304]{1,0:T(8,128)(2,1)}, bf16[384,2304]{1,0:T(8,128)(2,1)}, u32[]{:S(2)}, u32[]{:S(2)}) collective-permute-start(bf16[384,2304]{1,0:T(8,128)(2,1)} %bitcast.21.refs_5_), channel_id=1, source_target_pairs={{0,16},{16,0},{1,17},{17,1},{2,18},{18,2},{3,19},{19,3},{4,20},{20... | collective-permute-start | bytes 5308424 | tf_op jit(solution)/shard_map/ppermute | solution.py:540
  104.1 15.6 %collective-permute-start.26 = (bf16[4,2,24,1152]{3,2,1,0:T(8,128)(2,1)}, bf16[4,2,24,1152]{3,2,1,0:T(8,128)(2,1)}, u32[]{:S(2)}, u32[]{:S(2)}) collective-permute-start(bf16[4,2,24,1152]{3,2,1,0:T(8,128)(2,1)} %get-tuple-element.100), channel_id=1, source_target_pairs={{0,2},{1,3},{2,0},{3,1},{4,6},{5,7},{6,4},{7,5},{8,10},{9,11},{10,... | collective-permute-start | bytes 1327112 | tf_op jit(solution)/shard_map/ppermute | solution.py:544
  104.7 15.0 %collective-permute-start.27 = (bf16[4,2,24,1152]{3,2,1,0:T(8,128)(2,1)}, bf16[4,2,24,1152]{3,2,1,0:T(8,128)(2,1)}, u32[]{:S(2)}, u32[]{:S(2)}) collective-permute-start(bf16[4,2,24,1152]{3,2,1,0:T(8,128)(2,1)} %get-tuple-element.102), channel_id=1, source_target_pairs={{0,1},{1,0},{2,3},{3,2},{4,5},{5,4},{6,7},{7,6},{8,9},{9,8},{10,11... | collective-permute-start | bytes 1327112 | tf_op jit(solution)/shard_map/ppermute | solution.py:544
  111.1 24.0 %collective-permute-start.24 = (bf16[4,2,24,1152]{3,2,1,0:T(8,128)(2,1)}, bf16[4,2,24,1152]{3,2,1,0:T(8,128)(2,1)S(1)}, u32[]{:S(2)}, u32[]{:S(2)}) collective-permute-start(bf16[4,2,24,1152]{3,2,1,0:T(8,128)(2,1)} %get-tuple-element.96), channel_id=1, source_target_pairs={{0,2},{1,3},{2,0},{3,1},{4,6},{5,7},{6,4},{7,5},{8,10},{9,11},{10,... | collective-permute-start | bytes 1327112 | tf_op jit(solution)/shard_map/ppermute | solution.py:544
  112.5 22.6 %collective-permute-start.25 = (bf16[4,2,24,1152]{3,2,1,0:T(8,128)(2,1)}, bf16[4,2,24,1152]{3,2,1,0:T(8,128)(2,1)S(1)}, u32[]{:S(2)}, u32[]{:S(2)}) collective-permute-start(bf16[4,2,24,1152]{3,2,1,0:T(8,128)(2,1)} %get-tuple-element.98), channel_id=1, source_target_pairs={{0,1},{1,0},{2,3},{3,2},{4,5},{5,4},{6,7},{7,6},{8,9},{9,8},{10,11... | collective-permute-start | bytes 1327112 | tf_op jit(solution)/shard_map/ppermute | solution.py:544
  113.6 26.1 %all-to-all-start.1 = ((f32[32,1,2640]{2,1,0:T(1,128)}), f32[32,1,2640]{2,1,0:T(1,128)}, u32[]{:S(2)}, u32[]{:S(2)}) async-start(f32[32,1,2640]{2,1,0:T(1,128)} %broadcast_in_dim.65), calls=%async_computation.1 | async-start | bytes 688128 | tf_op jit(solution)/shard_map/all_to_all | solution.py:853
  122.1 11.7 %collective-permute-start.28 = (bf16[4,24,1152]{2,1,0:T(8,128)(2,1)S(1)}, bf16[4,24,1152]{2,1,0:T(8,128)(2,1)S(1)}, u32[]{:S(2)}, u32[]{:S(2)}) collective-permute-start(bf16[4,24,1152]{2,1,0:T(8,128)(2,1)S(1)} %get-tuple-element.104), channel_id=1, source_target_pairs={{0,1},{1,0},{2,3},{3,2},{4,5},{5,4},{6,7},{7,6},{8,9},{9,8},{10,11... | collective-permute-start | bytes 663560 | tf_op jit(solution)/shard_map/ppermute | solution.py:544
  123.4 10.4 %collective-permute-start.29 = (bf16[4,24,1152]{2,1,0:T(8,128)(2,1)S(1)}, bf16[4,24,1152]{2,1,0:T(8,128)(2,1)S(1)}, u32[]{:S(2)}, u32[]{:S(2)}) collective-permute-start(bf16[4,24,1152]{2,1,0:T(8,128)(2,1)S(1)} %get-tuple-element.106), channel_id=1, source_target_pairs={{0,2},{1,3},{2,0},{3,1},{4,6},{5,7},{6,4},{7,5},{8,10},{9,11},{10,... | collective-permute-start | bytes 663560 | tf_op jit(solution)/shard_map/ppermute | solution.py:544
  138.4 17.4 %collective-permute-start.30 = (bf16[4,1,128,384]{3,2,1,0:T(8,128)(2,1)S(1)}, bf16[4,1,128,384]{3,2,1,0:T(8,128)(2,1)}, u32[]{:S(2)}, u32[]{:S(2)}) collective-permute-start(bf16[4,1,128,384]{3,2,1,0:T(8,128)(2,1)S(1)} %get-tuple-element.136), channel_id=1, source_target_pairs={{0,1},{1,0},{2,3},{3,2},{4,5},{5,4},{6,7},{7,6},{8,9},{9,8},{10,11... | collective-permute-start | bytes 1179656 | tf_op jit(solution)/shard_map/ppermute | solution.py:540
  141.4 18.8 %collective-permute-start.33 = (bf16[4,24,1152]{2,1,0:T(8,128)(2,1)}, bf16[4,24,1152]{2,1,0:T(8,128)(2,1)S(1)}, u32[]{:S(2)}, u32[]{:S(2)}) collective-permute-start(bf16[4,24,1152]{2,1,0:T(8,128)(2,1)} %copy-done.22), channel_id=1, source_target_pairs={{0,1},{1,0},{2,3},{3,2},{4,5},{5,4},{6,7},{7,6},{8,9},{9,8},{10,11... | collective-permute-start | bytes 663560 | tf_op jit(solution)/shard_map/ppermute | solution.py:544
  141.6 18.5 %collective-permute-start.34 = (bf16[4,24,1152]{2,1,0:T(8,128)(2,1)}, bf16[4,24,1152]{2,1,0:T(8,128)(2,1)S(1)}, u32[]{:S(2)}, u32[]{:S(2)}) collective-permute-start(bf16[4,24,1152]{2,1,0:T(8,128)(2,1)} %copy-done.21), channel_id=1, source_target_pairs={{0,2},{1,3},{2,0},{3,1},{4,6},{5,7},{6,4},{7,5},{8,10},{9,11},{10,... | collective-permute-start | bytes 663560 | tf_op jit(solution)/shard_map/ppermute | solution.py:544
  142.6 17.6 %collective-permute-start.35 = (bf16[24,2304]{1,0:T(8,128)(2,1)}, bf16[24,2304]{1,0:T(8,128)(2,1)S(1)}, u32[]{:S(2)}, u32[]{:S(2)}) collective-permute-start(bf16[24,2304]{1,0:T(8,128)(2,1)} %copy-done.24), channel_id=1, source_target_pairs={{0,8},{1,9},{2,10},{3,11},{4,12},{5,13},{6,14},{7,15},{8,0},{9,1},... | collective-permute-start | bytes 331784 | tf_op jit(solution)/shard_map/ppermute | solution.py:544
  145.8 14.3 %collective-permute-start.36 = (bf16[24,2304]{1,0:T(8,128)(2,1)}, bf16[24,2304]{1,0:T(8,128)(2,1)S(1)}, u32[]{:S(2)}, u32[]{:S(2)}) collective-permute-start(bf16[24,2304]{1,0:T(8,128)(2,1)} %copy-done.23), channel_id=1, source_target_pairs={{0,12},{1,13},{2,14},{3,15},{4,0},{5,1},{6,2},{7,3},{8,4},{9,5},{1... | collective-permute-start | bytes 331784 | tf_op jit(solution)/shard_map/ppermute | solution.py:544
  149.3 16.1 %all-to-all-start.2 = ((f32[32,1,768]{2,1,0:T(1,128)}), f32[32,1,768]{2,1,0:T(1,128)S(1)}, u32[]{:S(2)}, u32[]{:S(2)}) async-start(f32[32,1,768]{2,1,0:T(1,128)} %broadcast_in_dim.67), calls=%async_computation.2 | async-start | bytes 196608 | tf_op jit(solution)/shard_map/all_to_all | solution.py:862
  158.3 19.0 %collective-permute-start.31 = (bf16[2,2,128,384]{3,2,1,0:T(8,128)(2,1)}, bf16[2,2,128,384]{3,2,1,0:T(8,128)(2,1)}, u32[]{:S(2)}, u32[]{:S(2)}) collective-permute-start(bf16[2,2,128,384]{3,2,1,0:T(8,128)(2,1)} %get-tuple-element.134), channel_id=1, source_target_pairs={{0,16},{16,0},{1,17},{17,1},{2,18},{18,2},{3,19},{19,3},{4,20},{20... | collective-permute-start | bytes 1179656 | tf_op jit(solution)/shard_map/ppermute | solution.py:540
  162.1 9.4 %collective-permute-start.38 = (bf16[24,2304]{1,0:T(8,128)(2,1)S(1)}, bf16[24,2304]{1,0:T(8,128)(2,1)S(1)}, u32[]{:S(2)}, u32[]{:S(2)}) collective-permute-start(bf16[24,2304]{1,0:T(8,128)(2,1)S(1)} %get-tuple-element.123), channel_id=1, source_target_pairs={{0,8},{1,9},{2,10},{3,11},{4,12},{5,13},{6,14},{7,15},{8,0},{9,1},... | collective-permute-start | bytes 331784 | tf_op jit(solution)/shard_map/ppermute | solution.py:544
  163.1 10.6 %collective-permute-start.39 = (bf16[24,2304]{1,0:T(8,128)(2,1)S(1)}, bf16[24,2304]{1,0:T(8,128)(2,1)S(1)}, u32[]{:S(2)}, u32[]{:S(2)}) collective-permute-start(bf16[24,2304]{1,0:T(8,128)(2,1)S(1)} %get-tuple-element.124), channel_id=1, source_target_pairs={{0,12},{1,13},{2,14},{3,15},{4,0},{5,1},{6,2},{7,3},{8,4},{9,5},{1... | collective-permute-start | bytes 331784 | tf_op jit(solution)/shard_map/ppermute | solution.py:544
  (50 other events, 295.3 us)

commit v11 on v9

--- a/solution.py
+++ b/solution.py
@@ -356,7 +356,7 @@
         out_specs=out_specs,
         scratch_shapes=scratch,
         compiler_params=pltpu.CompilerParams(
-            vmem_limit_bytes=(56 if length > 256 else 26 if forward and backward else 22)
+            vmem_limit_bytes=(56 if length > 256 else 36 if forward and backward else 36)
             * 1024
             * 1024
         ),
@@ -509,7 +509,7 @@
         down_ref[j * rows : (j + 1) * rows, :] = upper[:, (2 + j) * width : (3 + j) * width]
 
 
-def in_memory(kernel, shapes, operands, scratch=(), memory=pltpu.VMEM, after=(), limit=16):
+def in_memory(kernel, shapes, operands, scratch=(), memory=pltpu.VMEM, after=(), limit=32):
     specs = [pl.BlockSpec(memory_space=pltpu.SMEM)]
     specs += [pl.BlockSpec(memory_space=memory)] * (len(operands) - 1)
     specs += [pl.BlockSpec(memory_space=pl.ANY)] * len(after)
@@ -567,7 +567,7 @@
     return flip(first, size, 2), flip(second, size, 1)
 
 
-def gather_across(first, second, first_x, second_y, place, size, after=()):
+def gather_across(first, second, first_x, second_y, place, size):
     high, rows, lanes = first.shape
     first_y, second_x = flip(first, size, 1), flip(second, size, 2)
     first_both, second_both = flip(first_x, size, 1), flip(second_y, size, 2)
@@ -576,7 +576,6 @@
         [jax.ShapeDtypeStruct((high, 2, 2, rows, 2 * lanes), first.dtype)],
         [place, first, first_x, first_y, first_both, second, second_x, second_y, second_both],
         scratch=[pltpu.SemaphoreType.DMA((8,))],
-        after=after,
     )
     return full.reshape(size * rows, 2 * lanes)
 
@@ -757,14 +756,10 @@
     silu_all = jax.nn.silu(conditions).astype(jnp.bfloat16)
     silu_own = lax.dynamic_slice_in_dim(silu_all, ring_rank * rows, rows, 1)
     if compact:
-        *first_parts, second_shard = gather_along_z(
-            first_shard, place, ring_size, handed=(second_shard,)
+        *first_parts, second_shard, silu_late = gather_along_z(
+            first_shard, place, ring_size, handed=(second_shard, silu_own)
         )
         first_parts += first_flips(*first_parts, ring_size)
-        *second_parts, silu_late = gather_along_z(
-            second_shard, place, ring_size, handed=(silu_own,), after=(both, *first_parts[2:])
-        )
-        second_parts += first_flips(*second_parts, ring_size)
     else:
         silu_late = silu_own
 
@@ -780,7 +775,11 @@
     first_bias, second_bias = products[0, :, 6 * width :], products[1, :, 6 * width :]
 
     if compact:
-        first_pack = gather_across(*first_parts, place, ring_size, after=(products,))
+        second_parts = gather_along_z(
+            second_shard, place, ring_size, after=(both, *first_parts[2:])
+        )
+        second_parts += first_flips(*second_parts, ring_size)
+        first_pack = gather_across(*first_parts, place, ring_size)
         second_pack = gather_across(*second_parts, place, ring_size)
     else:
         first_pack = lax.all_gather(first_shard, RING, axis=0, tiled=True)
@@ -810,22 +809,21 @@
             ring_terms(second_keep), ring_terms(second_got), place, ring_size
         )
         second_received = scatter_flips(second_sorted, ring_size)
-        first_sorted = scatter_first(
+        *first_sorted, first_dmod, first_sums = scatter_first(
             ring_terms(first_keep),
             ring_terms(first_got),
             place,
             ring_size,
+            handed=(first_dmod, first_sums),
             after=(second_sorted[0],),
         )
         first_received = scatter_flips(first_sorted, ring_size)
-        second_turned, (first_dmod, first_sums) = scatter_second(
-            second_received, place, ring_size, handed=(first_dmod, first_sums)
+        second_turned, _ = scatter_second(second_received, place, ring_size)
+        first_turned, (first_grad,) = scatter_second(
+            first_received, place, ring_size, handed=(first_grad,), after=(second_turned[0],)
         )
-        second_sent = scatter_third(second_turned, place, ring_size)
+        second_sent = scatter_third(second_turned, place, ring_size, after=(first_turned[0],))
         second_pieces = scatter_along_z(second_sent, ring_size)
-        first_turned, (first_grad,) = scatter_second(
-            first_received, place, ring_size, handed=(first_grad,), after=(second_sent[0],)
-        )
 
     rows_back = jnp.concatenate(
         [
@@ -844,7 +842,7 @@
 
     if compact:
         *first_sent, columns = scatter_third(
-            first_turned, place, ring_size, handed=(columns,), after=tuple(second_pieces[1:])
+            first_turned, place, ring_size, handed=(columns,), after=(second_sent[0],)
         )
         first_pieces = scatter_along_z(first_sent, ring_size)
     else:

time: 194 us -> 191 us (0.985)
  local copies, waits for them, and re-layouts: 22 us -> 18.8 us
  waiting for transfers between devices: 62.4 us -> 59.5 us
    all_to_all x1, waiting for transfers between devices: 6.48 us -> 0.01 us  [per_device(): lax.all_to_all(rows_back[:, None], ('section', 'dp', 'seq'), 0, 0, tiled=...]
    all_to_all x1, waiting for transfers between devices: 0.01 us -> 4.65 us  [per_device(): lax.all_to_all(products[:, None], ('section', 'dp', 'seq'), 0, 0, tiled=T...]
    unnamed x88 -> x72, local copies, waits for them, and re-layouts: 15.3 us -> 12 us
    ppermute x32, starting transfers between devices: 30.3 us -> 27.7 us  [ring_exchange(): return lax.ppermute(block, RING, [(i, step(i)) for i in range(size)])]
  transfers between devices with their start and end apart: 44 -> 44, of which waited for: 17 -> 15; matrix products, arithmetic and copies ran while one was open for 7% -> 11% of each run, Pallas kernels for 13% -> 15%
where the time goes in v11:
time: 191 us; the launch traced here: 190 us
  waiting for transfers between devices  59.5 us (31%)
  starting transfers between devices  53.5 us (28%)
  Pallas kernels  43.9 us (23%)
  local copies, waits for them, and re-layouts  18.8 us (10%)
  other arithmetic  7.75 us (4%)
  matrix products  4.66 us (2%)
    ppermute x32, waiting for transfers between devices, ring_exchange(): return lax.ppermute(block, RING, [(i, step(i)) for i in range(size)])  54.8 us
    ppermute x32, starting transfers between devices, ring_exchange(): return lax.ppermute(block, RING, [(i, step(i)) for i in range(size)])  27.7 us
    pallas_call x3, Pallas kernels, run_section(): pl.pallas_call(partial(section_kernel, layout, forward, backward, len(aft...  26.1 us
    pallas_call x13, Pallas kernels, in_memory(): pl.pallas_call(body, out_shape=shapes, in_specs=specs, out_specs=[pl.Bloc...  17.8 us
    unnamed x72, local copies, waits for them, and re-layouts  12 us
    ppermute x9, starting transfers between devices, pair_swap(): return lax.ppermute(block, axis, [(0, 1), (1, 0)])  7.93 us
    all_to_all x1, starting transfers between devices, per_device(): lax.all_to_all(columns, ('section', 'dp', 'seq'), 0, 0, tiled=True)  6.39 us
    all_to_all x1, starting transfers between devices, per_device(): lax.all_to_all(rows_back[:, None], ('section', 'dp', 'seq'), 0, 0, tiled=...  6.39 us
  transfers between devices with their start and end apart: 44, of which 15 were waited for; matrix products, arithmetic and copies ran while one was open for 11% of the time, Pallas kernels for 15%

profile of v11, /device:TPU:9, one launch (start us, length us, event | category | flops | bytes accessed | tf_op | source)
XLA Modules:
  0.0 190.0 jit_solution(1087117638911091692)
XLA Ops:
  0.7 1.7 shard_map.178
  11.1 6.2 %collective-permute-done.3.refs_3_ = bf16[24,2304]{1,0:T(8,128)(2,1)S(1)} collective-permute-done((bf16[24,2304]{1,0:T(8,128)(2,1)S(1)}, bf16[24,2304]{1,0:T(8,128)(2,1)S(1)}, u32[]{:S(2)}, u32[]{:S(2)}) %collective-permute-start.3) | collective-permute-done | bytes 110624 | tf_op jit(solution)/shard_map/ppermute | solution.py:538
  17.3 2.4 %collective-permute-done.4.refs_4_ = bf16[24,2304]{1,0:T(8,128)(2,1)S(1)} collective-permute-done((bf16[24,2304]{1,0:T(8,128)(2,1)S(1)}, bf16[24,2304]{1,0:T(8,128)(2,1)S(1)}, u32[]{:S(2)}, u32[]{:S(2)}) %collective-permute-start.4) | collective-permute-done | bytes 110624 | tf_op jit(solution)/shard_map/ppermute | solution.py:538
  24.4 2.9 %collective-permute-done.12.refs_2_ = bf16[24,2304]{1,0:T(8,128)(2,1)S(1)} collective-permute-done((bf16[24,2304]{1,0:T(8,128)(2,1)S(1)}, bf16[24,2304]{1,0:T(8,128)(2,1)S(1)}, u32[]{:S(2)}, u32[]{:S(2)}) %collective-permute-start.12) | collective-permute-done | bytes 110624 | tf_op jit(solution)/shard_map/ppermute | solution.py:538
  29.2 5.9 %collective-permute-done.14.refs_4_ = bf16[24,2304]{1,0:T(8,128)(2,1)S(1)} collective-permute-done((bf16[24,2304]{1,0:T(8,128)(2,1)S(1)}, bf16[24,2304]{1,0:T(8,128)(2,1)S(1)}, u32[]{:S(2)}, u32[]{:S(2)}) %collective-permute-start.14) | collective-permute-done | bytes 110624 | tf_op jit(solution)/shard_map/ppermute | solution.py:538
  39.5 7.7 %collective-permute-done.10.refs_8_ = bf16[4,24,1152]{2,1,0:T(8,128)(2,1)S(1)} collective-permute-done((bf16[4,24,1152]{2,1,0:T(8,128)(2,1)S(1)}, bf16[4,24,1152]{2,1,0:T(8,128)(2,1)S(1)}, u32[]{:S(2)}, u32[]{:S(2)}) %collective-permute-start.10) | collective-permute-done | bytes 221216 | tf_op jit(solution)/shard_map/ppermute | solution.py:538
  48.2 3.0 %collective-permute-start.11 = (bf16[384,2304]{1,0:T(8,128)(2,1)S(1)}, bf16[384,2304]{1,0:T(8,128)(2,1)}, u32[]{:S(2)}, u32[]{:S(2)}) collective-permute-start(bf16[384,2304]{1,0:T(8,128)(2,1)S(1)} %bitcast.59), channel_id=1, source_target_pairs={{0,16},{16,0},{1,17},{17,1},{2,18},{18,2},{3,19},{19,3},{4,20},{20... | collective-permute-start | bytes 5308424 | tf_op jit(solution)/shard_map/ppermute | solution.py:534
  53.8 5.1 %all-to-all-start = ((f32[32,1,2640]{2,1,0:T(1,128)}), f32[32,1,2640]{2,1,0:T(1,128)}, u32[]{:S(2)}, u32[]{:S(2)}) async-start(f32[32,1,2640]{2,1,0:T(1,128)} %copy.22), calls=%async_computation | async-start | bytes 688128 | tf_op jit(solution)/shard_map/all_to_all | solution.py:769
  59.0 2.9 %shard_map.183 = bf16[4,2,2,24,2304]{4,3,2,1,0:T(8,128)(2,1)} custom-call(s32[3]{0:T(128)S(1)} %pad_add_fusion.refs_0_, bf16[4,24,1152]{2,1,0:T(8,128)(2,1)S(1)} %get-tuple-element.88.refs_1_, bf16[4,24,1152]{2,1,0:T(8,128)(2,1)} %collective-permute-done.15.refs_2_, bf16[4,24,1152]{2,1,0:T(8,128)(2,1)} %collective-permute-done.16.refs_3_, ...), custom_call_target="tpu_custom_call" | custom-call | bytes 5308416 | tf_op jit(solution)/shard_map/pallas_call | solution.py:522
  64.8 4.7 %all-to-all-done = f32[32,1,2640]{2,1,0:T(1,128)} async-done(((f32[32,1,2640]{2,1,0:T(1,128)}), f32[32,1,2640]{2,1,0:T(1,128)}, u32[]{:S(2)}, u32[]{:S(2)}) %all-to-all-start) | async-done | bytes 337952 | tf_op jit(solution)/shard_map/all_to_all | solution.py:769
  70.5 5.7 %shard_map.181 = (bf16[256,384]{1,0:T(8,128)(2,1)S(1)}, f32[1,2304]{1,0:T(1,128)S(1)}, bf16[256,1152]{1,0:T(8,128)(2,1)S(1)}, bf16[256,384]{1,0:T(8,128)(2,1)S(1...) custom-call(s32[1]{0:T(128)} %bitcast.refs_0_, ...), custom_call_target="tpu_custom_call" | custom-call | flops 1006632960 | bytes 5308416 | tf_op jit(solution)/shard_map/pallas_call | solution.py:352
  76.2 12.9 %shard_map.184 = (bf16[256,384]{1,0:T(8,128)(2,1)S(1)}, bf16[256,384]{1,0:T(8,128)(2,1)S(1)}, f32[1,2304]{1,0:T(1,128)S(1)}, f32[16,336]{1,0:T(8,128)S(1)}, bf16...) custom-call(s32[1]{0:T(128)} %bitcast.refs_0_, bf16[256,384]{1,0:T(8,128)(2,1)S(1)} %get-tuple-element.77.refs_1_, ...), custom_call_target="tpu_custom_call" | custom-call | flops 3019898880 | bytes 10616832 | tf_op jit(solution)/shard_map/pallas_call | solution.py:352
  91.0 7.5 %shard_map.185 = (bf16[256,384]{1,0:T(8,128)(2,1)S(1)}, f32[1,2304]{1,0:T(1,128)S(1)}, f32[16,336]{1,0:T(8,128)S(1)}, bf16[384,2304]{1,0:T(8,128)(2,1)S(1)}, bf16[384,2304]{1,0:T(8,128)(2,1)}) custom-call(s32[1]{0:T(128)} %bitcast.refs_0_, bf16[256,384]{1,0:T(8,128)(2,1)S(1)} %get-tuple-element.142.refs_1_, f32[1,2304]{1,0:T(1,128)S(1)} %get-tuple-element.78.refs_2_, ...), custom_call_target="tpu_custom_call" | custom-call | flops 2013265920 | bytes 10616832 | tf_op jit(solution)/shard_map/pallas_call | solution.py:352
  101.9 1.5 copy-done.4
  103.3 2.7 %shard_map.186 = (bf16[4,2,24,1152]{3,2,1,0:T(8,128)(2,1)S(1)}, bf16[4,2,24,1152]{3,2,1,0:T(8,128)(2,1)}, bf16[4,2,24,1152]{3,2,1,0:T(8,128)(2,1)S(1)}, bf16[4,2,24,1152]{3,2,1,0:T(8,128)(2,1)}) custom-call(s32[3]{0:T(128)S(1)} %pad_add_fusion.refs_0_, bf16[16,24,2304]{2,1,0:T(8,128)(2,1)S(1)} %bitcast.64, bf16[16,24,2304]{2,1,0:T(8,128)(2,1)} %bitcast.25.refs_2_), custom_call_target="tpu_custom_call" | custom-call | bytes 5308416 | tf_op jit(solution)/shard_map/pallas_call | solution.py:522
  107.7 1.7 shard_map.187
  113.4 6.4 %all-to-all-start.1 = ((f32[32,1,2640]{2,1,0:T(1,128)}), f32[32,1,2640]{2,1,0:T(1,128)}, u32[]{:S(2)}, u32[]{:S(2)}) async-start(f32[32,1,2640]{2,1,0:T(1,128)} %broadcast_in_dim.65), calls=%async_computation.1 | async-start | bytes 688128 | tf_op jit(solution)/shard_map/all_to_all | solution.py:836
  120.9 2.0 %shard_map.188 = (bf16[4,24,1152]{2,1,0:T(8,128)(2,1)S(1)}, bf16[4,24,1152]{2,1,0:T(8,128)(2,1)}, bf16[4,24,1152]{2,1,0:T(8,128)(2,1)S(1)}, bf16[4,24,1152]{2,1,0:T(8,128)(2,1)}) custom-call(s32[3]{0:T(128)S(1)} %pad_add_fusion.refs_0_, bf16[4,2,24,1152]{3,2,1,0:T(8,128)(2,1)S(1)} %get-tuple-element.97.refs_5_.refs_1_, ...), custom_call_target="tpu_custom_call" | custom-call | bytes 2654208 | tf_op jit(solution)/shard_map/pallas_call | solution.py:522
  122.9 6.7 %collective-permute-done.24.refs_2_ = bf16[4,2,24,1152]{3,2,1,0:T(8,128)(2,1)S(1)} collective-permute-done((bf16[4,2,24,1152]{3,2,1,0:T(8,128)(2,1)}, bf16[4,2,24,1152]{3,2,1,0:T(8,128)(2,1)S(1)}, u32[]{:S(2)}, u32[]{:S(2)}) %collective-permute-start.24) | collective-permute-done | bytes 442400 | tf_op jit(solution)/shard_map/ppermute | solution.py:538
  132.4 1.9 shard_map.189
  139.8 9.0 %collective-permute-done.32.refs_2_ = bf16[4,24,1152]{2,1,0:T(8,128)(2,1)S(1)} collective-permute-done((bf16[4,24,1152]{2,1,0:T(8,128)(2,1)}, bf16[4,24,1152]{2,1,0:T(8,128)(2,1)S(1)}, u32[]{:S(2)}, u32[]{:S(2)}) %collective-permute-start.32) | collective-permute-done | bytes 221216 | tf_op jit(solution)/shard_map/ppermute | solution.py:538
  149.5 4.0 %collective-permute-done.30.refs_2_ = bf16[4,24,1152]{2,1,0:T(8,128)(2,1)S(1)} collective-permute-done((bf16[4,24,1152]{2,1,0:T(8,128)(2,1)}, bf16[4,24,1152]{2,1,0:T(8,128)(2,1)S(1)}, u32[]{:S(2)}, u32[]{:S(2)}) %collective-permute-start.30) | collective-permute-done | bytes 221216 | tf_op jit(solution)/shard_map/ppermute | solution.py:538
  154.4 3.0 %collective-permute-start.35 = (bf16[24,2304]{1,0:T(8,128)(2,1)S(1)}, bf16[24,2304]{1,0:T(8,128)(2,1)S(1)}, u32[]{:S(2)}, u32[]{:S(2)}) collective-permute-start(bf16[24,2304]{1,0:T(8,128)(2,1)S(1)} %get-tuple-element.124), channel_id=1, source_target_pairs={{0,8},{1,9},{2,10},{3,11},{4,12},{5,13},{6,14},{7,15},{8,0},{9,1},... | collective-permute-start | bytes 331784 | tf_op jit(solution)/shard_map/ppermute | solution.py:538
  158.2 6.4 %all-to-all-start.2 = ((f32[32,1,768]{2,1,0:T(1,128)}), f32[32,1,768]{2,1,0:T(1,128)S(1)}, u32[]{:S(2)}, u32[]{:S(2)}) async-start(f32[32,1,768]{2,1,0:T(1,128)} %broadcast_in_dim.67), calls=%async_computation.2 | async-start | bytes 196608 | tf_op jit(solution)/shard_map/all_to_all | solution.py:898
  164.6 1.6 maximum_select_fusion
  168.9 1.5 collective-permute-start.37
  170.4 3.9 %collective-permute-start.38 = (bf16[24,2304]{1,0:T(8,128)(2,1)S(1)}, bf16[24,2304]{1,0:T(8,128)(2,1)S(1)}, u32[]{:S(2)}, u32[]{:S(2)}) collective-permute-start(bf16[24,2304]{1,0:T(8,128)(2,1)S(1)} %get-tuple-element.127), channel_id=1, source_target_pairs={{0,8},{1,9},{2,10},{3,11},{4,12},{5,13},{6,14},{7,15},{8,0},{9,1},... | collective-permute-start | bytes 331784 | tf_op jit(solution)/shard_map/ppermute | solution.py:538
  174.3 1.9 convolution_bitcast_fusion
  176.2 1.5 collective-permute-done.37.refs_6_
  177.7 1.8 collective-permute-done.38.refs_7_
  179.5 3.8 %collective-permute-done.39.refs_8_ = bf16[24,2304]{1,0:T(8,128)(2,1)S(1)} collective-permute-done((bf16[24,2304]{1,0:T(8,128)(2,1)S(1)}, bf16[24,2304]{1,0:T(8,128)(2,1)S(1)}, u32[]{:S(2)}, u32[]{:S(2)}) %collective-permute-start.39) | collective-permute-done | bytes 110624 | tf_op jit(solution)/shard_map/ppermute | solution.py:538
  185.7 2.2 %fusion.5 = f32[1000,384]{1,0:T(8,128)} fusion(s32[32]{0:T(128)S(1)} %copy-done.31, f32[32,384]{1,0:T(8,128)S(1)} %copy-done.28, f32[32,384]{1,0:T(8,128)S(1)} %reshape.76), kind=kOutput, calls=%fused_computation.27 | convolution fusion | flops 147598592 | bytes 1634432 | tf_op jit(solution)/shard_map/dot_general | solution.py:902
  (188 shorter events, 56.2 us)
Async XLA Ops:
  4.2 19.2 %collective-permute-start = (bf16[2,128,384]{2,1,0:T(8,128)(2,1)S(1)}, bf16[2,128,384]{2,1,0:T(8,128)(2,1)S(1)}, u32[]{:S(2)}, u32[]{:S(2)}) collective-permute-start(bf16[2,128,384]{2,1,0:T(8,128)(2,1)S(1)} %get-tuple-element.144), channel_id=1, source_target_pairs={{0,1},{1,0},{2,3},{3,2},{4,5},{5,4},{6,7},{7,6},{8,9},{9,8},{10,11... | collective-permute-start | bytes 589832 | tf_op jit(solution)/shard_map/ppermute | solution.py:534
  8.0 9.3 %collective-permute-start.3 = (bf16[24,2304]{1,0:T(8,128)(2,1)S(1)}, bf16[24,2304]{1,0:T(8,128)(2,1)S(1)}, u32[]{:S(2)}, u32[]{:S(2)}) collective-permute-start(bf16[24,2304]{1,0:T(8,128)(2,1)S(1)} %get-tuple-element.148.refs_1_), channel_id=1, source_target_pairs={{0,8},{1,9},{2,10},{3,11},{4,12},{5,13},{6,14},{7,15},{8,0},{9,1},... | collective-permute-start | bytes 331784 | tf_op jit(solution)/shard_map/ppermute | solution.py:538
  9.1 10.6 %collective-permute-start.4 = (bf16[24,2304]{1,0:T(8,128)(2,1)S(1)}, bf16[24,2304]{1,0:T(8,128)(2,1)S(1)}, u32[]{:S(2)}, u32[]{:S(2)}) collective-permute-start(bf16[24,2304]{1,0:T(8,128)(2,1)S(1)} %get-tuple-element.148.refs_1_), channel_id=1, source_target_pairs={{0,12},{1,13},{2,14},{3,15},{4,0},{5,1},{6,2},{7,3},{8,4},{9,5},{1... | collective-permute-start | bytes 331784 | tf_op jit(solution)/shard_map/ppermute | solution.py:538
  20.7 14.5 %collective-permute-start.5 = (bf16[4,24,1152]{2,1,0:T(8,128)(2,1)S(1)}, bf16[4,24,1152]{2,1,0:T(8,128)(2,1)S(1)}, u32[]{:S(2)}, u32[]{:S(2)}) collective-permute-start(bf16[4,24,1152]{2,1,0:T(8,128)(2,1)S(1)} %get-tuple-element.75.refs_1_), channel_id=1, source_target_pairs={{0,2},{1,3},{2,0},{3,1},{4,6},{5,7},{6,4},{7,5},{8,10},{9,11},{10,... | collective-permute-start | bytes 663560 | tf_op jit(solution)/shard_map/ppermute | solution.py:538
  21.9 15.8 %collective-permute-start.6 = (bf16[4,24,1152]{2,1,0:T(8,128)(2,1)S(1)}, bf16[4,24,1152]{2,1,0:T(8,128)(2,1)S(1)}, u32[]{:S(2)}, u32[]{:S(2)}) collective-permute-start(bf16[4,24,1152]{2,1,0:T(8,128)(2,1)S(1)} %get-tuple-element.75.refs_1_), channel_id=1, source_target_pairs={{0,1},{1,0},{2,3},{3,2},{4,5},{5,4},{6,7},{7,6},{8,9},{9,8},{10,11... | collective-permute-start | bytes 663560 | tf_op jit(solution)/shard_map/ppermute | solution.py:538
  22.2 13.0 %collective-permute-start.9 = (bf16[4,24,1152]{2,1,0:T(8,128)(2,1)S(1)}, bf16[4,24,1152]{2,1,0:T(8,128)(2,1)S(1)}, u32[]{:S(2)}, u32[]{:S(2)}) collective-permute-start(bf16[4,24,1152]{2,1,0:T(8,128)(2,1)S(1)} %get-tuple-element.76.refs_5_), channel_id=1, source_target_pairs={{0,1},{1,0},{2,3},{3,2},{4,5},{5,4},{6,7},{7,6},{8,9},{9,8},{10,11... | collective-permute-start | bytes 663560 | tf_op jit(solution)/shard_map/ppermute | solution.py:538
  29.0 10.2 %collective-permute-start.8 = (bf16[4,24,1152]{2,1,0:T(8,128)(2,1)S(1)}, bf16[4,24,1152]{2,1,0:T(8,128)(2,1)S(1)}, u32[]{:S(2)}, u32[]{:S(2)}) collective-permute-start(bf16[4,24,1152]{2,1,0:T(8,128)(2,1)S(1)} %get-tuple-element.76.refs_5_), channel_id=1, source_target_pairs={{0,2},{1,3},{2,0},{3,1},{4,6},{5,7},{6,4},{7,5},{8,10},{9,11},{10,... | collective-permute-start | bytes 663560 | tf_op jit(solution)/shard_map/ppermute | solution.py:538
  36.0 15.2 %collective-permute-start.15 = (bf16[4,24,1152]{2,1,0:T(8,128)(2,1)S(1)}, bf16[4,24,1152]{2,1,0:T(8,128)(2,1)}, u32[]{:S(2)}, u32[]{:S(2)}) collective-permute-start(bf16[4,24,1152]{2,1,0:T(8,128)(2,1)S(1)} %get-tuple-element.88.refs_1_), channel_id=1, source_target_pairs={{0,2},{1,3},{2,0},{3,1},{4,6},{5,7},{6,4},{7,5},{8,10},{9,11},{10,... | collective-permute-start | bytes 663560 | tf_op jit(solution)/shard_map/ppermute | solution.py:538
  36.3 15.2 %collective-permute-start.19 = (bf16[4,24,1152]{2,1,0:T(8,128)(2,1)S(1)}, bf16[4,24,1152]{2,1,0:T(8,128)(2,1)}, u32[]{:S(2)}, u32[]{:S(2)}) collective-permute-start(bf16[4,24,1152]{2,1,0:T(8,128)(2,1)S(1)} %get-tuple-element.89.refs_5_), channel_id=1, source_target_pairs={{0,1},{1,0},{2,3},{3,2},{4,5},{5,4},{6,7},{7,6},{8,9},{9,8},{10,11... | collective-permute-start | bytes 663560 | tf_op jit(solution)/shard_map/ppermute | solution.py:538
  36.5 10.6 %collective-permute-start.10 = (bf16[4,24,1152]{2,1,0:T(8,128)(2,1)S(1)}, bf16[4,24,1152]{2,1,0:T(8,128)(2,1)S(1)}, u32[]{:S(2)}, u32[]{:S(2)}) collective-permute-start(bf16[4,24,1152]{2,1,0:T(8,128)(2,1)S(1)} %collective-permute-done.9.refs_7_), channel_id=1, source_target_pairs={{0,2},{1,3},{2,0},{3,1},{4,6},{5,7},{6,4},{7,5},{8,10},{9,11},{10,... | collective-permute-start | bytes 663560 | tf_op jit(solution)/shard_map/ppermute | solution.py:538
  37.7 9.6 %collective-permute-start.7 = (bf16[4,24,1152]{2,1,0:T(8,128)(2,1)S(1)}, bf16[4,24,1152]{2,1,0:T(8,128)(2,1)S(1)}, u32[]{:S(2)}, u32[]{:S(2)}) collective-permute-start(bf16[4,24,1152]{2,1,0:T(8,128)(2,1)S(1)} %collective-permute-done.5.refs_2_.refs_6_), channel_id=1, source_target_pairs={{0,1},{1,0},{2,3},{3,2},{4,5},{5,4},{6,7},{7,6},{8,9},{9,8},{10,11... | collective-permute-start | bytes 663560 | tf_op jit(solution)/shard_map/ppermute | solution.py:538
  39.2 19.8 %collective-permute-start.16 = (bf16[4,24,1152]{2,1,0:T(8,128)(2,1)S(1)}, bf16[4,24,1152]{2,1,0:T(8,128)(2,1)}, u32[]{:S(2)}, u32[]{:S(2)}) collective-permute-start(bf16[4,24,1152]{2,1,0:T(8,128)(2,1)S(1)} %get-tuple-element.88.refs_1_), channel_id=1, source_target_pairs={{0,1},{1,0},{2,3},{3,2},{4,5},{5,4},{6,7},{7,6},{8,9},{9,8},{10,11... | collective-permute-start | bytes 663560 | tf_op jit(solution)/shard_map/ppermute | solution.py:538
  47.1 11.8 %collective-permute-start.18 = (bf16[4,24,1152]{2,1,0:T(8,128)(2,1)S(1)}, bf16[4,24,1152]{2,1,0:T(8,128)(2,1)}, u32[]{:S(2)}, u32[]{:S(2)}) collective-permute-start(bf16[4,24,1152]{2,1,0:T(8,128)(2,1)S(1)} %get-tuple-element.89.refs_5_), channel_id=1, source_target_pairs={{0,2},{1,3},{2,0},{3,1},{4,6},{5,7},{6,4},{7,5},{8,10},{9,11},{10,... | collective-permute-start | bytes 663560 | tf_op jit(solution)/shard_map/ppermute | solution.py:538
  48.2 22.3 %collective-permute-start.11 = (bf16[384,2304]{1,0:T(8,128)(2,1)S(1)}, bf16[384,2304]{1,0:T(8,128)(2,1)}, u32[]{:S(2)}, u32[]{:S(2)}) collective-permute-start(bf16[384,2304]{1,0:T(8,128)(2,1)S(1)} %bitcast.59), channel_id=1, source_target_pairs={{0,16},{16,0},{1,17},{17,1},{2,18},{18,2},{3,19},{19,3},{4,20},{20... | collective-permute-start | bytes 5308424 | tf_op jit(solution)/shard_map/ppermute | solution.py:534
  53.8 15.6 %all-to-all-start = ((f32[32,1,2640]{2,1,0:T(1,128)}), f32[32,1,2640]{2,1,0:T(1,128)}, u32[]{:S(2)}, u32[]{:S(2)}) async-start(f32[32,1,2640]{2,1,0:T(1,128)} %copy.22), calls=%async_computation | async-start | bytes 688128 | tf_op jit(solution)/shard_map/all_to_all | solution.py:769
  61.9 14.3 %collective-permute-start.21 = (bf16[384,2304]{1,0:T(8,128)(2,1)}, bf16[384,2304]{1,0:T(8,128)(2,1)}, u32[]{:S(2)}, u32[]{:S(2)}) collective-permute-start(bf16[384,2304]{1,0:T(8,128)(2,1)} %bitcast.21.refs_5_), channel_id=1, source_target_pairs={{0,16},{16,0},{1,17},{17,1},{2,18},{18,2},{3,19},{19,3},{4,20},{20... | collective-permute-start | bytes 5308424 | tf_op jit(solution)/shard_map/ppermute | solution.py:534
  90.4 11.5 %collective-permute-start.23 = (bf16[384,2304]{1,0:T(8,128)(2,1)}, bf16[384,2304]{1,0:T(8,128)(2,1)}, u32[]{:S(2)}, u32[]{:S(2)}) collective-permute-start(bf16[384,2304]{1,0:T(8,128)(2,1)} %get-tuple-element.96), channel_id=1, source_target_pairs={{0,16},{16,0},{1,17},{17,1},{2,18},{18,2},{3,19},{19,3},{4,20},{20... | collective-permute-start | bytes 5308424 | tf_op jit(solution)/shard_map/ppermute | solution.py:534
  106.1 13.7 %collective-permute-start.26 = (bf16[4,2,24,1152]{3,2,1,0:T(8,128)(2,1)}, bf16[4,2,24,1152]{3,2,1,0:T(8,128)(2,1)}, u32[]{:S(2)}, u32[]{:S(2)}) collective-permute-start(bf16[4,2,24,1152]{3,2,1,0:T(8,128)(2,1)} %get-tuple-element.103), channel_id=1, source_target_pairs={{0,2},{1,3},{2,0},{3,1},{4,6},{5,7},{6,4},{7,5},{8,10},{9,11},{10,... | collective-permute-start | bytes 1327112 | tf_op jit(solution)/shard_map/ppermute | solution.py:538
  107.2 12.6 %collective-permute-start.27 = (bf16[4,2,24,1152]{3,2,1,0:T(8,128)(2,1)}, bf16[4,2,24,1152]{3,2,1,0:T(8,128)(2,1)}, u32[]{:S(2)}, u32[]{:S(2)}) collective-permute-start(bf16[4,2,24,1152]{3,2,1,0:T(8,128)(2,1)} %get-tuple-element.105), channel_id=1, source_target_pairs={{0,1},{1,0},{2,3},{3,2},{4,5},{5,4},{6,7},{7,6},{8,9},{9,8},{10,11... | collective-permute-start | bytes 1327112 | tf_op jit(solution)/shard_map/ppermute | solution.py:538
  110.9 18.6 %collective-permute-start.24 = (bf16[4,2,24,1152]{3,2,1,0:T(8,128)(2,1)}, bf16[4,2,24,1152]{3,2,1,0:T(8,128)(2,1)S(1)}, u32[]{:S(2)}, u32[]{:S(2)}) collective-permute-start(bf16[4,2,24,1152]{3,2,1,0:T(8,128)(2,1)} %get-tuple-element.99), channel_id=1, source_target_pairs={{0,2},{1,3},{2,0},{3,1},{4,6},{5,7},{6,4},{7,5},{8,10},{9,11},{10,... | collective-permute-start | bytes 1327112 | tf_op jit(solution)/shard_map/ppermute | solution.py:538
  111.5 19.3 %collective-permute-start.25 = (bf16[4,2,24,1152]{3,2,1,0:T(8,128)(2,1)}, bf16[4,2,24,1152]{3,2,1,0:T(8,128)(2,1)}, u32[]{:S(2)}, u32[]{:S(2)}) collective-permute-start(bf16[4,2,24,1152]{3,2,1,0:T(8,128)(2,1)} %get-tuple-element.101), channel_id=1, source_target_pairs={{0,1},{1,0},{2,3},{3,2},{4,5},{5,4},{6,7},{7,6},{8,9},{9,8},{10,11... | collective-permute-start | bytes 1327112 | tf_op jit(solution)/shard_map/ppermute | solution.py:538
  113.4 25.2 %all-to-all-start.1 = ((f32[32,1,2640]{2,1,0:T(1,128)}), f32[32,1,2640]{2,1,0:T(1,128)}, u32[]{:S(2)}, u32[]{:S(2)}) async-start(f32[32,1,2640]{2,1,0:T(1,128)} %broadcast_in_dim.65), calls=%async_computation.1 | async-start | bytes 688128 | tf_op jit(solution)/shard_map/all_to_all | solution.py:836
  135.4 29.2 %collective-permute-start.28 = (bf16[4,1,128,384]{3,2,1,0:T(8,128)(2,1)}, bf16[4,1,128,384]{3,2,1,0:T(8,128)(2,1)}, u32[]{:S(2)}, u32[]{:S(2)}) collective-permute-start(bf16[4,1,128,384]{3,2,1,0:T(8,128)(2,1)} %get-tuple-element.140), channel_id=1, source_target_pairs={{0,1},{1,0},{2,3},{3,2},{4,5},{5,4},{6,7},{7,6},{8,9},{9,8},{10,11... | collective-permute-start | bytes 1179656 | tf_op jit(solution)/shard_map/ppermute | solution.py:534
  135.7 13.1 %collective-permute-start.32 = (bf16[4,24,1152]{2,1,0:T(8,128)(2,1)}, bf16[4,24,1152]{2,1,0:T(8,128)(2,1)S(1)}, u32[]{:S(2)}, u32[]{:S(2)}) collective-permute-start(bf16[4,24,1152]{2,1,0:T(8,128)(2,1)} %get-tuple-element.117), channel_id=1, source_target_pairs={{0,1},{1,0},{2,3},{3,2},{4,5},{5,4},{6,7},{7,6},{8,9},{9,8},{10,11... | collective-permute-start | bytes 663560 | tf_op jit(solution)/shard_map/ppermute | solution.py:538
  136.8 12.0 %collective-permute-start.33 = (bf16[4,24,1152]{2,1,0:T(8,128)(2,1)}, bf16[4,24,1152]{2,1,0:T(8,128)(2,1)S(1)}, u32[]{:S(2)}, u32[]{:S(2)}) collective-permute-start(bf16[4,24,1152]{2,1,0:T(8,128)(2,1)} %get-tuple-element.119), channel_id=1, source_target_pairs={{0,2},{1,3},{2,0},{3,1},{4,6},{5,7},{6,4},{7,5},{8,10},{9,11},{10,... | collective-permute-start | bytes 663560 | tf_op jit(solution)/shard_map/ppermute | solution.py:538
  137.0 16.4 %collective-permute-start.30 = (bf16[4,24,1152]{2,1,0:T(8,128)(2,1)}, bf16[4,24,1152]{2,1,0:T(8,128)(2,1)S(1)}, u32[]{:S(2)}, u32[]{:S(2)}) collective-permute-start(bf16[4,24,1152]{2,1,0:T(8,128)(2,1)} %get-tuple-element.110), channel_id=1, source_target_pairs={{0,1},{1,0},{2,3},{3,2},{4,5},{5,4},{6,7},{7,6},{8,9},{9,8},{10,11... | collective-permute-start | bytes 663560 | tf_op jit(solution)/shard_map/ppermute | solution.py:538
  137.5 15.9 %collective-permute-start.31 = (bf16[4,24,1152]{2,1,0:T(8,128)(2,1)}, bf16[4,24,1152]{2,1,0:T(8,128)(2,1)S(1)}, u32[]{:S(2)}, u32[]{:S(2)}) collective-permute-start(bf16[4,24,1152]{2,1,0:T(8,128)(2,1)} %get-tuple-element.112), channel_id=1, source_target_pairs={{0,2},{1,3},{2,0},{3,1},{4,6},{5,7},{6,4},{7,5},{8,10},{9,11},{10,... | collective-permute-start | bytes 663560 | tf_op jit(solution)/shard_map/ppermute | solution.py:538
  154.1 16.3 %collective-permute-start.34 = (bf16[24,2304]{1,0:T(8,128)(2,1)S(1)}, bf16[24,2304]{1,0:T(8,128)(2,1)S(1)}, u32[]{:S(2)}, u32[]{:S(2)}) collective-permute-start(bf16[24,2304]{1,0:T(8,128)(2,1)S(1)} %get-tuple-element.123), channel_id=1, source_target_pairs={{0,4},{1,5},{2,6},{3,7},{4,8},{5,9},{6,10},{7,11},{8,12},{9,13},{1... | collective-permute-start | bytes 331784 | tf_op jit(solution)/shard_map/ppermute | solution.py:538
  154.4 19.9 %collective-permute-start.35 = (bf16[24,2304]{1,0:T(8,128)(2,1)S(1)}, bf16[24,2304]{1,0:T(8,128)(2,1)S(1)}, u32[]{:S(2)}, u32[]{:S(2)}) collective-permute-start(bf16[24,2304]{1,0:T(8,128)(2,1)S(1)} %get-tuple-element.124), channel_id=1, source_target_pairs={{0,8},{1,9},{2,10},{3,11},{4,12},{5,13},{6,14},{7,15},{8,0},{9,1},... | collective-permute-start | bytes 331784 | tf_op jit(solution)/shard_map/ppermute | solution.py:538
  158.2 26.5 %all-to-all-start.2 = ((f32[32,1,768]{2,1,0:T(1,128)}), f32[32,1,768]{2,1,0:T(1,128)S(1)}, u32[]{:S(2)}, u32[]{:S(2)}) async-start(f32[32,1,768]{2,1,0:T(1,128)} %broadcast_in_dim.67), calls=%async_computation.2 | async-start | bytes 196608 | tf_op jit(solution)/shard_map/all_to_all | solution.py:898
  167.2 21.6 %collective-permute-start.29 = (bf16[2,2,128,384]{3,2,1,0:T(8,128)(2,1)}, bf16[2,2,128,384]{3,2,1,0:T(8,128)(2,1)S(1)}, u32[]{:S(2)}, u32[]{:S(2)}) collective-permute-start(bf16[2,2,128,384]{3,2,1,0:T(8,128)(2,1)} %get-tuple-element.138), channel_id=1, source_target_pairs={{0,16},{16,0},{1,17},{17,1},{2,18},{18,2},{3,19},{19,3},{4,20},{20... | collective-permute-start | bytes 1179656 | tf_op jit(solution)/shard_map/ppermute | solution.py:534
  170.4 9.1 %collective-permute-start.38 = (bf16[24,2304]{1,0:T(8,128)(2,1)S(1)}, bf16[24,2304]{1,0:T(8,128)(2,1)S(1)}, u32[]{:S(2)}, u32[]{:S(2)}) collective-permute-start(bf16[24,2304]{1,0:T(8,128)(2,1)S(1)} %get-tuple-element.127), channel_id=1, source_target_pairs={{0,8},{1,9},{2,10},{3,11},{4,12},{5,13},{6,14},{7,15},{8,0},{9,1},... | collective-permute-start | bytes 331784 | tf_op jit(solution)/shard_map/ppermute | solution.py:538
  (47 other events, 391.3 us)

commit v12 on v10

--- a/solution.py
+++ b/solution.py
@@ -565,8 +565,8 @@
         + [jax.ShapeDtypeStruct(block.shape, block.dtype) for block in handed],
         [place, *shards, *handed],
         scratch=[pltpu.SemaphoreType.DMA((high + len(handed), 2))],
-        memory=pl.ANY,
         after=after,
+        limit=32,
     )
 
 
@@ -583,7 +583,7 @@
         [jax.ShapeDtypeStruct((high, 2, 2, rows, 2 * lanes), first.dtype)],
         [place, first, first_x, first_y, first_both, second, second_x, second_y, second_both],
         scratch=[pltpu.SemaphoreType.DMA((8,))],
-        memory=pl.ANY,
+        limit=32,
     )
     return full.reshape(size * rows, 2 * lanes)
 
@@ -764,8 +764,9 @@
     silu_own = lax.dynamic_slice_in_dim(silu_all, ring_rank * rows, rows, 1)
     if compact:
         first_shards = rotations(first_shard, ring_size)
-        silu_late = hand_on(rank, silu_own, (first_shards[1],))
-        *first_parts, second_shard = gather_along_z(first_shards, place, handed=(second_shard,))
+        *first_parts, second_shard, silu_late = gather_along_z(
+            first_shards, place, handed=(second_shard, silu_own)
+        )
         first_parts += first_flips(*first_parts, ring_size)
     else:
         silu_late = silu_own
@@ -783,7 +784,7 @@
 
     if compact:
         second_parts = gather_along_z(
-            rotations(second_shard, ring_size), place, after=(products, both, *first_parts[2:])
+            rotations(second_shard, ring_size), place, after=(both, *first_parts[2:])
         )
         second_parts += first_flips(*second_parts, ring_size)
         first_pack = gather_across(*first_parts, place, ring_size)

time: 181 us -> 177 us (0.978)
  starting transfers between devices: 64.8 us -> 56.2 us
  waiting for transfers between devices: 39.5 us -> 46.3 us
  other arithmetic: 10 us -> 7.31 us
  local copies, waits for them, and re-layouts: 19.8 us -> 17.8 us
    ppermute x32, starting transfers between devices: 34.1 us -> 29.1 us  [ring_exchange(): return lax.ppermute(block, RING, [(i, step(i)) for i in range(size)])]
    all_to_all x1, waiting for transfers between devices: 0.01 us -> 4.65 us  [per_device(): lax.all_to_all(products[:, None], ('section', 'dp', 'seq'), 0, 0, tiled=T...]
    ppermute x9, starting transfers between devices: 11.6 us -> 7.44 us  [pair_swap(): return lax.ppermute(block, axis, [(0, 1), (1, 0)])]
    ppermute x32, waiting for transfers between devices: 39.5 us -> 41.6 us  [ring_exchange(): return lax.ppermute(block, RING, [(i, step(i)) for i in range(size)])]
    unnamed x78 -> x80, local copies, waits for them, and re-layouts: 12.6 us -> 11 us
    pallas_call x15 -> x14, Pallas kernels: 14 us -> 15.5 us  [in_memory(): pl.pallas_call(body, out_shape=shapes, in_specs=specs, out_specs=[pl.Bloc...]
  transfers between devices with their start and end apart: 44 -> 44, of which waited for: 10 -> 11; matrix products, arithmetic and copies ran while one was open for 10% -> 10% of each run, Pallas kernels for 14% -> 15%
where the time goes in v12:
time: 177 us; the launch traced here: 176 us
  starting transfers between devices  56.2 us (32%)
  waiting for transfers between devices  46.3 us (26%)
  Pallas kernels  41.4 us (23%)
  local copies, waits for them, and re-layouts  17.8 us (10%)
  other arithmetic  7.31 us (4%)
  matrix products  4.65 us (3%)
  between operations  2 us (1%)
    ppermute x32, waiting for transfers between devices, ring_exchange(): return lax.ppermute(block, RING, [(i, step(i)) for i in range(size)])  41.6 us
    ppermute x32, starting transfers between devices, ring_exchange(): return lax.ppermute(block, RING, [(i, step(i)) for i in range(size)])  29.1 us
    pallas_call x3, Pallas kernels, run_section(): pl.pallas_call(partial(section_kernel, layout, forward, backward, len(aft...  25.9 us
    pallas_call x14, Pallas kernels, in_memory(): pl.pallas_call(body, out_shape=shapes, in_specs=specs, out_specs=[pl.Bloc...  15.5 us
    unnamed x80, local copies, waits for them, and re-layouts  11 us
    all_to_all x1, starting transfers between devices, per_device(): lax.all_to_all(columns, ('section', 'dp', 'seq'), 0, 0, tiled=True)  7.84 us
    ppermute x9, starting transfers between devices, pair_swap(): return lax.ppermute(block, axis, [(0, 1), (1, 0)])  7.44 us
    all_to_all x1, starting transfers between devices, per_device(): lax.all_to_all(rows_back[:, None], ('section', 'dp', 'seq'), 0, 0, tiled=...  6.68 us
  transfers between devices with their start and end apart: 44, of which 11 were waited for; matrix products, arithmetic and copies ran while one was open for 10% of the time, Pallas kernels for 15%

profile of v12, /device:TPU:9, one launch (start us, length us, event | category | flops | bytes accessed | tf_op | source)
XLA Modules:
  0.0 175.7 jit_solution(1244430311486939280)
XLA Ops:
  0.7 1.7 shard_map.178
  4.2 1.3 collective-permute-start
  6.7 1.3 collective-permute-start.2
  9.1 1.4 collective-permute-start.4
  11.1 6.2 %collective-permute-done.3.refs_3_ = bf16[24,2304]{1,0:T(8,128)(2,1)S(1)} collective-permute-done((bf16[24,2304]{1,0:T(8,128)(2,1)S(1)}, bf16[24,2304]{1,0:T(8,128)(2,1)S(1)}, u32[]{:S(2)}, u32[]{:S(2)}) %collective-permute-start.3) | collective-permute-done | bytes 110624 | tf_op jit(solution)/shard_map/ppermute | solution.py:544
  17.3 2.4 %collective-permute-done.4.refs_4_ = bf16[24,2304]{1,0:T(8,128)(2,1)S(1)} collective-permute-done((bf16[24,2304]{1,0:T(8,128)(2,1)S(1)}, bf16[24,2304]{1,0:T(8,128)(2,1)S(1)}, u32[]{:S(2)}, u32[]{:S(2)}) %collective-permute-start.4) | collective-permute-done | bytes 110624 | tf_op jit(solution)/shard_map/ppermute | solution.py:544
  24.4 2.9 %collective-permute-done.12.refs_2_ = bf16[24,2304]{1,0:T(8,128)(2,1)S(1)} collective-permute-done((bf16[24,2304]{1,0:T(8,128)(2,1)S(1)}, bf16[24,2304]{1,0:T(8,128)(2,1)S(1)}, u32[]{:S(2)}, u32[]{:S(2)}) %collective-permute-start.12) | collective-permute-done | bytes 110624 | tf_op jit(solution)/shard_map/ppermute | solution.py:544
  29.3 5.9 %collective-permute-done.14.refs_4_ = bf16[24,2304]{1,0:T(8,128)(2,1)S(1)} collective-permute-done((bf16[24,2304]{1,0:T(8,128)(2,1)S(1)}, bf16[24,2304]{1,0:T(8,128)(2,1)S(1)}, u32[]{:S(2)}, u32[]{:S(2)}) %collective-permute-start.14) | collective-permute-done | bytes 110624 | tf_op jit(solution)/shard_map/ppermute | solution.py:544
  39.5 7.7 %collective-permute-done.10.refs_8_ = bf16[4,24,1152]{2,1,0:T(8,128)(2,1)S(1)} collective-permute-done((bf16[4,24,1152]{2,1,0:T(8,128)(2,1)S(1)}, bf16[4,24,1152]{2,1,0:T(8,128)(2,1)S(1)}, u32[]{:S(2)}, u32[]{:S(2)}) %collective-permute-start.10) | collective-permute-done | bytes 221216 | tf_op jit(solution)/shard_map/ppermute | solution.py:544
  48.2 3.0 %collective-permute-start.11 = (bf16[384,2304]{1,0:T(8,128)(2,1)S(1)}, bf16[384,2304]{1,0:T(8,128)(2,1)}, u32[]{:S(2)}, u32[]{:S(2)}) collective-permute-start(bf16[384,2304]{1,0:T(8,128)(2,1)S(1)} %bitcast.59), channel_id=1, source_target_pairs={{0,16},{16,0},{1,17},{17,1},{2,18},{18,2},{3,19},{19,3},{4,20},{20... | collective-permute-start | bytes 5308424 | tf_op jit(solution)/shard_map/ppermute | solution.py:540
  53.8 5.1 %all-to-all-start = ((f32[32,1,2640]{2,1,0:T(1,128)}), f32[32,1,2640]{2,1,0:T(1,128)}, u32[]{:S(2)}, u32[]{:S(2)}) async-start(f32[32,1,2640]{2,1,0:T(1,128)} %copy.22), calls=%async_computation | async-start | bytes 688128 | tf_op jit(solution)/shard_map/all_to_all | solution.py:777
  59.0 2.9 %shard_map.183 = bf16[4,2,2,24,2304]{4,3,2,1,0:T(8,128)(2,1)} custom-call(s32[3]{0:T(128)S(1)} %pad_add_fusion.refs_0_, bf16[4,24,1152]{2,1,0:T(8,128)(2,1)S(1)} %get-tuple-element.87.refs_1_, bf16[4,24,1152]{2,1,0:T(8,128)(2,1)} %collective-permute-done.15.refs_2_, bf16[4,24,1152]{2,1,0:T(8,128)(2,1)} %collective-permute-done.16.refs_3_, ...), custom_call_target="tpu_custom_call" | custom-call | bytes 5308416 | tf_op jit(solution)/shard_map/pallas_call | solution.py:519
  64.8 4.7 %all-to-all-done = f32[32,1,2640]{2,1,0:T(1,128)} async-done(((f32[32,1,2640]{2,1,0:T(1,128)}), f32[32,1,2640]{2,1,0:T(1,128)}, u32[]{:S(2)}, u32[]{:S(2)}) %all-to-all-start) | async-done | bytes 337952 | tf_op jit(solution)/shard_map/all_to_all | solution.py:777
  70.5 5.7 %shard_map.181 = (bf16[256,384]{1,0:T(8,128)(2,1)S(1)}, f32[1,2304]{1,0:T(1,128)S(1)}, bf16[256,1152]{1,0:T(8,128)(2,1)S(1)}, bf16[256,384]{1,0:T(8,128)(2,1)S(1...) custom-call(s32[1]{0:T(128)} %bitcast.refs_0_, ...), custom_call_target="tpu_custom_call" | custom-call | flops 1006632960 | bytes 5308416 | tf_op jit(solution)/shard_map/pallas_call | solution.py:352
  76.3 12.7 %shard_map.184 = (bf16[256,384]{1,0:T(8,128)(2,1)S(1)}, bf16[256,384]{1,0:T(8,128)(2,1)S(1)}, f32[1,2304]{1,0:T(1,128)S(1)}, f32[16,336]{1,0:T(8,128)S(1)}, bf16...) custom-call(s32[1]{0:T(128)} %bitcast.refs_0_, bf16[256,384]{1,0:T(8,128)(2,1)S(1)} %get-tuple-element.76.refs_1_, ...), custom_call_target="tpu_custom_call" | custom-call | flops 3019898880 | bytes 10616832 | tf_op jit(solution)/shard_map/pallas_call | solution.py:352
  89.6 7.5 %shard_map.185 = (bf16[256,384]{1,0:T(8,128)(2,1)S(1)}, f32[1,2304]{1,0:T(1,128)S(1)}, f32[16,336]{1,0:T(8,128)S(1)}, bf16[384,2304]{1,0:T(8,128)(2,1)S(1)}, bf16[384,2304]{1,0:T(8,128)(2,1)}) custom-call(s32[1]{0:T(128)} %bitcast.refs_0_, bf16[256,384]{1,0:T(8,128)(2,1)S(1)} %get-tuple-element.140.refs_1_, f32[1,2304]{1,0:T(1,128)S(1)} %get-tuple-element.77.refs_2_, ...), custom_call_target="tpu_custom_call" | custom-call | flops 2013265920 | bytes 10616832 | tf_op jit(solution)/shard_map/pallas_call | solution.py:352
  97.3 1.7 shard_map.186
  102.1 1.5 copy-done.2
  104.3 1.7 shard_map.187
  110.0 6.7 %all-to-all-start.1 = ((f32[32,1,2640]{2,1,0:T(1,128)}), f32[32,1,2640]{2,1,0:T(1,128)}, u32[]{:S(2)}, u32[]{:S(2)}) async-start(f32[32,1,2640]{2,1,0:T(1,128)} %broadcast_in_dim.65), calls=%async_computation.1 | async-start | bytes 688128 | tf_op jit(solution)/shard_map/all_to_all | solution.py:854
  117.7 1.4 shard_map.188
  119.1 1.3 collective-permute-start.28
  121.6 8.5 %collective-permute-done.28.refs_2_ = bf16[4,24,1152]{2,1,0:T(8,128)(2,1)S(1)} collective-permute-done((bf16[4,24,1152]{2,1,0:T(8,128)(2,1)S(1)}, bf16[4,24,1152]{2,1,0:T(8,128)(2,1)S(1)}, u32[]{:S(2)}, u32[]{:S(2)}) %collective-permute-start.28) | collective-permute-done | bytes 221216 | tf_op jit(solution)/shard_map/ppermute | solution.py:544
  139.2 3.4 %collective-permute-start.35 = (bf16[24,2304]{1,0:T(8,128)(2,1)}, bf16[24,2304]{1,0:T(8,128)(2,1)S(1)}, u32[]{:S(2)}, u32[]{:S(2)}) collective-permute-start(bf16[24,2304]{1,0:T(8,128)(2,1)} %copy-done.25), channel_id=1, source_target_pairs={{0,8},{1,9},{2,10},{3,11},{4,12},{5,13},{6,14},{7,15},{8,0},{9,1},... | collective-permute-start | bytes 331784 | tf_op jit(solution)/shard_map/ppermute | solution.py:544
  142.6 1.4 collective-permute-start.36
  144.8 7.8 %all-to-all-start.2 = ((f32[32,1,768]{2,1,0:T(1,128)}), f32[32,1,768]{2,1,0:T(1,128)S(1)}, u32[]{:S(2)}, u32[]{:S(2)}) async-start(f32[32,1,768]{2,1,0:T(1,128)} %broadcast_in_dim.67), calls=%async_computation.2 | async-start | bytes 196608 | tf_op jit(solution)/shard_map/all_to_all | solution.py:863
  152.6 1.6 maximum_select_fusion
  159.1 1.4 collective-permute-start.39
  160.5 1.9 %convolution_bitcast_fusion = f32[1,24,2304]{2,1,0:T(8,128)} fusion(bf16[32,24]{1,0:T(8,128)(2,1)S(1)} %fusion.19.refs_6_, f32[32,2640]{1,0:T(8,128)} %bitcast.70), kind=kOutput, calls=%fused_computation | convolution fusion | flops 3538944 | bytes 370176 | tf_op jit(solution)/shard_map/dot_general | solution.py:30
  163.3 4.1 %collective-permute-done.38.refs_3_ = bf16[24,2304]{1,0:T(8,128)(2,1)S(1)} collective-permute-done((bf16[24,2304]{1,0:T(8,128)(2,1)S(1)}, bf16[24,2304]{1,0:T(8,128)(2,1)S(1)}, u32[]{:S(2)}, u32[]{:S(2)}) %collective-permute-start.38) | collective-permute-done | bytes 110624 | tf_op jit(solution)/shard_map/ppermute | solution.py:544
  167.5 2.2 %collective-permute-done.39.refs_4_ = bf16[24,2304]{1,0:T(8,128)(2,1)S(1)} collective-permute-done((bf16[24,2304]{1,0:T(8,128)(2,1)S(1)}, bf16[24,2304]{1,0:T(8,128)(2,1)S(1)}, u32[]{:S(2)}, u32[]{:S(2)}) %collective-permute-start.39) | collective-permute-done | bytes 110624 | tf_op jit(solution)/shard_map/ppermute | solution.py:544
  170.3 2.2 %fusion.5 = f32[1000,384]{1,0:T(8,128)} fusion(s32[32]{0:T(128)S(1)} %copy-done.35, f32[32,384]{1,0:T(8,128)S(1)} %copy-done.32, f32[32,384]{1,0:T(8,128)S(1)} %reshape.76), kind=kOutput, calls=%fused_computation.27 | convolution fusion | flops 147598592 | bytes 1634432 | tf_op jit(solution)/shard_map/dot_general | solution.py:909
  (197 shorter events, 52.8 us)
Async XLA Ops:
  4.2 19.2 %collective-permute-start = (bf16[2,128,384]{2,1,0:T(8,128)(2,1)S(1)}, bf16[2,128,384]{2,1,0:T(8,128)(2,1)S(1)}, u32[]{:S(2)}, u32[]{:S(2)}) collective-permute-start(bf16[2,128,384]{2,1,0:T(8,128)(2,1)S(1)} %get-tuple-element.142), channel_id=1, source_target_pairs={{0,1},{1,0},{2,3},{3,2},{4,5},{5,4},{6,7},{7,6},{8,9},{9,8},{10,11... | collective-permute-start | bytes 589832 | tf_op jit(solution)/shard_map/ppermute | solution.py:540
  8.0 9.3 %collective-permute-start.3 = (bf16[24,2304]{1,0:T(8,128)(2,1)S(1)}, bf16[24,2304]{1,0:T(8,128)(2,1)S(1)}, u32[]{:S(2)}, u32[]{:S(2)}) collective-permute-start(bf16[24,2304]{1,0:T(8,128)(2,1)S(1)} %get-tuple-element.146.refs_1_), channel_id=1, source_target_pairs={{0,8},{1,9},{2,10},{3,11},{4,12},{5,13},{6,14},{7,15},{8,0},{9,1},... | collective-permute-start | bytes 331784 | tf_op jit(solution)/shard_map/ppermute | solution.py:544
  9.1 10.6 %collective-permute-start.4 = (bf16[24,2304]{1,0:T(8,128)(2,1)S(1)}, bf16[24,2304]{1,0:T(8,128)(2,1)S(1)}, u32[]{:S(2)}, u32[]{:S(2)}) collective-permute-start(bf16[24,2304]{1,0:T(8,128)(2,1)S(1)} %get-tuple-element.146.refs_1_), channel_id=1, source_target_pairs={{0,12},{1,13},{2,14},{3,15},{4,0},{5,1},{6,2},{7,3},{8,4},{9,5},{1... | collective-permute-start | bytes 331784 | tf_op jit(solution)/shard_map/ppermute | solution.py:544
  20.7 14.5 %collective-permute-start.5 = (bf16[4,24,1152]{2,1,0:T(8,128)(2,1)S(1)}, bf16[4,24,1152]{2,1,0:T(8,128)(2,1)S(1)}, u32[]{:S(2)}, u32[]{:S(2)}) collective-permute-start(bf16[4,24,1152]{2,1,0:T(8,128)(2,1)S(1)} %get-tuple-element.74.refs_1_), channel_id=1, source_target_pairs={{0,2},{1,3},{2,0},{3,1},{4,6},{5,7},{6,4},{7,5},{8,10},{9,11},{10,... | collective-permute-start | bytes 663560 | tf_op jit(solution)/shard_map/ppermute | solution.py:544
  21.9 15.8 %collective-permute-start.6 = (bf16[4,24,1152]{2,1,0:T(8,128)(2,1)S(1)}, bf16[4,24,1152]{2,1,0:T(8,128)(2,1)S(1)}, u32[]{:S(2)}, u32[]{:S(2)}) collective-permute-start(bf16[4,24,1152]{2,1,0:T(8,128)(2,1)S(1)} %get-tuple-element.74.refs_1_), channel_id=1, source_target_pairs={{0,1},{1,0},{2,3},{3,2},{4,5},{5,4},{6,7},{7,6},{8,9},{9,8},{10,11... | collective-permute-start | bytes 663560 | tf_op jit(solution)/shard_map/ppermute | solution.py:544
  22.2 13.0 %collective-permute-start.9 = (bf16[4,24,1152]{2,1,0:T(8,128)(2,1)S(1)}, bf16[4,24,1152]{2,1,0:T(8,128)(2,1)S(1)}, u32[]{:S(2)}, u32[]{:S(2)}) collective-permute-start(bf16[4,24,1152]{2,1,0:T(8,128)(2,1)S(1)} %get-tuple-element.75.refs_5_), channel_id=1, source_target_pairs={{0,1},{1,0},{2,3},{3,2},{4,5},{5,4},{6,7},{7,6},{8,9},{9,8},{10,11... | collective-permute-start | bytes 663560 | tf_op jit(solution)/shard_map/ppermute | solution.py:544
  29.0 10.2 %collective-permute-start.8 = (bf16[4,24,1152]{2,1,0:T(8,128)(2,1)S(1)}, bf16[4,24,1152]{2,1,0:T(8,128)(2,1)S(1)}, u32[]{:S(2)}, u32[]{:S(2)}) collective-permute-start(bf16[4,24,1152]{2,1,0:T(8,128)(2,1)S(1)} %get-tuple-element.75.refs_5_), channel_id=1, source_target_pairs={{0,2},{1,3},{2,0},{3,1},{4,6},{5,7},{6,4},{7,5},{8,10},{9,11},{10,... | collective-permute-start | bytes 663560 | tf_op jit(solution)/shard_map/ppermute | solution.py:544
  36.0 15.2 %collective-permute-start.15 = (bf16[4,24,1152]{2,1,0:T(8,128)(2,1)S(1)}, bf16[4,24,1152]{2,1,0:T(8,128)(2,1)}, u32[]{:S(2)}, u32[]{:S(2)}) collective-permute-start(bf16[4,24,1152]{2,1,0:T(8,128)(2,1)S(1)} %get-tuple-element.87.refs_1_), channel_id=1, source_target_pairs={{0,2},{1,3},{2,0},{3,1},{4,6},{5,7},{6,4},{7,5},{8,10},{9,11},{10,... | collective-permute-start | bytes 663560 | tf_op jit(solution)/shard_map/ppermute | solution.py:544
  36.3 15.2 %collective-permute-start.19 = (bf16[4,24,1152]{2,1,0:T(8,128)(2,1)S(1)}, bf16[4,24,1152]{2,1,0:T(8,128)(2,1)}, u32[]{:S(2)}, u32[]{:S(2)}) collective-permute-start(bf16[4,24,1152]{2,1,0:T(8,128)(2,1)S(1)} %get-tuple-element.88.refs_5_), channel_id=1, source_target_pairs={{0,1},{1,0},{2,3},{3,2},{4,5},{5,4},{6,7},{7,6},{8,9},{9,8},{10,11... | collective-permute-start | bytes 663560 | tf_op jit(solution)/shard_map/ppermute | solution.py:544
  36.5 10.6 %collective-permute-start.10 = (bf16[4,24,1152]{2,1,0:T(8,128)(2,1)S(1)}, bf16[4,24,1152]{2,1,0:T(8,128)(2,1)S(1)}, u32[]{:S(2)}, u32[]{:S(2)}) collective-permute-start(bf16[4,24,1152]{2,1,0:T(8,128)(2,1)S(1)} %collective-permute-done.9.refs_7_), channel_id=1, source_target_pairs={{0,2},{1,3},{2,0},{3,1},{4,6},{5,7},{6,4},{7,5},{8,10},{9,11},{10,... | collective-permute-start | bytes 663560 | tf_op jit(solution)/shard_map/ppermute | solution.py:544
  37.8 9.6 %collective-permute-start.7 = (bf16[4,24,1152]{2,1,0:T(8,128)(2,1)S(1)}, bf16[4,24,1152]{2,1,0:T(8,128)(2,1)S(1)}, u32[]{:S(2)}, u32[]{:S(2)}) collective-permute-start(bf16[4,24,1152]{2,1,0:T(8,128)(2,1)S(1)} %collective-permute-done.5.refs_2_.refs_6_), channel_id=1, source_target_pairs={{0,1},{1,0},{2,3},{3,2},{4,5},{5,4},{6,7},{7,6},{8,9},{9,8},{10,11... | collective-permute-start | bytes 663560 | tf_op jit(solution)/shard_map/ppermute | solution.py:544
  39.2 19.8 %collective-permute-start.16 = (bf16[4,24,1152]{2,1,0:T(8,128)(2,1)S(1)}, bf16[4,24,1152]{2,1,0:T(8,128)(2,1)}, u32[]{:S(2)}, u32[]{:S(2)}) collective-permute-start(bf16[4,24,1152]{2,1,0:T(8,128)(2,1)S(1)} %get-tuple-element.87.refs_1_), channel_id=1, source_target_pairs={{0,1},{1,0},{2,3},{3,2},{4,5},{5,4},{6,7},{7,6},{8,9},{9,8},{10,11... | collective-permute-start | bytes 663560 | tf_op jit(solution)/shard_map/ppermute | solution.py:544
  47.1 11.8 %collective-permute-start.18 = (bf16[4,24,1152]{2,1,0:T(8,128)(2,1)S(1)}, bf16[4,24,1152]{2,1,0:T(8,128)(2,1)}, u32[]{:S(2)}, u32[]{:S(2)}) collective-permute-start(bf16[4,24,1152]{2,1,0:T(8,128)(2,1)S(1)} %get-tuple-element.88.refs_5_), channel_id=1, source_target_pairs={{0,2},{1,3},{2,0},{3,1},{4,6},{5,7},{6,4},{7,5},{8,10},{9,11},{10,... | collective-permute-start | bytes 663560 | tf_op jit(solution)/shard_map/ppermute | solution.py:544
  48.2 22.3 %collective-permute-start.11 = (bf16[384,2304]{1,0:T(8,128)(2,1)S(1)}, bf16[384,2304]{1,0:T(8,128)(2,1)}, u32[]{:S(2)}, u32[]{:S(2)}) collective-permute-start(bf16[384,2304]{1,0:T(8,128)(2,1)S(1)} %bitcast.59), channel_id=1, source_target_pairs={{0,16},{16,0},{1,17},{17,1},{2,18},{18,2},{3,19},{19,3},{4,20},{20... | collective-permute-start | bytes 5308424 | tf_op jit(solution)/shard_map/ppermute | solution.py:540
  53.8 15.6 %all-to-all-start = ((f32[32,1,2640]{2,1,0:T(1,128)}), f32[32,1,2640]{2,1,0:T(1,128)}, u32[]{:S(2)}, u32[]{:S(2)}) async-start(f32[32,1,2640]{2,1,0:T(1,128)} %copy.22), calls=%async_computation | async-start | bytes 688128 | tf_op jit(solution)/shard_map/all_to_all | solution.py:777
  61.9 14.3 %collective-permute-start.21 = (bf16[384,2304]{1,0:T(8,128)(2,1)}, bf16[384,2304]{1,0:T(8,128)(2,1)}, u32[]{:S(2)}, u32[]{:S(2)}) collective-permute-start(bf16[384,2304]{1,0:T(8,128)(2,1)} %bitcast.21.refs_5_), channel_id=1, source_target_pairs={{0,16},{16,0},{1,17},{17,1},{2,18},{18,2},{3,19},{19,3},{4,20},{20... | collective-permute-start | bytes 5308424 | tf_op jit(solution)/shard_map/ppermute | solution.py:540
  99.8 16.9 %collective-permute-start.26 = (bf16[4,2,24,1152]{3,2,1,0:T(8,128)(2,1)}, bf16[4,2,24,1152]{3,2,1,0:T(8,128)(2,1)}, u32[]{:S(2)}, u32[]{:S(2)}) collective-permute-start(bf16[4,2,24,1152]{3,2,1,0:T(8,128)(2,1)} %get-tuple-element.102), channel_id=1, source_target_pairs={{0,2},{1,3},{2,0},{3,1},{4,6},{5,7},{6,4},{7,5},{8,10},{9,11},{10,... | collective-permute-start | bytes 1327112 | tf_op jit(solution)/shard_map/ppermute | solution.py:544
  100.9 15.7 %collective-permute-start.27 = (bf16[4,2,24,1152]{3,2,1,0:T(8,128)(2,1)}, bf16[4,2,24,1152]{3,2,1,0:T(8,128)(2,1)}, u32[]{:S(2)}, u32[]{:S(2)}) collective-permute-start(bf16[4,2,24,1152]{3,2,1,0:T(8,128)(2,1)} %get-tuple-element.104), channel_id=1, source_target_pairs={{0,1},{1,0},{2,3},{3,2},{4,5},{5,4},{6,7},{7,6},{8,9},{9,8},{10,11... | collective-permute-start | bytes 1327112 | tf_op jit(solution)/shard_map/ppermute | solution.py:544
  107.5 23.8 %collective-permute-start.24 = (bf16[4,2,24,1152]{3,2,1,0:T(8,128)(2,1)}, bf16[4,2,24,1152]{3,2,1,0:T(8,128)(2,1)S(1)}, u32[]{:S(2)}, u32[]{:S(2)}) collective-permute-start(bf16[4,2,24,1152]{3,2,1,0:T(8,128)(2,1)} %get-tuple-element.98), channel_id=1, source_target_pairs={{0,2},{1,3},{2,0},{3,1},{4,6},{5,7},{6,4},{7,5},{8,10},{9,11},{10,... | collective-permute-start | bytes 1327112 | tf_op jit(solution)/shard_map/ppermute | solution.py:544
  108.4 22.9 %collective-permute-start.25 = (bf16[4,2,24,1152]{3,2,1,0:T(8,128)(2,1)}, bf16[4,2,24,1152]{3,2,1,0:T(8,128)(2,1)S(1)}, u32[]{:S(2)}, u32[]{:S(2)}) collective-permute-start(bf16[4,2,24,1152]{3,2,1,0:T(8,128)(2,1)} %get-tuple-element.100), channel_id=1, source_target_pairs={{0,1},{1,0},{2,3},{3,2},{4,5},{5,4},{6,7},{7,6},{8,9},{9,8},{10,11... | collective-permute-start | bytes 1327112 | tf_op jit(solution)/shard_map/ppermute | solution.py:544
  110.0 25.9 %all-to-all-start.1 = ((f32[32,1,2640]{2,1,0:T(1,128)}), f32[32,1,2640]{2,1,0:T(1,128)}, u32[]{:S(2)}, u32[]{:S(2)}) async-start(f32[32,1,2640]{2,1,0:T(1,128)} %broadcast_in_dim.65), calls=%async_computation.1 | async-start | bytes 688128 | tf_op jit(solution)/shard_map/all_to_all | solution.py:854
  119.1 11.0 %collective-permute-start.28 = (bf16[4,24,1152]{2,1,0:T(8,128)(2,1)S(1)}, bf16[4,24,1152]{2,1,0:T(8,128)(2,1)S(1)}, u32[]{:S(2)}, u32[]{:S(2)}) collective-permute-start(bf16[4,24,1152]{2,1,0:T(8,128)(2,1)S(1)} %get-tuple-element.106), channel_id=1, source_target_pairs={{0,1},{1,0},{2,3},{3,2},{4,5},{5,4},{6,7},{7,6},{8,9},{9,8},{10,11... | collective-permute-start | bytes 663560 | tf_op jit(solution)/shard_map/ppermute | solution.py:544
  120.3 9.7 %collective-permute-start.29 = (bf16[4,24,1152]{2,1,0:T(8,128)(2,1)S(1)}, bf16[4,24,1152]{2,1,0:T(8,128)(2,1)S(1)}, u32[]{:S(2)}, u32[]{:S(2)}) collective-permute-start(bf16[4,24,1152]{2,1,0:T(8,128)(2,1)S(1)} %get-tuple-element.108), channel_id=1, source_target_pairs={{0,2},{1,3},{2,0},{3,1},{4,6},{5,7},{6,4},{7,5},{8,10},{9,11},{10,... | collective-permute-start | bytes 663560 | tf_op jit(solution)/shard_map/ppermute | solution.py:544
  135.4 17.2 %collective-permute-start.30 = (bf16[4,1,128,384]{3,2,1,0:T(8,128)(2,1)}, bf16[4,1,128,384]{3,2,1,0:T(8,128)(2,1)}, u32[]{:S(2)}, u32[]{:S(2)}) collective-permute-start(bf16[4,1,128,384]{3,2,1,0:T(8,128)(2,1)} %get-tuple-element.138), channel_id=1, source_target_pairs={{0,1},{1,0},{2,3},{3,2},{4,5},{5,4},{6,7},{7,6},{8,9},{9,8},{10,11... | collective-permute-start | bytes 1179656 | tf_op jit(solution)/shard_map/ppermute | solution.py:540
  137.8 18.3 %collective-permute-start.33 = (bf16[4,24,1152]{2,1,0:T(8,128)(2,1)}, bf16[4,24,1152]{2,1,0:T(8,128)(2,1)S(1)}, u32[]{:S(2)}, u32[]{:S(2)}) collective-permute-start(bf16[4,24,1152]{2,1,0:T(8,128)(2,1)} %copy-done.24), channel_id=1, source_target_pairs={{0,1},{1,0},{2,3},{3,2},{4,5},{5,4},{6,7},{7,6},{8,9},{9,8},{10,11... | collective-permute-start | bytes 663560 | tf_op jit(solution)/shard_map/ppermute | solution.py:544
  138.4 17.7 %collective-permute-start.34 = (bf16[4,24,1152]{2,1,0:T(8,128)(2,1)}, bf16[4,24,1152]{2,1,0:T(8,128)(2,1)S(1)}, u32[]{:S(2)}, u32[]{:S(2)}) collective-permute-start(bf16[4,24,1152]{2,1,0:T(8,128)(2,1)} %copy-done.23), channel_id=1, source_target_pairs={{0,2},{1,3},{2,0},{3,1},{4,6},{5,7},{6,4},{7,5},{8,10},{9,11},{10,... | collective-permute-start | bytes 663560 | tf_op jit(solution)/shard_map/ppermute | solution.py:544
  139.2 16.9 %collective-permute-start.35 = (bf16[24,2304]{1,0:T(8,128)(2,1)}, bf16[24,2304]{1,0:T(8,128)(2,1)S(1)}, u32[]{:S(2)}, u32[]{:S(2)}) collective-permute-start(bf16[24,2304]{1,0:T(8,128)(2,1)} %copy-done.25), channel_id=1, source_target_pairs={{0,8},{1,9},{2,10},{3,11},{4,12},{5,13},{6,14},{7,15},{8,0},{9,1},... | collective-permute-start | bytes 331784 | tf_op jit(solution)/shard_map/ppermute | solution.py:544
  142.6 13.5 %collective-permute-start.36 = (bf16[24,2304]{1,0:T(8,128)(2,1)S(1)}, bf16[24,2304]{1,0:T(8,128)(2,1)S(1)}, u32[]{:S(2)}, u32[]{:S(2)}) collective-permute-start(bf16[24,2304]{1,0:T(8,128)(2,1)S(1)} %get-tuple-element.122), channel_id=1, source_target_pairs={{0,12},{1,13},{2,14},{3,15},{4,0},{5,1},{6,2},{7,3},{8,4},{9,5},{1... | collective-permute-start | bytes 331784 | tf_op jit(solution)/shard_map/ppermute | solution.py:544
  144.8 17.5 %all-to-all-start.2 = ((f32[32,1,768]{2,1,0:T(1,128)}), f32[32,1,768]{2,1,0:T(1,128)S(1)}, u32[]{:S(2)}, u32[]{:S(2)}) async-start(f32[32,1,768]{2,1,0:T(1,128)} %broadcast_in_dim.67), calls=%async_computation.2 | async-start | bytes 196608 | tf_op jit(solution)/shard_map/all_to_all | solution.py:863
  155.1 18.2 %collective-permute-start.31 = (bf16[2,2,128,384]{3,2,1,0:T(8,128)(2,1)}, bf16[2,2,128,384]{3,2,1,0:T(8,128)(2,1)}, u32[]{:S(2)}, u32[]{:S(2)}) collective-permute-start(bf16[2,2,128,384]{3,2,1,0:T(8,128)(2,1)} %get-tuple-element.136), channel_id=1, source_target_pairs={{0,16},{16,0},{1,17},{17,1},{2,18},{18,2},{3,19},{19,3},{4,20},{20... | collective-permute-start | bytes 1179656 | tf_op jit(solution)/shard_map/ppermute | solution.py:540
  158.0 9.4 %collective-permute-start.38 = (bf16[24,2304]{1,0:T(8,128)(2,1)S(1)}, bf16[24,2304]{1,0:T(8,128)(2,1)S(1)}, u32[]{:S(2)}, u32[]{:S(2)}) collective-permute-start(bf16[24,2304]{1,0:T(8,128)(2,1)S(1)} %get-tuple-element.125), channel_id=1, source_target_pairs={{0,8},{1,9},{2,10},{3,11},{4,12},{5,13},{6,14},{7,15},{8,0},{9,1},... | collective-permute-start | bytes 331784 | tf_op jit(solution)/shard_map/ppermute | solution.py:544
  159.1 10.6 %collective-permute-start.39 = (bf16[24,2304]{1,0:T(8,128)(2,1)S(1)}, bf16[24,2304]{1,0:T(8,128)(2,1)S(1)}, u32[]{:S(2)}, u32[]{:S(2)}) collective-permute-start(bf16[24,2304]{1,0:T(8,128)(2,1)S(1)} %get-tuple-element.126), channel_id=1, source_target_pairs={{0,12},{1,13},{2,14},{3,15},{4,0},{5,1},{6,2},{7,3},{8,4},{9,5},{1... | collective-permute-start | bytes 331784 | tf_op jit(solution)/shard_map/ppermute | solution.py:544
  (51 other events, 437.6 us)

commit v13 on v12

--- a/solution.py
+++ b/solution.py
@@ -574,7 +574,7 @@
     return flip(first, size, 2), flip(second, size, 1)
 
 
-def gather_across(first, second, first_x, second_y, place, size):
+def gather_across(first, second, first_x, second_y, place, size, after=()):
     high, rows, lanes = first.shape
     first_y, second_x = flip(first, size, 1), flip(second, size, 2)
     first_both, second_both = flip(first_x, size, 1), flip(second_y, size, 2)
@@ -583,6 +583,7 @@
         [jax.ShapeDtypeStruct((high, 2, 2, rows, 2 * lanes), first.dtype)],
         [place, first, first_x, first_y, first_both, second, second_x, second_y, second_both],
         scratch=[pltpu.SemaphoreType.DMA((8,))],
+        after=after,
         limit=32,
     )
     return full.reshape(size * rows, 2 * lanes)
@@ -763,11 +764,17 @@
     silu_all = jax.nn.silu(conditions).astype(jnp.bfloat16)
     silu_own = lax.dynamic_slice_in_dim(silu_all, ring_rank * rows, rows, 1)
     if compact:
-        first_shards = rotations(first_shard, ring_size)
-        *first_parts, second_shard, silu_late = gather_along_z(
-            first_shards, place, handed=(second_shard, silu_own)
+        *first_parts, second_shard = gather_along_z(
+            rotations(first_shard, ring_size), place, handed=(second_shard,)
         )
         first_parts += first_flips(*first_parts, ring_size)
+        *second_parts, silu_late = gather_along_z(
+            rotations(second_shard, ring_size),
+            place,
+            handed=(silu_own,),
+            after=(both, *first_parts[2:]),
+        )
+        second_parts += first_flips(*second_parts, ring_size)
     else:
         silu_late = silu_own
 
@@ -783,12 +790,8 @@
     first_bias, second_bias = products[0, :, 6 * width :], products[1, :, 6 * width :]
 
     if compact:
-        second_parts = gather_along_z(
-            rotations(second_shard, ring_size), place, after=(both, *first_parts[2:])
-        )
-        second_parts += first_flips(*second_parts, ring_size)
         first_pack = gather_across(*first_parts, place, ring_size)
-        second_pack = gather_across(*second_parts, place, ring_size)
+        second_pack = gather_across(*second_parts, place, ring_size, after=(products,))
     else:
         first_pack = lax.all_gather(first_shard, RING, axis=0, tiled=True)
         second_pack = lax.all_gather(second_shard, RING, axis=0, tiled=True)
@@ -887,7 +890,7 @@
         partial(close_kernel, len(first_pieces)),
         [shard, shard],
         [rank, *first_pieces, *second_pieces],
-        after=(columns,),
+        after=(columns, outputs),
     )
     att, out, up, down = in_memory(
         spread_kernel,

time: 177 us -> 183 us (1.034)
  waiting for transfers between devices: 46.3 us -> 55.4 us
  starting transfers between devices: 56.2 us -> 53.8 us
    ppermute x32, waiting for transfers between devices: 41.6 us -> 55.3 us  [ring_exchange(): return lax.ppermute(block, RING, [(i, step(i)) for i in range(size)])]
    all_to_all x1, waiting for transfers between devices: 4.65 us -> 0.01 us  [per_device(): lax.all_to_all(products[:, None], ('section', 'dp', 'seq'), 0, 0, tiled=T...]
    unnamed x80 -> x68, local copies, waits for them, and re-layouts: 11 us -> 10.2 us
  transfers between devices with their start and end apart: 44 -> 44, of which waited for: 11 -> 14; matrix products, arithmetic and copies ran while one was open for 10% -> 11% of each run, Pallas kernels for 15% -> 14%
where the time goes in v13:
time: 183 us; the launch traced here: 182 us
  waiting for transfers between devices  55.4 us (30%)
  starting transfers between devices  53.8 us (29%)
  Pallas kernels  41.7 us (23%)
  local copies, waits for them, and re-layouts  17.8 us (10%)
  other arithmetic  7.35 us (4%)
  matrix products  3.7 us (2%)
  between operations  2.01 us (1%)
    ppermute x32, waiting for transfers between devices, ring_exchange(): return lax.ppermute(block, RING, [(i, step(i)) for i in range(size)])  55.3 us
    ppermute x32, starting transfers between devices, ring_exchange(): return lax.ppermute(block, RING, [(i, step(i)) for i in range(size)])  30.9 us
    pallas_call x3, Pallas kernels, run_section(): pl.pallas_call(partial(section_kernel, layout, forward, backward, len(aft...  25.9 us
    pallas_call x14, Pallas kernels, in_memory(): pl.pallas_call(body, out_shape=shapes, in_specs=specs, out_specs=[pl.Bloc...  15.8 us
    unnamed x68, local copies, waits for them, and re-layouts  10.2 us
    all_to_all x1, starting transfers between devices, per_device(): lax.all_to_all(columns, ('section', 'dp', 'seq'), 0, 0, tiled=True)  7.01 us
    all_to_all x1, starting transfers between devices, per_device(): lax.all_to_all(rows_back[:, None], ('section', 'dp', 'seq'), 0, 0, tiled=...  5.97 us
    ppermute x9, starting transfers between devices, pair_swap(): return lax.ppermute(block, axis, [(0, 1), (1, 0)])  5.82 us
  transfers between devices with their start and end apart: 44, of which 14 were waited for; matrix products, arithmetic and copies ran while one was open for 11% of the time, Pallas kernels for 14%

profile of v13, /device:TPU:9, one launch (start us, length us, event | category | flops | bytes accessed | tf_op | source)
XLA Modules:
  0.0 181.8 jit_solution(4218331648587876880)
XLA Ops:
  0.7 1.7 shard_map.178
  8.5 1.4 collective-permute-start.4
  10.4 6.2 %collective-permute-done.3.refs_3_ = bf16[24,2304]{1,0:T(8,128)(2,1)S(1)} collective-permute-done((bf16[24,2304]{1,0:T(8,128)(2,1)S(1)}, bf16[24,2304]{1,0:T(8,128)(2,1)S(1)}, u32[]{:S(2)}, u32[]{:S(2)}) %collective-permute-start.3) | collective-permute-done | bytes 110624 | tf_op jit(solution)/shard_map/ppermute | solution.py:544
  16.6 2.4 %collective-permute-done.4.refs_4_ = bf16[24,2304]{1,0:T(8,128)(2,1)S(1)} collective-permute-done((bf16[24,2304]{1,0:T(8,128)(2,1)S(1)}, bf16[24,2304]{1,0:T(8,128)(2,1)S(1)}, u32[]{:S(2)}, u32[]{:S(2)}) %collective-permute-start.4) | collective-permute-done | bytes 110624 | tf_op jit(solution)/shard_map/ppermute | solution.py:544
  23.9 1.6 collective-permute-done.5.refs_2_
  25.5 1.8 collective-permute-done.6.refs_3_
  27.3 6.2 %collective-permute-done.7.refs_4_ = bf16[24,2304]{1,0:T(8,128)(2,1)S(1)} collective-permute-done((bf16[24,2304]{1,0:T(8,128)(2,1)S(1)}, bf16[24,2304]{1,0:T(8,128)(2,1)S(1)}, u32[]{:S(2)}, u32[]{:S(2)}) %collective-permute-start.7) | collective-permute-done | bytes 110624 | tf_op jit(solution)/shard_map/ppermute | solution.py:544
  33.5 1.6 shard_map.180
  36.4 4.1 %all-to-all-start = ((f32[32,1,2640]{2,1,0:T(1,128)}), f32[32,1,2640]{2,1,0:T(1,128)}, u32[]{:S(2)}, u32[]{:S(2)}) async-start(f32[32,1,2640]{2,1,0:T(1,128)} %copy.22), calls=%async_computation | async-start | bytes 688128 | tf_op jit(solution)/shard_map/all_to_all | solution.py:784
  44.7 6.3 %collective-permute-done.10.refs_3_ = bf16[4,24,1152]{2,1,0:T(8,128)(2,1)S(1)} collective-permute-done((bf16[4,24,1152]{2,1,0:T(8,128)(2,1)S(1)}, bf16[4,24,1152]{2,1,0:T(8,128)(2,1)S(1)}, u32[]{:S(2)}, u32[]{:S(2)}) %collective-permute-start.10) | collective-permute-done | bytes 221216 | tf_op jit(solution)/shard_map/ppermute | solution.py:544
  51.0 1.4 collective-permute-start.13
  52.4 3.3 %collective-permute-done.15.refs_2_ = bf16[4,24,1152]{2,1,0:T(8,128)(2,1)} collective-permute-done((bf16[4,24,1152]{2,1,0:T(8,128)(2,1)}, bf16[4,24,1152]{2,1,0:T(8,128)(2,1)}, u32[]{:S(2)}, u32[]{:S(2)}) %collective-permute-start.15) | collective-permute-done | bytes 221216 | tf_op jit(solution)/shard_map/ppermute | solution.py:544
  57.2 3.3 %collective-permute-done.11.refs_4_ = bf16[4,24,1152]{2,1,0:T(8,128)(2,1)S(1)} collective-permute-done((bf16[4,24,1152]{2,1,0:T(8,128)(2,1)S(1)}, bf16[4,24,1152]{2,1,0:T(8,128)(2,1)S(1)}, u32[]{:S(2)}, u32[]{:S(2)}) %collective-permute-start.11) | collective-permute-done | bytes 221216 | tf_op jit(solution)/shard_map/ppermute | solution.py:544
  60.5 1.4 collective-permute-start.20
  66.8 3.3 %collective-permute-done.17.refs_4_ = bf16[4,24,1152]{2,1,0:T(8,128)(2,1)} collective-permute-done((bf16[4,24,1152]{2,1,0:T(8,128)(2,1)}, bf16[4,24,1152]{2,1,0:T(8,128)(2,1)}, u32[]{:S(2)}, u32[]{:S(2)}) %collective-permute-start.17) | collective-permute-done | bytes 221216 | tf_op jit(solution)/shard_map/ppermute | solution.py:544
  70.1 3.1 %shard_map.183 = bf16[4,2,2,24,2304]{4,3,2,1,0:T(8,128)(2,1)} custom-call(s32[3]{0:T(128)S(1)} %pad_add_fusion.refs_0_, bf16[4,24,1152]{2,1,0:T(8,128)(2,1)} %get-tuple-element.87.refs_1_, bf16[4,24,1152]{2,1,0:T(8,128)(2,1)} %collective-permute-done.15.refs_2_, bf16[4,24,1152]{2,1,0:T(8,128)(2,1)} %collective-permute-done.16.refs_3_, ...), custom_call_target="tpu_custom_call" | custom-call | bytes 5308416 | tf_op jit(solution)/shard_map/pallas_call | solution.py:519
  75.6 5.6 %shard_map.182 = (bf16[256,384]{1,0:T(8,128)(2,1)S(1)}, f32[1,2304]{1,0:T(1,128)S(1)}, bf16[256,1152]{1,0:T(8,128)(2,1)S(1)}, bf16[256,384]{1,0:T(8,128)(2,1)S(1...) custom-call(s32[1]{0:T(128)} %bitcast.refs_0_, ...), custom_call_target="tpu_custom_call" | custom-call | flops 1006632960 | bytes 5308416 | tf_op jit(solution)/shard_map/pallas_call | solution.py:352
  81.3 12.7 %shard_map.184 = (bf16[256,384]{1,0:T(8,128)(2,1)S(1)}, bf16[256,384]{1,0:T(8,128)(2,1)S(1)}, f32[1,2304]{1,0:T(1,128)S(1)}, f32[16,336]{1,0:T(8,128)S(1)}, bf16...) custom-call(s32[1]{0:T(128)} %bitcast.refs_0_, bf16[256,384]{1,0:T(8,128)(2,1)S(1)} %get-tuple-element.77.refs_1_, ...), custom_call_target="tpu_custom_call" | custom-call | flops 3019898880 | bytes 10616832 | tf_op jit(solution)/shard_map/pallas_call | solution.py:352
  94.0 7.6 %shard_map.185 = (bf16[256,384]{1,0:T(8,128)(2,1)S(1)}, f32[1,2304]{1,0:T(1,128)S(1)}, f32[16,336]{1,0:T(8,128)S(1)}, bf16[384,2304]{1,0:T(8,128)(2,1)S(1)}, bf16[384,2304]{1,0:T(8,128)(2,1)}) custom-call(s32[1]{0:T(128)} %bitcast.refs_0_, bf16[256,384]{1,0:T(8,128)(2,1)S(1)} %get-tuple-element.140.refs_1_, f32[1,2304]{1,0:T(1,128)S(1)} %get-tuple-element.78.refs_2_, ...), custom_call_target="tpu_custom_call" | custom-call | flops 2013265920 | bytes 10616832 | tf_op jit(solution)/shard_map/pallas_call | solution.py:352
  101.8 1.7 shard_map.186
  106.4 1.5 copy-done.2
  107.9 1.7 shard_map.187
  113.7 6.0 %all-to-all-start.1 = ((f32[32,1,2640]{2,1,0:T(1,128)}), f32[32,1,2640]{2,1,0:T(1,128)}, u32[]{:S(2)}, u32[]{:S(2)}) async-start(f32[32,1,2640]{2,1,0:T(1,128)} %broadcast_in_dim.65), calls=%async_computation.1 | async-start | bytes 688128 | tf_op jit(solution)/shard_map/all_to_all | solution.py:857
  124.6 9.8 %collective-permute-done.28.refs_2_ = bf16[4,24,1152]{2,1,0:T(8,128)(2,1)S(1)} collective-permute-done((bf16[4,24,1152]{2,1,0:T(8,128)(2,1)S(1)}, bf16[4,24,1152]{2,1,0:T(8,128)(2,1)S(1)}, u32[]{:S(2)}, u32[]{:S(2)}) %collective-permute-start.28) | collective-permute-done | bytes 221216 | tf_op jit(solution)/shard_map/ppermute | solution.py:544
  144.6 7.0 %all-to-all-start.2 = ((f32[32,1,768]{2,1,0:T(1,128)}), f32[32,1,768]{2,1,0:T(1,128)S(1)}, u32[]{:S(2)}, u32[]{:S(2)}) async-start(f32[32,1,768]{2,1,0:T(1,128)} %broadcast_in_dim.67), calls=%async_computation.2 | async-start | bytes 196608 | tf_op jit(solution)/shard_map/all_to_all | solution.py:866
  151.6 1.6 maximum_select_fusion
  155.1 2.1 %collective-permute-start.35 = (bf16[24,2304]{1,0:T(8,128)(2,1)S(1)}, bf16[24,2304]{1,0:T(8,128)(2,1)S(1)}, u32[]{:S(2)}, u32[]{:S(2)}) collective-permute-start(bf16[24,2304]{1,0:T(8,128)(2,1)S(1)} %copy-done.20), channel_id=1, source_target_pairs={{0,8},{1,9},{2,10},{3,11},{4,12},{5,13},{6,14},{7,15},{8,0},{9,1},... | collective-permute-start | bytes 331784 | tf_op jit(solution)/shard_map/ppermute | solution.py:544
  158.4 6.4 %collective-permute-done.35.refs_6_.refs_7_ = bf16[24,2304]{1,0:T(8,128)(2,1)S(1)} collective-permute-done((bf16[24,2304]{1,0:T(8,128)(2,1)S(1)}, bf16[24,2304]{1,0:T(8,128)(2,1)S(1)}, u32[]{:S(2)}, u32[]{:S(2)}) %collective-permute-start.35) | collective-permute-done | bytes 110624 | tf_op jit(solution)/shard_map/ppermute | solution.py:544
  165.5 3.2 %collective-permute-start.38 = (bf16[24,2304]{1,0:T(8,128)(2,1)S(1)}, bf16[24,2304]{1,0:T(8,128)(2,1)S(1)}, u32[]{:S(2)}, u32[]{:S(2)}) collective-permute-start(bf16[24,2304]{1,0:T(8,128)(2,1)S(1)} %get-tuple-element.125), channel_id=1, source_target_pairs={{0,8},{1,9},{2,10},{3,11},{4,12},{5,13},{6,14},{7,15},{8,0},{9,1},... | collective-permute-start | bytes 331784 | tf_op jit(solution)/shard_map/ppermute | solution.py:544
  168.7 1.4 collective-permute-start.39
  172.7 2.2 %fusion.5 = f32[1000,384]{1,0:T(8,128)} fusion(s32[32]{0:T(128)S(1)} %eq.24, f32[32,384]{1,0:T(8,128)S(1)} %copy-done.28, f32[32,384]{1,0:T(8,128)S(1)} %reshape.76), kind=kOutput, calls=%fused_computation.27 | convolution fusion | flops 147598592 | bytes 1634432 | tf_op jit(solution)/shard_map/dot_general | solution.py:912
  176.2 3.0 %collective-permute-done.39.refs_4_ = bf16[24,2304]{1,0:T(8,128)(2,1)S(1)} collective-permute-done((bf16[24,2304]{1,0:T(8,128)(2,1)S(1)}, bf16[24,2304]{1,0:T(8,128)(2,1)S(1)}, u32[]{:S(2)}, u32[]{:S(2)}) %collective-permute-start.39) | collective-permute-done | bytes 110624 | tf_op jit(solution)/shard_map/ppermute | solution.py:544
  (185 shorter events, 57.5 us)
Async XLA Ops:
  4.2 18.3 %collective-permute-start = (bf16[2,128,384]{2,1,0:T(8,128)(2,1)S(1)}, bf16[2,128,384]{2,1,0:T(8,128)(2,1)S(1)}, u32[]{:S(2)}, u32[]{:S(2)}) collective-permute-start(bf16[2,128,384]{2,1,0:T(8,128)(2,1)S(1)} %get-tuple-element.142), channel_id=1, source_target_pairs={{0,1},{1,0},{2,3},{3,2},{4,5},{5,4},{6,7},{7,6},{8,9},{9,8},{10,11... | collective-permute-start | bytes 589832 | tf_op jit(solution)/shard_map/ppermute | solution.py:540
  8.5 10.6 %collective-permute-start.4 = (bf16[24,2304]{1,0:T(8,128)(2,1)S(1)}, bf16[24,2304]{1,0:T(8,128)(2,1)S(1)}, u32[]{:S(2)}, u32[]{:S(2)}) collective-permute-start(bf16[24,2304]{1,0:T(8,128)(2,1)S(1)} %get-tuple-element.146.refs_1_), channel_id=1, source_target_pairs={{0,12},{1,13},{2,14},{3,15},{4,0},{5,1},{6,2},{7,3},{8,4},{9,5},{1... | collective-permute-start | bytes 331784 | tf_op jit(solution)/shard_map/ppermute | solution.py:544
  20.0 13.5 %collective-permute-start.8 = (bf16[4,24,1152]{2,1,0:T(8,128)(2,1)S(1)}, bf16[4,24,1152]{2,1,0:T(8,128)(2,1)S(1)}, u32[]{:S(2)}, u32[]{:S(2)}) collective-permute-start(bf16[4,24,1152]{2,1,0:T(8,128)(2,1)S(1)} %get-tuple-element.74.refs_1_), channel_id=1, source_target_pairs={{0,2},{1,3},{2,0},{3,1},{4,6},{5,7},{6,4},{7,5},{8,10},{9,11},{10,... | collective-permute-start | bytes 663560 | tf_op jit(solution)/shard_map/ppermute | solution.py:544
  21.3 12.2 %collective-permute-start.9 = (bf16[4,24,1152]{2,1,0:T(8,128)(2,1)S(1)}, bf16[4,24,1152]{2,1,0:T(8,128)(2,1)S(1)}, u32[]{:S(2)}, u32[]{:S(2)}) collective-permute-start(bf16[4,24,1152]{2,1,0:T(8,128)(2,1)S(1)} %get-tuple-element.75.refs_5_), channel_id=1, source_target_pairs={{0,1},{1,0},{2,3},{3,2},{4,5},{5,4},{6,7},{7,6},{8,9},{9,8},{10,11... | collective-permute-start | bytes 663560 | tf_op jit(solution)/shard_map/ppermute | solution.py:544
  22.5 11.0 %collective-permute-start.7 = (bf16[24,2304]{1,0:T(8,128)(2,1)S(1)}, bf16[24,2304]{1,0:T(8,128)(2,1)S(1)}, u32[]{:S(2)}, u32[]{:S(2)}) collective-permute-start(bf16[24,2304]{1,0:T(8,128)(2,1)S(1)} %get-tuple-element.73.refs_1_), channel_id=1, source_target_pairs={{0,12},{1,13},{2,14},{3,15},{4,0},{5,1},{6,2},{7,3},{8,4},{9,5},{1... | collective-permute-start | bytes 331784 | tf_op jit(solution)/shard_map/ppermute | solution.py:544
  36.4 29.4 %all-to-all-start = ((f32[32,1,2640]{2,1,0:T(1,128)}), f32[32,1,2640]{2,1,0:T(1,128)}, u32[]{:S(2)}, u32[]{:S(2)}) async-start(f32[32,1,2640]{2,1,0:T(1,128)} %copy.22), calls=%async_computation | async-start | bytes 688128 | tf_op jit(solution)/shard_map/all_to_all | solution.py:784
  40.5 10.5 %collective-permute-start.10 = (bf16[4,24,1152]{2,1,0:T(8,128)(2,1)S(1)}, bf16[4,24,1152]{2,1,0:T(8,128)(2,1)S(1)}, u32[]{:S(2)}, u32[]{:S(2)}) collective-permute-start(bf16[4,24,1152]{2,1,0:T(8,128)(2,1)S(1)} %get-tuple-element.74.refs_1_), channel_id=1, source_target_pairs={{0,1},{1,0},{2,3},{3,2},{4,5},{5,4},{6,7},{7,6},{8,9},{9,8},{10,11... | collective-permute-start | bytes 663560 | tf_op jit(solution)/shard_map/ppermute | solution.py:544
  41.8 10.6 %collective-permute-start.12 = (bf16[4,24,1152]{2,1,0:T(8,128)(2,1)S(1)}, bf16[4,24,1152]{2,1,0:T(8,128)(2,1)S(1)}, u32[]{:S(2)}, u32[]{:S(2)}) collective-permute-start(bf16[4,24,1152]{2,1,0:T(8,128)(2,1)S(1)} %get-tuple-element.75.refs_5_), channel_id=1, source_target_pairs={{0,2},{1,3},{2,0},{3,1},{4,6},{5,7},{6,4},{7,5},{8,10},{9,11},{10,... | collective-permute-start | bytes 663560 | tf_op jit(solution)/shard_map/ppermute | solution.py:544
  43.0 12.8 %collective-permute-start.15 = (bf16[4,24,1152]{2,1,0:T(8,128)(2,1)}, bf16[4,24,1152]{2,1,0:T(8,128)(2,1)}, u32[]{:S(2)}, u32[]{:S(2)}) collective-permute-start(bf16[4,24,1152]{2,1,0:T(8,128)(2,1)} %get-tuple-element.87.refs_1_), channel_id=1, source_target_pairs={{0,2},{1,3},{2,0},{3,1},{4,6},{5,7},{6,4},{7,5},{8,10},{9,11},{10,... | collective-permute-start | bytes 663560 | tf_op jit(solution)/shard_map/ppermute | solution.py:544
  43.3 13.3 %collective-permute-start.19 = (bf16[4,24,1152]{2,1,0:T(8,128)(2,1)}, bf16[4,24,1152]{2,1,0:T(8,128)(2,1)}, u32[]{:S(2)}, u32[]{:S(2)}) collective-permute-start(bf16[4,24,1152]{2,1,0:T(8,128)(2,1)} %get-tuple-element.88.refs_5_), channel_id=1, source_target_pairs={{0,1},{1,0},{2,3},{3,2},{4,5},{5,4},{6,7},{7,6},{8,9},{9,8},{10,11... | collective-permute-start | bytes 663560 | tf_op jit(solution)/shard_map/ppermute | solution.py:544
  43.5 17.0 %collective-permute-start.11 = (bf16[4,24,1152]{2,1,0:T(8,128)(2,1)S(1)}, bf16[4,24,1152]{2,1,0:T(8,128)(2,1)S(1)}, u32[]{:S(2)}, u32[]{:S(2)}) collective-permute-start(bf16[4,24,1152]{2,1,0:T(8,128)(2,1)S(1)} %collective-permute-done.8.refs_7_.refs_2_), channel_id=1, source_target_pairs={{0,1},{1,0},{2,3},{3,2},{4,5},{5,4},{6,7},{7,6},{8,9},{9,8},{10,11... | collective-permute-start | bytes 663560 | tf_op jit(solution)/shard_map/ppermute | solution.py:544
  51.0 10.9 %collective-permute-start.13 = (bf16[4,24,1152]{2,1,0:T(8,128)(2,1)S(1)}, bf16[4,24,1152]{2,1,0:T(8,128)(2,1)S(1)}, u32[]{:S(2)}, u32[]{:S(2)}) collective-permute-start(bf16[4,24,1152]{2,1,0:T(8,128)(2,1)S(1)} %collective-permute-done.9.refs_8_.refs_7_), channel_id=1, source_target_pairs={{0,2},{1,3},{2,0},{3,1},{4,6},{5,7},{6,4},{7,5},{8,10},{9,11},{10,... | collective-permute-start | bytes 663560 | tf_op jit(solution)/shard_map/ppermute | solution.py:544
  52.4 14.4 %collective-permute-start.16 = (bf16[4,24,1152]{2,1,0:T(8,128)(2,1)}, bf16[4,24,1152]{2,1,0:T(8,128)(2,1)}, u32[]{:S(2)}, u32[]{:S(2)}) collective-permute-start(bf16[4,24,1152]{2,1,0:T(8,128)(2,1)} %get-tuple-element.87.refs_1_), channel_id=1, source_target_pairs={{0,1},{1,0},{2,3},{3,2},{4,5},{5,4},{6,7},{7,6},{8,9},{9,8},{10,11... | collective-permute-start | bytes 663560 | tf_op jit(solution)/shard_map/ppermute | solution.py:544
  55.7 11.0 %collective-permute-start.18 = (bf16[4,24,1152]{2,1,0:T(8,128)(2,1)}, bf16[4,24,1152]{2,1,0:T(8,128)(2,1)}, u32[]{:S(2)}, u32[]{:S(2)}) collective-permute-start(bf16[4,24,1152]{2,1,0:T(8,128)(2,1)} %get-tuple-element.88.refs_5_), channel_id=1, source_target_pairs={{0,2},{1,3},{2,0},{3,1},{4,6},{5,7},{6,4},{7,5},{8,10},{9,11},{10,... | collective-permute-start | bytes 663560 | tf_op jit(solution)/shard_map/ppermute | solution.py:544
  56.6 13.5 %collective-permute-start.17 = (bf16[4,24,1152]{2,1,0:T(8,128)(2,1)}, bf16[4,24,1152]{2,1,0:T(8,128)(2,1)}, u32[]{:S(2)}, u32[]{:S(2)}) collective-permute-start(bf16[4,24,1152]{2,1,0:T(8,128)(2,1)} %collective-permute-done.15.refs_2_), channel_id=1, source_target_pairs={{0,1},{1,0},{2,3},{3,2},{4,5},{5,4},{6,7},{7,6},{8,9},{9,8},{10,11... | collective-permute-start | bytes 663560 | tf_op jit(solution)/shard_map/ppermute | solution.py:544
  64.6 11.0 %collective-permute-start.14 = (bf16[384,2304]{1,0:T(8,128)(2,1)S(1)}, bf16[384,2304]{1,0:T(8,128)(2,1)}, u32[]{:S(2)}, u32[]{:S(2)}) collective-permute-start(bf16[384,2304]{1,0:T(8,128)(2,1)S(1)} %bitcast.59), channel_id=1, source_target_pairs={{0,16},{16,0},{1,17},{17,1},{2,18},{18,2},{3,19},{19,3},{4,20},{20... | collective-permute-start | bytes 5308424 | tf_op jit(solution)/shard_map/ppermute | solution.py:540
  104.2 15.4 %collective-permute-start.26 = (bf16[4,2,24,1152]{3,2,1,0:T(8,128)(2,1)}, bf16[4,2,24,1152]{3,2,1,0:T(8,128)(2,1)}, u32[]{:S(2)}, u32[]{:S(2)}) collective-permute-start(bf16[4,2,24,1152]{3,2,1,0:T(8,128)(2,1)} %get-tuple-element.102), channel_id=1, source_target_pairs={{0,2},{1,3},{2,0},{3,1},{4,6},{5,7},{6,4},{7,5},{8,10},{9,11},{10,... | collective-permute-start | bytes 1327112 | tf_op jit(solution)/shard_map/ppermute | solution.py:544
  105.2 14.5 %collective-permute-start.27 = (bf16[4,2,24,1152]{3,2,1,0:T(8,128)(2,1)}, bf16[4,2,24,1152]{3,2,1,0:T(8,128)(2,1)}, u32[]{:S(2)}, u32[]{:S(2)}) collective-permute-start(bf16[4,2,24,1152]{3,2,1,0:T(8,128)(2,1)} %get-tuple-element.104), channel_id=1, source_target_pairs={{0,1},{1,0},{2,3},{3,2},{4,5},{5,4},{6,7},{7,6},{8,9},{9,8},{10,11... | collective-permute-start | bytes 1327112 | tf_op jit(solution)/shard_map/ppermute | solution.py:544
  111.1 23.9 %collective-permute-start.24 = (bf16[4,2,24,1152]{3,2,1,0:T(8,128)(2,1)}, bf16[4,2,24,1152]{3,2,1,0:T(8,128)(2,1)S(1)}, u32[]{:S(2)}, u32[]{:S(2)}) collective-permute-start(bf16[4,2,24,1152]{3,2,1,0:T(8,128)(2,1)} %get-tuple-element.98), channel_id=1, source_target_pairs={{0,2},{1,3},{2,0},{3,1},{4,6},{5,7},{6,4},{7,5},{8,10},{9,11},{10,... | collective-permute-start | bytes 1327112 | tf_op jit(solution)/shard_map/ppermute | solution.py:544
  112.1 22.9 %collective-permute-start.25 = (bf16[4,2,24,1152]{3,2,1,0:T(8,128)(2,1)}, bf16[4,2,24,1152]{3,2,1,0:T(8,128)(2,1)S(1)}, u32[]{:S(2)}, u32[]{:S(2)}) collective-permute-start(bf16[4,2,24,1152]{3,2,1,0:T(8,128)(2,1)} %get-tuple-element.100), channel_id=1, source_target_pairs={{0,1},{1,0},{2,3},{3,2},{4,5},{5,4},{6,7},{7,6},{8,9},{9,8},{10,11... | collective-permute-start | bytes 1327112 | tf_op jit(solution)/shard_map/ppermute | solution.py:544
  113.7 25.0 %all-to-all-start.1 = ((f32[32,1,2640]{2,1,0:T(1,128)}), f32[32,1,2640]{2,1,0:T(1,128)}, u32[]{:S(2)}, u32[]{:S(2)}) async-start(f32[32,1,2640]{2,1,0:T(1,128)} %broadcast_in_dim.65), calls=%async_computation.1 | async-start | bytes 688128 | tf_op jit(solution)/shard_map/all_to_all | solution.py:857
  122.1 12.2 %collective-permute-start.28 = (bf16[4,24,1152]{2,1,0:T(8,128)(2,1)S(1)}, bf16[4,24,1152]{2,1,0:T(8,128)(2,1)S(1)}, u32[]{:S(2)}, u32[]{:S(2)}) collective-permute-start(bf16[4,24,1152]{2,1,0:T(8,128)(2,1)S(1)} %get-tuple-element.106), channel_id=1, source_target_pairs={{0,1},{1,0},{2,3},{3,2},{4,5},{5,4},{6,7},{7,6},{8,9},{9,8},{10,11... | collective-permute-start | bytes 663560 | tf_op jit(solution)/shard_map/ppermute | solution.py:544
  123.4 11.0 %collective-permute-start.29 = (bf16[4,24,1152]{2,1,0:T(8,128)(2,1)S(1)}, bf16[4,24,1152]{2,1,0:T(8,128)(2,1)S(1)}, u32[]{:S(2)}, u32[]{:S(2)}) collective-permute-start(bf16[4,24,1152]{2,1,0:T(8,128)(2,1)S(1)} %get-tuple-element.108), channel_id=1, source_target_pairs={{0,2},{1,3},{2,0},{3,1},{4,6},{5,7},{6,4},{7,5},{8,10},{9,11},{10,... | collective-permute-start | bytes 663560 | tf_op jit(solution)/shard_map/ppermute | solution.py:544
  138.3 13.4 %collective-permute-start.30 = (bf16[4,1,128,384]{3,2,1,0:T(8,128)(2,1)S(1)}, bf16[4,1,128,384]{3,2,1,0:T(8,128)(2,1)}, u32[]{:S(2)}, u32[]{:S(2)}) collective-permute-start(bf16[4,1,128,384]{3,2,1,0:T(8,128)(2,1)S(1)} %get-tuple-element.138), channel_id=1, source_target_pairs={{0,1},{1,0},{2,3},{3,2},{4,5},{5,4},{6,7},{7,6},{8,9},{9,8},{10,11... | collective-permute-start | bytes 1179656 | tf_op jit(solution)/shard_map/ppermute | solution.py:540
  141.2 23.6 %collective-permute-start.33 = (bf16[4,24,1152]{2,1,0:T(8,128)(2,1)}, bf16[4,24,1152]{2,1,0:T(8,128)(2,1)S(1)}, u32[]{:S(2)}, u32[]{:S(2)}) collective-permute-start(bf16[4,24,1152]{2,1,0:T(8,128)(2,1)} %copy-done.18), channel_id=1, source_target_pairs={{0,1},{1,0},{2,3},{3,2},{4,5},{5,4},{6,7},{7,6},{8,9},{9,8},{10,11... | collective-permute-start | bytes 663560 | tf_op jit(solution)/shard_map/ppermute | solution.py:544
  142.2 22.6 %collective-permute-start.34 = (bf16[4,24,1152]{2,1,0:T(8,128)(2,1)}, bf16[4,24,1152]{2,1,0:T(8,128)(2,1)S(1)}, u32[]{:S(2)}, u32[]{:S(2)}) collective-permute-start(bf16[4,24,1152]{2,1,0:T(8,128)(2,1)} %copy-done.17), channel_id=1, source_target_pairs={{0,2},{1,3},{2,0},{3,1},{4,6},{5,7},{6,4},{7,5},{8,10},{9,11},{10,... | collective-permute-start | bytes 663560 | tf_op jit(solution)/shard_map/ppermute | solution.py:544
  144.6 25.5 %all-to-all-start.2 = ((f32[32,1,768]{2,1,0:T(1,128)}), f32[32,1,768]{2,1,0:T(1,128)S(1)}, u32[]{:S(2)}, u32[]{:S(2)}) async-start(f32[32,1,768]{2,1,0:T(1,128)} %broadcast_in_dim.67), calls=%async_computation.2 | async-start | bytes 196608 | tf_op jit(solution)/shard_map/all_to_all | solution.py:866
  154.2 20.8 %collective-permute-start.31 = (bf16[2,2,128,384]{3,2,1,0:T(8,128)(2,1)}, bf16[2,2,128,384]{3,2,1,0:T(8,128)(2,1)}, u32[]{:S(2)}, u32[]{:S(2)}) collective-permute-start(bf16[2,2,128,384]{3,2,1,0:T(8,128)(2,1)} %get-tuple-element.136), channel_id=1, source_target_pairs={{0,16},{16,0},{1,17},{17,1},{2,18},{18,2},{3,19},{19,3},{4,20},{20... | collective-permute-start | bytes 1179656 | tf_op jit(solution)/shard_map/ppermute | solution.py:540
  155.1 9.7 %collective-permute-start.35 = (bf16[24,2304]{1,0:T(8,128)(2,1)S(1)}, bf16[24,2304]{1,0:T(8,128)(2,1)S(1)}, u32[]{:S(2)}, u32[]{:S(2)}) collective-permute-start(bf16[24,2304]{1,0:T(8,128)(2,1)S(1)} %copy-done.20), channel_id=1, source_target_pairs={{0,8},{1,9},{2,10},{3,11},{4,12},{5,13},{6,14},{7,15},{8,0},{9,1},... | collective-permute-start | bytes 331784 | tf_op jit(solution)/shard_map/ppermute | solution.py:544
  165.5 10.8 %collective-permute-start.37 = (bf16[24,2304]{1,0:T(8,128)(2,1)S(1)}, bf16[24,2304]{1,0:T(8,128)(2,1)S(1)}, u32[]{:S(2)}, u32[]{:S(2)}) collective-permute-start(bf16[24,2304]{1,0:T(8,128)(2,1)S(1)} %get-tuple-element.124), channel_id=1, source_target_pairs={{0,4},{1,5},{2,6},{3,7},{4,8},{5,9},{6,10},{7,11},{8,12},{9,13},{1... | collective-permute-start | bytes 331784 | tf_op jit(solution)/shard_map/ppermute | solution.py:544
  165.5 10.7 %collective-permute-start.38 = (bf16[24,2304]{1,0:T(8,128)(2,1)S(1)}, bf16[24,2304]{1,0:T(8,128)(2,1)S(1)}, u32[]{:S(2)}, u32[]{:S(2)}) collective-permute-start(bf16[24,2304]{1,0:T(8,128)(2,1)S(1)} %get-tuple-element.125), channel_id=1, source_target_pairs={{0,8},{1,9},{2,10},{3,11},{4,12},{5,13},{6,14},{7,15},{8,0},{9,1},... | collective-permute-start | bytes 331784 | tf_op jit(solution)/shard_map/ppermute | solution.py:544
  168.7 10.6 %collective-permute-start.39 = (bf16[24,2304]{1,0:T(8,128)(2,1)S(1)}, bf16[24,2304]{1,0:T(8,128)(2,1)S(1)}, u32[]{:S(2)}, u32[]{:S(2)}) collective-permute-start(bf16[24,2304]{1,0:T(8,128)(2,1)S(1)} %get-tuple-element.126), channel_id=1, source_target_pairs={{0,12},{1,13},{2,14},{3,15},{4,0},{5,1},{6,2},{7,3},{8,4},{9,5},{1... | collective-permute-start | bytes 331784 | tf_op jit(solution)/shard_map/ppermute | solution.py:544
  (45 other events, 316.1 us)

commit v14 on v12

--- a/solution.py
+++ b/solution.py
@@ -153,13 +153,14 @@
 
         at = 6 * width
         arrivals[0].wait()
-        qkv_s[:, :width] = low(matmul(hidden_one, att_w[:, :width]) + bias(at, at + width))
+        queries = low(matmul(hidden_one, att_w[:, :width]) + bias(at, at + width))
+        qkv_s[:, :width] = low(queries.astype(jnp.float32) * SCALE)
         qkv_s[:, width : 2 * width] = low(matmul(hidden_one, att_w[:, width : 2 * width]))
         qkv_s[:, 2 * width :] = low(
             matmul(hidden_one, att_w[:, 2 * width :]) + bias(at + width, at + 2 * width)
         )
         for head in range(HEADS):
-            scores = matmul_transposed(part(qkv_s, 0, head), part(qkv_s, 1, head)) * SCALE
+            scores = matmul_transposed(part(qkv_s, 0, head), part(qkv_s, 1, head))
             raised = jnp.exp(scores - jnp.max(scores, axis=-1, keepdims=True))
             soft = raised * (1.0 / jnp.sum(raised, axis=-1, keepdims=True))
             soft_s[head] = soft
@@ -186,10 +187,10 @@
                 1.0 + (3.0 * CUBE) * square
             )
         arrivals[4].wait()
-        block_s[...] = down_p[...].astype(jnp.float32)
+        packed = down_p[...].astype(jnp.float32)
         for d in range(ring_size):
             for j in range(ratio):
-                down_s[(d * ratio + j) * rows : (d * ratio + j + 1) * rows, :] = block_s[
+                down_s[(d * ratio + j) * rows : (d * ratio + j + 1) * rows, :] = packed[
                     d * rows : (d + 1) * rows, j * width : (j + 1) * width
                 ]
         down_w[...] = low(down_s[...])
@@ -214,10 +215,10 @@
         )
     halves[0, :, 4 * width :] = low(outer_sum(hidden_two, da_s[:, :split]) * share)
     halves[1, :, : hidden - split] = low(outer_sum(hidden_two, da_s[:, split:]) * share)
-    down_s[...] = outer_sum(u_s[...], grad_branch) * share
+    down_grad = outer_sum(u_s[...], grad_branch) * share
     for d in range(ring_size):
         for j in range(ratio):
-            block_s[d * rows : (d + 1) * rows, j * width : (j + 1) * width] = down_s[
+            block_s[d * rows : (d + 1) * rows, j * width : (j + 1) * width] = down_grad[
                 (d * ratio + j) * rows : (d * ratio + j + 1) * rows, :
             ]
     halves[1, :, hidden - split :] = low(block_s[...])
@@ -258,7 +259,7 @@
         grad_scores = low(soft * (grad_soft - inner))
         grads = (
             matmul(grad_scores, part(qkv_s, 1, head)) * SCALE,
-            outer_sum(grad_scores, part(qkv_s, 0, head)) * SCALE,
+            outer_sum(grad_scores, part(qkv_s, 0, head)),
             outer_sum(low(soft), grad_head),
         )
         for member, grad in enumerate(grads):

time: 177 us -> 177 us (level)
  no operation moved by 1% of the time
where the time goes in v14:
time: 177 us; the launch traced here: 176 us
  starting transfers between devices  56.2 us (32%)
  waiting for transfers between devices  46.3 us (26%)
  Pallas kernels  41.5 us (23%)
  local copies, waits for them, and re-layouts  17.8 us (10%)
  other arithmetic  7.31 us (4%)
  matrix products  4.65 us (3%)
  between operations  2 us (1%)
    ppermute x32, waiting for transfers between devices, ring_exchange(): return lax.ppermute(block, RING, [(i, step(i)) for i in range(size)])  41.6 us
    ppermute x32, starting transfers between devices, ring_exchange(): return lax.ppermute(block, RING, [(i, step(i)) for i in range(size)])  29.1 us
    pallas_call x3, Pallas kernels, run_section(): pl.pallas_call(partial(section_kernel, layout, forward, backward, len(aft...  26 us
    pallas_call x14, Pallas kernels, in_memory(): pl.pallas_call(body, out_shape=shapes, in_specs=specs, out_specs=[pl.Bloc...  15.5 us
    unnamed x80, local copies, waits for them, and re-layouts  11 us
    all_to_all x1, starting transfers between devices, per_device(): lax.all_to_all(columns, ('section', 'dp', 'seq'), 0, 0, tiled=True)  7.85 us
    ppermute x9, starting transfers between devices, pair_swap(): return lax.ppermute(block, axis, [(0, 1), (1, 0)])  7.43 us
    all_to_all x1, starting transfers between devices, per_device(): lax.all_to_all(rows_back[:, None], ('section', 'dp', 'seq'), 0, 0, tiled=...  6.68 us
  transfers between devices with their start and end apart: 44, of which 11 were waited for; matrix products, arithmetic and copies ran while one was open for 10% of the time, Pallas kernels for 15%

profile of v14, /device:TPU:9, one launch (start us, length us, event | category | flops | bytes accessed | tf_op | source)
XLA Modules:
  0.0 175.8 jit_solution(15924447158215222457)
XLA Ops:
  0.7 1.7 shard_map.178
  4.2 1.3 collective-permute-start
  6.7 1.3 collective-permute-start.2
  9.1 1.4 collective-permute-start.4
  11.1 6.2 %collective-permute-done.3.refs_3_ = bf16[24,2304]{1,0:T(8,128)(2,1)S(1)} collective-permute-done((bf16[24,2304]{1,0:T(8,128)(2,1)S(1)}, bf16[24,2304]{1,0:T(8,128)(2,1)S(1)}, u32[]{:S(2)}, u32[]{:S(2)}) %collective-permute-start.3) | collective-permute-done | bytes 110624 | tf_op jit(solution)/shard_map/ppermute | solution.py:545
  17.3 2.4 %collective-permute-done.4.refs_4_ = bf16[24,2304]{1,0:T(8,128)(2,1)S(1)} collective-permute-done((bf16[24,2304]{1,0:T(8,128)(2,1)S(1)}, bf16[24,2304]{1,0:T(8,128)(2,1)S(1)}, u32[]{:S(2)}, u32[]{:S(2)}) %collective-permute-start.4) | collective-permute-done | bytes 110624 | tf_op jit(solution)/shard_map/ppermute | solution.py:545
  24.4 2.9 %collective-permute-done.12.refs_2_ = bf16[24,2304]{1,0:T(8,128)(2,1)S(1)} collective-permute-done((bf16[24,2304]{1,0:T(8,128)(2,1)S(1)}, bf16[24,2304]{1,0:T(8,128)(2,1)S(1)}, u32[]{:S(2)}, u32[]{:S(2)}) %collective-permute-start.12) | collective-permute-done | bytes 110624 | tf_op jit(solution)/shard_map/ppermute | solution.py:545
  29.3 5.9 %collective-permute-done.14.refs_4_ = bf16[24,2304]{1,0:T(8,128)(2,1)S(1)} collective-permute-done((bf16[24,2304]{1,0:T(8,128)(2,1)S(1)}, bf16[24,2304]{1,0:T(8,128)(2,1)S(1)}, u32[]{:S(2)}, u32[]{:S(2)}) %collective-permute-start.14) | collective-permute-done | bytes 110624 | tf_op jit(solution)/shard_map/ppermute | solution.py:545
  39.5 7.7 %collective-permute-done.10.refs_8_ = bf16[4,24,1152]{2,1,0:T(8,128)(2,1)S(1)} collective-permute-done((bf16[4,24,1152]{2,1,0:T(8,128)(2,1)S(1)}, bf16[4,24,1152]{2,1,0:T(8,128)(2,1)S(1)}, u32[]{:S(2)}, u32[]{:S(2)}) %collective-permute-start.10) | collective-permute-done | bytes 221216 | tf_op jit(solution)/shard_map/ppermute | solution.py:545
  48.2 3.0 %collective-permute-start.11 = (bf16[384,2304]{1,0:T(8,128)(2,1)S(1)}, bf16[384,2304]{1,0:T(8,128)(2,1)}, u32[]{:S(2)}, u32[]{:S(2)}) collective-permute-start(bf16[384,2304]{1,0:T(8,128)(2,1)S(1)} %bitcast.59), channel_id=1, source_target_pairs={{0,16},{16,0},{1,17},{17,1},{2,18},{18,2},{3,19},{19,3},{4,20},{20... | collective-permute-start | bytes 5308424 | tf_op jit(solution)/shard_map/ppermute | solution.py:541
  53.8 5.1 %all-to-all-start = ((f32[32,1,2640]{2,1,0:T(1,128)}), f32[32,1,2640]{2,1,0:T(1,128)}, u32[]{:S(2)}, u32[]{:S(2)}) async-start(f32[32,1,2640]{2,1,0:T(1,128)} %copy.22), calls=%async_computation | async-start | bytes 688128 | tf_op jit(solution)/shard_map/all_to_all | solution.py:778
  59.0 2.9 %shard_map.183 = bf16[4,2,2,24,2304]{4,3,2,1,0:T(8,128)(2,1)} custom-call(s32[3]{0:T(128)S(1)} %pad_add_fusion.refs_0_, bf16[4,24,1152]{2,1,0:T(8,128)(2,1)S(1)} %get-tuple-element.87.refs_1_, bf16[4,24,1152]{2,1,0:T(8,128)(2,1)} %collective-permute-done.15.refs_2_, bf16[4,24,1152]{2,1,0:T(8,128)(2,1)} %collective-permute-done.16.refs_3_, ...), custom_call_target="tpu_custom_call" | custom-call | bytes 5308416 | tf_op jit(solution)/shard_map/pallas_call | solution.py:520
  64.8 4.7 %all-to-all-done = f32[32,1,2640]{2,1,0:T(1,128)} async-done(((f32[32,1,2640]{2,1,0:T(1,128)}), f32[32,1,2640]{2,1,0:T(1,128)}, u32[]{:S(2)}, u32[]{:S(2)}) %all-to-all-start) | async-done | bytes 337952 | tf_op jit(solution)/shard_map/all_to_all | solution.py:778
  70.5 5.7 %shard_map.181 = (bf16[256,384]{1,0:T(8,128)(2,1)S(1)}, f32[1,2304]{1,0:T(1,128)S(1)}, bf16[256,1152]{1,0:T(8,128)(2,1)S(1)}, bf16[256,384]{1,0:T(8,128)(2,1)S(1...) custom-call(s32[1]{0:T(128)} %bitcast.refs_0_, ...), custom_call_target="tpu_custom_call" | custom-call | flops 1006632960 | bytes 5308416 | tf_op jit(solution)/shard_map/pallas_call | solution.py:353
  76.3 12.7 %shard_map.184 = (bf16[256,384]{1,0:T(8,128)(2,1)S(1)}, bf16[256,384]{1,0:T(8,128)(2,1)S(1)}, f32[1,2304]{1,0:T(1,128)S(1)}, f32[16,336]{1,0:T(8,128)S(1)}, bf16...) custom-call(s32[1]{0:T(128)} %bitcast.refs_0_, bf16[256,384]{1,0:T(8,128)(2,1)S(1)} %get-tuple-element.76.refs_1_, ...), custom_call_target="tpu_custom_call" | custom-call | flops 3019898880 | bytes 10616832 | tf_op jit(solution)/shard_map/pallas_call | solution.py:353
  89.7 7.5 %shard_map.185 = (bf16[256,384]{1,0:T(8,128)(2,1)S(1)}, f32[1,2304]{1,0:T(1,128)S(1)}, f32[16,336]{1,0:T(8,128)S(1)}, bf16[384,2304]{1,0:T(8,128)(2,1)S(1)}, bf16[384,2304]{1,0:T(8,128)(2,1)}) custom-call(s32[1]{0:T(128)} %bitcast.refs_0_, bf16[256,384]{1,0:T(8,128)(2,1)S(1)} %get-tuple-element.140.refs_1_, f32[1,2304]{1,0:T(1,128)S(1)} %get-tuple-element.77.refs_2_, ...), custom_call_target="tpu_custom_call" | custom-call | flops 2013265920 | bytes 10616832 | tf_op jit(solution)/shard_map/pallas_call | solution.py:353
  97.4 1.7 shard_map.186
  102.2 1.5 copy-done.2
  104.4 1.7 shard_map.187
  110.0 6.7 %all-to-all-start.1 = ((f32[32,1,2640]{2,1,0:T(1,128)}), f32[32,1,2640]{2,1,0:T(1,128)}, u32[]{:S(2)}, u32[]{:S(2)}) async-start(f32[32,1,2640]{2,1,0:T(1,128)} %broadcast_in_dim.65), calls=%async_computation.1 | async-start | bytes 688128 | tf_op jit(solution)/shard_map/all_to_all | solution.py:855
  117.8 1.4 shard_map.188
  119.1 1.3 collective-permute-start.28
  121.6 8.5 %collective-permute-done.28.refs_2_ = bf16[4,24,1152]{2,1,0:T(8,128)(2,1)S(1)} collective-permute-done((bf16[4,24,1152]{2,1,0:T(8,128)(2,1)S(1)}, bf16[4,24,1152]{2,1,0:T(8,128)(2,1)S(1)}, u32[]{:S(2)}, u32[]{:S(2)}) %collective-permute-start.28) | collective-permute-done | bytes 221216 | tf_op jit(solution)/shard_map/ppermute | solution.py:545
  139.3 3.4 %collective-permute-start.35 = (bf16[24,2304]{1,0:T(8,128)(2,1)}, bf16[24,2304]{1,0:T(8,128)(2,1)S(1)}, u32[]{:S(2)}, u32[]{:S(2)}) collective-permute-start(bf16[24,2304]{1,0:T(8,128)(2,1)} %copy-done.25), channel_id=1, source_target_pairs={{0,8},{1,9},{2,10},{3,11},{4,12},{5,13},{6,14},{7,15},{8,0},{9,1},... | collective-permute-start | bytes 331784 | tf_op jit(solution)/shard_map/ppermute | solution.py:545
  142.7 1.4 collective-permute-start.36
  144.8 7.9 %all-to-all-start.2 = ((f32[32,1,768]{2,1,0:T(1,128)}), f32[32,1,768]{2,1,0:T(1,128)S(1)}, u32[]{:S(2)}, u32[]{:S(2)}) async-start(f32[32,1,768]{2,1,0:T(1,128)} %broadcast_in_dim.67), calls=%async_computation.2 | async-start | bytes 196608 | tf_op jit(solution)/shard_map/all_to_all | solution.py:864
  152.7 1.6 maximum_select_fusion
  159.2 1.4 collective-permute-start.39
  160.5 1.9 %convolution_bitcast_fusion = f32[1,24,2304]{2,1,0:T(8,128)} fusion(bf16[32,24]{1,0:T(8,128)(2,1)S(1)} %fusion.19.refs_6_, f32[32,2640]{1,0:T(8,128)} %bitcast.70), kind=kOutput, calls=%fused_computation | convolution fusion | flops 3538944 | bytes 370176 | tf_op jit(solution)/shard_map/dot_general | solution.py:30
  163.4 4.1 %collective-permute-done.38.refs_3_ = bf16[24,2304]{1,0:T(8,128)(2,1)S(1)} collective-permute-done((bf16[24,2304]{1,0:T(8,128)(2,1)S(1)}, bf16[24,2304]{1,0:T(8,128)(2,1)S(1)}, u32[]{:S(2)}, u32[]{:S(2)}) %collective-permute-start.38) | collective-permute-done | bytes 110624 | tf_op jit(solution)/shard_map/ppermute | solution.py:545
  167.5 2.2 %collective-permute-done.39.refs_4_ = bf16[24,2304]{1,0:T(8,128)(2,1)S(1)} collective-permute-done((bf16[24,2304]{1,0:T(8,128)(2,1)S(1)}, bf16[24,2304]{1,0:T(8,128)(2,1)S(1)}, u32[]{:S(2)}, u32[]{:S(2)}) %collective-permute-start.39) | collective-permute-done | bytes 110624 | tf_op jit(solution)/shard_map/ppermute | solution.py:545
  170.4 2.2 %fusion.5 = f32[1000,384]{1,0:T(8,128)} fusion(s32[32]{0:T(128)S(1)} %copy-done.35, f32[32,384]{1,0:T(8,128)S(1)} %copy-done.32, f32[32,384]{1,0:T(8,128)S(1)} %reshape.76), kind=kOutput, calls=%fused_computation.27 | convolution fusion | flops 147598592 | bytes 1634432 | tf_op jit(solution)/shard_map/dot_general | solution.py:910
  (197 shorter events, 52.8 us)
Async XLA Ops:
  4.2 19.2 %collective-permute-start = (bf16[2,128,384]{2,1,0:T(8,128)(2,1)S(1)}, bf16[2,128,384]{2,1,0:T(8,128)(2,1)S(1)}, u32[]{:S(2)}, u32[]{:S(2)}) collective-permute-start(bf16[2,128,384]{2,1,0:T(8,128)(2,1)S(1)} %get-tuple-element.142), channel_id=1, source_target_pairs={{0,1},{1,0},{2,3},{3,2},{4,5},{5,4},{6,7},{7,6},{8,9},{9,8},{10,11... | collective-permute-start | bytes 589832 | tf_op jit(solution)/shard_map/ppermute | solution.py:541
  8.0 9.3 %collective-permute-start.3 = (bf16[24,2304]{1,0:T(8,128)(2,1)S(1)}, bf16[24,2304]{1,0:T(8,128)(2,1)S(1)}, u32[]{:S(2)}, u32[]{:S(2)}) collective-permute-start(bf16[24,2304]{1,0:T(8,128)(2,1)S(1)} %get-tuple-element.146.refs_1_), channel_id=1, source_target_pairs={{0,8},{1,9},{2,10},{3,11},{4,12},{5,13},{6,14},{7,15},{8,0},{9,1},... | collective-permute-start | bytes 331784 | tf_op jit(solution)/shard_map/ppermute | solution.py:545
  9.1 10.6 %collective-permute-start.4 = (bf16[24,2304]{1,0:T(8,128)(2,1)S(1)}, bf16[24,2304]{1,0:T(8,128)(2,1)S(1)}, u32[]{:S(2)}, u32[]{:S(2)}) collective-permute-start(bf16[24,2304]{1,0:T(8,128)(2,1)S(1)} %get-tuple-element.146.refs_1_), channel_id=1, source_target_pairs={{0,12},{1,13},{2,14},{3,15},{4,0},{5,1},{6,2},{7,3},{8,4},{9,5},{1... | collective-permute-start | bytes 331784 | tf_op jit(solution)/shard_map/ppermute | solution.py:545
  20.7 14.5 %collective-permute-start.5 = (bf16[4,24,1152]{2,1,0:T(8,128)(2,1)S(1)}, bf16[4,24,1152]{2,1,0:T(8,128)(2,1)S(1)}, u32[]{:S(2)}, u32[]{:S(2)}) collective-permute-start(bf16[4,24,1152]{2,1,0:T(8,128)(2,1)S(1)} %get-tuple-element.74.refs_1_), channel_id=1, source_target_pairs={{0,2},{1,3},{2,0},{3,1},{4,6},{5,7},{6,4},{7,5},{8,10},{9,11},{10,... | collective-permute-start | bytes 663560 | tf_op jit(solution)/shard_map/ppermute | solution.py:545
  21.9 15.8 %collective-permute-start.6 = (bf16[4,24,1152]{2,1,0:T(8,128)(2,1)S(1)}, bf16[4,24,1152]{2,1,0:T(8,128)(2,1)S(1)}, u32[]{:S(2)}, u32[]{:S(2)}) collective-permute-start(bf16[4,24,1152]{2,1,0:T(8,128)(2,1)S(1)} %get-tuple-element.74.refs_1_), channel_id=1, source_target_pairs={{0,1},{1,0},{2,3},{3,2},{4,5},{5,4},{6,7},{7,6},{8,9},{9,8},{10,11... | collective-permute-start | bytes 663560 | tf_op jit(solution)/shard_map/ppermute | solution.py:545
  22.2 13.0 %collective-permute-start.9 = (bf16[4,24,1152]{2,1,0:T(8,128)(2,1)S(1)}, bf16[4,24,1152]{2,1,0:T(8,128)(2,1)S(1)}, u32[]{:S(2)}, u32[]{:S(2)}) collective-permute-start(bf16[4,24,1152]{2,1,0:T(8,128)(2,1)S(1)} %get-tuple-element.75.refs_5_), channel_id=1, source_target_pairs={{0,1},{1,0},{2,3},{3,2},{4,5},{5,4},{6,7},{7,6},{8,9},{9,8},{10,11... | collective-permute-start | bytes 663560 | tf_op jit(solution)/shard_map/ppermute | solution.py:545
  29.0 10.2 %collective-permute-start.8 = (bf16[4,24,1152]{2,1,0:T(8,128)(2,1)S(1)}, bf16[4,24,1152]{2,1,0:T(8,128)(2,1)S(1)}, u32[]{:S(2)}, u32[]{:S(2)}) collective-permute-start(bf16[4,24,1152]{2,1,0:T(8,128)(2,1)S(1)} %get-tuple-element.75.refs_5_), channel_id=1, source_target_pairs={{0,2},{1,3},{2,0},{3,1},{4,6},{5,7},{6,4},{7,5},{8,10},{9,11},{10,... | collective-permute-start | bytes 663560 | tf_op jit(solution)/shard_map/ppermute | solution.py:545
  36.0 15.2 %collective-permute-start.15 = (bf16[4,24,1152]{2,1,0:T(8,128)(2,1)S(1)}, bf16[4,24,1152]{2,1,0:T(8,128)(2,1)}, u32[]{:S(2)}, u32[]{:S(2)}) collective-permute-start(bf16[4,24,1152]{2,1,0:T(8,128)(2,1)S(1)} %get-tuple-element.87.refs_1_), channel_id=1, source_target_pairs={{0,2},{1,3},{2,0},{3,1},{4,6},{5,7},{6,4},{7,5},{8,10},{9,11},{10,... | collective-permute-start | bytes 663560 | tf_op jit(solution)/shard_map/ppermute | solution.py:545
  36.3 15.2 %collective-permute-start.19 = (bf16[4,24,1152]{2,1,0:T(8,128)(2,1)S(1)}, bf16[4,24,1152]{2,1,0:T(8,128)(2,1)}, u32[]{:S(2)}, u32[]{:S(2)}) collective-permute-start(bf16[4,24,1152]{2,1,0:T(8,128)(2,1)S(1)} %get-tuple-element.88.refs_5_), channel_id=1, source_target_pairs={{0,1},{1,0},{2,3},{3,2},{4,5},{5,4},{6,7},{7,6},{8,9},{9,8},{10,11... | collective-permute-start | bytes 663560 | tf_op jit(solution)/shard_map/ppermute | solution.py:545
  36.5 10.6 %collective-permute-start.10 = (bf16[4,24,1152]{2,1,0:T(8,128)(2,1)S(1)}, bf16[4,24,1152]{2,1,0:T(8,128)(2,1)S(1)}, u32[]{:S(2)}, u32[]{:S(2)}) collective-permute-start(bf16[4,24,1152]{2,1,0:T(8,128)(2,1)S(1)} %collective-permute-done.9.refs_7_), channel_id=1, source_target_pairs={{0,2},{1,3},{2,0},{3,1},{4,6},{5,7},{6,4},{7,5},{8,10},{9,11},{10,... | collective-permute-start | bytes 663560 | tf_op jit(solution)/shard_map/ppermute | solution.py:545
  37.8 9.6 %collective-permute-start.7 = (bf16[4,24,1152]{2,1,0:T(8,128)(2,1)S(1)}, bf16[4,24,1152]{2,1,0:T(8,128)(2,1)S(1)}, u32[]{:S(2)}, u32[]{:S(2)}) collective-permute-start(bf16[4,24,1152]{2,1,0:T(8,128)(2,1)S(1)} %collective-permute-done.5.refs_2_.refs_6_), channel_id=1, source_target_pairs={{0,1},{1,0},{2,3},{3,2},{4,5},{5,4},{6,7},{7,6},{8,9},{9,8},{10,11... | collective-permute-start | bytes 663560 | tf_op jit(solution)/shard_map/ppermute | solution.py:545
  39.2 19.8 %collective-permute-start.16 = (bf16[4,24,1152]{2,1,0:T(8,128)(2,1)S(1)}, bf16[4,24,1152]{2,1,0:T(8,128)(2,1)}, u32[]{:S(2)}, u32[]{:S(2)}) collective-permute-start(bf16[4,24,1152]{2,1,0:T(8,128)(2,1)S(1)} %get-tuple-element.87.refs_1_), channel_id=1, source_target_pairs={{0,1},{1,0},{2,3},{3,2},{4,5},{5,4},{6,7},{7,6},{8,9},{9,8},{10,11... | collective-permute-start | bytes 663560 | tf_op jit(solution)/shard_map/ppermute | solution.py:545
  47.1 11.8 %collective-permute-start.18 = (bf16[4,24,1152]{2,1,0:T(8,128)(2,1)S(1)}, bf16[4,24,1152]{2,1,0:T(8,128)(2,1)}, u32[]{:S(2)}, u32[]{:S(2)}) collective-permute-start(bf16[4,24,1152]{2,1,0:T(8,128)(2,1)S(1)} %get-tuple-element.88.refs_5_), channel_id=1, source_target_pairs={{0,2},{1,3},{2,0},{3,1},{4,6},{5,7},{6,4},{7,5},{8,10},{9,11},{10,... | collective-permute-start | bytes 663560 | tf_op jit(solution)/shard_map/ppermute | solution.py:545
  48.2 22.3 %collective-permute-start.11 = (bf16[384,2304]{1,0:T(8,128)(2,1)S(1)}, bf16[384,2304]{1,0:T(8,128)(2,1)}, u32[]{:S(2)}, u32[]{:S(2)}) collective-permute-start(bf16[384,2304]{1,0:T(8,128)(2,1)S(1)} %bitcast.59), channel_id=1, source_target_pairs={{0,16},{16,0},{1,17},{17,1},{2,18},{18,2},{3,19},{19,3},{4,20},{20... | collective-permute-start | bytes 5308424 | tf_op jit(solution)/shard_map/ppermute | solution.py:541
  53.8 15.6 %all-to-all-start = ((f32[32,1,2640]{2,1,0:T(1,128)}), f32[32,1,2640]{2,1,0:T(1,128)}, u32[]{:S(2)}, u32[]{:S(2)}) async-start(f32[32,1,2640]{2,1,0:T(1,128)} %copy.22), calls=%async_computation | async-start | bytes 688128 | tf_op jit(solution)/shard_map/all_to_all | solution.py:778
  61.9 14.4 %collective-permute-start.21 = (bf16[384,2304]{1,0:T(8,128)(2,1)}, bf16[384,2304]{1,0:T(8,128)(2,1)}, u32[]{:S(2)}, u32[]{:S(2)}) collective-permute-start(bf16[384,2304]{1,0:T(8,128)(2,1)} %bitcast.21.refs_5_), channel_id=1, source_target_pairs={{0,16},{16,0},{1,17},{17,1},{2,18},{18,2},{3,19},{19,3},{4,20},{20... | collective-permute-start | bytes 5308424 | tf_op jit(solution)/shard_map/ppermute | solution.py:541
  99.9 16.9 %collective-permute-start.26 = (bf16[4,2,24,1152]{3,2,1,0:T(8,128)(2,1)}, bf16[4,2,24,1152]{3,2,1,0:T(8,128)(2,1)}, u32[]{:S(2)}, u32[]{:S(2)}) collective-permute-start(bf16[4,2,24,1152]{3,2,1,0:T(8,128)(2,1)} %get-tuple-element.102), channel_id=1, source_target_pairs={{0,2},{1,3},{2,0},{3,1},{4,6},{5,7},{6,4},{7,5},{8,10},{9,11},{10,... | collective-permute-start | bytes 1327112 | tf_op jit(solution)/shard_map/ppermute | solution.py:545
  101.0 15.7 %collective-permute-start.27 = (bf16[4,2,24,1152]{3,2,1,0:T(8,128)(2,1)}, bf16[4,2,24,1152]{3,2,1,0:T(8,128)(2,1)}, u32[]{:S(2)}, u32[]{:S(2)}) collective-permute-start(bf16[4,2,24,1152]{3,2,1,0:T(8,128)(2,1)} %get-tuple-element.104), channel_id=1, source_target_pairs={{0,1},{1,0},{2,3},{3,2},{4,5},{5,4},{6,7},{7,6},{8,9},{9,8},{10,11... | collective-permute-start | bytes 1327112 | tf_op jit(solution)/shard_map/ppermute | solution.py:545
  107.6 23.8 %collective-permute-start.24 = (bf16[4,2,24,1152]{3,2,1,0:T(8,128)(2,1)}, bf16[4,2,24,1152]{3,2,1,0:T(8,128)(2,1)S(1)}, u32[]{:S(2)}, u32[]{:S(2)}) collective-permute-start(bf16[4,2,24,1152]{3,2,1,0:T(8,128)(2,1)} %get-tuple-element.98), channel_id=1, source_target_pairs={{0,2},{1,3},{2,0},{3,1},{4,6},{5,7},{6,4},{7,5},{8,10},{9,11},{10,... | collective-permute-start | bytes 1327112 | tf_op jit(solution)/shard_map/ppermute | solution.py:545
  108.5 22.9 %collective-permute-start.25 = (bf16[4,2,24,1152]{3,2,1,0:T(8,128)(2,1)}, bf16[4,2,24,1152]{3,2,1,0:T(8,128)(2,1)S(1)}, u32[]{:S(2)}, u32[]{:S(2)}) collective-permute-start(bf16[4,2,24,1152]{3,2,1,0:T(8,128)(2,1)} %get-tuple-element.100), channel_id=1, source_target_pairs={{0,1},{1,0},{2,3},{3,2},{4,5},{5,4},{6,7},{7,6},{8,9},{9,8},{10,11... | collective-permute-start | bytes 1327112 | tf_op jit(solution)/shard_map/ppermute | solution.py:545
  110.0 25.9 %all-to-all-start.1 = ((f32[32,1,2640]{2,1,0:T(1,128)}), f32[32,1,2640]{2,1,0:T(1,128)}, u32[]{:S(2)}, u32[]{:S(2)}) async-start(f32[32,1,2640]{2,1,0:T(1,128)} %broadcast_in_dim.65), calls=%async_computation.1 | async-start | bytes 688128 | tf_op jit(solution)/shard_map/all_to_all | solution.py:855
  119.1 11.0 %collective-permute-start.28 = (bf16[4,24,1152]{2,1,0:T(8,128)(2,1)S(1)}, bf16[4,24,1152]{2,1,0:T(8,128)(2,1)S(1)}, u32[]{:S(2)}, u32[]{:S(2)}) collective-permute-start(bf16[4,24,1152]{2,1,0:T(8,128)(2,1)S(1)} %get-tuple-element.106), channel_id=1, source_target_pairs={{0,1},{1,0},{2,3},{3,2},{4,5},{5,4},{6,7},{7,6},{8,9},{9,8},{10,11... | collective-permute-start | bytes 663560 | tf_op jit(solution)/shard_map/ppermute | solution.py:545
  120.4 9.7 %collective-permute-start.29 = (bf16[4,24,1152]{2,1,0:T(8,128)(2,1)S(1)}, bf16[4,24,1152]{2,1,0:T(8,128)(2,1)S(1)}, u32[]{:S(2)}, u32[]{:S(2)}) collective-permute-start(bf16[4,24,1152]{2,1,0:T(8,128)(2,1)S(1)} %get-tuple-element.108), channel_id=1, source_target_pairs={{0,2},{1,3},{2,0},{3,1},{4,6},{5,7},{6,4},{7,5},{8,10},{9,11},{10,... | collective-permute-start | bytes 663560 | tf_op jit(solution)/shard_map/ppermute | solution.py:545
  135.5 17.2 %collective-permute-start.30 = (bf16[4,1,128,384]{3,2,1,0:T(8,128)(2,1)}, bf16[4,1,128,384]{3,2,1,0:T(8,128)(2,1)}, u32[]{:S(2)}, u32[]{:S(2)}) collective-permute-start(bf16[4,1,128,384]{3,2,1,0:T(8,128)(2,1)} %get-tuple-element.138), channel_id=1, source_target_pairs={{0,1},{1,0},{2,3},{3,2},{4,5},{5,4},{6,7},{7,6},{8,9},{9,8},{10,11... | collective-permute-start | bytes 1179656 | tf_op jit(solution)/shard_map/ppermute | solution.py:541
  137.9 18.3 %collective-permute-start.33 = (bf16[4,24,1152]{2,1,0:T(8,128)(2,1)}, bf16[4,24,1152]{2,1,0:T(8,128)(2,1)S(1)}, u32[]{:S(2)}, u32[]{:S(2)}) collective-permute-start(bf16[4,24,1152]{2,1,0:T(8,128)(2,1)} %copy-done.24), channel_id=1, source_target_pairs={{0,1},{1,0},{2,3},{3,2},{4,5},{5,4},{6,7},{7,6},{8,9},{9,8},{10,11... | collective-permute-start | bytes 663560 | tf_op jit(solution)/shard_map/ppermute | solution.py:545
  138.4 17.8 %collective-permute-start.34 = (bf16[4,24,1152]{2,1,0:T(8,128)(2,1)}, bf16[4,24,1152]{2,1,0:T(8,128)(2,1)S(1)}, u32[]{:S(2)}, u32[]{:S(2)}) collective-permute-start(bf16[4,24,1152]{2,1,0:T(8,128)(2,1)} %copy-done.23), channel_id=1, source_target_pairs={{0,2},{1,3},{2,0},{3,1},{4,6},{5,7},{6,4},{7,5},{8,10},{9,11},{10,... | collective-permute-start | bytes 663560 | tf_op jit(solution)/shard_map/ppermute | solution.py:545
  139.3 16.9 %collective-permute-start.35 = (bf16[24,2304]{1,0:T(8,128)(2,1)}, bf16[24,2304]{1,0:T(8,128)(2,1)S(1)}, u32[]{:S(2)}, u32[]{:S(2)}) collective-permute-start(bf16[24,2304]{1,0:T(8,128)(2,1)} %copy-done.25), channel_id=1, source_target_pairs={{0,8},{1,9},{2,10},{3,11},{4,12},{5,13},{6,14},{7,15},{8,0},{9,1},... | collective-permute-start | bytes 331784 | tf_op jit(solution)/shard_map/ppermute | solution.py:545
  142.7 13.5 %collective-permute-start.36 = (bf16[24,2304]{1,0:T(8,128)(2,1)S(1)}, bf16[24,2304]{1,0:T(8,128)(2,1)S(1)}, u32[]{:S(2)}, u32[]{:S(2)}) collective-permute-start(bf16[24,2304]{1,0:T(8,128)(2,1)S(1)} %get-tuple-element.122), channel_id=1, source_target_pairs={{0,12},{1,13},{2,14},{3,15},{4,0},{5,1},{6,2},{7,3},{8,4},{9,5},{1... | collective-permute-start | bytes 331784 | tf_op jit(solution)/shard_map/ppermute | solution.py:545
  144.8 17.6 %all-to-all-start.2 = ((f32[32,1,768]{2,1,0:T(1,128)}), f32[32,1,768]{2,1,0:T(1,128)S(1)}, u32[]{:S(2)}, u32[]{:S(2)}) async-start(f32[32,1,768]{2,1,0:T(1,128)} %broadcast_in_dim.67), calls=%async_computation.2 | async-start | bytes 196608 | tf_op jit(solution)/shard_map/all_to_all | solution.py:864
  155.2 18.2 %collective-permute-start.31 = (bf16[2,2,128,384]{3,2,1,0:T(8,128)(2,1)}, bf16[2,2,128,384]{3,2,1,0:T(8,128)(2,1)}, u32[]{:S(2)}, u32[]{:S(2)}) collective-permute-start(bf16[2,2,128,384]{3,2,1,0:T(8,128)(2,1)} %get-tuple-element.136), channel_id=1, source_target_pairs={{0,16},{16,0},{1,17},{17,1},{2,18},{18,2},{3,19},{19,3},{4,20},{20... | collective-permute-start | bytes 1179656 | tf_op jit(solution)/shard_map/ppermute | solution.py:541
  158.1 9.4 %collective-permute-start.38 = (bf16[24,2304]{1,0:T(8,128)(2,1)S(1)}, bf16[24,2304]{1,0:T(8,128)(2,1)S(1)}, u32[]{:S(2)}, u32[]{:S(2)}) collective-permute-start(bf16[24,2304]{1,0:T(8,128)(2,1)S(1)} %get-tuple-element.125), channel_id=1, source_target_pairs={{0,8},{1,9},{2,10},{3,11},{4,12},{5,13},{6,14},{7,15},{8,0},{9,1},... | collective-permute-start | bytes 331784 | tf_op jit(solution)/shard_map/ppermute | solution.py:545
  159.2 10.6 %collective-permute-start.39 = (bf16[24,2304]{1,0:T(8,128)(2,1)S(1)}, bf16[24,2304]{1,0:T(8,128)(2,1)S(1)}, u32[]{:S(2)}, u32[]{:S(2)}) collective-permute-start(bf16[24,2304]{1,0:T(8,128)(2,1)S(1)} %get-tuple-element.126), channel_id=1, source_target_pairs={{0,12},{1,13},{2,14},{3,15},{4,0},{5,1},{6,2},{7,3},{8,4},{9,5},{1... | collective-permute-start | bytes 331784 | tf_op jit(solution)/shard_map/ppermute | solution.py:545
  (51 other events, 437.7 us)
